TPU v7x, 256 devices: a whole 4x4x8 slice. The times are simulated.
256 devices in a mesh: fsdp: 64 (over y_hi, x, z), tp: 4 (over y_lo, core).
Axes of the slice: x: 4, y: 4 (y_hi: 2, y_lo: 2; y = y_hi * 2 + y_lo), z: 8, core: 2. Of those that a mesh axis runs over, the one named last changes fastest.
Arguments:
- tokens: bfloat16 [8192, 8192], P('fsdp', 'tp'), may hold values from -32 to 32
- gain: bfloat16 [8192], P('tp'), may hold values from 0.25 to 1.75
- w_query: bfloat16 [8192, 512], P('fsdp', 'tp'), may hold values from -0.055242717 to 0.055242717
- w_key: bfloat16 [8192, 128], P('fsdp'), may hold values from -1.2153398 to 1.2153398
- w_value: bfloat16 [8192, 128], P('fsdp'), may hold values from -0.0625 to 0.0625
- w_out: bfloat16 [512, 8192], P('tp', 'fsdp'), may hold values from -0.0625 to 0.0625
- cotangent: bfloat16 [8192, 8192], P('fsdp', 'tp'), may hold values from -6 to 6
Outputs:
- grad_input: float32 [8192, 8192], P('fsdp', 'tp')
- grad_gain: float32 [8192], P('tp')
- grad_query: float32 [8192, 512], P('fsdp', 'tp')
- grad_key: float32 [8192, 128], P('fsdp')
- grad_value: float32 [8192, 128], P('fsdp')
- grad_out: float32 [512, 8192], P('tp', 'fsdp')
All inputs are finite; a program needn't handle non-finite values.
Results may differ from a plain program's by a relative error of at most 0.024.
Values may be sent and summed in bfloat16 or wider, within the bound.
No kernel may reach another device: no remote copies, remote signals or barrier semaphores. Data moves between devices by JAX's collectives and lax.ppermute only.
A program may use at most 128 MiB of HBM per device.

v0:
```python
import functools
import math

import jax
import jax.numpy as jnp
from jax import lax
from jax.experimental import pallas as pl
from jax.experimental.pallas import tpu as pltpu
from jax.sharding import Mesh, PartitionSpec as P

HD = 128
NX = 4
NZ = 8
AXES = ("yh", "x", "z", "yl", "c")
FSDP = ("yh", "x", "z")
TP = ("yl", "c")
F32 = jnp.float32
BF16 = jnp.bfloat16
PIECE = 32
BLOCK = 2 * HD + 2 * PIECE
GROWS = 16
VMEM = pl.BlockSpec(memory_space=pltpu.VMEM)
SMEM = pl.BlockSpec(memory_space=pltpu.SMEM)


def flat(yh, x, z, yl, c):
    return (((yh * NX + x) * NZ + z) * 2 + yl) * 2 + c


def owner_perm(flip):
    pairs = []
    for yh in range(2):
        for x in range(NX):
            for z in range(NZ):
                for yl in range(2):
                    for c in range(2):
                        dest_x = (x % 2) * 2 + z // 4
                        dest_z = c * 4 + z % 4
                        pairs.append((flat(yh, x, z, yl, c), flat(yl ^ flip, dest_x, dest_z, yh, x // 2)))
    return pairs


def inverse(pairs):
    return [(d, s) for s, d in pairs]


def shift_x(value, by):
    return lax.ppermute(value, "x", [(i, (i + by) % NX) for i in range(NX)])


def shift_z(value, by):
    return lax.ppermute(value, "z", [(i, (i + by) % NZ) for i in range(NZ)])


def swap(value, axis):
    return lax.ppermute(value, axis, [(0, 1), (1, 0)])


def dot(a, b, ca, cb):
    return lax.dot_general(a, b, (((ca,), (cb,)), ((), ())), preferred_element_type=F32)


def lanes(start, size=HD):
    return pl.ds(pl.multiple_of(start, HD), size)


def call(body, outs, scratch, ids, *args, static=None):
    body = body if static is None else functools.partial(body, static)
    return pl.pallas_call(
        body,
        out_shape=[jax.ShapeDtypeStruct(s, d) for s, d in outs],
        in_specs=[SMEM] + [VMEM] * len(args),
        out_specs=[VMEM] * len(outs),
        scratch_shapes=[pltpu.VMEM(s, d) for s, d in scratch],
        compiler_params=pltpu.CompilerParams(vmem_limit_bytes=16 * 2**20),
    )(ids, *args)


def spread_kernel(ids, tokens, cot, *outs):
    x = ids[4]
    rows = tokens.shape[0]
    squares = jnp.zeros((rows, HD), F32)
    for at in range(0, tokens.shape[1], HD):
        value = tokens[:, at : at + HD].astype(F32)
        squares = squares + value * value
    total = jnp.sum(jnp.transpose(squares), axis=0, keepdims=True)
    high = total.astype(BF16).astype(F32)
    middle = (total - high).astype(BF16).astype(F32)
    extra = jnp.concatenate([high, middle, total - high - middle, jnp.zeros((GROWS - 3, HD), F32)], axis=0)
    for s in range(NX):
        block = lanes(((x + s) % NX) * 4 * HD, 4 * HD)
        outs[s][:rows] = tokens[:, block]
        outs[s][rows : 2 * rows] = cot[:, block]
        outs[s][2 * rows :, :HD] = extra.astype(BF16)
        outs[s][2 * rows :, HD:] = jnp.zeros((GROWS, 3 * HD), BF16)


def squares_kernel(ids, a, b, c, d, out):
    for s, ref in enumerate((a, b, c, d)):
        terms = ref[2 * HD :, :HD].astype(F32)
        out[s : s + 1] = (terms[2:3] + terms[1:2]) + terms[0:1]


def normalize_kernel(width, ids, *refs):
    parts, (totals, gain, unit, normed, cot) = refs[:4], refs[4:]
    for s in range(NX):
        rows = slice(s * HD, (s + 1) * HD)
        column = jnp.transpose(jnp.broadcast_to(totals[s : s + 1], (HD, HD)))
        inv = lax.rsqrt(column / width + 1e-05)
        for j in range(4):
            cols = slice(j * HD, (j + 1) * HD)
            value = parts[s][:HD, cols].astype(F32) * inv
            unit[rows, cols] = value
            normed[rows, cols] = (value * gain[:, cols]).astype(BF16)
        cot[rows] = parts[s][HD : 2 * HD]


def forward_pack_kernel(ids, both, prev, after, up, down, far_first, far_second):
    for out, ref in ((up, prev), (down, after)):
        out[: 2 * BLOCK] = both[...]
        out[2 * BLOCK :] = ref[...]
    far_first[...] = prev[:BLOCK]
    far_second[...] = after[BLOCK:]


def product(out, side, normed, cot, w_all, w_out):
    w_q = w_all[:, lanes(side * 2 * HD, 2 * HD)]
    w_kv = w_all[:, lanes((4 + side) * HD)]
    w_o = w_out[side]
    for r in range(0, 512, 256):
        rows = slice(r, r + 256)
        out[rows, : 2 * HD] = dot(normed[rows], w_q, 1, 0)
        out[rows, 2 * HD : 4 * HD] = dot(cot[rows], w_o, 1, 1)
        out[rows, 4 * HD :] = dot(normed[rows], w_kv, 1, 0)


def theirs_kernel(ids, both, prev1, next1, prev2, next2, far_first, far_second, normed, cot, out, w_all, w_out):
    z, c = ids[0], ids[2]

    def place(ref, base, d, half):
        zt = (z + d + NZ) % NZ
        side, j = zt // 4, zt % 4
        rows = pl.ds(pl.multiple_of(j * HD, HD), HD)
        w_all[rows, lanes(side * 2 * HD + half * HD)] = ref[base : base + HD]
        w_out[side, half * HD : (half + 1) * HD, lanes(j * HD)] = ref[base + HD : base + 2 * HD]
        part = pl.ds(pl.multiple_of(j * HD + (2 * half + side) * PIECE, PIECE), PIECE)
        w_all[part, 4 * HD : 5 * HD] = ref[base + 2 * HD : base + 2 * HD + PIECE]
        w_all[part, 5 * HD : 6 * HD] = ref[base + 2 * HD + PIECE : base + BLOCK]

    for ref, base, d in (
        (both, 0, 0),
        (prev1, 0, -1),
        (prev1, 2 * BLOCK, -3),
        (next1, 0, 1),
        (next1, 2 * BLOCK, 3),
        (prev2, 0, -2),
        (next2, 0, 2),
    ):
        place(ref, base, d, 0)
        place(ref, base + BLOCK, d, 1)
    place(far_first, 0, 4, 0)
    place(far_second, 0, 4, 1)
    product(out, 1 - c, normed, cot, w_all, w_out)


def mine_kernel(ids, normed, cot, w_all, w_out, out):
    product(out, ids[2], normed, cot, w_all, w_out)


def split_store(ref, total):
    for start, size, at in ((0, 2 * HD, 0), (4 * HD, HD, 6 * HD)):
        value = total[:, start : start + size]
        high = value.astype(BF16)
        ref[:, at : at + size] = high
        ref[:, at + size : at + 2 * size] = (value - high.astype(F32)).astype(BF16)
    ref[:, 4 * HD : 6 * HD] = total[:, 2 * HD : 4 * HD].astype(BF16)


def joined(ref):
    value = ref[...].astype(F32)
    return jnp.concatenate(
        [
            value[:, : 2 * HD] + value[:, 2 * HD : 4 * HD],
            value[:, 4 * HD : 6 * HD],
            value[:, 6 * HD : 7 * HD] + value[:, 7 * HD :],
        ],
        axis=1,
    )


def chunk_kernel(ids, mine, got, own, *outs):
    own[...] = mine[:HD] + got[:HD]
    for s in range(1, NX):
        rows = slice(s * HD, (s + 1) * HD)
        split_store(outs[s - 1], mine[rows] + got[rows])


def sum_kernel(ids, own, a, b, c, out):
    split_store(out, own[...] + joined(a) + joined(b) + joined(c))


def final_kernel(ids, mine, got, qa, kv):
    total = (joined(mine) + joined(got)).astype(BF16)
    qa[...] = total[:, : 4 * HD]
    kv[...] = total[:, 4 * HD :]


def attend_kernel(ids, qa, kv_mine, kv_theirs, out):
    first = ids[2] == 0
    mine, theirs = kv_mine[...].astype(F32), kv_theirs[...].astype(F32)
    key_rows = jnp.where(first, mine, theirs).astype(BF16)
    value_rows = jnp.where(first, theirs, mine).astype(BF16)
    causal = lax.broadcasted_iota(jnp.int32, (HD, HD), 0) >= lax.broadcasted_iota(jnp.int32, (HD, HD), 1)
    keys = jnp.zeros((HD, HD), F32)
    values = jnp.zeros((HD, HD), F32)
    for h in range(2):
        query = qa[:, h * HD : (h + 1) * HD]
        attn_grad = qa[:, (2 + h) * HD : (3 + h) * HD]
        scores = dot(query, key_rows, 1, 1) * HD ** (-0.5)
        scores = jnp.where(causal, scores, jnp.float32(-1e30))
        shifted = jnp.exp(scores - jnp.max(scores, axis=-1, keepdims=True))
        softmax_out = shifted / jnp.sum(shifted, axis=-1, keepdims=True)
        rounded = softmax_out.astype(BF16)
        dprob = dot(attn_grad, value_rows, 1, 1)
        dscore = softmax_out * (dprob - jnp.sum(dprob * softmax_out, axis=-1, keepdims=True)) * HD ** (-0.5)
        dscore = dscore.astype(BF16)
        out[:, h * HD : (h + 1) * HD] = dot(dscore, key_rows, 1, 0).astype(BF16)
        out[:, (2 + h) * HD : (3 + h) * HD] = dot(rounded, value_rows, 1, 0).astype(BF16)
        keys = keys + dot(dscore, query, 0, 0).astype(BF16).astype(F32)
        values = values + dot(rounded, attn_grad, 0, 0).astype(BF16).astype(F32)
    out[:, 4 * HD : 5 * HD] = keys.astype(BF16)
    out[:, 5 * HD :] = values.astype(BF16)


def gradient_kernel(ids, *refs):
    mine, theirs, (normed, cot, unit, w_all) = refs[:4], refs[4:8], refs[8:12]
    (t0, up, down, t2, m2, t4a, t4b), back = refs[12:19], refs[19:23]
    heads, attended, shared = refs[23:]
    z, c = ids[0], ids[2]
    for s in range(NX):
        rows = slice(s * HD, (s + 1) * HD)
        for ref, side in ((mine[s], c), (theirs[s], 1 - c)):
            heads[rows, lanes(side * 2 * HD, 2 * HD)] = ref[:, : 2 * HD]
            attended[rows, lanes(side * 2 * HD, 2 * HD)] = ref[:, 2 * HD : 4 * HD]
        total = mine[s][:, 4 * HD :].astype(F32) + theirs[s][:, 4 * HD :].astype(F32)
        heads[rows, 4 * HD :] = total.astype(BF16)

    gain_sum = jnp.zeros((1, 4 * HD), F32)
    for s in range(NX):
        rows = slice(s * HD, (s + 1) * HD)
        term = dot(heads[rows], w_all[...], 1, 1)
        back[s][...] = term.astype(BF16)
        gain_sum = gain_sum + jnp.sum(term * unit[rows], axis=0, keepdims=True)
    gain_rows = jnp.concatenate([gain_sum[:, j * HD : (j + 1) * HD] for j in range(4)], axis=0)
    high = gain_rows.astype(BF16).astype(F32)
    gain_rows = jnp.concatenate([high, gain_rows - high, jnp.zeros((8, HD), F32)], axis=0).astype(BF16)

    shared[...] = dot(normed[...], heads[:, 4 * HD :], 0, 0)
    g, n = GROWS, BLOCK
    for ref in (t0, up, down, t4a, t4b):
        ref[:g] = gain_rows
    for d, out_first, out_second in (
        (0, t0.at[g : g + n], t0.at[g + n :]),
        (1, up.at[g : g + n], up.at[g + n : g + 2 * n]),
        (3, up.at[g + 2 * n : g + 3 * n], up.at[g + 3 * n :]),
        (-1, down.at[g : g + n], down.at[g + n : g + 2 * n]),
        (-3, down.at[g + 2 * n : g + 3 * n], down.at[g + 3 * n :]),
        (2, t2.at[:n], t2.at[n:]),
        (-2, m2.at[:n], m2.at[n:]),
        (4, t4a.at[g:], t4b.at[g:]),
    ):
        zt = (z + d + NZ) % NZ
        side, j = zt // 4, zt % 4
        g_q = dot(normed[:, lanes(j * HD)], heads[:, lanes(side * 2 * HD, 2 * HD)], 0, 0).astype(BF16)
        g_o = dot(attended[:, lanes(side * 2 * HD, 2 * HD)], cot[:, lanes(j * HD)], 0, 0).astype(BF16)
        for half, out in enumerate((out_first, out_second)):
            out[:HD] = g_q[:, half * HD : (half + 1) * HD]
            out[HD : 2 * HD] = g_o[half * HD : (half + 1) * HD]
            part = shared[pl.ds(pl.multiple_of(j * HD + (2 * half + side) * PIECE, PIECE), PIECE), :].astype(BF16)
            out[2 * HD : 2 * HD + PIECE] = part[:, :HD]
            out[2 * HD + PIECE :] = part[:, HD:]


def relay_kernel(ids, t2, m2, a, b, c, d, up, down):
    g, n = GROWS, BLOCK
    up[:g] = a[:g]
    up[g : 2 * g] = c[:g]
    down[:g] = b[:g]
    down[g : 2 * g] = d[:g]
    total = t2[...].astype(F32) + a[g + 2 * n :].astype(F32)
    up[2 * g : 2 * g + n] = (total[:n] + c[g:].astype(F32)).astype(BF16)
    up[2 * g + n :] = total[n:].astype(BF16)
    total = m2[...].astype(F32) + b[g + 2 * n :].astype(F32)
    down[2 * g : 2 * g + n] = total[:n].astype(BF16)
    down[2 * g + n :] = (total[n:] + d[g:].astype(F32)).astype(BF16)


def finish_kernel(ids, t0, a, b, up, down, c, d, same, other, gain_out):
    g, n = GROWS, BLOCK
    flip = ids[3]
    near = slice(g, g + 2 * n)
    total = t0[near].astype(F32) + a[near].astype(F32) + b[near].astype(F32)
    total = total + up[2 * g :].astype(F32) + down[2 * g :].astype(F32)
    same[...] = jnp.where(flip == 0, total[:n], total[n:]).astype(BF16)
    other[...] = jnp.where(flip == 0, total[n:], total[:n]).astype(BF16)
    rows = up[g : 2 * g].astype(F32)
    for ref in (t0, a, b, c, d, up, down):
        rows = rows + ref[:g].astype(F32)
    gain_out[...] = rows[:4] + rows[4:8]


def gain_kernel(scale, ids, own, s1, s2, s3, out):
    for s, ref in enumerate((own, s1, s2, s3)):
        out[(ids[4] - s + NX) % NX] = ref[...] * scale


def row_kernel(width, ids, a, b, c, d, tokens, gain, totals, summed, row_sum):
    column = jnp.transpose(jnp.broadcast_to(totals[0:1], (HD, HD)))
    inv = lax.rsqrt(column / width + 1e-05)
    acc = jnp.zeros((HD, HD), F32)
    for s, ref in enumerate((a, b, c, d)):
        at = (ids[4] + s) % NX
        for j in range(4):
            cols = lanes(at * 4 * HD + j * HD)
            value = ref[:, j * HD : (j + 1) * HD]
            summed[:, cols] = value
            acc = acc + (value.astype(F32) * gain[:, cols]) * (tokens[:, cols].astype(F32) * inv)
    row_sum[...] = jnp.sum(jnp.transpose(acc), axis=0, keepdims=True)


def input_kernel(width, ids, summed, tokens, gain, totals, row_own, row_got, out):
    column = jnp.transpose(jnp.broadcast_to(totals[0:1], (HD, HD)))
    inv = lax.rsqrt(column / width + 1e-05)
    row_mean = jnp.transpose(jnp.broadcast_to(row_own[...] + row_got[...], (HD, HD))) / width
    for at in range(0, summed.shape[1], HD):
        cols = slice(at, at + HD)
        unit = tokens[:, cols].astype(F32) * inv
        out[:, cols] = inv * (summed[:, cols].astype(F32) * gain[:, cols] - unit * row_mean)


def owner_kernel(scale, ids, a, b, grad_query, grad_out, shared):
    total = a[...].astype(F32) + b[...].astype(F32)
    grad_query[...] = total[:HD] * scale
    grad_out[...] = total[HD : 2 * HD] * scale
    shared[...] = total[2 * HD :].astype(BF16)


def shared_kernel(scale, ids, own, by_c, by_yl, by_both, grad_key, grad_value):
    yl, c = ids[1], ids[2]
    for ref, at in ((own, 2 * yl + c), (by_c, 2 * yl + 1 - c), (by_yl, 2 - 2 * yl + c), (by_both, 3 - 2 * yl - c)):
        rows = pl.ds(pl.multiple_of(at * PIECE, PIECE), PIECE)
        grad_key[rows] = ref[:PIECE].astype(F32) * scale
        grad_value[rows] = ref[PIECE:].astype(F32) * scale


def local(tokens, gain, w_query, w_key, w_value, w_out, cotangent):
    rows, quarter = tokens.shape
    sub = quarter // NX
    width = quarter * 4
    yh, x, z, yl, c = (lax.axis_index(a) for a in AXES)
    ids = jnp.stack([z, yl, c, yh, x]).astype(jnp.int32)
    head = yl * 2 + c
    loss_scale = 1.0 / math.sqrt(rows * 64)

    pack = jnp.concatenate(
        [
            w_query,
            w_out,
            lax.dynamic_slice_in_dim(w_key, head * PIECE, PIECE, 0),
            lax.dynamic_slice_in_dim(w_value, head * PIECE, PIECE, 0),
        ],
        axis=0,
    )
    same = lax.ppermute(pack, AXES, owner_perm(0))
    other = lax.ppermute(pack, AXES, owner_perm(1))
    part_shape = ((2 * rows + GROWS, sub), BF16)
    parts = call(spread_kernel, [part_shape] * 4, [], ids, tokens, cotangent)
    same, other, *parts = lax.optimization_barrier((same, other, *parts))
    both = jnp.where(yh == 0, jnp.concatenate([same, other]), jnp.concatenate([other, same]))
    prev2, next2 = shift_z(both, 2), shift_z(both, -2)
    double, half_shape = ((4 * BLOCK, HD), BF16), ((BLOCK, HD), BF16)
    relays = call(forward_pack_kernel, [double] * 2 + [half_shape] * 2, [], ids, both, prev2, next2)
    prev1, next1 = shift_z(relays[0], 1), shift_z(relays[1], -1)
    far_first, far_second = shift_z(relays[2], 2), shift_z(relays[3], -2)
    weights = (both, prev1, next1, prev2, next2, far_first, far_second)

    parts = [parts[0]] + [shift_x(parts[s], s) for s in range(1, NX)]
    (totals,) = call(squares_kernel, [((NX, HD), F32)], [], ids, *parts)
    totals, *_ = lax.optimization_barrier((totals, relays[0]))
    totals = totals + swap(totals, "c")
    totals = totals + swap(totals, "yl")
    gain_f = gain.astype(F32)
    gain_sub = lax.dynamic_slice_in_dim(gain_f, x * sub, sub, 0).reshape(1, sub)
    unit_sw, normed_sw, cot_sw = call(
        normalize_kernel,
        [((512, sub), F32), ((512, sub), BF16), ((512, sub), BF16)],
        [],
        ids,
        *parts,
        totals,
        gain_sub,
        static=width,
    )

    theirs, w_all, w_heads = call(
        theirs_kernel,
        [((512, 5 * HD), F32), ((sub, 6 * HD), BF16), ((2, 2 * HD, sub), BF16)],
        [],
        ids,
        *weights,
        normed_sw,
        cot_sw,
    )
    (mine,) = call(mine_kernel, [((512, 5 * HD), F32)], [], ids, normed_sw, cot_sw, w_all, w_heads)
    split = ((rows, 8 * HD), BF16)
    own, *chunks = call(chunk_kernel, [((rows, 5 * HD), F32)] + [split] * 3, [], ids, mine, swap(theirs, "c"))
    chunks = [shift_x(chunks[s - 1], -s) for s in range(1, NX)]
    (partial,) = call(sum_kernel, [split], [], ids, own, *chunks)
    qa, kv = call(final_kernel, [((rows, 4 * HD), BF16), ((rows, HD), BF16)], [], ids, partial, swap(partial, "yl"))
    (heads,) = call(attend_kernel, [((rows, 6 * HD), BF16)], [], ids, qa, kv, swap(kv, "c"))
    heads = [heads] + [shift_x(heads, s) for s in range(1, NX)]

    g, n = GROWS, BLOCK
    t0, up, down, t2, m2, t4a, t4b, *back = call(
        gradient_kernel,
        [
            ((g + 2 * n, HD), BF16),
            ((g + 4 * n, HD), BF16),
            ((g + 4 * n, HD), BF16),
            ((2 * n, HD), BF16),
            ((2 * n, HD), BF16),
            ((g + n, HD), BF16),
            ((g + n, HD), BF16),
        ]
        + [((rows, sub), BF16)] * 4,
        [((512, 6 * HD), BF16), ((512, 4 * HD), BF16), ((sub, 2 * HD), F32)],
        ids,
        *heads,
        *[swap(h, "c") for h in heads],
        normed_sw,
        cot_sw,
        unit_sw,
        w_all,
    )
    c4, d4 = shift_z(t4a, 2), shift_z(t4b, -2)
    a, b = shift_z(up, 1), shift_z(down, -1)
    up, down = call(relay_kernel, [((2 * g + 2 * n, HD), BF16)] * 2, [], ids, t2, m2, a, b, c4, d4)
    *back, _ = lax.optimization_barrier((*back, swap(up[:g], "c")))
    up, down = shift_z(up, 2), shift_z(down, -2)
    to_same, to_other, gain_z = call(
        finish_kernel, [((n, HD), BF16)] * 2 + [((4, HD), F32)], [], ids, t0, a, b, up, down, c4, d4
    )
    gain_z, _ = lax.optimization_barrier((gain_z, swap(to_same[:g], "c")))
    arrived = (lax.ppermute(to_same, AXES, inverse(owner_perm(0))), lax.ppermute(to_other, AXES, inverse(owner_perm(1))))
    *sums, shared_own = call(
        owner_kernel,
        [((HD, HD), F32)] * 2 + [((2 * PIECE, HD), BF16)],
        [],
        ids,
        *arrived,
        static=loss_scale,
    )
    grad_query, grad_out = sums
    both_flip = lax.ppermute(shared_own, TP, [(i, 3 - i) for i in range(4)])
    grad_key, grad_value = call(
        shared_kernel,
        [((rows, HD), F32)] * 2,
        [],
        ids,
        shared_own,
        swap(shared_own, "c"),
        swap(shared_own, "yl"),
        both_flip,
        static=loss_scale,
    )

    gain_z = gain_z + swap(gain_z, "yh")
    (grad_gain,) = call(
        gain_kernel,
        [((NX, 4, HD), F32)],
        [],
        ids,
        gain_z,
        *[shift_x(gain_z, s) for s in range(1, NX)],
        static=loss_scale,
    )
    grad_gain = grad_gain.reshape(quarter)

    pieces = [back[0]] + [shift_x(back[s], -s) for s in range(1, NX)]
    gain_f = gain_f.reshape(1, quarter)
    summed, row_sum = call(
        row_kernel,
        [((rows, quarter), BF16), ((1, rows), F32)],
        [],
        ids,
        *pieces,
        tokens,
        gain_f,
        totals,
        static=width,
    )
    row_sum = row_sum + swap(row_sum, "c")
    (grad_input,) = call(
        input_kernel,
        [((rows, quarter), F32)],
        [],
        ids,
        summed,
        tokens,
        gain_f,
        totals,
        row_sum,
        swap(row_sum, "yl"),
        static=width,
    )
    return (grad_input, grad_gain, grad_query, grad_key, grad_value, grad_out)


def solution(mesh):
    fine = Mesh(mesh.devices.reshape(2, NX, NZ, 2, 2), AXES)
    in_specs = (P(FSDP, TP), P(TP), P(FSDP, TP), P(FSDP, None), P(FSDP, None), P(TP, FSDP), P(FSDP, TP))
    out_specs = (P(FSDP, TP), P(TP), P(FSDP, TP), P(FSDP, None), P(FSDP, None), P(TP, FSDP))
    return jax.shard_map(local, mesh=fine, in_specs=in_specs, out_specs=out_specs, check_vma=False)
```

profile of v0, /device:TPU:8, one launch (start us, length us, event | category | flops | bytes accessed | tf_op | source)
XLA Modules:
  0.0 166.1 jit_solution(3835888385913060321)
XLA Ops:
  2.1 3.5 %collective-permute-start = (bf16[320,128]{1,0:T(8,128)(2,1)S(1)}, bf16[320,128]{1,0:T(8,128)(2,1)S(1)}, u32[]{:S(2)}, u32[]{:S(2)}) collective-permute-start(bf16[320,128]{1,0:T(8,128)(2,1)S(1)} %pad_maximum_fusion), channel_id=1, source_target_pairs={{0,0},{1,16},{2,128},{3,144},{4,4},{5,20},{6,132},{7,148},{8,8},{9... | collective-permute-start | bytes 245768 | tf_op jit(solution)/shard_map/ppermute | solution.py:374
  8.6 3.0 %collective-permute-done.1 = bf16[320,128]{1,0:T(8,128)(2,1)S(1)} collective-permute-done((bf16[320,128]{1,0:T(8,128)(2,1)S(1)}, bf16[320,128]{1,0:T(8,128)(2,1)S(1)}, u32[]{:S(2)}, u32[]{:S(2)}) %collective-permute-start.1) | collective-permute-done | bytes 81952 | tf_op jit(solution)/shard_map/ppermute | solution.py:375
  11.7 3.3 %collective-permute-start.5 = (bf16[640,128]{1,0:T(8,128)(2,1)S(1)}, bf16[640,128]{1,0:T(8,128)(2,1)S(1)}, u32[]{:S(2)}, u32[]{:S(2)}) collective-permute-start(bf16[640,128]{1,0:T(8,128)(2,1)S(1)} %maximum_select_fusion.both), channel_id=1, source_target_pairs={{0,8},{4,12},{8,16},{12,20},{16,24},{20,28},{24,0},{28,4},{1,9},{5... | collective-permute-start | bytes 491528 | tf_op jit(solution)/shard_map/ppermute | solution.py:52
  15.0 8.6 %collective-permute-start.6 = (bf16[640,128]{1,0:T(8,128)(2,1)S(1)}, bf16[640,128]{1,0:T(8,128)(2,1)S(1)}, u32[]{:S(2)}, u32[]{:S(2)}) collective-permute-start(bf16[640,128]{1,0:T(8,128)(2,1)S(1)} %maximum_select_fusion.both), channel_id=1, source_target_pairs={{0,24},{4,28},{8,0},{12,4},{16,8},{20,12},{24,16},{28,20},{1,25},{... | collective-permute-start | bytes 491528 | tf_op jit(solution)/shard_map/ppermute | solution.py:52
  24.0 3.0 %collective-permute-start.3 = (bf16[272,512]{1,0:T(8,128)(2,1)S(1)}, bf16[272,512]{1,0:T(8,128)(2,1)S(1)}, u32[]{:S(2)}, u32[]{:S(2)}) collective-permute-start(bf16[272,512]{1,0:T(8,128)(2,1)S(1)} %get-tuple-element.66), channel_id=1, source_target_pairs={{0,64},{32,96},{64,0},{96,32},{1,65},{33,97},{65,1},{97,33},{2,66}... | collective-permute-start | bytes 835592 | tf_op jit(solution)/shard_map/ppermute | solution.py:48
  27.8 4.3 %collective-permute-done.6.after.next2 = bf16[640,128]{1,0:T(8,128)(2,1)S(1)} collective-permute-done((bf16[640,128]{1,0:T(8,128)(2,1)S(1)}, bf16[640,128]{1,0:T(8,128)(2,1)S(1)}, u32[]{:S(2)}, u32[]{:S(2)}) %collective-permute-start.6) | collective-permute-done | bytes 163872 | tf_op jit(solution)/shard_map/ppermute | solution.py:52
  32.7 4.0 %collective-permute-start.10 = (bf16[1280,128]{1,0:T(8,128)(2,1)S(1)}, bf16[1280,128]{1,0:T(8,128)(2,1)S(1)}, u32[]{:S(2)}, u32[]{:S(2)}) collective-permute-start(bf16[1280,128]{1,0:T(8,128)(2,1)S(1)} %get-tuple-element.74), channel_id=1, source_target_pairs={{0,28},{4,0},{8,4},{12,8},{16,12},{20,16},{24,20},{28,24},{1,29},{... | collective-permute-start | bytes 983048 | tf_op jit(solution)/shard_map/ppermute | solution.py:52
  36.7 3.0 %collective-permute-start.4 = (bf16[272,512]{1,0:T(8,128)(2,1)S(1)}, bf16[272,512]{1,0:T(8,128)(2,1)S(1)}, u32[]{:S(2)}, u32[]{:S(2)}) collective-permute-start(bf16[272,512]{1,0:T(8,128)(2,1)S(1)} %get-tuple-element.67), channel_id=1, source_target_pairs={{0,96},{32,0},{64,32},{96,64},{1,97},{33,1},{65,33},{97,65},{2,98}... | collective-permute-start | bytes 835592 | tf_op jit(solution)/shard_map/ppermute | solution.py:48
  39.8 4.0 %collective-permute-start.12 = (bf16[320,128]{1,0:T(8,128)(2,1)S(1)}, bf16[320,128]{1,0:T(8,128)(2,1)S(1)}, u32[]{:S(2)}, u32[]{:S(2)}) collective-permute-start(bf16[320,128]{1,0:T(8,128)(2,1)S(1)} %get-tuple-element.76), channel_id=1, source_target_pairs={{0,24},{4,28},{8,0},{12,4},{16,8},{20,12},{24,16},{28,20},{1,25},{... | collective-permute-start | bytes 245768 | tf_op jit(solution)/shard_map/ppermute | solution.py:52
  43.8 1.8 %collective-permute-done.4.d.refs_3_ = bf16[272,512]{1,0:T(8,128)(2,1)S(1)} collective-permute-done((bf16[272,512]{1,0:T(8,128)(2,1)S(1)}, bf16[272,512]{1,0:T(8,128)(2,1)S(1)}, u32[]{:S(2)}, u32[]{:S(2)}) %collective-permute-start.4) | collective-permute-done | bytes 278560 | tf_op jit(solution)/shard_map/ppermute | solution.py:48
  47.6 3.5 %collective-permute-done.8 = f32[4,128]{1,0:T(4,128)S(1)} collective-permute-done((f32[4,128]{1,0:T(4,128)S(1)}, f32[4,128]{1,0:T(4,128)S(1)}, u32[]{:S(2)}, u32[]{:S(2)}) %collective-permute-start.8) | collective-permute-done | bytes 2080 | tf_op jit(solution)/shard_map/ppermute | solution.py:56
  54.6 1.9 %collective-permute-done.13.got = f32[512,640]{1,0:T(8,128)S(1)} collective-permute-done((f32[512,640]{1,0:T(8,128)S(1)}, f32[512,640]{1,0:T(8,128)S(1)}, u32[]{:S(2)}, u32[]{:S(2)}) %collective-permute-start.13) | collective-permute-done | bytes 1310752 | tf_op jit(solution)/shard_map/ppermute | solution.py:56
  57.2 3.9 %collective-permute-start.14 = (bf16[128,1024]{1,0:T(8,128)(2,1)S(1)}, bf16[128,1024]{1,0:T(8,128)(2,1)S(1)}, u32[]{:S(2)}, u32[]{:S(2)}) collective-permute-start(bf16[128,1024]{1,0:T(8,128)(2,1)S(1)} %get-tuple-element.81), channel_id=1, source_target_pairs={{0,96},{32,0},{64,32},{96,64},{1,97},{33,1},{65,33},{97,65},{2,98}... | collective-permute-start | bytes 786440 | tf_op jit(solution)/shard_map/ppermute | solution.py:48
  62.1 10.5 %collective-permute-done.14.a = bf16[128,1024]{1,0:T(8,128)(2,1)S(1)} collective-permute-done((bf16[128,1024]{1,0:T(8,128)(2,1)S(1)}, bf16[128,1024]{1,0:T(8,128)(2,1)S(1)}, u32[]{:S(2)}, u32[]{:S(2)}) %collective-permute-start.14) | collective-permute-done | bytes 262176 | tf_op jit(solution)/shard_map/ppermute | solution.py:48
  72.6 3.4 %collective-permute-done.16.c = bf16[128,1024]{1,0:T(8,128)(2,1)S(1)} collective-permute-done((bf16[128,1024]{1,0:T(8,128)(2,1)S(1)}, bf16[128,1024]{1,0:T(8,128)(2,1)S(1)}, u32[]{:S(2)}, u32[]{:S(2)}) %collective-permute-start.16) | collective-permute-done | bytes 262176 | tf_op jit(solution)/shard_map/ppermute | solution.py:48
  76.8 7.9 %collective-permute-done.17.got = bf16[128,1024]{1,0:T(8,128)(2,1)S(1)} collective-permute-done((bf16[128,1024]{1,0:T(8,128)(2,1)S(1)}, bf16[128,1024]{1,0:T(8,128)(2,1)S(1)}, u32[]{:S(2)}, u32[]{:S(2)}) %collective-permute-start.17) | collective-permute-done | bytes 262176 | tf_op jit(solution)/shard_map/ppermute | solution.py:56
  90.0 1.8 %collective-permute-start.21 = (bf16[128,768]{1,0:T(8,128)(2,1)S(1)}, bf16[128,768]{1,0:T(8,128)(2,1)S(1)}, u32[]{:S(2)}, u32[]{:S(2)}) collective-permute-start(bf16[128,768]{1,0:T(8,128)(2,1)S(1)} %shard_map.127.refs_0_), channel_id=1, source_target_pairs={{0,96},{32,0},{64,32},{96,64},{1,97},{33,1},{65,33},{97,65},{2,98}... | collective-permute-start | bytes 589832 | tf_op jit(solution)/shard_map/ppermute | solution.py:48
  91.8 8.9 %collective-permute-done.19.refs_1_ = bf16[128,768]{1,0:T(8,128)(2,1)S(1)} collective-permute-done((bf16[128,768]{1,0:T(8,128)(2,1)S(1)}, bf16[128,768]{1,0:T(8,128)(2,1)S(1)}, u32[]{:S(2)}, u32[]{:S(2)}) %collective-permute-start.19) | collective-permute-done | bytes 196640 | tf_op jit(solution)/shard_map/ppermute | solution.py:48
  102.8 2.8 %shard_map.128 = (bf16[656,128]{1,0:T(8,128)(2,1)S(1)}, bf16[1296,128]{1,0:T(8,128)(2,1)S(1)}, bf16[1296,128]{1,0:T(8,128)(2,1)S(1)}, bf16[640,128]{1,0:T(8,128)...) custom-call(s32[5]{0:T(128)S(1)} %stack.23.ids, ...), custom_call_target="tpu_custom_call" | custom-call | tf_op jit(solution)/shard_map/pallas_call | solution.py:69
  105.9 3.0 %collective-permute-start.32 = (bf16[1296,128]{1,0:T(8,128)(2,1)S(1)}, bf16[1296,128]{1,0:T(8,128)(2,1)S(1)}, u32[]{:S(2)}, u32[]{:S(2)}) collective-permute-start(bf16[1296,128]{1,0:T(8,128)(2,1)S(1)} %get-tuple-element.99), channel_id=1, source_target_pairs={{0,28},{4,0},{8,4},{12,8},{16,12},{20,16},{24,20},{28,24},{1,29},{... | collective-permute-start | bytes 995336 | tf_op jit(solution)/shard_map/ppermute | solution.py:52
  108.8 4.1 %collective-permute-start.34 = (bf16[336,128]{1,0:T(8,128)(2,1)S(1)}, bf16[336,128]{1,0:T(8,128)(2,1)S(1)}, u32[]{:S(2)}, u32[]{:S(2)}) collective-permute-start(bf16[336,128]{1,0:T(8,128)(2,1)S(1)} %get-tuple-element.103), channel_id=1, source_target_pairs={{0,24},{4,28},{8,0},{12,4},{16,8},{20,12},{24,16},{28,20},{1,25},{... | collective-permute-start | bytes 258056 | tf_op jit(solution)/shard_map/ppermute | solution.py:52
  113.0 8.6 %collective-permute-done.33.c = bf16[336,128]{1,0:T(8,128)(2,1)S(1)} collective-permute-done((bf16[336,128]{1,0:T(8,128)(2,1)S(1)}, bf16[336,128]{1,0:T(8,128)(2,1)S(1)}, u32[]{:S(2)}, u32[]{:S(2)}) %collective-permute-start.33) | collective-permute-done | bytes 86048 | tf_op jit(solution)/shard_map/ppermute | solution.py:52
  122.8 3.7 %collective-permute-start.36 = (bf16[672,128]{1,0:T(8,128)(2,1)S(1)}, bf16[672,128]{1,0:T(8,128)(2,1)S(1)}, u32[]{:S(2)}, u32[]{:S(2)}) collective-permute-start(bf16[672,128]{1,0:T(8,128)(2,1)S(1)} %get-tuple-element.105), channel_id=1, source_target_pairs={{0,24},{4,28},{8,0},{12,4},{16,8},{20,12},{24,16},{28,20},{1,25},{... | collective-permute-start | bytes 516104 | tf_op jit(solution)/shard_map/ppermute | solution.py:52
  126.4 2.3 %collective-permute-start.26 = (bf16[128,512]{1,0:T(8,128)(2,1)S(1)}, bf16[128,512]{1,0:T(8,128)(2,1)S(1)}, u32[]{:S(2)}, u32[]{:S(2)}) collective-permute-start(bf16[128,512]{1,0:T(8,128)(2,1)S(1)} %get-tuple-element.92), channel_id=1, source_target_pairs={{0,96},{32,0},{64,32},{96,64},{1,97},{33,1},{65,33},{97,65},{2,98}... | collective-permute-start | bytes 393224 | tf_op jit(solution)/shard_map/ppermute | solution.py:48
  129.6 2.5 %collective-permute-done.35.up = bf16[672,128]{1,0:T(8,128)(2,1)S(1)} collective-permute-done((bf16[672,128]{1,0:T(8,128)(2,1)S(1)}, bf16[672,128]{1,0:T(8,128)(2,1)S(1)}, u32[]{:S(2)}, u32[]{:S(2)}) %collective-permute-start.35) | collective-permute-done | bytes 172064 | tf_op jit(solution)/shard_map/ppermute | solution.py:52
  132.8 2.1 %collective-permute-start.41 = (bf16[320,128]{1,0:T(8,128)(2,1)S(1)}, bf16[320,128]{1,0:T(8,128)(2,1)S(1)}, u32[]{:S(2)}, u32[]{:S(2)}) collective-permute-start(bf16[320,128]{1,0:T(8,128)(2,1)S(1)} %get-tuple-element.107), channel_id=1, source_target_pairs={{0,0},{16,1},{128,2},{144,3},{4,4},{20,5},{132,6},{148,7},{8,8},{2... | collective-permute-start | bytes 245768 | tf_op jit(solution)/shard_map/ppermute | solution.py:454
  135.0 4.2 %collective-permute-done.41.a = bf16[320,128]{1,0:T(8,128)(2,1)S(1)} collective-permute-done((bf16[320,128]{1,0:T(8,128)(2,1)S(1)}, bf16[320,128]{1,0:T(8,128)(2,1)S(1)}, u32[]{:S(2)}, u32[]{:S(2)}) %collective-permute-start.41) | collective-permute-done | bytes 81952 | tf_op jit(solution)/shard_map/ppermute | solution.py:454
  140.6 4.7 %collective-permute-start.43 = (bf16[64,128]{1,0:T(8,128)(2,1)S(1)}, bf16[64,128]{1,0:T(8,128)(2,1)S(1)}, u32[]{:S(2)}, u32[]{:S(2)}) collective-permute-start(bf16[64,128]{1,0:T(8,128)(2,1)S(1)} %get-tuple-element.110.own), channel_id=1, source_target_pairs={{0,1},{1,0},{2,3},{3,2},{4,5},{5,4},{6,7},{7,6},{8,9},{9,8},{10,11... | collective-permute-start | bytes 49160 | tf_op jit(solution)/shard_map/ppermute | solution.py:56
  145.3 2.2 %collective-permute-start.44 = (bf16[64,128]{1,0:T(8,128)(2,1)S(1)}, bf16[64,128]{1,0:T(8,128)(2,1)S(1)}, u32[]{:S(2)}, u32[]{:S(2)}) collective-permute-start(bf16[64,128]{1,0:T(8,128)(2,1)S(1)} %get-tuple-element.110.own), channel_id=1, source_target_pairs={{0,2},{2,0},{1,3},{3,1},{4,6},{6,4},{5,7},{7,5},{8,10},{10,8},{9,1... | collective-permute-start | bytes 49160 | tf_op jit(solution)/shard_map/ppermute | solution.py:56
  147.5 3.8 %collective-permute-start.38 = (f32[4,128]{1,0:T(4,128)S(1)}, f32[4,128]{1,0:T(4,128)S(1)}, u32[]{:S(2)}, u32[]{:S(2)}) collective-permute-start(f32[4,128]{1,0:T(4,128)S(1)} %add.28.own), channel_id=1, source_target_pairs={{0,32},{32,64},{64,96},{96,0},{1,33},{33,65},{65,97},{97,1},{2,34}... | collective-permute-start | bytes 6152 | tf_op jit(solution)/shard_map/ppermute | solution.py:48
  155.1 2.1 %collective-permute-done.30.row_got = f32[1,128]{1,0:T(1,128)S(1)} collective-permute-done((f32[1,128]{1,0:T(1,128)S(1)}, f32[1,128]{1,0:T(1,128)S(1)}, u32[]{:S(2)}, u32[]{:S(2)}) %collective-permute-start.30) | collective-permute-done | bytes 544 | tf_op jit(solution)/shard_map/ppermute | solution.py:56
  157.1 3.0 %collective-permute-start.39 = (f32[4,128]{1,0:T(4,128)S(1)}, f32[4,128]{1,0:T(4,128)S(1)}, u32[]{:S(2)}, u32[]{:S(2)}) collective-permute-start(f32[4,128]{1,0:T(4,128)S(1)} %add.28.own), channel_id=1, source_target_pairs={{0,64},{32,96},{64,0},{96,32},{1,65},{33,97},{65,1},{97,33},{2,66}... | collective-permute-start | bytes 6152 | tf_op jit(solution)/shard_map/ppermute | solution.py:48
  (96 shorter events, 35.8 us)
Async XLA Ops:
  2.1 6.5 %collective-permute-start = (bf16[320,128]{1,0:T(8,128)(2,1)S(1)}, bf16[320,128]{1,0:T(8,128)(2,1)S(1)}, u32[]{:S(2)}, u32[]{:S(2)}) collective-permute-start(bf16[320,128]{1,0:T(8,128)(2,1)S(1)} %pad_maximum_fusion), channel_id=1, source_target_pairs={{0,0},{1,16},{2,128},{3,144},{4,4},{5,20},{6,132},{7,148},{8,8},{9... | collective-permute-start | bytes 245768 | tf_op jit(solution)/shard_map/ppermute | solution.py:374
  11.7 16.1 %collective-permute-start.5 = (bf16[640,128]{1,0:T(8,128)(2,1)S(1)}, bf16[640,128]{1,0:T(8,128)(2,1)S(1)}, u32[]{:S(2)}, u32[]{:S(2)}) collective-permute-start(bf16[640,128]{1,0:T(8,128)(2,1)S(1)} %maximum_select_fusion.both), channel_id=1, source_target_pairs={{0,8},{4,12},{8,16},{12,20},{16,24},{20,28},{24,0},{28,4},{1,9},{5... | collective-permute-start | bytes 491528 | tf_op jit(solution)/shard_map/ppermute | solution.py:52
  15.0 17.0 %collective-permute-start.6 = (bf16[640,128]{1,0:T(8,128)(2,1)S(1)}, bf16[640,128]{1,0:T(8,128)(2,1)S(1)}, u32[]{:S(2)}, u32[]{:S(2)}) collective-permute-start(bf16[640,128]{1,0:T(8,128)(2,1)S(1)} %maximum_select_fusion.both), channel_id=1, source_target_pairs={{0,24},{4,28},{8,0},{12,4},{16,8},{20,12},{24,16},{28,20},{1,25},{... | collective-permute-start | bytes 491528 | tf_op jit(solution)/shard_map/ppermute | solution.py:52
  23.6 16.1 %collective-permute-start.2 = (bf16[272,512]{1,0:T(8,128)(2,1)S(1)}, bf16[272,512]{1,0:T(8,128)(2,1)S(1)}, u32[]{:S(2)}, u32[]{:S(2)}) collective-permute-start(bf16[272,512]{1,0:T(8,128)(2,1)S(1)} %get-tuple-element.65), channel_id=1, source_target_pairs={{0,32},{32,64},{64,96},{96,0},{1,33},{33,65},{65,97},{97,1},{2,34}... | collective-permute-start | bytes 835592 | tf_op jit(solution)/shard_map/ppermute | solution.py:48
  24.0 15.8 %collective-permute-start.3 = (bf16[272,512]{1,0:T(8,128)(2,1)S(1)}, bf16[272,512]{1,0:T(8,128)(2,1)S(1)}, u32[]{:S(2)}, u32[]{:S(2)}) collective-permute-start(bf16[272,512]{1,0:T(8,128)(2,1)S(1)} %get-tuple-element.66), channel_id=1, source_target_pairs={{0,64},{32,96},{64,0},{96,32},{1,65},{33,97},{65,1},{97,33},{2,66}... | collective-permute-start | bytes 835592 | tf_op jit(solution)/shard_map/ppermute | solution.py:48
  32.7 19.2 %collective-permute-start.10 = (bf16[1280,128]{1,0:T(8,128)(2,1)S(1)}, bf16[1280,128]{1,0:T(8,128)(2,1)S(1)}, u32[]{:S(2)}, u32[]{:S(2)}) collective-permute-start(bf16[1280,128]{1,0:T(8,128)(2,1)S(1)} %get-tuple-element.74), channel_id=1, source_target_pairs={{0,28},{4,0},{8,4},{12,8},{16,12},{20,16},{24,20},{28,24},{1,29},{... | collective-permute-start | bytes 983048 | tf_op jit(solution)/shard_map/ppermute | solution.py:52
  36.7 15.2 %collective-permute-start.9 = (bf16[1280,128]{1,0:T(8,128)(2,1)S(1)}, bf16[1280,128]{1,0:T(8,128)(2,1)S(1)}, u32[]{:S(2)}, u32[]{:S(2)}) collective-permute-start(bf16[1280,128]{1,0:T(8,128)(2,1)S(1)} %get-tuple-element.70), channel_id=1, source_target_pairs={{0,4},{4,8},{8,12},{12,16},{16,20},{20,24},{24,28},{28,0},{1,5},{5... | collective-permute-start | bytes 983048 | tf_op jit(solution)/shard_map/ppermute | solution.py:52
  36.7 9.0 %collective-permute-start.4 = (bf16[272,512]{1,0:T(8,128)(2,1)S(1)}, bf16[272,512]{1,0:T(8,128)(2,1)S(1)}, u32[]{:S(2)}, u32[]{:S(2)}) collective-permute-start(bf16[272,512]{1,0:T(8,128)(2,1)S(1)} %get-tuple-element.67), channel_id=1, source_target_pairs={{0,96},{32,0},{64,32},{96,64},{1,97},{33,1},{65,33},{97,65},{2,98}... | collective-permute-start | bytes 835592 | tf_op jit(solution)/shard_map/ppermute | solution.py:48
  39.7 12.2 %collective-permute-start.11 = (bf16[320,128]{1,0:T(8,128)(2,1)S(1)}, bf16[320,128]{1,0:T(8,128)(2,1)S(1)}, u32[]{:S(2)}, u32[]{:S(2)}) collective-permute-start(bf16[320,128]{1,0:T(8,128)(2,1)S(1)} %get-tuple-element.75), channel_id=1, source_target_pairs={{0,8},{4,12},{8,16},{12,20},{16,24},{20,28},{24,0},{28,4},{1,9},{5... | collective-permute-start | bytes 245768 | tf_op jit(solution)/shard_map/ppermute | solution.py:52
  39.8 12.0 %collective-permute-start.12 = (bf16[320,128]{1,0:T(8,128)(2,1)S(1)}, bf16[320,128]{1,0:T(8,128)(2,1)S(1)}, u32[]{:S(2)}, u32[]{:S(2)}) collective-permute-start(bf16[320,128]{1,0:T(8,128)(2,1)S(1)} %get-tuple-element.76), channel_id=1, source_target_pairs={{0,24},{4,28},{8,0},{12,4},{16,8},{20,12},{24,16},{28,20},{1,25},{... | collective-permute-start | bytes 245768 | tf_op jit(solution)/shard_map/ppermute | solution.py:52
  57.2 15.4 %collective-permute-start.14 = (bf16[128,1024]{1,0:T(8,128)(2,1)S(1)}, bf16[128,1024]{1,0:T(8,128)(2,1)S(1)}, u32[]{:S(2)}, u32[]{:S(2)}) collective-permute-start(bf16[128,1024]{1,0:T(8,128)(2,1)S(1)} %get-tuple-element.81), channel_id=1, source_target_pairs={{0,96},{32,0},{64,32},{96,64},{1,97},{33,1},{65,33},{97,65},{2,98}... | collective-permute-start | bytes 786440 | tf_op jit(solution)/shard_map/ppermute | solution.py:48
  61.1 11.5 %collective-permute-start.15 = (bf16[128,1024]{1,0:T(8,128)(2,1)S(1)}, bf16[128,1024]{1,0:T(8,128)(2,1)S(1)}, u32[]{:S(2)}, u32[]{:S(2)}) collective-permute-start(bf16[128,1024]{1,0:T(8,128)(2,1)S(1)} %get-tuple-element.82), channel_id=1, source_target_pairs={{0,64},{32,96},{64,0},{96,32},{1,65},{33,97},{65,1},{97,33},{2,66}... | collective-permute-start | bytes 786440 | tf_op jit(solution)/shard_map/ppermute | solution.py:48
  61.1 14.9 %collective-permute-start.16 = (bf16[128,1024]{1,0:T(8,128)(2,1)S(1)}, bf16[128,1024]{1,0:T(8,128)(2,1)S(1)}, u32[]{:S(2)}, u32[]{:S(2)}) collective-permute-start(bf16[128,1024]{1,0:T(8,128)(2,1)S(1)} %get-tuple-element.83), channel_id=1, source_target_pairs={{0,32},{32,64},{64,96},{96,0},{1,33},{33,65},{65,97},{97,1},{2,34}... | collective-permute-start | bytes 786440 | tf_op jit(solution)/shard_map/ppermute | solution.py:48
  76.7 8.0 %collective-permute-start.17 = (bf16[128,1024]{1,0:T(8,128)(2,1)S(1)}, bf16[128,1024]{1,0:T(8,128)(2,1)S(1)}, u32[]{:S(2)}, u32[]{:S(2)}) collective-permute-start(bf16[128,1024]{1,0:T(8,128)(2,1)S(1)} %shard_map.125.mine), channel_id=1, source_target_pairs={{0,2},{2,0},{1,3},{3,1},{4,6},{6,4},{5,7},{7,5},{8,10},{10,8},{9,1... | collective-permute-start | bytes 786440 | tf_op jit(solution)/shard_map/ppermute | solution.py:56
  88.2 12.5 %collective-permute-start.19 = (bf16[128,768]{1,0:T(8,128)(2,1)S(1)}, bf16[128,768]{1,0:T(8,128)(2,1)S(1)}, u32[]{:S(2)}, u32[]{:S(2)}) collective-permute-start(bf16[128,768]{1,0:T(8,128)(2,1)S(1)} %shard_map.127.refs_0_), channel_id=1, source_target_pairs={{0,32},{32,64},{64,96},{96,0},{1,33},{33,65},{65,97},{97,1},{2,34}... | collective-permute-start | bytes 589832 | tf_op jit(solution)/shard_map/ppermute | solution.py:48
  88.3 12.4 %collective-permute-start.20 = (bf16[128,768]{1,0:T(8,128)(2,1)S(1)}, bf16[128,768]{1,0:T(8,128)(2,1)S(1)}, u32[]{:S(2)}, u32[]{:S(2)}) collective-permute-start(bf16[128,768]{1,0:T(8,128)(2,1)S(1)} %shard_map.127.refs_0_), channel_id=1, source_target_pairs={{0,64},{32,96},{64,0},{96,32},{1,65},{33,97},{65,1},{97,33},{2,66}... | collective-permute-start | bytes 589832 | tf_op jit(solution)/shard_map/ppermute | solution.py:48
  90.0 11.3 %collective-permute-start.21 = (bf16[128,768]{1,0:T(8,128)(2,1)S(1)}, bf16[128,768]{1,0:T(8,128)(2,1)S(1)}, u32[]{:S(2)}, u32[]{:S(2)}) collective-permute-start(bf16[128,768]{1,0:T(8,128)(2,1)S(1)} %shard_map.127.refs_0_), channel_id=1, source_target_pairs={{0,96},{32,0},{64,32},{96,64},{1,97},{33,1},{65,33},{97,65},{2,98}... | collective-permute-start | bytes 589832 | tf_op jit(solution)/shard_map/ppermute | solution.py:48
  91.8 9.5 %collective-permute-start.22 = (bf16[128,768]{1,0:T(8,128)(2,1)S(1)}, bf16[128,768]{1,0:T(8,128)(2,1)S(1)}, u32[]{:S(2)}, u32[]{:S(2)}) collective-permute-start(bf16[128,768]{1,0:T(8,128)(2,1)S(1)} %shard_map.127.refs_0_), channel_id=1, source_target_pairs={{0,1},{1,0},{2,3},{3,2},{4,5},{5,4},{6,7},{7,6},{8,9},{9,8},{10,11... | collective-permute-start | bytes 589832 | tf_op jit(solution)/shard_map/ppermute | solution.py:56
  105.5 16.0 %collective-permute-start.31 = (bf16[1296,128]{1,0:T(8,128)(2,1)S(1)}, bf16[1296,128]{1,0:T(8,128)(2,1)S(1)}, u32[]{:S(2)}, u32[]{:S(2)}) collective-permute-start(bf16[1296,128]{1,0:T(8,128)(2,1)S(1)} %get-tuple-element.98), channel_id=1, source_target_pairs={{0,4},{4,8},{8,12},{12,16},{16,20},{20,24},{24,28},{28,0},{1,5},{5... | collective-permute-start | bytes 995336 | tf_op jit(solution)/shard_map/ppermute | solution.py:52
  105.9 15.7 %collective-permute-start.32 = (bf16[1296,128]{1,0:T(8,128)(2,1)S(1)}, bf16[1296,128]{1,0:T(8,128)(2,1)S(1)}, u32[]{:S(2)}, u32[]{:S(2)}) collective-permute-start(bf16[1296,128]{1,0:T(8,128)(2,1)S(1)} %get-tuple-element.99), channel_id=1, source_target_pairs={{0,28},{4,0},{8,4},{12,8},{16,12},{20,16},{24,20},{28,24},{1,29},{... | collective-permute-start | bytes 995336 | tf_op jit(solution)/shard_map/ppermute | solution.py:52
  108.8 12.7 %collective-permute-start.33 = (bf16[336,128]{1,0:T(8,128)(2,1)S(1)}, bf16[336,128]{1,0:T(8,128)(2,1)S(1)}, u32[]{:S(2)}, u32[]{:S(2)}) collective-permute-start(bf16[336,128]{1,0:T(8,128)(2,1)S(1)} %get-tuple-element.102), channel_id=1, source_target_pairs={{0,8},{4,12},{8,16},{12,20},{16,24},{20,28},{24,0},{28,4},{1,9},{5... | collective-permute-start | bytes 258056 | tf_op jit(solution)/shard_map/ppermute | solution.py:52
  108.8 12.7 %collective-permute-start.34 = (bf16[336,128]{1,0:T(8,128)(2,1)S(1)}, bf16[336,128]{1,0:T(8,128)(2,1)S(1)}, u32[]{:S(2)}, u32[]{:S(2)}) collective-permute-start(bf16[336,128]{1,0:T(8,128)(2,1)S(1)} %get-tuple-element.103), channel_id=1, source_target_pairs={{0,24},{4,28},{8,0},{12,4},{16,8},{20,12},{24,16},{28,20},{1,25},{... | collective-permute-start | bytes 258056 | tf_op jit(solution)/shard_map/ppermute | solution.py:52
  122.2 9.9 %collective-permute-start.35 = (bf16[672,128]{1,0:T(8,128)(2,1)S(1)}, bf16[672,128]{1,0:T(8,128)(2,1)S(1)}, u32[]{:S(2)}, u32[]{:S(2)}) collective-permute-start(bf16[672,128]{1,0:T(8,128)(2,1)S(1)} %get-tuple-element.104), channel_id=1, source_target_pairs={{0,8},{4,12},{8,16},{12,20},{16,24},{20,28},{24,0},{28,4},{1,9},{5... | collective-permute-start | bytes 516104 | tf_op jit(solution)/shard_map/ppermute | solution.py:52
  122.8 9.4 %collective-permute-start.36 = (bf16[672,128]{1,0:T(8,128)(2,1)S(1)}, bf16[672,128]{1,0:T(8,128)(2,1)S(1)}, u32[]{:S(2)}, u32[]{:S(2)}) collective-permute-start(bf16[672,128]{1,0:T(8,128)(2,1)S(1)} %get-tuple-element.105), channel_id=1, source_target_pairs={{0,24},{4,28},{8,0},{12,4},{16,8},{20,12},{24,16},{28,20},{1,25},{... | collective-permute-start | bytes 516104 | tf_op jit(solution)/shard_map/ppermute | solution.py:52
  126.4 18.8 %collective-permute-start.26 = (bf16[128,512]{1,0:T(8,128)(2,1)S(1)}, bf16[128,512]{1,0:T(8,128)(2,1)S(1)}, u32[]{:S(2)}, u32[]{:S(2)}) collective-permute-start(bf16[128,512]{1,0:T(8,128)(2,1)S(1)} %get-tuple-element.92), channel_id=1, source_target_pairs={{0,96},{32,0},{64,32},{96,64},{1,97},{33,1},{65,33},{97,65},{2,98}... | collective-permute-start | bytes 393224 | tf_op jit(solution)/shard_map/ppermute | solution.py:48
  128.7 18.8 %collective-permute-start.27 = (bf16[128,512]{1,0:T(8,128)(2,1)S(1)}, bf16[128,512]{1,0:T(8,128)(2,1)S(1)}, u32[]{:S(2)}, u32[]{:S(2)}) collective-permute-start(bf16[128,512]{1,0:T(8,128)(2,1)S(1)} %get-tuple-element.93), channel_id=1, source_target_pairs={{0,64},{32,96},{64,0},{96,32},{1,65},{33,97},{65,1},{97,33},{2,66}... | collective-permute-start | bytes 393224 | tf_op jit(solution)/shard_map/ppermute | solution.py:48
  128.7 22.6 %collective-permute-start.28 = (bf16[128,512]{1,0:T(8,128)(2,1)S(1)}, bf16[128,512]{1,0:T(8,128)(2,1)S(1)}, u32[]{:S(2)}, u32[]{:S(2)}) collective-permute-start(bf16[128,512]{1,0:T(8,128)(2,1)S(1)} %get-tuple-element.94), channel_id=1, source_target_pairs={{0,32},{32,64},{64,96},{96,0},{1,33},{33,65},{65,97},{97,1},{2,34}... | collective-permute-start | bytes 393224 | tf_op jit(solution)/shard_map/ppermute | solution.py:48
  139.1 8.4 %collective-permute-start.37 = (f32[4,128]{1,0:T(4,128)S(1)}, f32[4,128]{1,0:T(4,128)S(1)}, u32[]{:S(2)}, u32[]{:S(2)}) collective-permute-start(f32[4,128]{1,0:T(4,128)S(1)} %get-tuple-element.106), channel_id=1, source_target_pairs={{0,128},{128,0},{1,129},{129,1},{2,130},{130,2},{3,131},{131,3},{4... | collective-permute-start | bytes 6152 | tf_op jit(solution)/shard_map/ppermute | solution.py:56
  140.6 24.3 %collective-permute-start.43 = (bf16[64,128]{1,0:T(8,128)(2,1)S(1)}, bf16[64,128]{1,0:T(8,128)(2,1)S(1)}, u32[]{:S(2)}, u32[]{:S(2)}) collective-permute-start(bf16[64,128]{1,0:T(8,128)(2,1)S(1)} %get-tuple-element.110.own), channel_id=1, source_target_pairs={{0,1},{1,0},{2,3},{3,2},{4,5},{5,4},{6,7},{7,6},{8,9},{9,8},{10,11... | collective-permute-start | bytes 49160 | tf_op jit(solution)/shard_map/ppermute | solution.py:56
  145.3 19.6 %collective-permute-start.44 = (bf16[64,128]{1,0:T(8,128)(2,1)S(1)}, bf16[64,128]{1,0:T(8,128)(2,1)S(1)}, u32[]{:S(2)}, u32[]{:S(2)}) collective-permute-start(bf16[64,128]{1,0:T(8,128)(2,1)S(1)} %get-tuple-element.110.own), channel_id=1, source_target_pairs={{0,2},{2,0},{1,3},{3,1},{4,6},{6,4},{5,7},{7,5},{8,10},{10,8},{9,1... | collective-permute-start | bytes 49160 | tf_op jit(solution)/shard_map/ppermute | solution.py:56
  147.5 17.4 %collective-permute-start.45 = (bf16[64,128]{1,0:T(8,128)(2,1)S(1)}, bf16[64,128]{1,0:T(8,128)(2,1)S(1)}, u32[]{:S(2)}, u32[]{:S(2)}) collective-permute-start(bf16[64,128]{1,0:T(8,128)(2,1)S(1)} %get-tuple-element.110.own), channel_id=1, source_target_pairs={{0,3},{1,2},{2,1},{3,0},{4,7},{5,6},{6,5},{7,4},{8,11},{9,10},{10,... | collective-permute-start | bytes 49160 | tf_op jit(solution)/shard_map/ppermute | solution.py:464
  147.5 12.6 %collective-permute-start.38 = (f32[4,128]{1,0:T(4,128)S(1)}, f32[4,128]{1,0:T(4,128)S(1)}, u32[]{:S(2)}, u32[]{:S(2)}) collective-permute-start(f32[4,128]{1,0:T(4,128)S(1)} %add.28.own), channel_id=1, source_target_pairs={{0,32},{32,64},{64,96},{96,0},{1,33},{33,65},{65,97},{97,1},{2,34}... | collective-permute-start | bytes 6152 | tf_op jit(solution)/shard_map/ppermute | solution.py:48
  (18 other events, 116.0 us)
where the time goes:
time: 168 us; the launch traced here: 166 us
  starting transfers between devices  72.3 us (43%)
  waiting for transfers between devices  69.7 us (41%)
  Pallas kernels  19.3 us (11%)
  local copies, waits for them, and re-layouts  2.98 us (2%)
    ppermute x12, starting transfers between devices, shift_z(): return lax.ppermute(value, 'z', [(i, (i + by) % NZ) for i in range(NZ)])  31.7 us
    ppermute x15, waiting for transfers between devices, shift_x(): return lax.ppermute(value, 'x', [(i, (i + by) % NX) for i in range(NX)])  25.9 us
    ppermute x15, starting transfers between devices, shift_x(): return lax.ppermute(value, 'x', [(i, (i + by) % NX) for i in range(NX)])  25.6 us
    ppermute x14, waiting for transfers between devices, swap(): return lax.ppermute(value, axis, [(0, 1), (1, 0)])  20.3 us
    pallas_call x18, Pallas kernels, call(): pl.pallas_call(body, out_shape=[jax.ShapeDtypeStruct(s, d) for s, d in ou...  19.3 us
    ppermute x12, waiting for transfers between devices, shift_z(): return lax.ppermute(value, 'z', [(i, (i + by) % NZ) for i in range(NZ)])  16.1 us
    ppermute x14, starting transfers between devices, swap(): return lax.ppermute(value, axis, [(0, 1), (1, 0)])  9.34 us
    ppermute x1, waiting for transfers between devices, local(): lax.ppermute(to_same, AXES, inverse(owner_perm(0)))  4.16 us
  transfers between devices with their start and end apart: 46, of which 23 were waited for; matrix products, arithmetic and copies ran while one was open for 0% of the time, Pallas kernels for 6%

commit v1 on v0

--- a/solution.py
+++ b/solution.py
@@ -34,8 +34,8 @@
             for z in range(NZ):
                 for yl in range(2):
                     for c in range(2):
-                        dest_x = (x % 2) * 2 + z // 4
-                        dest_z = c * 4 + z % 4
+                        dest_x = (x % 2) * 2 + z % 2
+                        dest_z = (z // 2) * 2 + c
                         pairs.append((flat(yh, x, z, yl, c), flat(yl ^ flip, dest_x, dest_z, yh, x // 2)))
     return pairs
 
@@ -62,6 +62,10 @@
 
 def lanes(start, size=HD):
     return pl.ds(pl.multiple_of(start, HD), size)
+
+
+def feature(at, j):
+    return ((at // 2) * 8 + 2 * j + at % 2) * HD
 
 
 def call(body, outs, scratch, ids, *args, static=None):
@@ -76,42 +80,42 @@
     )(ids, *args)
 
 
-def spread_kernel(ids, tokens, cot, *outs):
-    x = ids[4]
-    rows = tokens.shape[0]
-    squares = jnp.zeros((rows, HD), F32)
+def squares_kernel(ids, tokens, out):
+    squares = jnp.zeros((tokens.shape[0], HD), F32)
     for at in range(0, tokens.shape[1], HD):
         value = tokens[:, at : at + HD].astype(F32)
         squares = squares + value * value
-    total = jnp.sum(jnp.transpose(squares), axis=0, keepdims=True)
+    out[...] = jnp.sum(jnp.transpose(squares), axis=0, keepdims=True)
+
+
+def spread_kernel(ids, tokens, cot, total, *outs):
+    rows = tokens.shape[0]
+    total = total[...]
     high = total.astype(BF16).astype(F32)
     middle = (total - high).astype(BF16).astype(F32)
     extra = jnp.concatenate([high, middle, total - high - middle, jnp.zeros((GROWS - 3, HD), F32)], axis=0)
     for s in range(NX):
-        block = lanes(((x + s) % NX) * 4 * HD, 4 * HD)
-        outs[s][:rows] = tokens[:, block]
-        outs[s][rows : 2 * rows] = cot[:, block]
-        outs[s][2 * rows :, :HD] = extra.astype(BF16)
-        outs[s][2 * rows :, HD:] = jnp.zeros((GROWS, 3 * HD), BF16)
-
-
-def squares_kernel(ids, a, b, c, d, out):
-    for s, ref in enumerate((a, b, c, d)):
-        terms = ref[2 * HD :, :HD].astype(F32)
-        out[s : s + 1] = (terms[2:3] + terms[1:2]) + terms[0:1]
+        at = (ids[4] + s) % NX
+        for j in range(4):
+            block, cols = lanes(feature(at, j)), slice(j * HD, (j + 1) * HD)
+            outs[s][:rows, cols] = tokens[:, block]
+            outs[s][rows : 2 * rows, cols] = cot[:, block]
+            outs[s][2 * rows :, cols] = extra.astype(BF16)
 
 
 def normalize_kernel(width, ids, *refs):
-    parts, (totals, gain, unit, normed, cot) = refs[:4], refs[4:]
+    parts, (gain, unit, normed, cot) = refs[:4], refs[4:]
     for s in range(NX):
         rows = slice(s * HD, (s + 1) * HD)
-        column = jnp.transpose(jnp.broadcast_to(totals[s : s + 1], (HD, HD)))
+        terms = parts[s][2 * HD :, :HD].astype(F32)
+        total = (terms[2:3] + terms[1:2]) + terms[0:1]
+        column = jnp.transpose(jnp.broadcast_to(total, (HD, HD)))
         inv = lax.rsqrt(column / width + 1e-05)
         for j in range(4):
             cols = slice(j * HD, (j + 1) * HD)
             value = parts[s][:HD, cols].astype(F32) * inv
             unit[rows, cols] = value
-            normed[rows, cols] = (value * gain[:, cols]).astype(BF16)
+            normed[rows, cols] = (value * gain[:, lanes(feature(ids[4], j))]).astype(BF16)
         cot[rows] = parts[s][HD : 2 * HD]
 
 
@@ -139,7 +143,7 @@
 
     def place(ref, base, d, half):
         zt = (z + d + NZ) % NZ
-        side, j = zt // 4, zt % 4
+        side, j = zt % 2, zt // 2
         rows = pl.ds(pl.multiple_of(j * HD, HD), HD)
         w_all[rows, lanes(side * 2 * HD + half * HD)] = ref[base : base + HD]
         w_out[side, half * HD : (half + 1) * HD, lanes(j * HD)] = ref[base + HD : base + 2 * HD]
@@ -270,7 +274,7 @@
         (4, t4a.at[g:], t4b.at[g:]),
     ):
         zt = (z + d + NZ) % NZ
-        side, j = zt // 4, zt % 4
+        side, j = zt % 2, zt // 2
         g_q = dot(normed[:, lanes(j * HD)], heads[:, lanes(side * 2 * HD, 2 * HD)], 0, 0).astype(BF16)
         g_o = dot(attended[:, lanes(side * 2 * HD, 2 * HD)], cot[:, lanes(j * HD)], 0, 0).astype(BF16)
         for half, out in enumerate((out_first, out_second)):
@@ -311,25 +315,27 @@
 
 def gain_kernel(scale, ids, own, s1, s2, s3, out):
     for s, ref in enumerate((own, s1, s2, s3)):
-        out[(ids[4] - s + NX) % NX] = ref[...] * scale
-
-
-def row_kernel(width, ids, a, b, c, d, tokens, gain, totals, summed, row_sum):
-    column = jnp.transpose(jnp.broadcast_to(totals[0:1], (HD, HD)))
+        at = (ids[4] - s + NX) % NX
+        for j in range(4):
+            out[(at // 2) * 8 + 2 * j + at % 2] = ref[j : j + 1] * scale
+
+
+def row_kernel(width, ids, a, b, c, d, tokens, gain, total, summed, row_sum):
+    column = jnp.transpose(jnp.broadcast_to(total[...], (HD, HD)))
     inv = lax.rsqrt(column / width + 1e-05)
     acc = jnp.zeros((HD, HD), F32)
     for s, ref in enumerate((a, b, c, d)):
         at = (ids[4] + s) % NX
         for j in range(4):
-            cols = lanes(at * 4 * HD + j * HD)
+            cols = lanes(feature(at, j))
             value = ref[:, j * HD : (j + 1) * HD]
             summed[:, cols] = value
             acc = acc + (value.astype(F32) * gain[:, cols]) * (tokens[:, cols].astype(F32) * inv)
     row_sum[...] = jnp.sum(jnp.transpose(acc), axis=0, keepdims=True)
 
 
-def input_kernel(width, ids, summed, tokens, gain, totals, row_own, row_got, out):
-    column = jnp.transpose(jnp.broadcast_to(totals[0:1], (HD, HD)))
+def input_kernel(width, ids, summed, tokens, gain, total, row_own, row_got, out):
+    column = jnp.transpose(jnp.broadcast_to(total[...], (HD, HD)))
     inv = lax.rsqrt(column / width + 1e-05)
     row_mean = jnp.transpose(jnp.broadcast_to(row_own[...] + row_got[...], (HD, HD))) / width
     for at in range(0, summed.shape[1], HD):
@@ -338,14 +344,16 @@
         out[:, cols] = inv * (summed[:, cols].astype(F32) * gain[:, cols] - unit * row_mean)
 
 
-def owner_kernel(scale, ids, a, b, grad_query, grad_out, shared):
-    total = a[...].astype(F32) + b[...].astype(F32)
-    grad_query[...] = total[:HD] * scale
-    grad_out[...] = total[HD : 2 * HD] * scale
-    shared[...] = total[2 * HD :].astype(BF16)
-
-
-def shared_kernel(scale, ids, own, by_c, by_yl, by_both, grad_key, grad_value):
+def owner_kernel(scale, ids, a, b, grad_query, grad_out):
+    for out, rows in ((grad_query, slice(0, HD)), (grad_out, slice(HD, 2 * HD))):
+        out[...] = (a[rows].astype(F32) + b[rows].astype(F32)) * scale
+
+
+def shared_kernel(ids, a, b, shared):
+    shared[...] = (a[2 * HD :].astype(F32) + b[2 * HD :].astype(F32)).astype(BF16)
+
+
+def join_kernel(scale, ids, own, by_c, by_yl, by_both, grad_key, grad_value):
     yl, c = ids[1], ids[2]
     for ref, at in ((own, 2 * yl + c), (by_c, 2 * yl + 1 - c), (by_yl, 2 - 2 * yl + c), (by_both, 3 - 2 * yl - c)):
         rows = pl.ds(pl.multiple_of(at * PIECE, PIECE), PIECE)
@@ -373,9 +381,10 @@
     )
     same = lax.ppermute(pack, AXES, owner_perm(0))
     other = lax.ppermute(pack, AXES, owner_perm(1))
-    part_shape = ((2 * rows + GROWS, sub), BF16)
-    parts = call(spread_kernel, [part_shape] * 4, [], ids, tokens, cotangent)
-    same, other, *parts = lax.optimization_barrier((same, other, *parts))
+    (total,) = call(squares_kernel, [((1, rows), F32)], [], ids, tokens)
+    total = total + swap(total, "c")
+    same, other, total = lax.optimization_barrier((same, other, total))
+    total = total + swap(total, "yl")
     both = jnp.where(yh == 0, jnp.concatenate([same, other]), jnp.concatenate([other, same]))
     prev2, next2 = shift_z(both, 2), shift_z(both, -2)
     double, half_shape = ((4 * BLOCK, HD), BF16), ((BLOCK, HD), BF16)
@@ -384,21 +393,18 @@
     far_first, far_second = shift_z(relays[2], 2), shift_z(relays[3], -2)
     weights = (both, prev1, next1, prev2, next2, far_first, far_second)
 
+    total, _ = lax.optimization_barrier((total, both))
+    part_shape = ((2 * rows + GROWS, sub), BF16)
+    parts = call(spread_kernel, [part_shape] * 4, [], ids, tokens, cotangent, total)
     parts = [parts[0]] + [shift_x(parts[s], s) for s in range(1, NX)]
-    (totals,) = call(squares_kernel, [((NX, HD), F32)], [], ids, *parts)
-    totals, *_ = lax.optimization_barrier((totals, relays[0]))
-    totals = totals + swap(totals, "c")
-    totals = totals + swap(totals, "yl")
-    gain_f = gain.astype(F32)
-    gain_sub = lax.dynamic_slice_in_dim(gain_f, x * sub, sub, 0).reshape(1, sub)
+    gain_f = gain.astype(F32).reshape(1, quarter)
     unit_sw, normed_sw, cot_sw = call(
         normalize_kernel,
         [((512, sub), F32), ((512, sub), BF16), ((512, sub), BF16)],
         [],
         ids,
         *parts,
-        totals,
-        gain_sub,
+        gain_f,
         static=width,
     )
 
@@ -445,49 +451,9 @@
     c4, d4 = shift_z(t4a, 2), shift_z(t4b, -2)
     a, b = shift_z(up, 1), shift_z(down, -1)
     up, down = call(relay_kernel, [((2 * g + 2 * n, HD), BF16)] * 2, [], ids, t2, m2, a, b, c4, d4)
-    *back, _ = lax.optimization_barrier((*back, swap(up[:g], "c")))
     up, down = shift_z(up, 2), shift_z(down, -2)
-    to_same, to_other, gain_z = call(
-        finish_kernel, [((n, HD), BF16)] * 2 + [((4, HD), F32)], [], ids, t0, a, b, up, down, c4, d4
-    )
-    gain_z, _ = lax.optimization_barrier((gain_z, swap(to_same[:g], "c")))
-    arrived = (lax.ppermute(to_same, AXES, inverse(owner_perm(0))), lax.ppermute(to_other, AXES, inverse(owner_perm(1))))
-    *sums, shared_own = call(
-        owner_kernel,
-        [((HD, HD), F32)] * 2 + [((2 * PIECE, HD), BF16)],
-        [],
-        ids,
-        *arrived,
-        static=loss_scale,
-    )
-    grad_query, grad_out = sums
-    both_flip = lax.ppermute(shared_own, TP, [(i, 3 - i) for i in range(4)])
-    grad_key, grad_value = call(
-        shared_kernel,
-        [((rows, HD), F32)] * 2,
-        [],
-        ids,
-        shared_own,
-        swap(shared_own, "c"),
-        swap(shared_own, "yl"),
-        both_flip,
-        static=loss_scale,
-    )
-
-    gain_z = gain_z + swap(gain_z, "yh")
-    (grad_gain,) = call(
-        gain_kernel,
-        [((NX, 4, HD), F32)],
-        [],
-        ids,
-        gain_z,
-        *[shift_x(gain_z, s) for s in range(1, NX)],
-        static=loss_scale,
-    )
-    grad_gain = grad_gain.reshape(quarter)
 
     pieces = [back[0]] + [shift_x(back[s], -s) for s in range(1, NX)]
-    gain_f = gain_f.reshape(1, quarter)
     summed, row_sum = call(
         row_kernel,
         [((rows, quarter), BF16), ((1, rows), F32)],
@@ -496,10 +462,15 @@
         *pieces,
         tokens,
         gain_f,
-        totals,
+        total,
         static=width,
     )
     row_sum = row_sum + swap(row_sum, "c")
+    up, down, row_sum = lax.optimization_barrier((up, down, row_sum))
+    to_same, to_other, gain_z = call(
+        finish_kernel, [((n, HD), BF16)] * 2 + [((4, HD), F32)], [], ids, t0, a, b, up, down, c4, d4
+    )
+    gain_z, _ = lax.optimization_barrier((gain_z, swap(to_same[:g], "c")))
     (grad_input,) = call(
         input_kernel,
         [((rows, quarter), F32)],
@@ -508,11 +479,40 @@
         summed,
         tokens,
         gain_f,
-        totals,
+        total,
         row_sum,
         swap(row_sum, "yl"),
         static=width,
     )
+    arrived = (lax.ppermute(to_same, AXES, inverse(owner_perm(0))), lax.ppermute(to_other, AXES, inverse(owner_perm(1))))
+    gain_z = gain_z + swap(gain_z, "yh")
+    *arrived, grad_input, gain_z = lax.optimization_barrier((*arrived, grad_input, gain_z))
+    (shared_own,) = call(shared_kernel, [((2 * PIECE, HD), BF16)], [], ids, *arrived)
+    grad_query, grad_out = call(owner_kernel, [((HD, HD), F32)] * 2, [], ids, *arrived, static=loss_scale)
+    shared_yl = swap(shared_own, "yl")
+    grad_key, grad_value = call(
+        join_kernel,
+        [((rows, HD), F32)] * 2,
+        [],
+        ids,
+        shared_own,
+        swap(shared_own, "c"),
+        shared_yl,
+        swap(shared_yl, "c"),
+        static=loss_scale,
+    )
+
+    (grad_gain,) = call(
+        gain_kernel,
+        [((4 * NX, 1, HD), F32)],
+        [],
+        ids,
+        gain_z,
+        *[shift_x(gain_z, s) for s in range(1, NX)],
+        static=loss_scale,
+    )
+    grad_gain = grad_gain.reshape(quarter)
+
     return (grad_input, grad_gain, grad_query, grad_key, grad_value, grad_out)
 
 

time: 168 us -> 163 us (0.970)
  starting transfers between devices: 72.3 us -> 60 us
  waiting for transfers between devices: 69.7 us -> 76.3 us
    ppermute x15, waiting for transfers between devices: 25.9 us -> 37.5 us  [shift_x(): return lax.ppermute(value, 'x', [(i, (i + by) % NX) for i in range(NX)])]
    ppermute x12, starting transfers between devices: 31.7 us -> 24.4 us  [shift_z(): return lax.ppermute(value, 'z', [(i, (i + by) % NZ) for i in range(NZ)])]
    ppermute x15, starting transfers between devices: 25.6 us -> 21.4 us  [shift_x(): return lax.ppermute(value, 'x', [(i, (i + by) % NX) for i in range(NX)])]
    ppermute x1, waiting for transfers between devices: 4.16 us -> 0.01 us  [local(): lax.ppermute(to_same, AXES, inverse(owner_perm(0)))]
    ppermute x14 -> x15, waiting for transfers between devices: 20.3 us -> 22.7 us  [swap(): return lax.ppermute(value, axis, [(0, 1), (1, 0)])]
    ppermute x12, waiting for transfers between devices: 16.1 us -> 14.3 us  [shift_z(): return lax.ppermute(value, 'z', [(i, (i + by) % NZ) for i in range(NZ)])]
    ppermute x14 -> x15, starting transfers between devices: 9.34 us -> 8.3 us  [swap(): return lax.ppermute(value, axis, [(0, 1), (1, 0)])]
    pallas_call x18 -> x19, Pallas kernels: 19.3 us -> 20.2 us  [call(): pl.pallas_call(body, out_shape=[jax.ShapeDtypeStruct(s, d) for s, d in ou...]
  transfers between devices with their start and end apart: 46 -> 46, of which waited for: 23 -> 27; matrix products, arithmetic and copies ran while one was open for 0% -> 0% of each run, Pallas kernels for 6% -> 6%
where the time goes in v1:
time: 163 us; the launch traced here: 162 us
  waiting for transfers between devices  76.3 us (47%)
  starting transfers between devices  60 us (37%)
  Pallas kernels  20.2 us (12%)
  local copies, waits for them, and re-layouts  3.94 us (2%)
    ppermute x15, waiting for transfers between devices, shift_x(): return lax.ppermute(value, 'x', [(i, (i + by) % NX) for i in range(NX)])  37.5 us
    ppermute x12, starting transfers between devices, shift_z(): return lax.ppermute(value, 'z', [(i, (i + by) % NZ) for i in range(NZ)])  24.4 us
    ppermute x15, waiting for transfers between devices, swap(): return lax.ppermute(value, axis, [(0, 1), (1, 0)])  22.7 us
    ppermute x15, starting transfers between devices, shift_x(): return lax.ppermute(value, 'x', [(i, (i + by) % NX) for i in range(NX)])  21.4 us
    pallas_call x19, Pallas kernels, call(): pl.pallas_call(body, out_shape=[jax.ShapeDtypeStruct(s, d) for s, d in ou...  20.2 us
    ppermute x12, waiting for transfers between devices, shift_z(): return lax.ppermute(value, 'z', [(i, (i + by) % NZ) for i in range(NZ)])  14.3 us
    ppermute x15, starting transfers between devices, swap(): return lax.ppermute(value, axis, [(0, 1), (1, 0)])  8.3 us
    ppermute x1, starting transfers between devices, local(): same = lax.ppermute(pack, AXES, owner_perm(0))  3.47 us
  transfers between devices with their start and end apart: 46, of which 27 were waited for; matrix products, arithmetic and copies ran while one was open for 0% of the time, Pallas kernels for 6%

profile of v1, /device:TPU:8, one launch (start us, length us, event | category | flops | bytes accessed | tf_op | source)
XLA Modules:
  0.0 162.2 jit_solution(11905987613848676139)
XLA Ops:
  2.2 3.5 %collective-permute-start = (bf16[320,128]{1,0:T(8,128)(2,1)S(1)}, bf16[320,128]{1,0:T(8,128)(2,1)S(1)}, u32[]{:S(2)}, u32[]{:S(2)}) collective-permute-start(bf16[320,128]{1,0:T(8,128)(2,1)S(1)} %pad_maximum_fusion), channel_id=1, source_target_pairs={{0,0},{1,4},{2,128},{3,132},{4,32},{5,36},{6,160},{7,164},{8,8},{9... | collective-permute-start | bytes 245768 | tf_op jit(solution)/shard_map/ppermute | solution.py:382
  11.7 3.3 %collective-permute-start.7 = (bf16[640,128]{1,0:T(8,128)(2,1)S(1)}, bf16[640,128]{1,0:T(8,128)(2,1)S(1)}, u32[]{:S(2)}, u32[]{:S(2)}) collective-permute-start(bf16[640,128]{1,0:T(8,128)(2,1)S(1)} %maximum_select_fusion.both), channel_id=1, source_target_pairs={{0,8},{4,12},{8,16},{12,20},{16,24},{20,28},{24,0},{28,4},{1,9},{5... | collective-permute-start | bytes 491528 | tf_op jit(solution)/shard_map/ppermute | solution.py:52
  15.1 3.1 %collective-permute-start.8 = (bf16[640,128]{1,0:T(8,128)(2,1)S(1)}, bf16[640,128]{1,0:T(8,128)(2,1)S(1)}, u32[]{:S(2)}, u32[]{:S(2)}) collective-permute-start(bf16[640,128]{1,0:T(8,128)(2,1)S(1)} %maximum_select_fusion.both), channel_id=1, source_target_pairs={{0,24},{4,28},{8,0},{12,4},{16,8},{20,12},{24,16},{28,20},{1,25},{... | collective-permute-start | bytes 491528 | tf_op jit(solution)/shard_map/ppermute | solution.py:52
  19.5 2.3 %collective-permute-done.3 = f32[1,128]{1,0:T(1,128)S(1)} collective-permute-done((f32[1,128]{1,0:T(1,128)S(1)}, f32[1,128]{1,0:T(1,128)S(1)}, u32[]{:S(2)}, u32[]{:S(2)}) %collective-permute-start.3) | collective-permute-done | bytes 544 | tf_op jit(solution)/shard_map/ppermute | solution.py:56
  24.7 5.0 %collective-permute-start.4 = (bf16[272,512]{1,0:T(8,128)(2,1)S(1)}, bf16[272,512]{1,0:T(8,128)(2,1)S(1)}, u32[]{:S(2)}, u32[]{:S(2)}) collective-permute-start(bf16[272,512]{1,0:T(8,128)(2,1)S(1)} %get-tuple-element.64), channel_id=1, source_target_pairs={{0,32},{32,64},{64,96},{96,0},{1,33},{33,65},{65,97},{97,1},{2,34}... | collective-permute-start | bytes 835592 | tf_op jit(solution)/shard_map/ppermute | solution.py:48
  29.7 2.3 %collective-permute-start.5 = (bf16[272,512]{1,0:T(8,128)(2,1)S(1)}, bf16[272,512]{1,0:T(8,128)(2,1)S(1)}, u32[]{:S(2)}, u32[]{:S(2)}) collective-permute-start(bf16[272,512]{1,0:T(8,128)(2,1)S(1)} %get-tuple-element.65), channel_id=1, source_target_pairs={{0,64},{32,96},{64,0},{96,32},{1,65},{33,97},{65,1},{97,33},{2,66}... | collective-permute-start | bytes 835592 | tf_op jit(solution)/shard_map/ppermute | solution.py:48
  35.2 6.6 %collective-permute-done.4.refs_1_ = bf16[272,512]{1,0:T(8,128)(2,1)S(1)} collective-permute-done((bf16[272,512]{1,0:T(8,128)(2,1)S(1)}, bf16[272,512]{1,0:T(8,128)(2,1)S(1)}, u32[]{:S(2)}, u32[]{:S(2)}) %collective-permute-start.4) | collective-permute-done | bytes 278560 | tf_op jit(solution)/shard_map/ppermute | solution.py:48
  42.8 3.1 %collective-permute-start.12 = (bf16[320,128]{1,0:T(8,128)(2,1)S(1)}, bf16[320,128]{1,0:T(8,128)(2,1)S(1)}, u32[]{:S(2)}, u32[]{:S(2)}) collective-permute-start(bf16[320,128]{1,0:T(8,128)(2,1)S(1)} %get-tuple-element.72), channel_id=1, source_target_pairs={{0,24},{4,28},{8,0},{12,4},{16,8},{20,12},{24,16},{28,20},{1,25},{... | collective-permute-start | bytes 245768 | tf_op jit(solution)/shard_map/ppermute | solution.py:52
  46.7 2.4 %collective-permute-done.11.far_first = bf16[320,128]{1,0:T(8,128)(2,1)S(1)} collective-permute-done((bf16[320,128]{1,0:T(8,128)(2,1)S(1)}, bf16[320,128]{1,0:T(8,128)(2,1)S(1)}, u32[]{:S(2)}, u32[]{:S(2)}) %collective-permute-start.11) | collective-permute-done | bytes 81952 | tf_op jit(solution)/shard_map/ppermute | solution.py:52
  49.1 2.0 %collective-permute-done.12.far_second = bf16[320,128]{1,0:T(8,128)(2,1)S(1)} collective-permute-done((bf16[320,128]{1,0:T(8,128)(2,1)S(1)}, bf16[320,128]{1,0:T(8,128)(2,1)S(1)}, u32[]{:S(2)}, u32[]{:S(2)}) %collective-permute-start.12) | collective-permute-done | bytes 81952 | tf_op jit(solution)/shard_map/ppermute | solution.py:52
  53.7 1.9 %collective-permute-done.13.got = f32[512,640]{1,0:T(8,128)S(1)} collective-permute-done((f32[512,640]{1,0:T(8,128)S(1)}, f32[512,640]{1,0:T(8,128)S(1)}, u32[]{:S(2)}, u32[]{:S(2)}) %collective-permute-start.13) | collective-permute-done | bytes 1310752 | tf_op jit(solution)/shard_map/ppermute | solution.py:56
  56.7 1.9 %collective-permute-start.16 = (bf16[128,1024]{1,0:T(8,128)(2,1)S(1)}, bf16[128,1024]{1,0:T(8,128)(2,1)S(1)}, u32[]{:S(2)}, u32[]{:S(2)}) collective-permute-start(bf16[128,1024]{1,0:T(8,128)(2,1)S(1)} %get-tuple-element.79), channel_id=1, source_target_pairs={{0,32},{32,64},{64,96},{96,0},{1,33},{33,65},{65,97},{97,1},{2,34}... | collective-permute-start | bytes 786440 | tf_op jit(solution)/shard_map/ppermute | solution.py:48
  58.6 7.1 %collective-permute-done.14.a = bf16[128,1024]{1,0:T(8,128)(2,1)S(1)} collective-permute-done((bf16[128,1024]{1,0:T(8,128)(2,1)S(1)}, bf16[128,1024]{1,0:T(8,128)(2,1)S(1)}, u32[]{:S(2)}, u32[]{:S(2)}) %collective-permute-start.14) | collective-permute-done | bytes 262176 | tf_op jit(solution)/shard_map/ppermute | solution.py:48
  67.4 4.8 %collective-permute-done.16.c = bf16[128,1024]{1,0:T(8,128)(2,1)S(1)} collective-permute-done((bf16[128,1024]{1,0:T(8,128)(2,1)S(1)}, bf16[128,1024]{1,0:T(8,128)(2,1)S(1)}, u32[]{:S(2)}, u32[]{:S(2)}) %collective-permute-start.16) | collective-permute-done | bytes 262176 | tf_op jit(solution)/shard_map/ppermute | solution.py:48
  72.9 8.2 %collective-permute-done.17.got = bf16[128,1024]{1,0:T(8,128)(2,1)S(1)} collective-permute-done((bf16[128,1024]{1,0:T(8,128)(2,1)S(1)}, bf16[128,1024]{1,0:T(8,128)(2,1)S(1)}, u32[]{:S(2)}, u32[]{:S(2)}) %collective-permute-start.17) | collective-permute-done | bytes 262176 | tf_op jit(solution)/shard_map/ppermute | solution.py:56
  84.8 1.8 %collective-permute-start.20 = (bf16[128,768]{1,0:T(8,128)(2,1)S(1)}, bf16[128,768]{1,0:T(8,128)(2,1)S(1)}, u32[]{:S(2)}, u32[]{:S(2)}) collective-permute-start(bf16[128,768]{1,0:T(8,128)(2,1)S(1)} %shard_map.127.refs_0_), channel_id=1, source_target_pairs={{0,64},{32,96},{64,0},{96,32},{1,65},{33,97},{65,1},{97,33},{2,66}... | collective-permute-start | bytes 589832 | tf_op jit(solution)/shard_map/ppermute | solution.py:48
  88.0 9.1 %collective-permute-done.19.refs_1_ = bf16[128,768]{1,0:T(8,128)(2,1)S(1)} collective-permute-done((bf16[128,768]{1,0:T(8,128)(2,1)S(1)}, bf16[128,768]{1,0:T(8,128)(2,1)S(1)}, u32[]{:S(2)}, u32[]{:S(2)}) %collective-permute-start.19) | collective-permute-done | bytes 196640 | tf_op jit(solution)/shard_map/ppermute | solution.py:48
  99.2 2.8 %shard_map.128 = (bf16[656,128]{1,0:T(8,128)(2,1)S(1)}, bf16[1296,128]{1,0:T(8,128)(2,1)S(1)}, bf16[1296,128]{1,0:T(8,128)(2,1)S(1)}, bf16[640,128]{1,0:T(8,128)...) custom-call(s32[5]{0:T(128)S(1)} %stack.23.ids, ...), custom_call_target="tpu_custom_call" | custom-call | tf_op jit(solution)/shard_map/pallas_call | solution.py:73
  102.2 3.1 %collective-permute-start.27 = (bf16[1296,128]{1,0:T(8,128)(2,1)S(1)}, bf16[1296,128]{1,0:T(8,128)(2,1)S(1)}, u32[]{:S(2)}, u32[]{:S(2)}) collective-permute-start(bf16[1296,128]{1,0:T(8,128)(2,1)S(1)} %get-tuple-element.85), channel_id=1, source_target_pairs={{0,28},{4,0},{8,4},{12,8},{16,12},{20,16},{24,20},{28,24},{1,29},{... | collective-permute-start | bytes 995336 | tf_op jit(solution)/shard_map/ppermute | solution.py:52
  105.3 2.8 %collective-permute-start.28 = (bf16[336,128]{1,0:T(8,128)(2,1)S(1)}, bf16[336,128]{1,0:T(8,128)(2,1)S(1)}, u32[]{:S(2)}, u32[]{:S(2)}) collective-permute-start(bf16[336,128]{1,0:T(8,128)(2,1)S(1)} %get-tuple-element.88), channel_id=1, source_target_pairs={{0,8},{4,12},{8,16},{12,20},{16,24},{20,28},{24,0},{28,4},{1,9},{5... | collective-permute-start | bytes 258056 | tf_op jit(solution)/shard_map/ppermute | solution.py:52
  109.4 7.4 %collective-permute-done.28.c = bf16[336,128]{1,0:T(8,128)(2,1)S(1)} collective-permute-done((bf16[336,128]{1,0:T(8,128)(2,1)S(1)}, bf16[336,128]{1,0:T(8,128)(2,1)S(1)}, u32[]{:S(2)}, u32[]{:S(2)}) %collective-permute-start.28) | collective-permute-done | bytes 86048 | tf_op jit(solution)/shard_map/ppermute | solution.py:52
  116.8 2.6 %collective-permute-done.29.d = bf16[336,128]{1,0:T(8,128)(2,1)S(1)} collective-permute-done((bf16[336,128]{1,0:T(8,128)(2,1)S(1)}, bf16[336,128]{1,0:T(8,128)(2,1)S(1)}, u32[]{:S(2)}, u32[]{:S(2)}) %collective-permute-start.29) | collective-permute-done | bytes 86048 | tf_op jit(solution)/shard_map/ppermute | solution.py:52
  121.4 2.9 %collective-permute-start.31 = (bf16[672,128]{1,0:T(8,128)(2,1)S(1)}, bf16[672,128]{1,0:T(8,128)(2,1)S(1)}, u32[]{:S(2)}, u32[]{:S(2)}) collective-permute-start(bf16[672,128]{1,0:T(8,128)(2,1)S(1)} %get-tuple-element.91), channel_id=1, source_target_pairs={{0,24},{4,28},{8,0},{12,4},{16,8},{20,12},{24,16},{28,20},{1,25},{... | collective-permute-start | bytes 516104 | tf_op jit(solution)/shard_map/ppermute | solution.py:52
  124.3 2.3 %collective-permute-start.32 = (bf16[128,512]{1,0:T(8,128)(2,1)S(1)}, bf16[128,512]{1,0:T(8,128)(2,1)S(1)}, u32[]{:S(2)}, u32[]{:S(2)}) collective-permute-start(bf16[128,512]{1,0:T(8,128)(2,1)S(1)} %get-tuple-element.93), channel_id=1, source_target_pairs={{0,96},{32,0},{64,32},{96,64},{1,97},{33,1},{65,33},{97,65},{2,98}... | collective-permute-start | bytes 393224 | tf_op jit(solution)/shard_map/ppermute | solution.py:48
  127.4 3.1 %collective-permute-done.32.b = bf16[128,512]{1,0:T(8,128)(2,1)S(1)} collective-permute-done((bf16[128,512]{1,0:T(8,128)(2,1)S(1)}, bf16[128,512]{1,0:T(8,128)(2,1)S(1)}, u32[]{:S(2)}, u32[]{:S(2)}) %collective-permute-start.32) | collective-permute-done | bytes 131104 | tf_op jit(solution)/shard_map/ppermute | solution.py:48
  130.5 2.7 %collective-permute-done.33.c = bf16[128,512]{1,0:T(8,128)(2,1)S(1)} collective-permute-done((bf16[128,512]{1,0:T(8,128)(2,1)S(1)}, bf16[128,512]{1,0:T(8,128)(2,1)S(1)}, u32[]{:S(2)}, u32[]{:S(2)}) %collective-permute-start.33) | collective-permute-done | bytes 131104 | tf_op jit(solution)/shard_map/ppermute | solution.py:48
  137.1 2.4 %collective-permute-start.36 = (bf16[320,128]{1,0:T(8,128)(2,1)S(1)}, bf16[320,128]{1,0:T(8,128)(2,1)S(1)}, u32[]{:S(2)}, u32[]{:S(2)}) collective-permute-start(bf16[320,128]{1,0:T(8,128)(2,1)S(1)} %get-tuple-element.99), channel_id=1, source_target_pairs={{0,0},{4,1},{128,2},{132,3},{32,4},{36,5},{160,6},{164,7},{8,8},{1... | collective-permute-start | bytes 245768 | tf_op jit(solution)/shard_map/ppermute | solution.py:487
  139.5 3.0 %collective-permute-start.39 = (f32[4,128]{1,0:T(4,128)S(1)}, f32[4,128]{1,0:T(4,128)S(1)}, u32[]{:S(2)}, u32[]{:S(2)}) collective-permute-start(f32[4,128]{1,0:T(4,128)S(1)} %get-tuple-element.103), channel_id=1, source_target_pairs={{0,128},{128,0},{1,129},{129,1},{2,130},{130,2},{3,131},{131,3},{4... | collective-permute-start | bytes 6152 | tf_op jit(solution)/shard_map/ppermute | solution.py:56
  143.3 2.8 %collective-permute-done.38.row_got = f32[1,128]{1,0:T(1,128)S(1)} collective-permute-done((f32[1,128]{1,0:T(1,128)S(1)}, f32[1,128]{1,0:T(1,128)S(1)}, u32[]{:S(2)}, u32[]{:S(2)}) %collective-permute-start.38) | collective-permute-done | bytes 544 | tf_op jit(solution)/shard_map/ppermute | solution.py:56
  146.1 1.8 %shard_map.132 = f32[128,2048]{1,0:T(8,128)} custom-call(s32[5]{0:T(128)S(1)} %stack.23.ids, bf16[128,2048]{1,0:T(8,128)(2,1)S(1)} %get-tuple-element.101.summed, bf16[128,2048]{1,0:T(8,128)(2,1)S(1)} %copy-done.2, f32[1,2048]{1,0:T(1,128)S(1)} %bitcast.9, f32[1,128]{1,0:T(1,128)S(1)} %add.22.total, f32[1,128]{1,0:T(1,128)S(1)} %add.23.row_own, ...), custom_call_target="tpu_custom_call" | custom-call | tf_op jit(solution)/shard_map/pallas_call | solution.py:73
  149.3 3.0 %collective-permute-done.44.by_yl = bf16[64,128]{1,0:T(8,128)(2,1)S(1)} collective-permute-done((bf16[64,128]{1,0:T(8,128)(2,1)S(1)}, bf16[64,128]{1,0:T(8,128)(2,1)S(1)}, u32[]{:S(2)}, u32[]{:S(2)}) %collective-permute-start.44) | collective-permute-done | bytes 16416 | tf_op jit(solution)/shard_map/ppermute | solution.py:56
  152.3 2.2 %collective-permute-start.40 = (f32[4,128]{1,0:T(4,128)S(1)}, f32[4,128]{1,0:T(4,128)S(1)}, u32[]{:S(2)}, u32[]{:S(2)}) collective-permute-start(f32[4,128]{1,0:T(4,128)S(1)} %add.24.own), channel_id=1, source_target_pairs={{0,32},{32,64},{64,96},{96,0},{1,33},{33,65},{65,97},{97,1},{2,34}... | collective-permute-start | bytes 6152 | tf_op jit(solution)/shard_map/ppermute | solution.py:48
  (98 shorter events, 48.2 us)
Async XLA Ops:
  2.2 7.8 %collective-permute-start = (bf16[320,128]{1,0:T(8,128)(2,1)S(1)}, bf16[320,128]{1,0:T(8,128)(2,1)S(1)}, u32[]{:S(2)}, u32[]{:S(2)}) collective-permute-start(bf16[320,128]{1,0:T(8,128)(2,1)S(1)} %pad_maximum_fusion), channel_id=1, source_target_pairs={{0,0},{1,4},{2,128},{3,132},{4,32},{5,36},{6,160},{7,164},{8,8},{9... | collective-permute-start | bytes 245768 | tf_op jit(solution)/shard_map/ppermute | solution.py:382
  11.7 20.3 %collective-permute-start.7 = (bf16[640,128]{1,0:T(8,128)(2,1)S(1)}, bf16[640,128]{1,0:T(8,128)(2,1)S(1)}, u32[]{:S(2)}, u32[]{:S(2)}) collective-permute-start(bf16[640,128]{1,0:T(8,128)(2,1)S(1)} %maximum_select_fusion.both), channel_id=1, source_target_pairs={{0,8},{4,12},{8,16},{12,20},{16,24},{20,28},{24,0},{28,4},{1,9},{5... | collective-permute-start | bytes 491528 | tf_op jit(solution)/shard_map/ppermute | solution.py:52
  15.1 16.9 %collective-permute-start.8 = (bf16[640,128]{1,0:T(8,128)(2,1)S(1)}, bf16[640,128]{1,0:T(8,128)(2,1)S(1)}, u32[]{:S(2)}, u32[]{:S(2)}) collective-permute-start(bf16[640,128]{1,0:T(8,128)(2,1)S(1)} %maximum_select_fusion.both), channel_id=1, source_target_pairs={{0,24},{4,28},{8,0},{12,4},{16,8},{20,12},{24,16},{28,20},{1,25},{... | collective-permute-start | bytes 491528 | tf_op jit(solution)/shard_map/ppermute | solution.py:52
  24.7 17.1 %collective-permute-start.4 = (bf16[272,512]{1,0:T(8,128)(2,1)S(1)}, bf16[272,512]{1,0:T(8,128)(2,1)S(1)}, u32[]{:S(2)}, u32[]{:S(2)}) collective-permute-start(bf16[272,512]{1,0:T(8,128)(2,1)S(1)} %get-tuple-element.64), channel_id=1, source_target_pairs={{0,32},{32,64},{64,96},{96,0},{1,33},{33,65},{65,97},{97,1},{2,34}... | collective-permute-start | bytes 835592 | tf_op jit(solution)/shard_map/ppermute | solution.py:48
  29.7 13.2 %collective-permute-start.5 = (bf16[272,512]{1,0:T(8,128)(2,1)S(1)}, bf16[272,512]{1,0:T(8,128)(2,1)S(1)}, u32[]{:S(2)}, u32[]{:S(2)}) collective-permute-start(bf16[272,512]{1,0:T(8,128)(2,1)S(1)} %get-tuple-element.65), channel_id=1, source_target_pairs={{0,64},{32,96},{64,0},{96,32},{1,65},{33,97},{65,1},{97,33},{2,66}... | collective-permute-start | bytes 835592 | tf_op jit(solution)/shard_map/ppermute | solution.py:48
  32.6 18.4 %collective-permute-start.10 = (bf16[1280,128]{1,0:T(8,128)(2,1)S(1)}, bf16[1280,128]{1,0:T(8,128)(2,1)S(1)}, u32[]{:S(2)}, u32[]{:S(2)}) collective-permute-start(bf16[1280,128]{1,0:T(8,128)(2,1)S(1)} %get-tuple-element.70), channel_id=1, source_target_pairs={{0,28},{4,0},{8,4},{12,8},{16,12},{20,16},{24,20},{28,24},{1,29},{... | collective-permute-start | bytes 983048 | tf_op jit(solution)/shard_map/ppermute | solution.py:52
  33.8 17.3 %collective-permute-start.9 = (bf16[1280,128]{1,0:T(8,128)(2,1)S(1)}, bf16[1280,128]{1,0:T(8,128)(2,1)S(1)}, u32[]{:S(2)}, u32[]{:S(2)}) collective-permute-start(bf16[1280,128]{1,0:T(8,128)(2,1)S(1)} %get-tuple-element.69), channel_id=1, source_target_pairs={{0,4},{4,8},{8,12},{12,16},{16,20},{20,24},{24,28},{28,0},{1,5},{5... | collective-permute-start | bytes 983048 | tf_op jit(solution)/shard_map/ppermute | solution.py:52
  34.7 11.2 %collective-permute-start.6 = (bf16[272,512]{1,0:T(8,128)(2,1)S(1)}, bf16[272,512]{1,0:T(8,128)(2,1)S(1)}, u32[]{:S(2)}, u32[]{:S(2)}) collective-permute-start(bf16[272,512]{1,0:T(8,128)(2,1)S(1)} %get-tuple-element.66), channel_id=1, source_target_pairs={{0,96},{32,0},{64,32},{96,64},{1,97},{33,1},{65,33},{97,65},{2,98}... | collective-permute-start | bytes 835592 | tf_op jit(solution)/shard_map/ppermute | solution.py:48
  41.7 7.4 %collective-permute-start.11 = (bf16[320,128]{1,0:T(8,128)(2,1)S(1)}, bf16[320,128]{1,0:T(8,128)(2,1)S(1)}, u32[]{:S(2)}, u32[]{:S(2)}) collective-permute-start(bf16[320,128]{1,0:T(8,128)(2,1)S(1)} %get-tuple-element.71), channel_id=1, source_target_pairs={{0,8},{4,12},{8,16},{12,20},{16,24},{20,28},{24,0},{28,4},{1,9},{5... | collective-permute-start | bytes 245768 | tf_op jit(solution)/shard_map/ppermute | solution.py:52
  42.8 8.2 %collective-permute-start.12 = (bf16[320,128]{1,0:T(8,128)(2,1)S(1)}, bf16[320,128]{1,0:T(8,128)(2,1)S(1)}, u32[]{:S(2)}, u32[]{:S(2)}) collective-permute-start(bf16[320,128]{1,0:T(8,128)(2,1)S(1)} %get-tuple-element.72), channel_id=1, source_target_pairs={{0,24},{4,28},{8,0},{12,4},{16,8},{20,12},{24,16},{28,20},{1,25},{... | collective-permute-start | bytes 245768 | tf_op jit(solution)/shard_map/ppermute | solution.py:52
  56.3 9.4 %collective-permute-start.14 = (bf16[128,1024]{1,0:T(8,128)(2,1)S(1)}, bf16[128,1024]{1,0:T(8,128)(2,1)S(1)}, u32[]{:S(2)}, u32[]{:S(2)}) collective-permute-start(bf16[128,1024]{1,0:T(8,128)(2,1)S(1)} %get-tuple-element.77), channel_id=1, source_target_pairs={{0,96},{32,0},{64,32},{96,64},{1,97},{33,1},{65,33},{97,65},{2,98}... | collective-permute-start | bytes 786440 | tf_op jit(solution)/shard_map/ppermute | solution.py:48
  56.6 10.8 %collective-permute-start.15 = (bf16[128,1024]{1,0:T(8,128)(2,1)S(1)}, bf16[128,1024]{1,0:T(8,128)(2,1)S(1)}, u32[]{:S(2)}, u32[]{:S(2)}) collective-permute-start(bf16[128,1024]{1,0:T(8,128)(2,1)S(1)} %get-tuple-element.78), channel_id=1, source_target_pairs={{0,64},{32,96},{64,0},{96,32},{1,65},{33,97},{65,1},{97,33},{2,66}... | collective-permute-start | bytes 786440 | tf_op jit(solution)/shard_map/ppermute | solution.py:48
  56.7 15.5 %collective-permute-start.16 = (bf16[128,1024]{1,0:T(8,128)(2,1)S(1)}, bf16[128,1024]{1,0:T(8,128)(2,1)S(1)}, u32[]{:S(2)}, u32[]{:S(2)}) collective-permute-start(bf16[128,1024]{1,0:T(8,128)(2,1)S(1)} %get-tuple-element.79), channel_id=1, source_target_pairs={{0,32},{32,64},{64,96},{96,0},{1,33},{33,65},{65,97},{97,1},{2,34}... | collective-permute-start | bytes 786440 | tf_op jit(solution)/shard_map/ppermute | solution.py:48
  72.8 8.3 %collective-permute-start.17 = (bf16[128,1024]{1,0:T(8,128)(2,1)S(1)}, bf16[128,1024]{1,0:T(8,128)(2,1)S(1)}, u32[]{:S(2)}, u32[]{:S(2)}) collective-permute-start(bf16[128,1024]{1,0:T(8,128)(2,1)S(1)} %shard_map.125.mine), channel_id=1, source_target_pairs={{0,2},{2,0},{1,3},{3,1},{4,6},{6,4},{5,7},{7,5},{8,10},{10,8},{9,1... | collective-permute-start | bytes 786440 | tf_op jit(solution)/shard_map/ppermute | solution.py:56
  84.7 12.5 %collective-permute-start.19 = (bf16[128,768]{1,0:T(8,128)(2,1)S(1)}, bf16[128,768]{1,0:T(8,128)(2,1)S(1)}, u32[]{:S(2)}, u32[]{:S(2)}) collective-permute-start(bf16[128,768]{1,0:T(8,128)(2,1)S(1)} %shard_map.127.refs_0_), channel_id=1, source_target_pairs={{0,32},{32,64},{64,96},{96,0},{1,33},{33,65},{65,97},{97,1},{2,34}... | collective-permute-start | bytes 589832 | tf_op jit(solution)/shard_map/ppermute | solution.py:48
  84.8 12.4 %collective-permute-start.20 = (bf16[128,768]{1,0:T(8,128)(2,1)S(1)}, bf16[128,768]{1,0:T(8,128)(2,1)S(1)}, u32[]{:S(2)}, u32[]{:S(2)}) collective-permute-start(bf16[128,768]{1,0:T(8,128)(2,1)S(1)} %shard_map.127.refs_0_), channel_id=1, source_target_pairs={{0,64},{32,96},{64,0},{96,32},{1,65},{33,97},{65,1},{97,33},{2,66}... | collective-permute-start | bytes 589832 | tf_op jit(solution)/shard_map/ppermute | solution.py:48
  86.6 11.2 %collective-permute-start.21 = (bf16[128,768]{1,0:T(8,128)(2,1)S(1)}, bf16[128,768]{1,0:T(8,128)(2,1)S(1)}, u32[]{:S(2)}, u32[]{:S(2)}) collective-permute-start(bf16[128,768]{1,0:T(8,128)(2,1)S(1)} %shard_map.127.refs_0_), channel_id=1, source_target_pairs={{0,96},{32,0},{64,32},{96,64},{1,97},{33,1},{65,33},{97,65},{2,98}... | collective-permute-start | bytes 589832 | tf_op jit(solution)/shard_map/ppermute | solution.py:48
  88.0 9.8 %collective-permute-start.22 = (bf16[128,768]{1,0:T(8,128)(2,1)S(1)}, bf16[128,768]{1,0:T(8,128)(2,1)S(1)}, u32[]{:S(2)}, u32[]{:S(2)}) collective-permute-start(bf16[128,768]{1,0:T(8,128)(2,1)S(1)} %shard_map.127.refs_0_), channel_id=1, source_target_pairs={{0,1},{1,0},{2,3},{3,2},{4,5},{5,4},{6,7},{7,6},{8,9},{9,8},{10,11... | collective-permute-start | bytes 589832 | tf_op jit(solution)/shard_map/ppermute | solution.py:56
  102.0 17.4 %collective-permute-start.26 = (bf16[1296,128]{1,0:T(8,128)(2,1)S(1)}, bf16[1296,128]{1,0:T(8,128)(2,1)S(1)}, u32[]{:S(2)}, u32[]{:S(2)}) collective-permute-start(bf16[1296,128]{1,0:T(8,128)(2,1)S(1)} %get-tuple-element.84), channel_id=1, source_target_pairs={{0,4},{4,8},{8,12},{12,16},{16,20},{20,24},{24,28},{28,0},{1,5},{5... | collective-permute-start | bytes 995336 | tf_op jit(solution)/shard_map/ppermute | solution.py:52
  102.2 17.2 %collective-permute-start.27 = (bf16[1296,128]{1,0:T(8,128)(2,1)S(1)}, bf16[1296,128]{1,0:T(8,128)(2,1)S(1)}, u32[]{:S(2)}, u32[]{:S(2)}) collective-permute-start(bf16[1296,128]{1,0:T(8,128)(2,1)S(1)} %get-tuple-element.85), channel_id=1, source_target_pairs={{0,28},{4,0},{8,4},{12,8},{16,12},{20,16},{24,20},{28,24},{1,29},{... | collective-permute-start | bytes 995336 | tf_op jit(solution)/shard_map/ppermute | solution.py:52
  105.3 11.5 %collective-permute-start.28 = (bf16[336,128]{1,0:T(8,128)(2,1)S(1)}, bf16[336,128]{1,0:T(8,128)(2,1)S(1)}, u32[]{:S(2)}, u32[]{:S(2)}) collective-permute-start(bf16[336,128]{1,0:T(8,128)(2,1)S(1)} %get-tuple-element.88), channel_id=1, source_target_pairs={{0,8},{4,12},{8,16},{12,20},{16,24},{20,28},{24,0},{28,4},{1,9},{5... | collective-permute-start | bytes 258056 | tf_op jit(solution)/shard_map/ppermute | solution.py:52
  108.1 11.3 %collective-permute-start.29 = (bf16[336,128]{1,0:T(8,128)(2,1)S(1)}, bf16[336,128]{1,0:T(8,128)(2,1)S(1)}, u32[]{:S(2)}, u32[]{:S(2)}) collective-permute-start(bf16[336,128]{1,0:T(8,128)(2,1)S(1)} %get-tuple-element.89), channel_id=1, source_target_pairs={{0,24},{4,28},{8,0},{12,4},{16,8},{20,12},{24,16},{28,20},{1,25},{... | collective-permute-start | bytes 258056 | tf_op jit(solution)/shard_map/ppermute | solution.py:52
  120.0 16.3 %collective-permute-start.30 = (bf16[672,128]{1,0:T(8,128)(2,1)S(1)}, bf16[672,128]{1,0:T(8,128)(2,1)S(1)}, u32[]{:S(2)}, u32[]{:S(2)}) collective-permute-start(bf16[672,128]{1,0:T(8,128)(2,1)S(1)} %get-tuple-element.90), channel_id=1, source_target_pairs={{0,8},{4,12},{8,16},{12,20},{16,24},{20,28},{24,0},{28,4},{1,9},{5... | collective-permute-start | bytes 516104 | tf_op jit(solution)/shard_map/ppermute | solution.py:52
  121.4 15.0 %collective-permute-start.31 = (bf16[672,128]{1,0:T(8,128)(2,1)S(1)}, bf16[672,128]{1,0:T(8,128)(2,1)S(1)}, u32[]{:S(2)}, u32[]{:S(2)}) collective-permute-start(bf16[672,128]{1,0:T(8,128)(2,1)S(1)} %get-tuple-element.91), channel_id=1, source_target_pairs={{0,24},{4,28},{8,0},{12,4},{16,8},{20,12},{24,16},{28,20},{1,25},{... | collective-permute-start | bytes 516104 | tf_op jit(solution)/shard_map/ppermute | solution.py:52
  124.3 6.2 %collective-permute-start.32 = (bf16[128,512]{1,0:T(8,128)(2,1)S(1)}, bf16[128,512]{1,0:T(8,128)(2,1)S(1)}, u32[]{:S(2)}, u32[]{:S(2)}) collective-permute-start(bf16[128,512]{1,0:T(8,128)(2,1)S(1)} %get-tuple-element.93), channel_id=1, source_target_pairs={{0,96},{32,0},{64,32},{96,64},{1,97},{33,1},{65,33},{97,65},{2,98}... | collective-permute-start | bytes 393224 | tf_op jit(solution)/shard_map/ppermute | solution.py:48
  126.6 6.6 %collective-permute-start.33 = (bf16[128,512]{1,0:T(8,128)(2,1)S(1)}, bf16[128,512]{1,0:T(8,128)(2,1)S(1)}, u32[]{:S(2)}, u32[]{:S(2)}) collective-permute-start(bf16[128,512]{1,0:T(8,128)(2,1)S(1)} %get-tuple-element.94), channel_id=1, source_target_pairs={{0,64},{32,96},{64,0},{96,32},{1,65},{33,97},{65,1},{97,33},{2,66}... | collective-permute-start | bytes 393224 | tf_op jit(solution)/shard_map/ppermute | solution.py:48
  126.6 7.6 %collective-permute-start.34 = (bf16[128,512]{1,0:T(8,128)(2,1)S(1)}, bf16[128,512]{1,0:T(8,128)(2,1)S(1)}, u32[]{:S(2)}, u32[]{:S(2)}) collective-permute-start(bf16[128,512]{1,0:T(8,128)(2,1)S(1)} %get-tuple-element.95), channel_id=1, source_target_pairs={{0,32},{32,64},{64,96},{96,0},{1,33},{33,65},{65,97},{97,1},{2,34}... | collective-permute-start | bytes 393224 | tf_op jit(solution)/shard_map/ppermute | solution.py:48
  137.1 10.9 %collective-permute-start.36 = (bf16[320,128]{1,0:T(8,128)(2,1)S(1)}, bf16[320,128]{1,0:T(8,128)(2,1)S(1)}, u32[]{:S(2)}, u32[]{:S(2)}) collective-permute-start(bf16[320,128]{1,0:T(8,128)(2,1)S(1)} %get-tuple-element.99), channel_id=1, source_target_pairs={{0,0},{4,1},{128,2},{132,3},{32,4},{36,5},{160,6},{164,7},{8,8},{1... | collective-permute-start | bytes 245768 | tf_op jit(solution)/shard_map/ppermute | solution.py:487
  139.4 8.5 %collective-permute-start.37 = (bf16[320,128]{1,0:T(8,128)(2,1)S(1)}, bf16[320,128]{1,0:T(8,128)(2,1)S(1)}, u32[]{:S(2)}, u32[]{:S(2)}) collective-permute-start(bf16[320,128]{1,0:T(8,128)(2,1)S(1)} %get-tuple-element.100), channel_id=1, source_target_pairs={{128,0},{132,1},{0,2},{4,3},{160,4},{164,5},{32,6},{36,7},{136,8},... | collective-permute-start | bytes 245768 | tf_op jit(solution)/shard_map/ppermute | solution.py:487
  139.5 8.4 %collective-permute-start.39 = (f32[4,128]{1,0:T(4,128)S(1)}, f32[4,128]{1,0:T(4,128)S(1)}, u32[]{:S(2)}, u32[]{:S(2)}) collective-permute-start(f32[4,128]{1,0:T(4,128)S(1)} %get-tuple-element.103), channel_id=1, source_target_pairs={{0,128},{128,0},{1,129},{129,1},{2,130},{130,2},{3,131},{131,3},{4... | collective-permute-start | bytes 6152 | tf_op jit(solution)/shard_map/ppermute | solution.py:56
  149.3 11.7 %collective-permute-start.43 = (bf16[64,128]{1,0:T(8,128)(2,1)S(1)}, bf16[64,128]{1,0:T(8,128)(2,1)S(1)}, u32[]{:S(2)}, u32[]{:S(2)}) collective-permute-start(bf16[64,128]{1,0:T(8,128)(2,1)S(1)} %shard_map.135.own), channel_id=1, source_target_pairs={{0,1},{1,0},{2,3},{3,2},{4,5},{5,4},{6,7},{7,6},{8,9},{9,8},{10,11... | collective-permute-start | bytes 49160 | tf_op jit(solution)/shard_map/ppermute | solution.py:56
  152.3 8.7 %collective-permute-start.45 = (bf16[64,128]{1,0:T(8,128)(2,1)S(1)}, bf16[64,128]{1,0:T(8,128)(2,1)S(1)}, u32[]{:S(2)}, u32[]{:S(2)}) collective-permute-start(bf16[64,128]{1,0:T(8,128)(2,1)S(1)} %collective-permute-done.44.by_yl), channel_id=1, source_target_pairs={{0,1},{1,0},{2,3},{3,2},{4,5},{5,4},{6,7},{7,6},{8,9},{9,8},{10,11... | collective-permute-start | bytes 49160 | tf_op jit(solution)/shard_map/ppermute | solution.py:56
  (19 other events, 124.1 us)

commit v2 on v1

--- a/solution.py
+++ b/solution.py
@@ -68,39 +68,41 @@
     return ((at // 2) * 8 + 2 * j + at % 2) * HD
 
 
-def call(body, outs, scratch, ids, *args, static=None):
+def call(body, outs, scratch, ids, *args, static=None, aliases={}):
     body = body if static is None else functools.partial(body, static)
     return pl.pallas_call(
         body,
         out_shape=[jax.ShapeDtypeStruct(s, d) for s, d in outs],
         in_specs=[SMEM] + [VMEM] * len(args),
         out_specs=[VMEM] * len(outs),
+        input_output_aliases=aliases,
         scratch_shapes=[pltpu.VMEM(s, d) for s, d in scratch],
         compiler_params=pltpu.CompilerParams(vmem_limit_bytes=16 * 2**20),
     )(ids, *args)
 
 
-def squares_kernel(ids, tokens, out):
-    squares = jnp.zeros((tokens.shape[0], HD), F32)
-    for at in range(0, tokens.shape[1], HD):
-        value = tokens[:, at : at + HD].astype(F32)
-        squares = squares + value * value
-    out[...] = jnp.sum(jnp.transpose(squares), axis=0, keepdims=True)
-
-
-def spread_kernel(ids, tokens, cot, total, *outs):
+def spread_kernel(ids, tokens, cot, total_out, *outs):
     rows = tokens.shape[0]
+    squares = jnp.zeros((rows, HD), F32)
+    for s in range(NX):
+        at = (ids[4] + s) % NX
+        for j in range(4):
+            block, cols = lanes(feature(at, j)), slice(j * HD, (j + 1) * HD)
+            value = tokens[:, block]
+            squares = squares + value.astype(F32) * value.astype(F32)
+            outs[s][:rows, cols] = value
+            outs[s][rows : 2 * rows, cols] = cot[:, block]
+    total_out[...] = jnp.sum(jnp.transpose(squares), axis=0, keepdims=True)
+
+
+def stamp_kernel(ids, total, *refs):
     total = total[...]
     high = total.astype(BF16).astype(F32)
     middle = (total - high).astype(BF16).astype(F32)
     extra = jnp.concatenate([high, middle, total - high - middle, jnp.zeros((GROWS - 3, HD), F32)], axis=0)
-    for s in range(NX):
-        at = (ids[4] + s) % NX
-        for j in range(4):
-            block, cols = lanes(feature(at, j)), slice(j * HD, (j + 1) * HD)
-            outs[s][:rows, cols] = tokens[:, block]
-            outs[s][rows : 2 * rows, cols] = cot[:, block]
-            outs[s][2 * rows :, cols] = extra.astype(BF16)
+    extra = jnp.concatenate([extra] * 4, axis=1).astype(BF16)
+    for out in refs[NX:]:
+        out[2 * HD :] = extra
 
 
 def normalize_kernel(width, ids, *refs):
@@ -209,7 +211,7 @@
     kv[...] = total[:, 4 * HD :]
 
 
-def attend_kernel(ids, qa, kv_mine, kv_theirs, out):
+def attend_kernel(ids, qa, kv_mine, kv_theirs, out, row_out):
     first = ids[2] == 0
     mine, theirs = kv_mine[...].astype(F32), kv_theirs[...].astype(F32)
     key_rows = jnp.where(first, mine, theirs).astype(BF16)
@@ -217,6 +219,7 @@
     causal = lax.broadcasted_iota(jnp.int32, (HD, HD), 0) >= lax.broadcasted_iota(jnp.int32, (HD, HD), 1)
     keys = jnp.zeros((HD, HD), F32)
     values = jnp.zeros((HD, HD), F32)
+    row_terms = jnp.zeros((HD, HD), F32)
     for h in range(2):
         query = qa[:, h * HD : (h + 1) * HD]
         attn_grad = qa[:, (2 + h) * HD : (3 + h) * HD]
@@ -228,12 +231,16 @@
         dprob = dot(attn_grad, value_rows, 1, 1)
         dscore = softmax_out * (dprob - jnp.sum(dprob * softmax_out, axis=-1, keepdims=True)) * HD ** (-0.5)
         dscore = dscore.astype(BF16)
-        out[:, h * HD : (h + 1) * HD] = dot(dscore, key_rows, 1, 0).astype(BF16)
+        d_query = dot(dscore, key_rows, 1, 0).astype(BF16)
+        out[:, h * HD : (h + 1) * HD] = d_query
+        row_terms = row_terms + d_query.astype(F32) * query.astype(F32)
         out[:, (2 + h) * HD : (3 + h) * HD] = dot(rounded, value_rows, 1, 0).astype(BF16)
         keys = keys + dot(dscore, query, 0, 0).astype(BF16).astype(F32)
         values = values + dot(rounded, attn_grad, 0, 0).astype(BF16).astype(F32)
     out[:, 4 * HD : 5 * HD] = keys.astype(BF16)
     out[:, 5 * HD :] = values.astype(BF16)
+    row_terms = row_terms + keys * key_rows.astype(F32) + values * value_rows.astype(F32)
+    row_out[...] = jnp.sum(jnp.transpose(row_terms), axis=0, keepdims=True)
 
 
 def gradient_kernel(ids, *refs):
@@ -313,35 +320,16 @@
     gain_out[...] = rows[:4] + rows[4:8]
 
 
-def gain_kernel(scale, ids, own, s1, s2, s3, out):
-    for s, ref in enumerate((own, s1, s2, s3)):
-        at = (ids[4] - s + NX) % NX
-        for j in range(4):
-            out[(at // 2) * 8 + 2 * j + at % 2] = ref[j : j + 1] * scale
-
-
-def row_kernel(width, ids, a, b, c, d, tokens, gain, total, summed, row_sum):
-    column = jnp.transpose(jnp.broadcast_to(total[...], (HD, HD)))
-    inv = lax.rsqrt(column / width + 1e-05)
-    acc = jnp.zeros((HD, HD), F32)
+def input_kernel(width, ids, a, b, c, d, tokens, gain, total, row_sum, out):
+    inv = lax.rsqrt(jnp.transpose(jnp.broadcast_to(total[...], (HD, HD))) / width + 1e-05)
+    row_mean = jnp.transpose(jnp.broadcast_to(row_sum[...], (HD, HD))) / width
     for s, ref in enumerate((a, b, c, d)):
         at = (ids[4] + s) % NX
         for j in range(4):
             cols = lanes(feature(at, j))
-            value = ref[:, j * HD : (j + 1) * HD]
-            summed[:, cols] = value
-            acc = acc + (value.astype(F32) * gain[:, cols]) * (tokens[:, cols].astype(F32) * inv)
-    row_sum[...] = jnp.sum(jnp.transpose(acc), axis=0, keepdims=True)
-
-
-def input_kernel(width, ids, summed, tokens, gain, total, row_own, row_got, out):
-    column = jnp.transpose(jnp.broadcast_to(total[...], (HD, HD)))
-    inv = lax.rsqrt(column / width + 1e-05)
-    row_mean = jnp.transpose(jnp.broadcast_to(row_own[...] + row_got[...], (HD, HD))) / width
-    for at in range(0, summed.shape[1], HD):
-        cols = slice(at, at + HD)
-        unit = tokens[:, cols].astype(F32) * inv
-        out[:, cols] = inv * (summed[:, cols].astype(F32) * gain[:, cols] - unit * row_mean)
+            unit = tokens[:, cols].astype(F32) * inv
+            scaled = ref[:, j * HD : (j + 1) * HD].astype(F32) * gain[:, cols]
+            out[:, cols] = inv * (scaled - unit * row_mean)
 
 
 def owner_kernel(scale, ids, a, b, grad_query, grad_out):
@@ -353,12 +341,16 @@
     shared[...] = (a[2 * HD :].astype(F32) + b[2 * HD :].astype(F32)).astype(BF16)
 
 
-def join_kernel(scale, ids, own, by_c, by_yl, by_both, grad_key, grad_value):
-    yl, c = ids[1], ids[2]
+def join_kernel(scale, ids, own, by_c, by_yl, by_both, g0, g1, g2, g3, grad_key, grad_value, grad_gain):
+    yl, c, x = ids[1], ids[2], ids[4]
     for ref, at in ((own, 2 * yl + c), (by_c, 2 * yl + 1 - c), (by_yl, 2 - 2 * yl + c), (by_both, 3 - 2 * yl - c)):
         rows = pl.ds(pl.multiple_of(at * PIECE, PIECE), PIECE)
         grad_key[rows] = ref[:PIECE].astype(F32) * scale
         grad_value[rows] = ref[PIECE:].astype(F32) * scale
+    for s, ref in enumerate((g0, g1, g2, g3)):
+        at = (x - s + NX) % NX
+        for j in range(4):
+            grad_gain[(at // 2) * 8 + 2 * j + at % 2] = ref[j : j + 1] * scale
 
 
 def local(tokens, gain, w_query, w_key, w_value, w_out, cotangent):
@@ -381,7 +373,8 @@
     )
     same = lax.ppermute(pack, AXES, owner_perm(0))
     other = lax.ppermute(pack, AXES, owner_perm(1))
-    (total,) = call(squares_kernel, [((1, rows), F32)], [], ids, tokens)
+    part_shape = ((2 * rows + GROWS, sub), BF16)
+    total, *parts = call(spread_kernel, [((1, rows), F32)] + [part_shape] * 4, [], ids, tokens, cotangent)
     total = total + swap(total, "c")
     same, other, total = lax.optimization_barrier((same, other, total))
     total = total + swap(total, "yl")
@@ -393,9 +386,7 @@
     far_first, far_second = shift_z(relays[2], 2), shift_z(relays[3], -2)
     weights = (both, prev1, next1, prev2, next2, far_first, far_second)
 
-    total, _ = lax.optimization_barrier((total, both))
-    part_shape = ((2 * rows + GROWS, sub), BF16)
-    parts = call(spread_kernel, [part_shape] * 4, [], ids, tokens, cotangent, total)
+    parts = call(stamp_kernel, [part_shape] * 4, [], ids, total, *parts, aliases={2 + s: s for s in range(4)})
     parts = [parts[0]] + [shift_x(parts[s], s) for s in range(1, NX)]
     gain_f = gain.astype(F32).reshape(1, quarter)
     unit_sw, normed_sw, cot_sw = call(
@@ -423,7 +414,10 @@
     chunks = [shift_x(chunks[s - 1], -s) for s in range(1, NX)]
     (partial,) = call(sum_kernel, [split], [], ids, own, *chunks)
     qa, kv = call(final_kernel, [((rows, 4 * HD), BF16), ((rows, HD), BF16)], [], ids, partial, swap(partial, "yl"))
-    (heads,) = call(attend_kernel, [((rows, 6 * HD), BF16)], [], ids, qa, kv, swap(kv, "c"))
+    heads, row_sum = call(
+        attend_kernel, [((rows, 6 * HD), BF16), ((1, rows), F32)], [], ids, qa, kv, swap(kv, "c")
+    )
+    row_sum = row_sum + swap(row_sum, "c")
     heads = [heads] + [shift_x(heads, s) for s in range(1, NX)]
 
     g, n = GROWS, BLOCK
@@ -454,65 +448,42 @@
     up, down = shift_z(up, 2), shift_z(down, -2)
 
     pieces = [back[0]] + [shift_x(back[s], -s) for s in range(1, NX)]
-    summed, row_sum = call(
-        row_kernel,
-        [((rows, quarter), BF16), ((1, rows), F32)],
+    to_same, to_other, gain_z = call(
+        finish_kernel, [((n, HD), BF16)] * 2 + [((4, HD), F32)], [], ids, t0, a, b, up, down, c4, d4
+    )
+    gain_z, _ = lax.optimization_barrier((gain_z, swap(to_same[:g], "c")))
+    (grad_input,) = call(
+        input_kernel,
+        [((rows, quarter), F32)],
         [],
         ids,
         *pieces,
         tokens,
         gain_f,
         total,
-        static=width,
-    )
-    row_sum = row_sum + swap(row_sum, "c")
-    up, down, row_sum = lax.optimization_barrier((up, down, row_sum))
-    to_same, to_other, gain_z = call(
-        finish_kernel, [((n, HD), BF16)] * 2 + [((4, HD), F32)], [], ids, t0, a, b, up, down, c4, d4
-    )
-    gain_z, _ = lax.optimization_barrier((gain_z, swap(to_same[:g], "c")))
-    (grad_input,) = call(
-        input_kernel,
-        [((rows, quarter), F32)],
-        [],
-        ids,
-        summed,
-        tokens,
-        gain_f,
-        total,
         row_sum,
-        swap(row_sum, "yl"),
         static=width,
     )
     arrived = (lax.ppermute(to_same, AXES, inverse(owner_perm(0))), lax.ppermute(to_other, AXES, inverse(owner_perm(1))))
     gain_z = gain_z + swap(gain_z, "yh")
+    gain_x = [gain_z] + [shift_x(gain_z, s) for s in range(1, NX)]
     *arrived, grad_input, gain_z = lax.optimization_barrier((*arrived, grad_input, gain_z))
     (shared_own,) = call(shared_kernel, [((2 * PIECE, HD), BF16)], [], ids, *arrived)
     grad_query, grad_out = call(owner_kernel, [((HD, HD), F32)] * 2, [], ids, *arrived, static=loss_scale)
     shared_yl = swap(shared_own, "yl")
-    grad_key, grad_value = call(
+    grad_key, grad_value, grad_gain = call(
         join_kernel,
-        [((rows, HD), F32)] * 2,
+        [((rows, HD), F32)] * 2 + [((4 * NX, 1, HD), F32)],
         [],
         ids,
         shared_own,
         swap(shared_own, "c"),
         shared_yl,
         swap(shared_yl, "c"),
+        *gain_x,
         static=loss_scale,
     )
-
-    (grad_gain,) = call(
-        gain_kernel,
-        [((4 * NX, 1, HD), F32)],
-        [],
-        ids,
-        gain_z,
-        *[shift_x(gain_z, s) for s in range(1, NX)],
-        static=loss_scale,
-    )
     grad_gain = grad_gain.reshape(quarter)
-
     return (grad_input, grad_gain, grad_query, grad_key, grad_value, grad_out)
 
 

time: 163 us -> 153 us (0.939)
  waiting for transfers between devices: 76.3 us -> 67.5 us
  Pallas kernels: 20.2 us -> 18.2 us
    ppermute x15, waiting for transfers between devices: 37.5 us -> 29.9 us  [shift_x(): return lax.ppermute(value, 'x', [(i, (i + by) % NX) for i in range(NX)])]
    ppermute x12, waiting for transfers between devices: 14.3 us -> 17.8 us  [shift_z(): return lax.ppermute(value, 'z', [(i, (i + by) % NZ) for i in range(NZ)])]
    ppermute x15 -> x14, waiting for transfers between devices: 22.7 us -> 19.4 us  [swap(): return lax.ppermute(value, axis, [(0, 1), (1, 0)])]
    pallas_call x19 -> x17, Pallas kernels: 20.2 us -> 18.2 us  [call(): pl.pallas_call(body, out_shape=[jax.ShapeDtypeStruct(s, d) for s, d in ou...]
    ppermute x15 -> x14, starting transfers between devices: 8.3 us -> 9.08 us  [swap(): return lax.ppermute(value, axis, [(0, 1), (1, 0)])]
  transfers between devices with their start and end apart: 46 -> 45, of which waited for: 27 -> 24; matrix products, arithmetic and copies ran while one was open for 0% -> 0% of each run, Pallas kernels for 6% -> 5%
where the time goes in v2:
time: 153 us; the launch traced here: 151 us
  waiting for transfers between devices  67.5 us (44%)
  starting transfers between devices  61.1 us (40%)
  Pallas kernels  18.2 us (12%)
  local copies, waits for them, and re-layouts  2.9 us (2%)
    ppermute x15, waiting for transfers between devices, shift_x(): return lax.ppermute(value, 'x', [(i, (i + by) % NX) for i in range(NX)])  29.9 us
    ppermute x12, starting transfers between devices, shift_z(): return lax.ppermute(value, 'z', [(i, (i + by) % NZ) for i in range(NZ)])  24.7 us
    ppermute x15, starting transfers between devices, shift_x(): return lax.ppermute(value, 'x', [(i, (i + by) % NX) for i in range(NX)])  21.8 us
    ppermute x14, waiting for transfers between devices, swap(): return lax.ppermute(value, axis, [(0, 1), (1, 0)])  19.4 us
    pallas_call x17, Pallas kernels, call(): pl.pallas_call(body, out_shape=[jax.ShapeDtypeStruct(s, d) for s, d in ou...  18.2 us
    ppermute x12, waiting for transfers between devices, shift_z(): return lax.ppermute(value, 'z', [(i, (i + by) % NZ) for i in range(NZ)])  17.8 us
    ppermute x14, starting transfers between devices, swap(): return lax.ppermute(value, axis, [(0, 1), (1, 0)])  9.08 us
    ppermute x1, starting transfers between devices, local(): same = lax.ppermute(pack, AXES, owner_perm(0))  3.47 us
  transfers between devices with their start and end apart: 45, of which 24 were waited for; matrix products, arithmetic and copies ran while one was open for 0% of the time, Pallas kernels for 5%

profile of v2, /device:TPU:8, one launch (start us, length us, event | category | flops | bytes accessed | tf_op | source)
XLA Modules:
  0.0 151.4 jit_solution(11963451022356346440)
XLA Ops:
  2.1 3.5 %collective-permute-start = (bf16[320,128]{1,0:T(8,128)(2,1)S(1)}, bf16[320,128]{1,0:T(8,128)(2,1)S(1)}, u32[]{:S(2)}, u32[]{:S(2)}) collective-permute-start(bf16[320,128]{1,0:T(8,128)(2,1)S(1)} %pad_maximum_fusion), channel_id=1, source_target_pairs={{0,0},{1,4},{2,128},{3,132},{4,32},{5,36},{6,160},{7,164},{8,8},{9... | collective-permute-start | bytes 245768 | tf_op jit(solution)/shard_map/ppermute | solution.py:374
  11.7 3.3 %collective-permute-start.7 = (bf16[640,128]{1,0:T(8,128)(2,1)S(1)}, bf16[640,128]{1,0:T(8,128)(2,1)S(1)}, u32[]{:S(2)}, u32[]{:S(2)}) collective-permute-start(bf16[640,128]{1,0:T(8,128)(2,1)S(1)} %maximum_select_fusion.both), channel_id=1, source_target_pairs={{0,8},{4,12},{8,16},{12,20},{16,24},{20,28},{24,0},{28,4},{1,9},{5... | collective-permute-start | bytes 491528 | tf_op jit(solution)/shard_map/ppermute | solution.py:52
  15.0 3.1 %collective-permute-start.8 = (bf16[640,128]{1,0:T(8,128)(2,1)S(1)}, bf16[640,128]{1,0:T(8,128)(2,1)S(1)}, u32[]{:S(2)}, u32[]{:S(2)}) collective-permute-start(bf16[640,128]{1,0:T(8,128)(2,1)S(1)} %maximum_select_fusion.both), channel_id=1, source_target_pairs={{0,24},{4,28},{8,0},{12,4},{16,8},{20,12},{24,16},{28,20},{1,25},{... | collective-permute-start | bytes 491528 | tf_op jit(solution)/shard_map/ppermute | solution.py:52
  18.2 2.5 %collective-permute-start.3 = (f32[1,128]{1,0:T(1,128)S(1)}, f32[1,128]{1,0:T(1,128)S(1)}, u32[]{:S(2)}, u32[]{:S(2)}) collective-permute-start(f32[1,128]{1,0:T(1,128)S(1)} %add.21), channel_id=1, source_target_pairs={{0,2},{2,0},{1,3},{3,1},{4,6},{6,4},{5,7},{7,5},{8,10},{10,8},{9,1... | collective-permute-start | bytes 1544 | tf_op jit(solution)/shard_map/ppermute | solution.py:56
  22.8 4.5 %collective-permute-start.4 = (bf16[272,512]{1,0:T(8,128)(2,1)S(1)}, bf16[272,512]{1,0:T(8,128)(2,1)S(1)}, u32[]{:S(2)}, u32[]{:S(2)}) collective-permute-start(bf16[272,512]{1,0:T(8,128)(2,1)S(1)} %get-tuple-element.67), channel_id=1, source_target_pairs={{0,32},{32,64},{64,96},{96,0},{1,33},{33,65},{65,97},{97,1},{2,34}... | collective-permute-start | bytes 835592 | tf_op jit(solution)/shard_map/ppermute | solution.py:48
  27.3 2.3 %collective-permute-start.5 = (bf16[272,512]{1,0:T(8,128)(2,1)S(1)}, bf16[272,512]{1,0:T(8,128)(2,1)S(1)}, u32[]{:S(2)}, u32[]{:S(2)}) collective-permute-start(bf16[272,512]{1,0:T(8,128)(2,1)S(1)} %get-tuple-element.68), channel_id=1, source_target_pairs={{0,64},{32,96},{64,0},{96,32},{1,65},{33,97},{65,1},{97,33},{2,66}... | collective-permute-start | bytes 835592 | tf_op jit(solution)/shard_map/ppermute | solution.py:48
  33.0 6.4 %collective-permute-done.4.refs_1_ = bf16[272,512]{1,0:T(8,128)(2,1)S(1)} collective-permute-done((bf16[272,512]{1,0:T(8,128)(2,1)S(1)}, bf16[272,512]{1,0:T(8,128)(2,1)S(1)}, u32[]{:S(2)}, u32[]{:S(2)}) %collective-permute-start.4) | collective-permute-done | bytes 278560 | tf_op jit(solution)/shard_map/ppermute | solution.py:48
  40.4 3.1 %collective-permute-start.12 = (bf16[320,128]{1,0:T(8,128)(2,1)S(1)}, bf16[320,128]{1,0:T(8,128)(2,1)S(1)}, u32[]{:S(2)}, u32[]{:S(2)}) collective-permute-start(bf16[320,128]{1,0:T(8,128)(2,1)S(1)} %get-tuple-element.77), channel_id=1, source_target_pairs={{0,24},{4,28},{8,0},{12,4},{16,8},{20,12},{24,16},{28,20},{1,25},{... | collective-permute-start | bytes 245768 | tf_op jit(solution)/shard_map/ppermute | solution.py:52
  44.3 2.3 %collective-permute-done.11.far_first = bf16[320,128]{1,0:T(8,128)(2,1)S(1)} collective-permute-done((bf16[320,128]{1,0:T(8,128)(2,1)S(1)}, bf16[320,128]{1,0:T(8,128)(2,1)S(1)}, u32[]{:S(2)}, u32[]{:S(2)}) %collective-permute-start.11) | collective-permute-done | bytes 81952 | tf_op jit(solution)/shard_map/ppermute | solution.py:52
  50.2 1.9 %collective-permute-done.13.got = f32[512,640]{1,0:T(8,128)S(1)} collective-permute-done((f32[512,640]{1,0:T(8,128)S(1)}, f32[512,640]{1,0:T(8,128)S(1)}, u32[]{:S(2)}, u32[]{:S(2)}) %collective-permute-start.13) | collective-permute-done | bytes 1310752 | tf_op jit(solution)/shard_map/ppermute | solution.py:56
  53.0 1.7 %collective-permute-start.15 = (bf16[128,1024]{1,0:T(8,128)(2,1)S(1)}, bf16[128,1024]{1,0:T(8,128)(2,1)S(1)}, u32[]{:S(2)}, u32[]{:S(2)}) collective-permute-start(bf16[128,1024]{1,0:T(8,128)(2,1)S(1)} %get-tuple-element.83), channel_id=1, source_target_pairs={{0,64},{32,96},{64,0},{96,32},{1,65},{33,97},{65,1},{97,33},{2,66}... | collective-permute-start | bytes 786440 | tf_op jit(solution)/shard_map/ppermute | solution.py:48
  55.2 7.0 %collective-permute-done.14.a = bf16[128,1024]{1,0:T(8,128)(2,1)S(1)} collective-permute-done((bf16[128,1024]{1,0:T(8,128)(2,1)S(1)}, bf16[128,1024]{1,0:T(8,128)(2,1)S(1)}, u32[]{:S(2)}, u32[]{:S(2)}) %collective-permute-start.14) | collective-permute-done | bytes 262176 | tf_op jit(solution)/shard_map/ppermute | solution.py:48
  62.2 1.6 %collective-permute-done.15.b = bf16[128,1024]{1,0:T(8,128)(2,1)S(1)} collective-permute-done((bf16[128,1024]{1,0:T(8,128)(2,1)S(1)}, bf16[128,1024]{1,0:T(8,128)(2,1)S(1)}, u32[]{:S(2)}, u32[]{:S(2)}) %collective-permute-start.15) | collective-permute-done | bytes 262176 | tf_op jit(solution)/shard_map/ppermute | solution.py:48
  63.8 4.8 %collective-permute-done.16.c = bf16[128,1024]{1,0:T(8,128)(2,1)S(1)} collective-permute-done((bf16[128,1024]{1,0:T(8,128)(2,1)S(1)}, bf16[128,1024]{1,0:T(8,128)(2,1)S(1)}, u32[]{:S(2)}, u32[]{:S(2)}) %collective-permute-start.16) | collective-permute-done | bytes 262176 | tf_op jit(solution)/shard_map/ppermute | solution.py:48
  69.4 8.2 %collective-permute-done.17.got = bf16[128,1024]{1,0:T(8,128)(2,1)S(1)} collective-permute-done((bf16[128,1024]{1,0:T(8,128)(2,1)S(1)}, bf16[128,1024]{1,0:T(8,128)(2,1)S(1)}, u32[]{:S(2)}, u32[]{:S(2)}) %collective-permute-start.17) | collective-permute-done | bytes 262176 | tf_op jit(solution)/shard_map/ppermute | solution.py:56
  79.5 1.7 %shard_map.127 = (bf16[128,768]{1,0:T(8,128)(2,1)S(1)}, f32[1,128]{1,0:T(1,128)S(1)}) custom-call(s32[5]{0:T(128)S(1)} %stack.23.ids, bf16[128,512]{1,0:T(8,128)(2,1)S(1)} %get-tuple-element.85.qa, bf16[128,128]{1,0:T(8,128)(2,1)S(1)} %get-tuple-element.86.kv_mine, bf16[128,128]{1,0:T(8,128)(2,1)S(1)} %collective-permute-done.18.kv_theirs), custom_call_target="tpu_custom_call" | custom-call | tf_op jit(solution)/shard_map/pallas_call | solution.py:73
  81.3 1.8 %collective-permute-start.20 = (bf16[128,768]{1,0:T(8,128)(2,1)S(1)}, bf16[128,768]{1,0:T(8,128)(2,1)S(1)}, u32[]{:S(2)}, u32[]{:S(2)}) collective-permute-start(bf16[128,768]{1,0:T(8,128)(2,1)S(1)} %get-tuple-element.87.refs_0_), channel_id=1, source_target_pairs={{0,64},{32,96},{64,0},{96,32},{1,65},{33,97},{65,1},{97,33},{2,66}... | collective-permute-start | bytes 589832 | tf_op jit(solution)/shard_map/ppermute | solution.py:48
  83.1 2.2 %collective-permute-start.21 = (bf16[128,768]{1,0:T(8,128)(2,1)S(1)}, bf16[128,768]{1,0:T(8,128)(2,1)S(1)}, u32[]{:S(2)}, u32[]{:S(2)}) collective-permute-start(bf16[128,768]{1,0:T(8,128)(2,1)S(1)} %get-tuple-element.87.refs_0_), channel_id=1, source_target_pairs={{0,96},{32,0},{64,32},{96,64},{1,97},{33,1},{65,33},{97,65},{2,98}... | collective-permute-start | bytes 589832 | tf_op jit(solution)/shard_map/ppermute | solution.py:48
  85.2 8.4 %collective-permute-done.19.refs_1_ = bf16[128,768]{1,0:T(8,128)(2,1)S(1)} collective-permute-done((bf16[128,768]{1,0:T(8,128)(2,1)S(1)}, bf16[128,768]{1,0:T(8,128)(2,1)S(1)}, u32[]{:S(2)}, u32[]{:S(2)}) %collective-permute-start.19) | collective-permute-done | bytes 196640 | tf_op jit(solution)/shard_map/ppermute | solution.py:48
  95.7 2.8 %shard_map.128 = (bf16[656,128]{1,0:T(8,128)(2,1)S(1)}, bf16[1296,128]{1,0:T(8,128)(2,1)S(1)}, bf16[1296,128]{1,0:T(8,128)(2,1)S(1)}, bf16[640,128]{1,0:T(8,128)...) custom-call(s32[5]{0:T(128)S(1)} %stack.23.ids, ...), custom_call_target="tpu_custom_call" | custom-call | tf_op jit(solution)/shard_map/pallas_call | solution.py:73
  99.9 2.2 %collective-permute-start.27 = (bf16[1296,128]{1,0:T(8,128)(2,1)S(1)}, bf16[1296,128]{1,0:T(8,128)(2,1)S(1)}, u32[]{:S(2)}, u32[]{:S(2)}) collective-permute-start(bf16[1296,128]{1,0:T(8,128)(2,1)S(1)} %get-tuple-element.91), channel_id=1, source_target_pairs={{0,28},{4,0},{8,4},{12,8},{16,12},{20,16},{24,20},{28,24},{1,29},{... | collective-permute-start | bytes 995336 | tf_op jit(solution)/shard_map/ppermute | solution.py:52
  102.1 3.7 %collective-permute-start.28 = (bf16[336,128]{1,0:T(8,128)(2,1)S(1)}, bf16[336,128]{1,0:T(8,128)(2,1)S(1)}, u32[]{:S(2)}, u32[]{:S(2)}) collective-permute-start(bf16[336,128]{1,0:T(8,128)(2,1)S(1)} %get-tuple-element.94), channel_id=1, source_target_pairs={{0,8},{4,12},{8,16},{12,20},{16,24},{20,28},{24,0},{28,4},{1,9},{5... | collective-permute-start | bytes 258056 | tf_op jit(solution)/shard_map/ppermute | solution.py:52
  106.3 8.8 %collective-permute-done.28.c = bf16[336,128]{1,0:T(8,128)(2,1)S(1)} collective-permute-done((bf16[336,128]{1,0:T(8,128)(2,1)S(1)}, bf16[336,128]{1,0:T(8,128)(2,1)S(1)}, u32[]{:S(2)}, u32[]{:S(2)}) %collective-permute-start.28) | collective-permute-done | bytes 86048 | tf_op jit(solution)/shard_map/ppermute | solution.py:52
  115.0 2.0 %collective-permute-done.29.d = bf16[336,128]{1,0:T(8,128)(2,1)S(1)} collective-permute-done((bf16[336,128]{1,0:T(8,128)(2,1)S(1)}, bf16[336,128]{1,0:T(8,128)(2,1)S(1)}, u32[]{:S(2)}, u32[]{:S(2)}) %collective-permute-start.29) | collective-permute-done | bytes 86048 | tf_op jit(solution)/shard_map/ppermute | solution.py:52
  119.1 2.9 %collective-permute-start.31 = (bf16[672,128]{1,0:T(8,128)(2,1)S(1)}, bf16[672,128]{1,0:T(8,128)(2,1)S(1)}, u32[]{:S(2)}, u32[]{:S(2)}) collective-permute-start(bf16[672,128]{1,0:T(8,128)(2,1)S(1)} %get-tuple-element.97), channel_id=1, source_target_pairs={{0,24},{4,28},{8,0},{12,4},{16,8},{20,12},{24,16},{28,20},{1,25},{... | collective-permute-start | bytes 516104 | tf_op jit(solution)/shard_map/ppermute | solution.py:52
  121.9 2.3 %collective-permute-start.34 = (bf16[128,512]{1,0:T(8,128)(2,1)S(1)}, bf16[128,512]{1,0:T(8,128)(2,1)S(1)}, u32[]{:S(2)}, u32[]{:S(2)}) collective-permute-start(bf16[128,512]{1,0:T(8,128)(2,1)S(1)} %get-tuple-element.101), channel_id=1, source_target_pairs={{0,96},{32,0},{64,32},{96,64},{1,97},{33,1},{65,33},{97,65},{2,98}... | collective-permute-start | bytes 393224 | tf_op jit(solution)/shard_map/ppermute | solution.py:48
  125.1 3.3 %collective-permute-done.30.up = bf16[672,128]{1,0:T(8,128)(2,1)S(1)} collective-permute-done((bf16[672,128]{1,0:T(8,128)(2,1)S(1)}, bf16[672,128]{1,0:T(8,128)(2,1)S(1)}, u32[]{:S(2)}, u32[]{:S(2)}) %collective-permute-start.30) | collective-permute-done | bytes 172064 | tf_op jit(solution)/shard_map/ppermute | solution.py:52
  129.6 1.9 %collective-permute-start.32 = (bf16[320,128]{1,0:T(8,128)(2,1)S(1)}, bf16[320,128]{1,0:T(8,128)(2,1)S(1)}, u32[]{:S(2)}, u32[]{:S(2)}) collective-permute-start(bf16[320,128]{1,0:T(8,128)(2,1)S(1)} %get-tuple-element.98), channel_id=1, source_target_pairs={{0,0},{4,1},{128,2},{132,3},{32,4},{36,5},{160,6},{164,7},{8,8},{1... | collective-permute-start | bytes 245768 | tf_op jit(solution)/shard_map/ppermute | solution.py:467
  131.6 3.5 %collective-permute-start.38 = (f32[4,128]{1,0:T(4,128)S(1)}, f32[4,128]{1,0:T(4,128)S(1)}, u32[]{:S(2)}, u32[]{:S(2)}) collective-permute-start(f32[4,128]{1,0:T(4,128)S(1)} %get-tuple-element.105), channel_id=1, source_target_pairs={{0,128},{128,0},{1,129},{129,1},{2,130},{130,2},{3,131},{131,3},{4... | collective-permute-start | bytes 6152 | tf_op jit(solution)/shard_map/ppermute | solution.py:56
  135.1 1.9 %shard_map.131 = f32[128,2048]{1,0:T(8,128)} custom-call(s32[5]{0:T(128)S(1)} %stack.23.ids, bf16[128,512]{1,0:T(8,128)(2,1)S(1)} %get-tuple-element.100.a, bf16[128,512]{1,0:T(8,128)(2,1)S(1)} %collective-permute-done.34.b, bf16[128,512]{1,0:T(8,128)(2,1)S(1)} %collective-permute-done.35.c, bf16[128,512]{1,0:T(8,128)(2,1)S(1)} %collective-permute-done.36.d, ...), custom_call_target="tpu_custom_call" | custom-call | tf_op jit(solution)/shard_map/pallas_call | solution.py:73
  139.6 3.1 %collective-permute-done.40.by_yl = bf16[64,128]{1,0:T(8,128)(2,1)S(1)} collective-permute-done((bf16[64,128]{1,0:T(8,128)(2,1)S(1)}, bf16[64,128]{1,0:T(8,128)(2,1)S(1)}, u32[]{:S(2)}, u32[]{:S(2)}) %collective-permute-start.40) | collective-permute-done | bytes 16416 | tf_op jit(solution)/shard_map/ppermute | solution.py:56
  143.4 3.2 %collective-permute-start.43 = (f32[4,128]{1,0:T(4,128)S(1)}, f32[4,128]{1,0:T(4,128)S(1)}, u32[]{:S(2)}, u32[]{:S(2)}) collective-permute-start(f32[4,128]{1,0:T(4,128)S(1)} %add.24.g0), channel_id=1, source_target_pairs={{0,64},{32,96},{64,0},{96,32},{1,65},{33,97},{65,1},{97,33},{2,66}... | collective-permute-start | bytes 6152 | tf_op jit(solution)/shard_map/ppermute | solution.py:48
  (92 shorter events, 38.8 us)
Async XLA Ops:
  2.1 9.1 %collective-permute-start = (bf16[320,128]{1,0:T(8,128)(2,1)S(1)}, bf16[320,128]{1,0:T(8,128)(2,1)S(1)}, u32[]{:S(2)}, u32[]{:S(2)}) collective-permute-start(bf16[320,128]{1,0:T(8,128)(2,1)S(1)} %pad_maximum_fusion), channel_id=1, source_target_pairs={{0,0},{1,4},{2,128},{3,132},{4,32},{5,36},{6,160},{7,164},{8,8},{9... | collective-permute-start | bytes 245768 | tf_op jit(solution)/shard_map/ppermute | solution.py:374
  11.7 17.9 %collective-permute-start.7 = (bf16[640,128]{1,0:T(8,128)(2,1)S(1)}, bf16[640,128]{1,0:T(8,128)(2,1)S(1)}, u32[]{:S(2)}, u32[]{:S(2)}) collective-permute-start(bf16[640,128]{1,0:T(8,128)(2,1)S(1)} %maximum_select_fusion.both), channel_id=1, source_target_pairs={{0,8},{4,12},{8,16},{12,20},{16,24},{20,28},{24,0},{28,4},{1,9},{5... | collective-permute-start | bytes 491528 | tf_op jit(solution)/shard_map/ppermute | solution.py:52
  15.0 14.5 %collective-permute-start.8 = (bf16[640,128]{1,0:T(8,128)(2,1)S(1)}, bf16[640,128]{1,0:T(8,128)(2,1)S(1)}, u32[]{:S(2)}, u32[]{:S(2)}) collective-permute-start(bf16[640,128]{1,0:T(8,128)(2,1)S(1)} %maximum_select_fusion.both), channel_id=1, source_target_pairs={{0,24},{4,28},{8,0},{12,4},{16,8},{20,12},{24,16},{28,20},{1,25},{... | collective-permute-start | bytes 491528 | tf_op jit(solution)/shard_map/ppermute | solution.py:52
  22.8 16.6 %collective-permute-start.4 = (bf16[272,512]{1,0:T(8,128)(2,1)S(1)}, bf16[272,512]{1,0:T(8,128)(2,1)S(1)}, u32[]{:S(2)}, u32[]{:S(2)}) collective-permute-start(bf16[272,512]{1,0:T(8,128)(2,1)S(1)} %get-tuple-element.67), channel_id=1, source_target_pairs={{0,32},{32,64},{64,96},{96,0},{1,33},{33,65},{65,97},{97,1},{2,34}... | collective-permute-start | bytes 835592 | tf_op jit(solution)/shard_map/ppermute | solution.py:48
  27.3 13.2 %collective-permute-start.5 = (bf16[272,512]{1,0:T(8,128)(2,1)S(1)}, bf16[272,512]{1,0:T(8,128)(2,1)S(1)}, u32[]{:S(2)}, u32[]{:S(2)}) collective-permute-start(bf16[272,512]{1,0:T(8,128)(2,1)S(1)} %get-tuple-element.68), channel_id=1, source_target_pairs={{0,64},{32,96},{64,0},{96,32},{1,65},{33,97},{65,1},{97,33},{2,66}... | collective-permute-start | bytes 835592 | tf_op jit(solution)/shard_map/ppermute | solution.py:48
  30.2 17.3 %collective-permute-start.10 = (bf16[1280,128]{1,0:T(8,128)(2,1)S(1)}, bf16[1280,128]{1,0:T(8,128)(2,1)S(1)}, u32[]{:S(2)}, u32[]{:S(2)}) collective-permute-start(bf16[1280,128]{1,0:T(8,128)(2,1)S(1)} %get-tuple-element.75), channel_id=1, source_target_pairs={{0,28},{4,0},{8,4},{12,8},{16,12},{20,16},{24,20},{28,24},{1,29},{... | collective-permute-start | bytes 983048 | tf_op jit(solution)/shard_map/ppermute | solution.py:52
  31.5 16.0 %collective-permute-start.9 = (bf16[1280,128]{1,0:T(8,128)(2,1)S(1)}, bf16[1280,128]{1,0:T(8,128)(2,1)S(1)}, u32[]{:S(2)}, u32[]{:S(2)}) collective-permute-start(bf16[1280,128]{1,0:T(8,128)(2,1)S(1)} %get-tuple-element.74), channel_id=1, source_target_pairs={{0,4},{4,8},{8,12},{12,16},{16,20},{20,24},{24,28},{28,0},{1,5},{5... | collective-permute-start | bytes 983048 | tf_op jit(solution)/shard_map/ppermute | solution.py:52
  32.3 11.2 %collective-permute-start.6 = (bf16[272,512]{1,0:T(8,128)(2,1)S(1)}, bf16[272,512]{1,0:T(8,128)(2,1)S(1)}, u32[]{:S(2)}, u32[]{:S(2)}) collective-permute-start(bf16[272,512]{1,0:T(8,128)(2,1)S(1)} %get-tuple-element.69), channel_id=1, source_target_pairs={{0,96},{32,0},{64,32},{96,64},{1,97},{33,1},{65,33},{97,65},{2,98}... | collective-permute-start | bytes 835592 | tf_op jit(solution)/shard_map/ppermute | solution.py:48
  39.4 7.3 %collective-permute-start.11 = (bf16[320,128]{1,0:T(8,128)(2,1)S(1)}, bf16[320,128]{1,0:T(8,128)(2,1)S(1)}, u32[]{:S(2)}, u32[]{:S(2)}) collective-permute-start(bf16[320,128]{1,0:T(8,128)(2,1)S(1)} %get-tuple-element.76), channel_id=1, source_target_pairs={{0,8},{4,12},{8,16},{12,20},{16,24},{20,28},{24,0},{28,4},{1,9},{5... | collective-permute-start | bytes 245768 | tf_op jit(solution)/shard_map/ppermute | solution.py:52
  40.4 7.1 %collective-permute-start.12 = (bf16[320,128]{1,0:T(8,128)(2,1)S(1)}, bf16[320,128]{1,0:T(8,128)(2,1)S(1)}, u32[]{:S(2)}, u32[]{:S(2)}) collective-permute-start(bf16[320,128]{1,0:T(8,128)(2,1)S(1)} %get-tuple-element.77), channel_id=1, source_target_pairs={{0,24},{4,28},{8,0},{12,4},{16,8},{20,12},{24,16},{28,20},{1,25},{... | collective-permute-start | bytes 245768 | tf_op jit(solution)/shard_map/ppermute | solution.py:52
  52.8 9.4 %collective-permute-start.14 = (bf16[128,1024]{1,0:T(8,128)(2,1)S(1)}, bf16[128,1024]{1,0:T(8,128)(2,1)S(1)}, u32[]{:S(2)}, u32[]{:S(2)}) collective-permute-start(bf16[128,1024]{1,0:T(8,128)(2,1)S(1)} %get-tuple-element.82), channel_id=1, source_target_pairs={{0,96},{32,0},{64,32},{96,64},{1,97},{33,1},{65,33},{97,65},{2,98}... | collective-permute-start | bytes 786440 | tf_op jit(solution)/shard_map/ppermute | solution.py:48
  53.0 10.8 %collective-permute-start.15 = (bf16[128,1024]{1,0:T(8,128)(2,1)S(1)}, bf16[128,1024]{1,0:T(8,128)(2,1)S(1)}, u32[]{:S(2)}, u32[]{:S(2)}) collective-permute-start(bf16[128,1024]{1,0:T(8,128)(2,1)S(1)} %get-tuple-element.83), channel_id=1, source_target_pairs={{0,64},{32,96},{64,0},{96,32},{1,65},{33,97},{65,1},{97,33},{2,66}... | collective-permute-start | bytes 786440 | tf_op jit(solution)/shard_map/ppermute | solution.py:48
  54.8 13.8 %collective-permute-start.16 = (bf16[128,1024]{1,0:T(8,128)(2,1)S(1)}, bf16[128,1024]{1,0:T(8,128)(2,1)S(1)}, u32[]{:S(2)}, u32[]{:S(2)}) collective-permute-start(bf16[128,1024]{1,0:T(8,128)(2,1)S(1)} %get-tuple-element.84), channel_id=1, source_target_pairs={{0,32},{32,64},{64,96},{96,0},{1,33},{33,65},{65,97},{97,1},{2,34}... | collective-permute-start | bytes 786440 | tf_op jit(solution)/shard_map/ppermute | solution.py:48
  69.3 8.3 %collective-permute-start.17 = (bf16[128,1024]{1,0:T(8,128)(2,1)S(1)}, bf16[128,1024]{1,0:T(8,128)(2,1)S(1)}, u32[]{:S(2)}, u32[]{:S(2)}) collective-permute-start(bf16[128,1024]{1,0:T(8,128)(2,1)S(1)} %shard_map.125.mine), channel_id=1, source_target_pairs={{0,2},{2,0},{1,3},{3,1},{4,6},{6,4},{5,7},{7,5},{8,10},{10,8},{9,1... | collective-permute-start | bytes 786440 | tf_op jit(solution)/shard_map/ppermute | solution.py:56
  81.2 12.5 %collective-permute-start.19 = (bf16[128,768]{1,0:T(8,128)(2,1)S(1)}, bf16[128,768]{1,0:T(8,128)(2,1)S(1)}, u32[]{:S(2)}, u32[]{:S(2)}) collective-permute-start(bf16[128,768]{1,0:T(8,128)(2,1)S(1)} %get-tuple-element.87.refs_0_), channel_id=1, source_target_pairs={{0,32},{32,64},{64,96},{96,0},{1,33},{33,65},{65,97},{97,1},{2,34}... | collective-permute-start | bytes 589832 | tf_op jit(solution)/shard_map/ppermute | solution.py:48
  81.3 12.4 %collective-permute-start.20 = (bf16[128,768]{1,0:T(8,128)(2,1)S(1)}, bf16[128,768]{1,0:T(8,128)(2,1)S(1)}, u32[]{:S(2)}, u32[]{:S(2)}) collective-permute-start(bf16[128,768]{1,0:T(8,128)(2,1)S(1)} %get-tuple-element.87.refs_0_), channel_id=1, source_target_pairs={{0,64},{32,96},{64,0},{96,32},{1,65},{33,97},{65,1},{97,33},{2,66}... | collective-permute-start | bytes 589832 | tf_op jit(solution)/shard_map/ppermute | solution.py:48
  83.1 11.2 %collective-permute-start.21 = (bf16[128,768]{1,0:T(8,128)(2,1)S(1)}, bf16[128,768]{1,0:T(8,128)(2,1)S(1)}, u32[]{:S(2)}, u32[]{:S(2)}) collective-permute-start(bf16[128,768]{1,0:T(8,128)(2,1)S(1)} %get-tuple-element.87.refs_0_), channel_id=1, source_target_pairs={{0,96},{32,0},{64,32},{96,64},{1,97},{33,1},{65,33},{97,65},{2,98}... | collective-permute-start | bytes 589832 | tf_op jit(solution)/shard_map/ppermute | solution.py:48
  85.2 9.0 %collective-permute-start.22 = (bf16[128,768]{1,0:T(8,128)(2,1)S(1)}, bf16[128,768]{1,0:T(8,128)(2,1)S(1)}, u32[]{:S(2)}, u32[]{:S(2)}) collective-permute-start(bf16[128,768]{1,0:T(8,128)(2,1)S(1)} %get-tuple-element.87.refs_0_), channel_id=1, source_target_pairs={{0,1},{1,0},{2,3},{3,2},{4,5},{5,4},{6,7},{7,6},{8,9},{9,8},{10,11... | collective-permute-start | bytes 589832 | tf_op jit(solution)/shard_map/ppermute | solution.py:56
  98.5 18.6 %collective-permute-start.26 = (bf16[1296,128]{1,0:T(8,128)(2,1)S(1)}, bf16[1296,128]{1,0:T(8,128)(2,1)S(1)}, u32[]{:S(2)}, u32[]{:S(2)}) collective-permute-start(bf16[1296,128]{1,0:T(8,128)(2,1)S(1)} %get-tuple-element.90), channel_id=1, source_target_pairs={{0,4},{4,8},{8,12},{12,16},{16,20},{20,24},{24,28},{28,0},{1,5},{5... | collective-permute-start | bytes 995336 | tf_op jit(solution)/shard_map/ppermute | solution.py:52
  99.9 17.1 %collective-permute-start.27 = (bf16[1296,128]{1,0:T(8,128)(2,1)S(1)}, bf16[1296,128]{1,0:T(8,128)(2,1)S(1)}, u32[]{:S(2)}, u32[]{:S(2)}) collective-permute-start(bf16[1296,128]{1,0:T(8,128)(2,1)S(1)} %get-tuple-element.91), channel_id=1, source_target_pairs={{0,28},{4,0},{8,4},{12,8},{16,12},{20,16},{24,20},{28,24},{1,29},{... | collective-permute-start | bytes 995336 | tf_op jit(solution)/shard_map/ppermute | solution.py:52
  102.1 12.9 %collective-permute-start.28 = (bf16[336,128]{1,0:T(8,128)(2,1)S(1)}, bf16[336,128]{1,0:T(8,128)(2,1)S(1)}, u32[]{:S(2)}, u32[]{:S(2)}) collective-permute-start(bf16[336,128]{1,0:T(8,128)(2,1)S(1)} %get-tuple-element.94), channel_id=1, source_target_pairs={{0,8},{4,12},{8,16},{12,20},{16,24},{20,28},{24,0},{28,4},{1,9},{5... | collective-permute-start | bytes 258056 | tf_op jit(solution)/shard_map/ppermute | solution.py:52
  105.8 11.3 %collective-permute-start.29 = (bf16[336,128]{1,0:T(8,128)(2,1)S(1)}, bf16[336,128]{1,0:T(8,128)(2,1)S(1)}, u32[]{:S(2)}, u32[]{:S(2)}) collective-permute-start(bf16[336,128]{1,0:T(8,128)(2,1)S(1)} %get-tuple-element.95), channel_id=1, source_target_pairs={{0,24},{4,28},{8,0},{12,4},{16,8},{20,12},{24,16},{28,20},{1,25},{... | collective-permute-start | bytes 258056 | tf_op jit(solution)/shard_map/ppermute | solution.py:52
  117.7 10.7 %collective-permute-start.30 = (bf16[672,128]{1,0:T(8,128)(2,1)S(1)}, bf16[672,128]{1,0:T(8,128)(2,1)S(1)}, u32[]{:S(2)}, u32[]{:S(2)}) collective-permute-start(bf16[672,128]{1,0:T(8,128)(2,1)S(1)} %get-tuple-element.96), channel_id=1, source_target_pairs={{0,8},{4,12},{8,16},{12,20},{16,24},{20,28},{24,0},{28,4},{1,9},{5... | collective-permute-start | bytes 516104 | tf_op jit(solution)/shard_map/ppermute | solution.py:52
  119.1 9.9 %collective-permute-start.31 = (bf16[672,128]{1,0:T(8,128)(2,1)S(1)}, bf16[672,128]{1,0:T(8,128)(2,1)S(1)}, u32[]{:S(2)}, u32[]{:S(2)}) collective-permute-start(bf16[672,128]{1,0:T(8,128)(2,1)S(1)} %get-tuple-element.97), channel_id=1, source_target_pairs={{0,24},{4,28},{8,0},{12,4},{16,8},{20,12},{24,16},{28,20},{1,25},{... | collective-permute-start | bytes 516104 | tf_op jit(solution)/shard_map/ppermute | solution.py:52
  121.9 9.7 %collective-permute-start.34 = (bf16[128,512]{1,0:T(8,128)(2,1)S(1)}, bf16[128,512]{1,0:T(8,128)(2,1)S(1)}, u32[]{:S(2)}, u32[]{:S(2)}) collective-permute-start(bf16[128,512]{1,0:T(8,128)(2,1)S(1)} %get-tuple-element.101), channel_id=1, source_target_pairs={{0,96},{32,0},{64,32},{96,64},{1,97},{33,1},{65,33},{97,65},{2,98}... | collective-permute-start | bytes 393224 | tf_op jit(solution)/shard_map/ppermute | solution.py:48
  124.2 10.9 %collective-permute-start.35 = (bf16[128,512]{1,0:T(8,128)(2,1)S(1)}, bf16[128,512]{1,0:T(8,128)(2,1)S(1)}, u32[]{:S(2)}, u32[]{:S(2)}) collective-permute-start(bf16[128,512]{1,0:T(8,128)(2,1)S(1)} %get-tuple-element.102), channel_id=1, source_target_pairs={{0,64},{32,96},{64,0},{96,32},{1,65},{33,97},{65,1},{97,33},{2,66}... | collective-permute-start | bytes 393224 | tf_op jit(solution)/shard_map/ppermute | solution.py:48
  124.2 10.9 %collective-permute-start.36 = (bf16[128,512]{1,0:T(8,128)(2,1)S(1)}, bf16[128,512]{1,0:T(8,128)(2,1)S(1)}, u32[]{:S(2)}, u32[]{:S(2)}) collective-permute-start(bf16[128,512]{1,0:T(8,128)(2,1)S(1)} %get-tuple-element.103), channel_id=1, source_target_pairs={{0,32},{32,64},{64,96},{96,0},{1,33},{33,65},{65,97},{97,1},{2,34}... | collective-permute-start | bytes 393224 | tf_op jit(solution)/shard_map/ppermute | solution.py:48
  129.6 8.7 %collective-permute-start.32 = (bf16[320,128]{1,0:T(8,128)(2,1)S(1)}, bf16[320,128]{1,0:T(8,128)(2,1)S(1)}, u32[]{:S(2)}, u32[]{:S(2)}) collective-permute-start(bf16[320,128]{1,0:T(8,128)(2,1)S(1)} %get-tuple-element.98), channel_id=1, source_target_pairs={{0,0},{4,1},{128,2},{132,3},{32,4},{36,5},{160,6},{164,7},{8,8},{1... | collective-permute-start | bytes 245768 | tf_op jit(solution)/shard_map/ppermute | solution.py:467
  131.5 6.8 %collective-permute-start.33 = (bf16[320,128]{1,0:T(8,128)(2,1)S(1)}, bf16[320,128]{1,0:T(8,128)(2,1)S(1)}, u32[]{:S(2)}, u32[]{:S(2)}) collective-permute-start(bf16[320,128]{1,0:T(8,128)(2,1)S(1)} %get-tuple-element.99), channel_id=1, source_target_pairs={{128,0},{132,1},{0,2},{4,3},{160,4},{164,5},{32,6},{36,7},{136,8},... | collective-permute-start | bytes 245768 | tf_op jit(solution)/shard_map/ppermute | solution.py:467
  131.6 6.7 %collective-permute-start.38 = (f32[4,128]{1,0:T(4,128)S(1)}, f32[4,128]{1,0:T(4,128)S(1)}, u32[]{:S(2)}, u32[]{:S(2)}) collective-permute-start(f32[4,128]{1,0:T(4,128)S(1)} %get-tuple-element.105), channel_id=1, source_target_pairs={{0,128},{128,0},{1,129},{129,1},{2,130},{130,2},{3,131},{131,3},{4... | collective-permute-start | bytes 6152 | tf_op jit(solution)/shard_map/ppermute | solution.py:56
  139.6 10.6 %collective-permute-start.39 = (bf16[64,128]{1,0:T(8,128)(2,1)S(1)}, bf16[64,128]{1,0:T(8,128)(2,1)S(1)}, u32[]{:S(2)}, u32[]{:S(2)}) collective-permute-start(bf16[64,128]{1,0:T(8,128)(2,1)S(1)} %shard_map.132.own), channel_id=1, source_target_pairs={{0,1},{1,0},{2,3},{3,2},{4,5},{5,4},{6,7},{7,6},{8,9},{9,8},{10,11... | collective-permute-start | bytes 49160 | tf_op jit(solution)/shard_map/ppermute | solution.py:56
  142.7 7.5 %collective-permute-start.41 = (bf16[64,128]{1,0:T(8,128)(2,1)S(1)}, bf16[64,128]{1,0:T(8,128)(2,1)S(1)}, u32[]{:S(2)}, u32[]{:S(2)}) collective-permute-start(bf16[64,128]{1,0:T(8,128)(2,1)S(1)} %collective-permute-done.40.by_yl), channel_id=1, source_target_pairs={{0,1},{1,0},{2,3},{3,2},{4,5},{5,4},{6,7},{7,6},{8,9},{9,8},{10,11... | collective-permute-start | bytes 49160 | tf_op jit(solution)/shard_map/ppermute | solution.py:56
  (17 other events, 117.4 us)

commit v3 on v2

--- a/solution.py
+++ b/solution.py
@@ -260,7 +260,7 @@
     for s in range(NX):
         rows = slice(s * HD, (s + 1) * HD)
         term = dot(heads[rows], w_all[...], 1, 1)
-        back[s][...] = term.astype(BF16)
+        back[s][:HD] = term.astype(BF16)
         gain_sum = gain_sum + jnp.sum(term * unit[rows], axis=0, keepdims=True)
     gain_rows = jnp.concatenate([gain_sum[:, j * HD : (j + 1) * HD] for j in range(4)], axis=0)
     high = gain_rows.astype(BF16).astype(F32)
@@ -292,35 +292,50 @@
             out[2 * HD + PIECE :] = part[:, HD:]
 
 
-def relay_kernel(ids, t2, m2, a, b, c, d, up, down):
+def relay_kernel(ids, t2, m2, a, b, c, d, t0, *refs):
+    up, down, *back = refs[NX:]
     g, n = GROWS, BLOCK
-    up[:g] = a[:g]
-    up[g : 2 * g] = c[:g]
-    down[:g] = b[:g]
-    down[g : 2 * g] = d[:g]
     total = t2[...].astype(F32) + a[g + 2 * n :].astype(F32)
-    up[2 * g : 2 * g + n] = (total[:n] + c[g:].astype(F32)).astype(BF16)
-    up[2 * g + n :] = total[n:].astype(BF16)
+    up[:n] = (total[:n] + c[g:].astype(F32)).astype(BF16)
+    up[n:] = total[n:].astype(BF16)
     total = m2[...].astype(F32) + b[g + 2 * n :].astype(F32)
-    down[2 * g : 2 * g + n] = total[:n].astype(BF16)
-    down[2 * g + n :] = (total[n:] + d[g:].astype(F32)).astype(BF16)
-
-
-def finish_kernel(ids, t0, a, b, up, down, c, d, same, other, gain_out):
+    down[:n] = total[:n].astype(BF16)
+    down[n:] = (total[n:] + d[g:].astype(F32)).astype(BF16)
+    three = t0[:g].astype(F32) + a[:g].astype(F32) + b[:g].astype(F32)
+    five = three + c[:g].astype(F32) + d[:g].astype(F32)
+    terms = []
+    for rows in (five, three):
+        value = rows[:4] + rows[4:8]
+        high = value.astype(BF16).astype(F32)
+        terms += [high, value - high]
+    for j in range(4):
+        rows = jnp.concatenate([t[j : j + 1] for t in terms] + [jnp.zeros((g - 4, HD), F32)], axis=0).astype(BF16)
+        for ref in back:
+            ref[HD:, j * HD : (j + 1) * HD] = rows
+
+
+def finish_kernel(ids, t0, a, b, up, down, same, other):
     g, n = GROWS, BLOCK
     flip = ids[3]
     near = slice(g, g + 2 * n)
     total = t0[near].astype(F32) + a[near].astype(F32) + b[near].astype(F32)
-    total = total + up[2 * g :].astype(F32) + down[2 * g :].astype(F32)
+    total = total + up[...].astype(F32) + down[...].astype(F32)
     same[...] = jnp.where(flip == 0, total[:n], total[n:]).astype(BF16)
     other[...] = jnp.where(flip == 0, total[n:], total[:n]).astype(BF16)
-    rows = up[g : 2 * g].astype(F32)
-    for ref in (t0, a, b, c, d, up, down):
-        rows = rows + ref[:g].astype(F32)
-    gain_out[...] = rows[:4] + rows[4:8]
-
-
-def input_kernel(width, ids, a, b, c, d, tokens, gain, total, row_sum, out):
+
+
+def gain_kernel(ids, *refs):
+    five, three = refs[NX:]
+    for s in range(NX):
+        rows = refs[s][HD:].astype(F32)
+        for out, at in ((five, 0), (three, 2)):
+            value = rows[at : at + 1] + rows[at + 1 : at + 2]
+            for j in range(4):
+                out[4 * s + j : 4 * s + j + 1] = value[:, j * HD : (j + 1) * HD]
+
+
+def input_kernel(sizes, ids, a, b, c, d, tokens, gain, total, row_sum, same, other, out, grad_query, grad_out):
+    width, scale = sizes
     inv = lax.rsqrt(jnp.transpose(jnp.broadcast_to(total[...], (HD, HD))) / width + 1e-05)
     row_mean = jnp.transpose(jnp.broadcast_to(row_sum[...], (HD, HD))) / width
     for s, ref in enumerate((a, b, c, d)):
@@ -328,29 +343,26 @@
         for j in range(4):
             cols = lanes(feature(at, j))
             unit = tokens[:, cols].astype(F32) * inv
-            scaled = ref[:, j * HD : (j + 1) * HD].astype(F32) * gain[:, cols]
+            scaled = ref[:HD, j * HD : (j + 1) * HD].astype(F32) * gain[:, cols]
             out[:, cols] = inv * (scaled - unit * row_mean)
-
-
-def owner_kernel(scale, ids, a, b, grad_query, grad_out):
-    for out, rows in ((grad_query, slice(0, HD)), (grad_out, slice(HD, 2 * HD))):
-        out[...] = (a[rows].astype(F32) + b[rows].astype(F32)) * scale
+    for grad, at in ((grad_query, slice(0, HD)), (grad_out, slice(HD, 2 * HD))):
+        grad[...] = (same[at].astype(F32) + other[at].astype(F32)) * scale
 
 
 def shared_kernel(ids, a, b, shared):
     shared[...] = (a[2 * HD :].astype(F32) + b[2 * HD :].astype(F32)).astype(BF16)
 
 
-def join_kernel(scale, ids, own, by_c, by_yl, by_both, g0, g1, g2, g3, grad_key, grad_value, grad_gain):
+def join_kernel(scale, ids, own, by_c, by_yl, by_both, gains, grad_key, grad_value, grad_gain):
     yl, c, x = ids[1], ids[2], ids[4]
     for ref, at in ((own, 2 * yl + c), (by_c, 2 * yl + 1 - c), (by_yl, 2 - 2 * yl + c), (by_both, 3 - 2 * yl - c)):
         rows = pl.ds(pl.multiple_of(at * PIECE, PIECE), PIECE)
         grad_key[rows] = ref[:PIECE].astype(F32) * scale
         grad_value[rows] = ref[PIECE:].astype(F32) * scale
-    for s, ref in enumerate((g0, g1, g2, g3)):
-        at = (x - s + NX) % NX
+    for s in range(NX):
+        at = (x + s) % NX
         for j in range(4):
-            grad_gain[(at // 2) * 8 + 2 * j + at % 2] = ref[j : j + 1] * scale
+            grad_gain[(at // 2) * 8 + 2 * j + at % 2] = gains[4 * s + j : 4 * s + j + 1] * scale
 
 
 def local(tokens, gain, w_query, w_key, w_value, w_out, cotangent):
@@ -432,7 +444,7 @@
             ((g + n, HD), BF16),
             ((g + n, HD), BF16),
         ]
-        + [((rows, sub), BF16)] * 4,
+        + [((rows + GROWS, sub), BF16)] * 4,
         [((512, 6 * HD), BF16), ((512, 4 * HD), BF16), ((sub, 2 * HD), F32)],
         ids,
         *heads,
@@ -444,17 +456,34 @@
     )
     c4, d4 = shift_z(t4a, 2), shift_z(t4b, -2)
     a, b = shift_z(up, 1), shift_z(down, -1)
-    up, down = call(relay_kernel, [((2 * g + 2 * n, HD), BF16)] * 2, [], ids, t2, m2, a, b, c4, d4)
+    up, down, *back = call(
+        relay_kernel,
+        [((2 * n, HD), BF16)] * 2 + [((rows + g, sub), BF16)] * 4,
+        [],
+        ids,
+        t2,
+        m2,
+        a,
+        b,
+        c4,
+        d4,
+        t0,
+        *back,
+        aliases={8 + s: 2 + s for s in range(NX)},
+    )
     up, down = shift_z(up, 2), shift_z(down, -2)
 
     pieces = [back[0]] + [shift_x(back[s], -s) for s in range(1, NX)]
-    to_same, to_other, gain_z = call(
-        finish_kernel, [((n, HD), BF16)] * 2 + [((4, HD), F32)], [], ids, t0, a, b, up, down, c4, d4
-    )
-    gain_z, _ = lax.optimization_barrier((gain_z, swap(to_same[:g], "c")))
-    (grad_input,) = call(
+    to_same, to_other = call(finish_kernel, [((n, HD), BF16)] * 2, [], ids, t0, a, b, up, down)
+    arrived = (lax.ppermute(to_same, AXES, inverse(owner_perm(0))), lax.ppermute(to_other, AXES, inverse(owner_perm(1))))
+    gain_five, gain_three = call(gain_kernel, [((4 * NX, HD), F32)] * 2, [], ids, *pieces)
+    gain_z = gain_five + shift_z(gain_three, 4)
+    *arrived, gain_z = lax.optimization_barrier((*arrived, gain_z))
+    gain_z = gain_z + swap(gain_z, "yh")
+    (shared_own,) = call(shared_kernel, [((2 * PIECE, HD), BF16)], [], ids, *arrived)
+    grad_input, grad_query, grad_out = call(
         input_kernel,
-        [((rows, quarter), F32)],
+        [((rows, quarter), F32)] + [((HD, HD), F32)] * 2,
         [],
         ids,
         *pieces,
@@ -462,14 +491,9 @@
         gain_f,
         total,
         row_sum,
-        static=width,
-    )
-    arrived = (lax.ppermute(to_same, AXES, inverse(owner_perm(0))), lax.ppermute(to_other, AXES, inverse(owner_perm(1))))
-    gain_z = gain_z + swap(gain_z, "yh")
-    gain_x = [gain_z] + [shift_x(gain_z, s) for s in range(1, NX)]
-    *arrived, grad_input, gain_z = lax.optimization_barrier((*arrived, grad_input, gain_z))
-    (shared_own,) = call(shared_kernel, [((2 * PIECE, HD), BF16)], [], ids, *arrived)
-    grad_query, grad_out = call(owner_kernel, [((HD, HD), F32)] * 2, [], ids, *arrived, static=loss_scale)
+        *arrived,
+        static=(width, loss_scale),
+    )
     shared_yl = swap(shared_own, "yl")
     grad_key, grad_value, grad_gain = call(
         join_kernel,
@@ -480,7 +504,7 @@
         swap(shared_own, "c"),
         shared_yl,
         swap(shared_yl, "c"),
-        *gain_x,
+        gain_z,
         static=loss_scale,
     )
     grad_gain = grad_gain.reshape(quarter)

time: 153 us -> 153 us (level)
  waiting for transfers between devices: 67.5 us -> 72.2 us
  starting transfers between devices: 61.1 us -> 57.4 us
    ppermute x12 -> x13, waiting for transfers between devices: 17.8 us -> 23.9 us  [shift_z(): return lax.ppermute(value, 'z', [(i, (i + by) % NZ) for i in range(NZ)])]
    ppermute x15 -> x12, starting transfers between devices: 21.8 us -> 17.1 us  [shift_x(): return lax.ppermute(value, 'x', [(i, (i + by) % NX) for i in range(NX)])]
    ppermute x12 -> x13, starting transfers between devices: 24.7 us -> 25.9 us  [shift_z(): return lax.ppermute(value, 'z', [(i, (i + by) % NZ) for i in range(NZ)])]
    ppermute x15 -> x12, waiting for transfers between devices: 29.9 us -> 29.2 us  [shift_x(): return lax.ppermute(value, 'x', [(i, (i + by) % NX) for i in range(NX)])]
  transfers between devices with their start and end apart: 45 -> 43, of which waited for: 24 -> 25; matrix products, arithmetic and copies ran while one was open for 0% -> 0% of each run, Pallas kernels for 5% -> 5%
where the time goes in v3:
time: 153 us; the launch traced here: 152 us
  waiting for transfers between devices  72.2 us (47%)
  starting transfers between devices  57.4 us (38%)
  Pallas kernels  17.5 us (11%)
  local copies, waits for them, and re-layouts  2.9 us (2%)
    ppermute x12, waiting for transfers between devices, shift_x(): return lax.ppermute(value, 'x', [(i, (i + by) % NX) for i in range(NX)])  29.2 us
    ppermute x13, starting transfers between devices, shift_z(): return lax.ppermute(value, 'z', [(i, (i + by) % NZ) for i in range(NZ)])  25.9 us
    ppermute x13, waiting for transfers between devices, shift_z(): return lax.ppermute(value, 'z', [(i, (i + by) % NZ) for i in range(NZ)])  23.9 us
    ppermute x14, waiting for transfers between devices, swap(): return lax.ppermute(value, axis, [(0, 1), (1, 0)])  18.6 us
    pallas_call x17, Pallas kernels, call(): pl.pallas_call(body, out_shape=[jax.ShapeDtypeStruct(s, d) for s, d in ou...  17.5 us
    ppermute x12, starting transfers between devices, shift_x(): return lax.ppermute(value, 'x', [(i, (i + by) % NX) for i in range(NX)])  17.1 us
    ppermute x14, starting transfers between devices, swap(): return lax.ppermute(value, axis, [(0, 1), (1, 0)])  8.82 us
    ppermute x1, starting transfers between devices, local(): same = lax.ppermute(pack, AXES, owner_perm(0))  3.47 us
  transfers between devices with their start and end apart: 43, of which 25 were waited for; matrix products, arithmetic and copies ran while one was open for 0% of the time, Pallas kernels for 5%

profile of v3, /device:TPU:8, one launch (start us, length us, event | category | flops | bytes accessed | tf_op | source)
XLA Modules:
  0.0 151.7 jit_solution(16132922579800277081)
XLA Ops:
  2.1 3.5 %collective-permute-start = (bf16[320,128]{1,0:T(8,128)(2,1)S(1)}, bf16[320,128]{1,0:T(8,128)(2,1)S(1)}, u32[]{:S(2)}, u32[]{:S(2)}) collective-permute-start(bf16[320,128]{1,0:T(8,128)(2,1)S(1)} %pad_maximum_fusion), channel_id=1, source_target_pairs={{0,0},{1,4},{2,128},{3,132},{4,32},{5,36},{6,160},{7,164},{8,8},{9... | collective-permute-start | bytes 245768 | tf_op jit(solution)/shard_map/ppermute | solution.py:386
  11.7 3.3 %collective-permute-start.7 = (bf16[640,128]{1,0:T(8,128)(2,1)S(1)}, bf16[640,128]{1,0:T(8,128)(2,1)S(1)}, u32[]{:S(2)}, u32[]{:S(2)}) collective-permute-start(bf16[640,128]{1,0:T(8,128)(2,1)S(1)} %maximum_select_fusion.both), channel_id=1, source_target_pairs={{0,8},{4,12},{8,16},{12,20},{16,24},{20,28},{24,0},{28,4},{1,9},{5... | collective-permute-start | bytes 491528 | tf_op jit(solution)/shard_map/ppermute | solution.py:52
  15.0 3.1 %collective-permute-start.8 = (bf16[640,128]{1,0:T(8,128)(2,1)S(1)}, bf16[640,128]{1,0:T(8,128)(2,1)S(1)}, u32[]{:S(2)}, u32[]{:S(2)}) collective-permute-start(bf16[640,128]{1,0:T(8,128)(2,1)S(1)} %maximum_select_fusion.both), channel_id=1, source_target_pairs={{0,24},{4,28},{8,0},{12,4},{16,8},{20,12},{24,16},{28,20},{1,25},{... | collective-permute-start | bytes 491528 | tf_op jit(solution)/shard_map/ppermute | solution.py:52
  18.2 2.5 %collective-permute-start.3 = (f32[1,128]{1,0:T(1,128)S(1)}, f32[1,128]{1,0:T(1,128)S(1)}, u32[]{:S(2)}, u32[]{:S(2)}) collective-permute-start(f32[1,128]{1,0:T(1,128)S(1)} %add.24), channel_id=1, source_target_pairs={{0,2},{2,0},{1,3},{3,1},{4,6},{6,4},{5,7},{7,5},{8,10},{10,8},{9,1... | collective-permute-start | bytes 1544 | tf_op jit(solution)/shard_map/ppermute | solution.py:56
  22.8 4.5 %collective-permute-start.4 = (bf16[272,512]{1,0:T(8,128)(2,1)S(1)}, bf16[272,512]{1,0:T(8,128)(2,1)S(1)}, u32[]{:S(2)}, u32[]{:S(2)}) collective-permute-start(bf16[272,512]{1,0:T(8,128)(2,1)S(1)} %get-tuple-element.73), channel_id=1, source_target_pairs={{0,32},{32,64},{64,96},{96,0},{1,33},{33,65},{65,97},{97,1},{2,34}... | collective-permute-start | bytes 835592 | tf_op jit(solution)/shard_map/ppermute | solution.py:48
  27.3 2.3 %collective-permute-start.5 = (bf16[272,512]{1,0:T(8,128)(2,1)S(1)}, bf16[272,512]{1,0:T(8,128)(2,1)S(1)}, u32[]{:S(2)}, u32[]{:S(2)}) collective-permute-start(bf16[272,512]{1,0:T(8,128)(2,1)S(1)} %get-tuple-element.74), channel_id=1, source_target_pairs={{0,64},{32,96},{64,0},{96,32},{1,65},{33,97},{65,1},{97,33},{2,66}... | collective-permute-start | bytes 835592 | tf_op jit(solution)/shard_map/ppermute | solution.py:48
  33.0 6.4 %collective-permute-done.4.refs_1_ = bf16[272,512]{1,0:T(8,128)(2,1)S(1)} collective-permute-done((bf16[272,512]{1,0:T(8,128)(2,1)S(1)}, bf16[272,512]{1,0:T(8,128)(2,1)S(1)}, u32[]{:S(2)}, u32[]{:S(2)}) %collective-permute-start.4) | collective-permute-done | bytes 278560 | tf_op jit(solution)/shard_map/ppermute | solution.py:48
  40.4 3.1 %collective-permute-start.12 = (bf16[320,128]{1,0:T(8,128)(2,1)S(1)}, bf16[320,128]{1,0:T(8,128)(2,1)S(1)}, u32[]{:S(2)}, u32[]{:S(2)}) collective-permute-start(bf16[320,128]{1,0:T(8,128)(2,1)S(1)} %get-tuple-element.83), channel_id=1, source_target_pairs={{0,24},{4,28},{8,0},{12,4},{16,8},{20,12},{24,16},{28,20},{1,25},{... | collective-permute-start | bytes 245768 | tf_op jit(solution)/shard_map/ppermute | solution.py:52
  44.3 2.3 %collective-permute-done.11.far_first = bf16[320,128]{1,0:T(8,128)(2,1)S(1)} collective-permute-done((bf16[320,128]{1,0:T(8,128)(2,1)S(1)}, bf16[320,128]{1,0:T(8,128)(2,1)S(1)}, u32[]{:S(2)}, u32[]{:S(2)}) %collective-permute-start.11) | collective-permute-done | bytes 81952 | tf_op jit(solution)/shard_map/ppermute | solution.py:52
  50.2 1.9 %collective-permute-done.13.got = f32[512,640]{1,0:T(8,128)S(1)} collective-permute-done((f32[512,640]{1,0:T(8,128)S(1)}, f32[512,640]{1,0:T(8,128)S(1)}, u32[]{:S(2)}, u32[]{:S(2)}) %collective-permute-start.13) | collective-permute-done | bytes 1310752 | tf_op jit(solution)/shard_map/ppermute | solution.py:56
  53.0 1.7 %collective-permute-start.15 = (bf16[128,1024]{1,0:T(8,128)(2,1)S(1)}, bf16[128,1024]{1,0:T(8,128)(2,1)S(1)}, u32[]{:S(2)}, u32[]{:S(2)}) collective-permute-start(bf16[128,1024]{1,0:T(8,128)(2,1)S(1)} %get-tuple-element.89), channel_id=1, source_target_pairs={{0,64},{32,96},{64,0},{96,32},{1,65},{33,97},{65,1},{97,33},{2,66}... | collective-permute-start | bytes 786440 | tf_op jit(solution)/shard_map/ppermute | solution.py:48
  55.2 7.0 %collective-permute-done.14.a = bf16[128,1024]{1,0:T(8,128)(2,1)S(1)} collective-permute-done((bf16[128,1024]{1,0:T(8,128)(2,1)S(1)}, bf16[128,1024]{1,0:T(8,128)(2,1)S(1)}, u32[]{:S(2)}, u32[]{:S(2)}) %collective-permute-start.14) | collective-permute-done | bytes 262176 | tf_op jit(solution)/shard_map/ppermute | solution.py:48
  62.2 1.6 %collective-permute-done.15.b = bf16[128,1024]{1,0:T(8,128)(2,1)S(1)} collective-permute-done((bf16[128,1024]{1,0:T(8,128)(2,1)S(1)}, bf16[128,1024]{1,0:T(8,128)(2,1)S(1)}, u32[]{:S(2)}, u32[]{:S(2)}) %collective-permute-start.15) | collective-permute-done | bytes 262176 | tf_op jit(solution)/shard_map/ppermute | solution.py:48
  63.8 4.8 %collective-permute-done.16.c = bf16[128,1024]{1,0:T(8,128)(2,1)S(1)} collective-permute-done((bf16[128,1024]{1,0:T(8,128)(2,1)S(1)}, bf16[128,1024]{1,0:T(8,128)(2,1)S(1)}, u32[]{:S(2)}, u32[]{:S(2)}) %collective-permute-start.16) | collective-permute-done | bytes 262176 | tf_op jit(solution)/shard_map/ppermute | solution.py:48
  69.4 8.2 %collective-permute-done.17.got = bf16[128,1024]{1,0:T(8,128)(2,1)S(1)} collective-permute-done((bf16[128,1024]{1,0:T(8,128)(2,1)S(1)}, bf16[128,1024]{1,0:T(8,128)(2,1)S(1)}, u32[]{:S(2)}, u32[]{:S(2)}) %collective-permute-start.17) | collective-permute-done | bytes 262176 | tf_op jit(solution)/shard_map/ppermute | solution.py:56
  79.5 1.7 %shard_map.127 = (bf16[128,768]{1,0:T(8,128)(2,1)S(1)}, f32[1,128]{1,0:T(1,128)S(1)}) custom-call(s32[5]{0:T(128)S(1)} %stack.23.ids, bf16[128,512]{1,0:T(8,128)(2,1)S(1)} %get-tuple-element.91.qa, bf16[128,128]{1,0:T(8,128)(2,1)S(1)} %get-tuple-element.92.kv_mine, bf16[128,128]{1,0:T(8,128)(2,1)S(1)} %collective-permute-done.18.kv_theirs), custom_call_target="tpu_custom_call" | custom-call | tf_op jit(solution)/shard_map/pallas_call | solution.py:73
  81.3 1.8 %collective-permute-start.20 = (bf16[128,768]{1,0:T(8,128)(2,1)S(1)}, bf16[128,768]{1,0:T(8,128)(2,1)S(1)}, u32[]{:S(2)}, u32[]{:S(2)}) collective-permute-start(bf16[128,768]{1,0:T(8,128)(2,1)S(1)} %get-tuple-element.93.refs_0_), channel_id=1, source_target_pairs={{0,64},{32,96},{64,0},{96,32},{1,65},{33,97},{65,1},{97,33},{2,66}... | collective-permute-start | bytes 589832 | tf_op jit(solution)/shard_map/ppermute | solution.py:48
  83.1 2.2 %collective-permute-start.21 = (bf16[128,768]{1,0:T(8,128)(2,1)S(1)}, bf16[128,768]{1,0:T(8,128)(2,1)S(1)}, u32[]{:S(2)}, u32[]{:S(2)}) collective-permute-start(bf16[128,768]{1,0:T(8,128)(2,1)S(1)} %get-tuple-element.93.refs_0_), channel_id=1, source_target_pairs={{0,96},{32,0},{64,32},{96,64},{1,97},{33,1},{65,33},{97,65},{2,98}... | collective-permute-start | bytes 589832 | tf_op jit(solution)/shard_map/ppermute | solution.py:48
  85.2 8.4 %collective-permute-done.19.refs_1_ = bf16[128,768]{1,0:T(8,128)(2,1)S(1)} collective-permute-done((bf16[128,768]{1,0:T(8,128)(2,1)S(1)}, bf16[128,768]{1,0:T(8,128)(2,1)S(1)}, u32[]{:S(2)}, u32[]{:S(2)}) %collective-permute-start.19) | collective-permute-done | bytes 196640 | tf_op jit(solution)/shard_map/ppermute | solution.py:48
  95.7 2.8 %shard_map.128 = (bf16[656,128]{1,0:T(8,128)(2,1)S(1)}, bf16[1296,128]{1,0:T(8,128)(2,1)S(1)}, bf16[1296,128]{1,0:T(8,128)(2,1)S(1)}, bf16[640,128]{1,0:T(8,128)...) custom-call(s32[5]{0:T(128)S(1)} %stack.23.ids, ...), custom_call_target="tpu_custom_call" | custom-call | tf_op jit(solution)/shard_map/pallas_call | solution.py:73
  99.9 2.2 %collective-permute-start.27 = (bf16[1296,128]{1,0:T(8,128)(2,1)S(1)}, bf16[1296,128]{1,0:T(8,128)(2,1)S(1)}, u32[]{:S(2)}, u32[]{:S(2)}) collective-permute-start(bf16[1296,128]{1,0:T(8,128)(2,1)S(1)} %get-tuple-element.98), channel_id=1, source_target_pairs={{0,28},{4,0},{8,4},{12,8},{16,12},{20,16},{24,20},{28,24},{1,29},{... | collective-permute-start | bytes 995336 | tf_op jit(solution)/shard_map/ppermute | solution.py:52
  102.1 3.7 %collective-permute-start.28 = (bf16[336,128]{1,0:T(8,128)(2,1)S(1)}, bf16[336,128]{1,0:T(8,128)(2,1)S(1)}, u32[]{:S(2)}, u32[]{:S(2)}) collective-permute-start(bf16[336,128]{1,0:T(8,128)(2,1)S(1)} %get-tuple-element.99), channel_id=1, source_target_pairs={{0,8},{4,12},{8,16},{12,20},{16,24},{20,28},{24,0},{28,4},{1,9},{5... | collective-permute-start | bytes 258056 | tf_op jit(solution)/shard_map/ppermute | solution.py:52
  106.3 8.8 %collective-permute-done.28.c = bf16[336,128]{1,0:T(8,128)(2,1)S(1)} collective-permute-done((bf16[336,128]{1,0:T(8,128)(2,1)S(1)}, bf16[336,128]{1,0:T(8,128)(2,1)S(1)}, u32[]{:S(2)}, u32[]{:S(2)}) %collective-permute-start.28) | collective-permute-done | bytes 86048 | tf_op jit(solution)/shard_map/ppermute | solution.py:52
  115.0 2.0 %collective-permute-done.29.d = bf16[336,128]{1,0:T(8,128)(2,1)S(1)} collective-permute-done((bf16[336,128]{1,0:T(8,128)(2,1)S(1)}, bf16[336,128]{1,0:T(8,128)(2,1)S(1)}, u32[]{:S(2)}, u32[]{:S(2)}) %collective-permute-start.29) | collective-permute-done | bytes 86048 | tf_op jit(solution)/shard_map/ppermute | solution.py:52
  119.1 2.9 %collective-permute-start.35 = (bf16[640,128]{1,0:T(8,128)(2,1)S(1)}, bf16[640,128]{1,0:T(8,128)(2,1)S(1)}, u32[]{:S(2)}, u32[]{:S(2)}) collective-permute-start(bf16[640,128]{1,0:T(8,128)(2,1)S(1)} %get-tuple-element.112), channel_id=1, source_target_pairs={{0,24},{4,28},{8,0},{12,4},{16,8},{20,12},{24,16},{28,20},{1,25},{... | collective-permute-start | bytes 491528 | tf_op jit(solution)/shard_map/ppermute | solution.py:52
  121.9 2.3 %collective-permute-start.30 = (bf16[144,512]{1,0:T(8,128)(2,1)S(1)}, bf16[144,512]{1,0:T(8,128)(2,1)S(1)}, u32[]{:S(2)}, u32[]{:S(2)}) collective-permute-start(bf16[144,512]{1,0:T(8,128)(2,1)S(1)} %get-tuple-element.107), channel_id=1, source_target_pairs={{0,96},{32,0},{64,32},{96,64},{1,97},{33,1},{65,33},{97,65},{2,98}... | collective-permute-start | bytes 442376 | tf_op jit(solution)/shard_map/ppermute | solution.py:48
  125.1 2.8 %collective-permute-done.34.up = bf16[640,128]{1,0:T(8,128)(2,1)S(1)} collective-permute-done((bf16[640,128]{1,0:T(8,128)(2,1)S(1)}, bf16[640,128]{1,0:T(8,128)(2,1)S(1)}, u32[]{:S(2)}, u32[]{:S(2)}) %collective-permute-start.34) | collective-permute-done | bytes 163872 | tf_op jit(solution)/shard_map/ppermute | solution.py:52
  129.2 1.9 %collective-permute-start.36 = (bf16[320,128]{1,0:T(8,128)(2,1)S(1)}, bf16[320,128]{1,0:T(8,128)(2,1)S(1)}, u32[]{:S(2)}, u32[]{:S(2)}) collective-permute-start(bf16[320,128]{1,0:T(8,128)(2,1)S(1)} %get-tuple-element.113), channel_id=1, source_target_pairs={{0,0},{4,1},{128,2},{132,3},{32,4},{36,5},{160,6},{164,7},{8,8},{1... | collective-permute-start | bytes 245768 | tf_op jit(solution)/shard_map/ppermute | solution.py:478
  134.0 6.4 %collective-permute-done.38 = f32[16,128]{1,0:T(8,128)S(1)} collective-permute-done((f32[16,128]{1,0:T(8,128)S(1)}, f32[16,128]{1,0:T(8,128)S(1)}, u32[]{:S(2)}, u32[]{:S(2)}) %collective-permute-start.38) | collective-permute-done | bytes 8224 | tf_op jit(solution)/shard_map/ppermute | solution.py:52
  142.2 2.7 %collective-permute-done.40.by_yl = bf16[64,128]{1,0:T(8,128)(2,1)S(1)} collective-permute-done((bf16[64,128]{1,0:T(8,128)(2,1)S(1)}, bf16[64,128]{1,0:T(8,128)(2,1)S(1)}, u32[]{:S(2)}, u32[]{:S(2)}) %collective-permute-start.40) | collective-permute-done | bytes 16416 | tf_op jit(solution)/shard_map/ppermute | solution.py:56
  144.8 2.5 %collective-permute-start.42 = (f32[16,128]{1,0:T(8,128)S(1)}, f32[16,128]{1,0:T(8,128)S(1)}, u32[]{:S(2)}, u32[]{:S(2)}) collective-permute-start(f32[16,128]{1,0:T(8,128)S(1)} %add.27), channel_id=1, source_target_pairs={{0,128},{128,0},{1,129},{129,1},{2,130},{130,2},{3,131},{131,3},{4... | collective-permute-start | bytes 24584 | tf_op jit(solution)/shard_map/ppermute | solution.py:56
  148.5 2.0 %shard_map.132 = (f32[128,2048]{1,0:T(8,128)}, f32[128,128]{1,0:T(8,128)}, f32[128,128]{1,0:T(8,128)}) custom-call(s32[5]{0:T(128)S(1)} %stack.23.ids, bf16[144,512]{1,0:T(8,128)(2,1)S(1)} %get-tuple-element.106.refs_0_.a, bf16[144,512]{1,0:T(8,128)(2,1)S(1)} %collective-permute-done.30.refs_1_.b, bf16[144,512]{1,0:T(8,128)(2,1)S(1)} %collective-permute-done.31.refs_2_.c, ...), custom_call_target="tpu_custom_call" | custom-call | tf_op jit(solution)/shard_map/pallas_call | solution.py:73
  (89 shorter events, 37.6 us)
Async XLA Ops:
  2.1 9.1 %collective-permute-start = (bf16[320,128]{1,0:T(8,128)(2,1)S(1)}, bf16[320,128]{1,0:T(8,128)(2,1)S(1)}, u32[]{:S(2)}, u32[]{:S(2)}) collective-permute-start(bf16[320,128]{1,0:T(8,128)(2,1)S(1)} %pad_maximum_fusion), channel_id=1, source_target_pairs={{0,0},{1,4},{2,128},{3,132},{4,32},{5,36},{6,160},{7,164},{8,8},{9... | collective-permute-start | bytes 245768 | tf_op jit(solution)/shard_map/ppermute | solution.py:386
  5.6 6.0 %collective-permute-start.1 = (bf16[320,128]{1,0:T(8,128)(2,1)S(1)}, bf16[320,128]{1,0:T(8,128)(2,1)S(1)}, u32[]{:S(2)}, u32[]{:S(2)}) collective-permute-start(bf16[320,128]{1,0:T(8,128)(2,1)S(1)} %pad_maximum_fusion), channel_id=1, source_target_pairs={{0,128},{1,132},{2,0},{3,4},{4,160},{5,164},{6,32},{7,36},{8,136},... | collective-permute-start | bytes 245768 | tf_op jit(solution)/shard_map/ppermute | solution.py:387
  11.7 17.9 %collective-permute-start.7 = (bf16[640,128]{1,0:T(8,128)(2,1)S(1)}, bf16[640,128]{1,0:T(8,128)(2,1)S(1)}, u32[]{:S(2)}, u32[]{:S(2)}) collective-permute-start(bf16[640,128]{1,0:T(8,128)(2,1)S(1)} %maximum_select_fusion.both), channel_id=1, source_target_pairs={{0,8},{4,12},{8,16},{12,20},{16,24},{20,28},{24,0},{28,4},{1,9},{5... | collective-permute-start | bytes 491528 | tf_op jit(solution)/shard_map/ppermute | solution.py:52
  15.0 14.5 %collective-permute-start.8 = (bf16[640,128]{1,0:T(8,128)(2,1)S(1)}, bf16[640,128]{1,0:T(8,128)(2,1)S(1)}, u32[]{:S(2)}, u32[]{:S(2)}) collective-permute-start(bf16[640,128]{1,0:T(8,128)(2,1)S(1)} %maximum_select_fusion.both), channel_id=1, source_target_pairs={{0,24},{4,28},{8,0},{12,4},{16,8},{20,12},{24,16},{28,20},{1,25},{... | collective-permute-start | bytes 491528 | tf_op jit(solution)/shard_map/ppermute | solution.py:52
  22.8 16.6 %collective-permute-start.4 = (bf16[272,512]{1,0:T(8,128)(2,1)S(1)}, bf16[272,512]{1,0:T(8,128)(2,1)S(1)}, u32[]{:S(2)}, u32[]{:S(2)}) collective-permute-start(bf16[272,512]{1,0:T(8,128)(2,1)S(1)} %get-tuple-element.73), channel_id=1, source_target_pairs={{0,32},{32,64},{64,96},{96,0},{1,33},{33,65},{65,97},{97,1},{2,34}... | collective-permute-start | bytes 835592 | tf_op jit(solution)/shard_map/ppermute | solution.py:48
  27.3 13.2 %collective-permute-start.5 = (bf16[272,512]{1,0:T(8,128)(2,1)S(1)}, bf16[272,512]{1,0:T(8,128)(2,1)S(1)}, u32[]{:S(2)}, u32[]{:S(2)}) collective-permute-start(bf16[272,512]{1,0:T(8,128)(2,1)S(1)} %get-tuple-element.74), channel_id=1, source_target_pairs={{0,64},{32,96},{64,0},{96,32},{1,65},{33,97},{65,1},{97,33},{2,66}... | collective-permute-start | bytes 835592 | tf_op jit(solution)/shard_map/ppermute | solution.py:48
  30.2 17.3 %collective-permute-start.10 = (bf16[1280,128]{1,0:T(8,128)(2,1)S(1)}, bf16[1280,128]{1,0:T(8,128)(2,1)S(1)}, u32[]{:S(2)}, u32[]{:S(2)}) collective-permute-start(bf16[1280,128]{1,0:T(8,128)(2,1)S(1)} %get-tuple-element.81), channel_id=1, source_target_pairs={{0,28},{4,0},{8,4},{12,8},{16,12},{20,16},{24,20},{28,24},{1,29},{... | collective-permute-start | bytes 983048 | tf_op jit(solution)/shard_map/ppermute | solution.py:52
  31.5 16.0 %collective-permute-start.9 = (bf16[1280,128]{1,0:T(8,128)(2,1)S(1)}, bf16[1280,128]{1,0:T(8,128)(2,1)S(1)}, u32[]{:S(2)}, u32[]{:S(2)}) collective-permute-start(bf16[1280,128]{1,0:T(8,128)(2,1)S(1)} %get-tuple-element.80), channel_id=1, source_target_pairs={{0,4},{4,8},{8,12},{12,16},{16,20},{20,24},{24,28},{28,0},{1,5},{5... | collective-permute-start | bytes 983048 | tf_op jit(solution)/shard_map/ppermute | solution.py:52
  32.3 11.2 %collective-permute-start.6 = (bf16[272,512]{1,0:T(8,128)(2,1)S(1)}, bf16[272,512]{1,0:T(8,128)(2,1)S(1)}, u32[]{:S(2)}, u32[]{:S(2)}) collective-permute-start(bf16[272,512]{1,0:T(8,128)(2,1)S(1)} %get-tuple-element.75), channel_id=1, source_target_pairs={{0,96},{32,0},{64,32},{96,64},{1,97},{33,1},{65,33},{97,65},{2,98}... | collective-permute-start | bytes 835592 | tf_op jit(solution)/shard_map/ppermute | solution.py:48
  39.4 7.3 %collective-permute-start.11 = (bf16[320,128]{1,0:T(8,128)(2,1)S(1)}, bf16[320,128]{1,0:T(8,128)(2,1)S(1)}, u32[]{:S(2)}, u32[]{:S(2)}) collective-permute-start(bf16[320,128]{1,0:T(8,128)(2,1)S(1)} %get-tuple-element.82), channel_id=1, source_target_pairs={{0,8},{4,12},{8,16},{12,20},{16,24},{20,28},{24,0},{28,4},{1,9},{5... | collective-permute-start | bytes 245768 | tf_op jit(solution)/shard_map/ppermute | solution.py:52
  40.4 7.1 %collective-permute-start.12 = (bf16[320,128]{1,0:T(8,128)(2,1)S(1)}, bf16[320,128]{1,0:T(8,128)(2,1)S(1)}, u32[]{:S(2)}, u32[]{:S(2)}) collective-permute-start(bf16[320,128]{1,0:T(8,128)(2,1)S(1)} %get-tuple-element.83), channel_id=1, source_target_pairs={{0,24},{4,28},{8,0},{12,4},{16,8},{20,12},{24,16},{28,20},{1,25},{... | collective-permute-start | bytes 245768 | tf_op jit(solution)/shard_map/ppermute | solution.py:52
  52.8 9.4 %collective-permute-start.14 = (bf16[128,1024]{1,0:T(8,128)(2,1)S(1)}, bf16[128,1024]{1,0:T(8,128)(2,1)S(1)}, u32[]{:S(2)}, u32[]{:S(2)}) collective-permute-start(bf16[128,1024]{1,0:T(8,128)(2,1)S(1)} %get-tuple-element.88), channel_id=1, source_target_pairs={{0,96},{32,0},{64,32},{96,64},{1,97},{33,1},{65,33},{97,65},{2,98}... | collective-permute-start | bytes 786440 | tf_op jit(solution)/shard_map/ppermute | solution.py:48
  53.0 10.8 %collective-permute-start.15 = (bf16[128,1024]{1,0:T(8,128)(2,1)S(1)}, bf16[128,1024]{1,0:T(8,128)(2,1)S(1)}, u32[]{:S(2)}, u32[]{:S(2)}) collective-permute-start(bf16[128,1024]{1,0:T(8,128)(2,1)S(1)} %get-tuple-element.89), channel_id=1, source_target_pairs={{0,64},{32,96},{64,0},{96,32},{1,65},{33,97},{65,1},{97,33},{2,66}... | collective-permute-start | bytes 786440 | tf_op jit(solution)/shard_map/ppermute | solution.py:48
  54.8 13.8 %collective-permute-start.16 = (bf16[128,1024]{1,0:T(8,128)(2,1)S(1)}, bf16[128,1024]{1,0:T(8,128)(2,1)S(1)}, u32[]{:S(2)}, u32[]{:S(2)}) collective-permute-start(bf16[128,1024]{1,0:T(8,128)(2,1)S(1)} %get-tuple-element.90), channel_id=1, source_target_pairs={{0,32},{32,64},{64,96},{96,0},{1,33},{33,65},{65,97},{97,1},{2,34}... | collective-permute-start | bytes 786440 | tf_op jit(solution)/shard_map/ppermute | solution.py:48
  69.3 8.3 %collective-permute-start.17 = (bf16[128,1024]{1,0:T(8,128)(2,1)S(1)}, bf16[128,1024]{1,0:T(8,128)(2,1)S(1)}, u32[]{:S(2)}, u32[]{:S(2)}) collective-permute-start(bf16[128,1024]{1,0:T(8,128)(2,1)S(1)} %shard_map.125.mine), channel_id=1, source_target_pairs={{0,2},{2,0},{1,3},{3,1},{4,6},{6,4},{5,7},{7,5},{8,10},{10,8},{9,1... | collective-permute-start | bytes 786440 | tf_op jit(solution)/shard_map/ppermute | solution.py:56
  81.2 12.5 %collective-permute-start.19 = (bf16[128,768]{1,0:T(8,128)(2,1)S(1)}, bf16[128,768]{1,0:T(8,128)(2,1)S(1)}, u32[]{:S(2)}, u32[]{:S(2)}) collective-permute-start(bf16[128,768]{1,0:T(8,128)(2,1)S(1)} %get-tuple-element.93.refs_0_), channel_id=1, source_target_pairs={{0,32},{32,64},{64,96},{96,0},{1,33},{33,65},{65,97},{97,1},{2,34}... | collective-permute-start | bytes 589832 | tf_op jit(solution)/shard_map/ppermute | solution.py:48
  81.3 12.4 %collective-permute-start.20 = (bf16[128,768]{1,0:T(8,128)(2,1)S(1)}, bf16[128,768]{1,0:T(8,128)(2,1)S(1)}, u32[]{:S(2)}, u32[]{:S(2)}) collective-permute-start(bf16[128,768]{1,0:T(8,128)(2,1)S(1)} %get-tuple-element.93.refs_0_), channel_id=1, source_target_pairs={{0,64},{32,96},{64,0},{96,32},{1,65},{33,97},{65,1},{97,33},{2,66}... | collective-permute-start | bytes 589832 | tf_op jit(solution)/shard_map/ppermute | solution.py:48
  83.1 11.2 %collective-permute-start.21 = (bf16[128,768]{1,0:T(8,128)(2,1)S(1)}, bf16[128,768]{1,0:T(8,128)(2,1)S(1)}, u32[]{:S(2)}, u32[]{:S(2)}) collective-permute-start(bf16[128,768]{1,0:T(8,128)(2,1)S(1)} %get-tuple-element.93.refs_0_), channel_id=1, source_target_pairs={{0,96},{32,0},{64,32},{96,64},{1,97},{33,1},{65,33},{97,65},{2,98}... | collective-permute-start | bytes 589832 | tf_op jit(solution)/shard_map/ppermute | solution.py:48
  85.2 9.0 %collective-permute-start.22 = (bf16[128,768]{1,0:T(8,128)(2,1)S(1)}, bf16[128,768]{1,0:T(8,128)(2,1)S(1)}, u32[]{:S(2)}, u32[]{:S(2)}) collective-permute-start(bf16[128,768]{1,0:T(8,128)(2,1)S(1)} %get-tuple-element.93.refs_0_), channel_id=1, source_target_pairs={{0,1},{1,0},{2,3},{3,2},{4,5},{5,4},{6,7},{7,6},{8,9},{9,8},{10,11... | collective-permute-start | bytes 589832 | tf_op jit(solution)/shard_map/ppermute | solution.py:56
  98.5 18.6 %collective-permute-start.26 = (bf16[1296,128]{1,0:T(8,128)(2,1)S(1)}, bf16[1296,128]{1,0:T(8,128)(2,1)S(1)}, u32[]{:S(2)}, u32[]{:S(2)}) collective-permute-start(bf16[1296,128]{1,0:T(8,128)(2,1)S(1)} %get-tuple-element.97), channel_id=1, source_target_pairs={{0,4},{4,8},{8,12},{12,16},{16,20},{20,24},{24,28},{28,0},{1,5},{5... | collective-permute-start | bytes 995336 | tf_op jit(solution)/shard_map/ppermute | solution.py:52
  99.9 17.1 %collective-permute-start.27 = (bf16[1296,128]{1,0:T(8,128)(2,1)S(1)}, bf16[1296,128]{1,0:T(8,128)(2,1)S(1)}, u32[]{:S(2)}, u32[]{:S(2)}) collective-permute-start(bf16[1296,128]{1,0:T(8,128)(2,1)S(1)} %get-tuple-element.98), channel_id=1, source_target_pairs={{0,28},{4,0},{8,4},{12,8},{16,12},{20,16},{24,20},{28,24},{1,29},{... | collective-permute-start | bytes 995336 | tf_op jit(solution)/shard_map/ppermute | solution.py:52
  102.1 12.9 %collective-permute-start.28 = (bf16[336,128]{1,0:T(8,128)(2,1)S(1)}, bf16[336,128]{1,0:T(8,128)(2,1)S(1)}, u32[]{:S(2)}, u32[]{:S(2)}) collective-permute-start(bf16[336,128]{1,0:T(8,128)(2,1)S(1)} %get-tuple-element.99), channel_id=1, source_target_pairs={{0,8},{4,12},{8,16},{12,20},{16,24},{20,28},{24,0},{28,4},{1,9},{5... | collective-permute-start | bytes 258056 | tf_op jit(solution)/shard_map/ppermute | solution.py:52
  105.8 11.3 %collective-permute-start.29 = (bf16[336,128]{1,0:T(8,128)(2,1)S(1)}, bf16[336,128]{1,0:T(8,128)(2,1)S(1)}, u32[]{:S(2)}, u32[]{:S(2)}) collective-permute-start(bf16[336,128]{1,0:T(8,128)(2,1)S(1)} %get-tuple-element.100), channel_id=1, source_target_pairs={{0,24},{4,28},{8,0},{12,4},{16,8},{20,12},{24,16},{28,20},{1,25},{... | collective-permute-start | bytes 258056 | tf_op jit(solution)/shard_map/ppermute | solution.py:52
  117.7 10.2 %collective-permute-start.34 = (bf16[640,128]{1,0:T(8,128)(2,1)S(1)}, bf16[640,128]{1,0:T(8,128)(2,1)S(1)}, u32[]{:S(2)}, u32[]{:S(2)}) collective-permute-start(bf16[640,128]{1,0:T(8,128)(2,1)S(1)} %get-tuple-element.111), channel_id=1, source_target_pairs={{0,8},{4,12},{8,16},{12,20},{16,24},{20,28},{24,0},{28,4},{1,9},{5... | collective-permute-start | bytes 491528 | tf_op jit(solution)/shard_map/ppermute | solution.py:52
  119.1 9.5 %collective-permute-start.35 = (bf16[640,128]{1,0:T(8,128)(2,1)S(1)}, bf16[640,128]{1,0:T(8,128)(2,1)S(1)}, u32[]{:S(2)}, u32[]{:S(2)}) collective-permute-start(bf16[640,128]{1,0:T(8,128)(2,1)S(1)} %get-tuple-element.112), channel_id=1, source_target_pairs={{0,24},{4,28},{8,0},{12,4},{16,8},{20,12},{24,16},{28,20},{1,25},{... | collective-permute-start | bytes 491528 | tf_op jit(solution)/shard_map/ppermute | solution.py:52
  121.9 9.3 %collective-permute-start.30 = (bf16[144,512]{1,0:T(8,128)(2,1)S(1)}, bf16[144,512]{1,0:T(8,128)(2,1)S(1)}, u32[]{:S(2)}, u32[]{:S(2)}) collective-permute-start(bf16[144,512]{1,0:T(8,128)(2,1)S(1)} %get-tuple-element.107), channel_id=1, source_target_pairs={{0,96},{32,0},{64,32},{96,64},{1,97},{33,1},{65,33},{97,65},{2,98}... | collective-permute-start | bytes 442376 | tf_op jit(solution)/shard_map/ppermute | solution.py:48
  124.3 7.0 %collective-permute-start.31 = (bf16[144,512]{1,0:T(8,128)(2,1)S(1)}, bf16[144,512]{1,0:T(8,128)(2,1)S(1)}, u32[]{:S(2)}, u32[]{:S(2)}) collective-permute-start(bf16[144,512]{1,0:T(8,128)(2,1)S(1)} %get-tuple-element.108), channel_id=1, source_target_pairs={{0,64},{32,96},{64,0},{96,32},{1,65},{33,97},{65,1},{97,33},{2,66}... | collective-permute-start | bytes 442376 | tf_op jit(solution)/shard_map/ppermute | solution.py:48
  124.3 8.0 %collective-permute-start.32 = (bf16[144,512]{1,0:T(8,128)(2,1)S(1)}, bf16[144,512]{1,0:T(8,128)(2,1)S(1)}, u32[]{:S(2)}, u32[]{:S(2)}) collective-permute-start(bf16[144,512]{1,0:T(8,128)(2,1)S(1)} %get-tuple-element.109), channel_id=1, source_target_pairs={{0,32},{32,64},{64,96},{96,0},{1,33},{33,65},{65,97},{97,1},{2,34}... | collective-permute-start | bytes 442376 | tf_op jit(solution)/shard_map/ppermute | solution.py:48
  129.2 11.2 %collective-permute-start.36 = (bf16[320,128]{1,0:T(8,128)(2,1)S(1)}, bf16[320,128]{1,0:T(8,128)(2,1)S(1)}, u32[]{:S(2)}, u32[]{:S(2)}) collective-permute-start(bf16[320,128]{1,0:T(8,128)(2,1)S(1)} %get-tuple-element.113), channel_id=1, source_target_pairs={{0,0},{4,1},{128,2},{132,3},{32,4},{36,5},{160,6},{164,7},{8,8},{1... | collective-permute-start | bytes 245768 | tf_op jit(solution)/shard_map/ppermute | solution.py:478
  131.2 9.3 %collective-permute-start.37 = (bf16[320,128]{1,0:T(8,128)(2,1)S(1)}, bf16[320,128]{1,0:T(8,128)(2,1)S(1)}, u32[]{:S(2)}, u32[]{:S(2)}) collective-permute-start(bf16[320,128]{1,0:T(8,128)(2,1)S(1)} %get-tuple-element.114), channel_id=1, source_target_pairs={{128,0},{132,1},{0,2},{4,3},{160,4},{164,5},{32,6},{36,7},{136,8},... | collective-permute-start | bytes 245768 | tf_op jit(solution)/shard_map/ppermute | solution.py:478
  132.8 7.7 %collective-permute-start.38 = (f32[16,128]{1,0:T(8,128)S(1)}, f32[16,128]{1,0:T(8,128)S(1)}, u32[]{:S(2)}, u32[]{:S(2)}) collective-permute-start(f32[16,128]{1,0:T(8,128)S(1)} %get-tuple-element.116), channel_id=1, source_target_pairs={{0,16},{4,20},{8,24},{12,28},{16,0},{20,4},{24,8},{28,12},{1,17},{... | collective-permute-start | bytes 24584 | tf_op jit(solution)/shard_map/ppermute | solution.py:52
  142.2 8.3 %collective-permute-start.39 = (bf16[64,128]{1,0:T(8,128)(2,1)S(1)}, bf16[64,128]{1,0:T(8,128)(2,1)S(1)}, u32[]{:S(2)}, u32[]{:S(2)}) collective-permute-start(bf16[64,128]{1,0:T(8,128)(2,1)S(1)} %shard_map.133.own), channel_id=1, source_target_pairs={{0,1},{1,0},{2,3},{3,2},{4,5},{5,4},{6,7},{7,6},{8,9},{9,8},{10,11... | collective-permute-start | bytes 49160 | tf_op jit(solution)/shard_map/ppermute | solution.py:56
  (15 other events, 100.1 us)

commit v4 on v3

--- a/solution.py
+++ b/solution.py
@@ -129,18 +129,24 @@
     far_second[...] = after[BLOCK:]
 
 
-def product(out, side, normed, cot, w_all, w_out):
+def product(outs, side, normed, cot, w_all, w_out):
     w_q = w_all[:, lanes(side * 2 * HD, 2 * HD)]
     w_kv = w_all[:, lanes((4 + side) * HD)]
     w_o = w_out[side]
     for r in range(0, 512, 256):
         rows = slice(r, r + 256)
-        out[rows, : 2 * HD] = dot(normed[rows], w_q, 1, 0)
-        out[rows, 2 * HD : 4 * HD] = dot(cot[rows], w_o, 1, 1)
-        out[rows, 4 * HD :] = dot(normed[rows], w_kv, 1, 0)
-
-
-def theirs_kernel(ids, both, prev1, next1, prev2, next2, far_first, far_second, normed, cot, out, w_all, w_out):
+        query = dot(normed[rows], w_q, 1, 0)
+        attn_grad = dot(cot[rows], w_o, 1, 1)
+        shared = dot(normed[rows], w_kv, 1, 0)
+        for half in range(2):
+            out, part = outs[r // HD + half], slice(half * HD, (half + 1) * HD)
+            out[:, : 2 * HD] = query[part]
+            out[:, 2 * HD : 4 * HD] = attn_grad[part]
+            out[:, 4 * HD :] = shared[part]
+
+
+def theirs_kernel(ids, both, prev1, next1, prev2, next2, far_first, far_second, normed, cot, *refs):
+    outs, w_all, w_out = refs[:NX], refs[NX], refs[NX + 1]
     z, c = ids[0], ids[2]
 
     def place(ref, base, d, half):
@@ -166,11 +172,16 @@
         place(ref, base + BLOCK, d, 1)
     place(far_first, 0, 4, 0)
     place(far_second, 0, 4, 1)
-    product(out, 1 - c, normed, cot, w_all, w_out)
-
-
-def mine_kernel(ids, normed, cot, w_all, w_out, out):
-    product(out, ids[2], normed, cot, w_all, w_out)
+    product(outs, 1 - c, normed, cot, w_all, w_out)
+
+
+def mine_kernel(ids, normed, cot, w_all, w_out, *refs):
+    outs, normed_t = refs[:NX], refs[NX]
+    product(outs, ids[2], normed, cot, w_all, w_out)
+    for s in range(NX):
+        for j in range(4):
+            rows, cols = slice(s * HD, (s + 1) * HD), slice(j * HD, (j + 1) * HD)
+            normed_t[cols, rows] = jnp.transpose(normed[rows, cols])
 
 
 def split_store(ref, total):
@@ -194,11 +205,12 @@
     )
 
 
-def chunk_kernel(ids, mine, got, own, *outs):
-    own[...] = mine[:HD] + got[:HD]
-    for s in range(1, NX):
-        rows = slice(s * HD, (s + 1) * HD)
-        split_store(outs[s - 1], mine[rows] + got[rows])
+def chunk_kernel(ids, mine, got, out):
+    split_store(out, mine[...] + got[...])
+
+
+def own_kernel(ids, mine, got, out):
+    out[...] = mine[...] + got[...]
 
 
 def sum_kernel(ids, own, a, b, c, out):
@@ -244,7 +256,7 @@
 
 
 def gradient_kernel(ids, *refs):
-    mine, theirs, (normed, cot, unit, w_all) = refs[:4], refs[4:8], refs[8:12]
+    mine, theirs, (normed_t, cot, unit, w_all) = refs[:4], refs[4:8], refs[8:12]
     (t0, up, down, t2, m2, t4a, t4b), back = refs[12:19], refs[19:23]
     heads, attended, shared = refs[23:]
     z, c = ids[0], ids[2]
@@ -252,7 +264,9 @@
         rows = slice(s * HD, (s + 1) * HD)
         for ref, side in ((mine[s], c), (theirs[s], 1 - c)):
             heads[rows, lanes(side * 2 * HD, 2 * HD)] = ref[:, : 2 * HD]
-            attended[rows, lanes(side * 2 * HD, 2 * HD)] = ref[:, 2 * HD : 4 * HD]
+            for half in range(2):
+                at = pl.ds(pl.multiple_of((2 * side + half) * HD, HD), HD)
+                attended[at, rows] = jnp.transpose(ref[:, (2 + half) * HD : (3 + half) * HD])
         total = mine[s][:, 4 * HD :].astype(F32) + theirs[s][:, 4 * HD :].astype(F32)
         heads[rows, 4 * HD :] = total.astype(BF16)
 
@@ -266,7 +280,7 @@
     high = gain_rows.astype(BF16).astype(F32)
     gain_rows = jnp.concatenate([high, gain_rows - high, jnp.zeros((8, HD), F32)], axis=0).astype(BF16)
 
-    shared[...] = dot(normed[...], heads[:, 4 * HD :], 0, 0)
+    shared[...] = dot(normed_t[...], heads[:, 4 * HD :], 1, 0)
     g, n = GROWS, BLOCK
     for ref in (t0, up, down, t4a, t4b):
         ref[:g] = gain_rows
@@ -282,8 +296,8 @@
     ):
         zt = (z + d + NZ) % NZ
         side, j = zt % 2, zt // 2
-        g_q = dot(normed[:, lanes(j * HD)], heads[:, lanes(side * 2 * HD, 2 * HD)], 0, 0).astype(BF16)
-        g_o = dot(attended[:, lanes(side * 2 * HD, 2 * HD)], cot[:, lanes(j * HD)], 0, 0).astype(BF16)
+        g_q = dot(normed_t[pl.ds(pl.multiple_of(j * HD, HD), HD)], heads[:, lanes(side * 2 * HD, 2 * HD)], 1, 0).astype(BF16)
+        g_o = dot(attended[pl.ds(pl.multiple_of(side * 2 * HD, 2 * HD), 2 * HD)], cot[:, lanes(j * HD)], 1, 0).astype(BF16)
         for half, out in enumerate((out_first, out_second)):
             out[:HD] = g_q[:, half * HD : (half + 1) * HD]
             out[HD : 2 * HD] = g_o[half * HD : (half + 1) * HD]
@@ -334,8 +348,7 @@
                 out[4 * s + j : 4 * s + j + 1] = value[:, j * HD : (j + 1) * HD]
 
 
-def input_kernel(sizes, ids, a, b, c, d, tokens, gain, total, row_sum, same, other, out, grad_query, grad_out):
-    width, scale = sizes
+def input_kernel(width, ids, a, b, c, d, tokens, gain, total, row_sum, out):
     inv = lax.rsqrt(jnp.transpose(jnp.broadcast_to(total[...], (HD, HD))) / width + 1e-05)
     row_mean = jnp.transpose(jnp.broadcast_to(row_sum[...], (HD, HD))) / width
     for s, ref in enumerate((a, b, c, d)):
@@ -345,6 +358,9 @@
             unit = tokens[:, cols].astype(F32) * inv
             scaled = ref[:HD, j * HD : (j + 1) * HD].astype(F32) * gain[:, cols]
             out[:, cols] = inv * (scaled - unit * row_mean)
+
+
+def owner_kernel(scale, ids, same, other, grad_query, grad_out):
     for grad, at in ((grad_query, slice(0, HD)), (grad_out, slice(HD, 2 * HD))):
         grad[...] = (same[at].astype(F32) + other[at].astype(F32)) * scale
 
@@ -411,19 +427,30 @@
         static=width,
     )
 
-    theirs, w_all, w_heads = call(
+    *theirs, w_all, w_heads = call(
         theirs_kernel,
-        [((512, 5 * HD), F32), ((sub, 6 * HD), BF16), ((2, 2 * HD, sub), BF16)],
+        [((rows, 5 * HD), F32)] * 4 + [((sub, 6 * HD), BF16), ((2, 2 * HD, sub), BF16)],
         [],
         ids,
         *weights,
         normed_sw,
         cot_sw,
     )
-    (mine,) = call(mine_kernel, [((512, 5 * HD), F32)], [], ids, normed_sw, cot_sw, w_all, w_heads)
+    got = [None] + [swap(theirs[s], "c") for s in range(1, NX)]
+    got[0] = swap(theirs[0], "c")
+    *mine, normed_t = call(
+        mine_kernel,
+        [((rows, 5 * HD), F32)] * 4 + [((sub, 512), BF16)],
+        [],
+        ids,
+        normed_sw,
+        cot_sw,
+        w_all,
+        w_heads,
+    )
     split = ((rows, 8 * HD), BF16)
-    own, *chunks = call(chunk_kernel, [((rows, 5 * HD), F32)] + [split] * 3, [], ids, mine, swap(theirs, "c"))
-    chunks = [shift_x(chunks[s - 1], -s) for s in range(1, NX)]
+    chunks = [shift_x(call(chunk_kernel, [split], [], ids, mine[s], got[s])[0], -s) for s in range(1, NX)]
+    (own,) = call(own_kernel, [((rows, 5 * HD), F32)], [], ids, mine[0], got[0])
     (partial,) = call(sum_kernel, [split], [], ids, own, *chunks)
     qa, kv = call(final_kernel, [((rows, 4 * HD), BF16), ((rows, HD), BF16)], [], ids, partial, swap(partial, "yl"))
     heads, row_sum = call(
@@ -449,13 +476,14 @@
         ids,
         *heads,
         *[swap(h, "c") for h in heads],
-        normed_sw,
+        normed_t,
         cot_sw,
         unit_sw,
         w_all,
     )
     c4, d4 = shift_z(t4a, 2), shift_z(t4b, -2)
     a, b = shift_z(up, 1), shift_z(down, -1)
+    a, row_sum = lax.optimization_barrier((a, row_sum))
     up, down, *back = call(
         relay_kernel,
         [((2 * n, HD), BF16)] * 2 + [((rows + g, sub), BF16)] * 4,
@@ -478,12 +506,9 @@
     arrived = (lax.ppermute(to_same, AXES, inverse(owner_perm(0))), lax.ppermute(to_other, AXES, inverse(owner_perm(1))))
     gain_five, gain_three = call(gain_kernel, [((4 * NX, HD), F32)] * 2, [], ids, *pieces)
     gain_z = gain_five + shift_z(gain_three, 4)
-    *arrived, gain_z = lax.optimization_barrier((*arrived, gain_z))
-    gain_z = gain_z + swap(gain_z, "yh")
-    (shared_own,) = call(shared_kernel, [((2 * PIECE, HD), BF16)], [], ids, *arrived)
-    grad_input, grad_query, grad_out = call(
+    (grad_input,) = call(
         input_kernel,
-        [((rows, quarter), F32)] + [((HD, HD), F32)] * 2,
+        [((rows, quarter), F32)],
         [],
         ids,
         *pieces,
@@ -491,10 +516,13 @@
         gain_f,
         total,
         row_sum,
-        *arrived,
-        static=(width, loss_scale),
-    )
+        static=width,
+    )
+    *arrived, grad_input, gain_z = lax.optimization_barrier((*arrived, grad_input, gain_z))
+    (shared_own,) = call(shared_kernel, [((2 * PIECE, HD), BF16)], [], ids, *arrived)
+    grad_query, grad_out = call(owner_kernel, [((HD, HD), F32)] * 2, [], ids, *arrived, static=loss_scale)
     shared_yl = swap(shared_own, "yl")
+    gain_z = gain_z + swap(gain_z, "yh")
     grad_key, grad_value, grad_gain = call(
         join_kernel,
         [((rows, HD), F32)] * 2 + [((4 * NX, 1, HD), F32)],

time: 153 us -> 149 us (0.974)
  waiting for transfers between devices: 72.2 us -> 59.2 us
  starting transfers between devices: 57.4 us -> 63.1 us
  Pallas kernels: 17.5 us -> 20.3 us
    ppermute x12, waiting for transfers between devices: 29.2 us -> 23.1 us  [shift_x(): return lax.ppermute(value, 'x', [(i, (i + by) % NX) for i in range(NX)])]
    ppermute x13, waiting for transfers between devices: 23.9 us -> 19.2 us  [shift_z(): return lax.ppermute(value, 'z', [(i, (i + by) % NZ) for i in range(NZ)])]
    ppermute x13, starting transfers between devices: 25.9 us -> 29.5 us  [shift_z(): return lax.ppermute(value, 'z', [(i, (i + by) % NZ) for i in range(NZ)])]
    pallas_call x17 -> x21, Pallas kernels: 17.5 us -> 20.3 us  [call(): pl.pallas_call(body, out_shape=[jax.ShapeDtypeStruct(s, d) for s, d in ou...]
    ppermute x1, starting transfers between devices: 0.09 us -> 2.19 us  [local(): other = lax.ppermute(pack, AXES, owner_perm(1))]
    ppermute x14 -> x17, starting transfers between devices: 8.82 us -> 10.6 us  [swap(): return lax.ppermute(value, axis, [(0, 1), (1, 0)])]
    ppermute x14 -> x17, waiting for transfers between devices: 18.6 us -> 16.9 us  [swap(): return lax.ppermute(value, axis, [(0, 1), (1, 0)])]
  transfers between devices with their start and end apart: 43 -> 46, of which waited for: 25 -> 25; matrix products, arithmetic and copies ran while one was open for 0% -> 0% of each run, Pallas kernels for 5% -> 7%
where the time goes in v4:
time: 149 us; the launch traced here: 147 us
  starting transfers between devices  63.1 us (42%)
  waiting for transfers between devices  59.2 us (40%)
  Pallas kernels  20.3 us (14%)
  local copies, waits for them, and re-layouts  2.92 us (2%)
    ppermute x13, starting transfers between devices, shift_z(): return lax.ppermute(value, 'z', [(i, (i + by) % NZ) for i in range(NZ)])  29.5 us
    ppermute x12, waiting for transfers between devices, shift_x(): return lax.ppermute(value, 'x', [(i, (i + by) % NX) for i in range(NX)])  23.1 us
    pallas_call x21, Pallas kernels, call(): pl.pallas_call(body, out_shape=[jax.ShapeDtypeStruct(s, d) for s, d in ou...  20.3 us
    ppermute x13, waiting for transfers between devices, shift_z(): return lax.ppermute(value, 'z', [(i, (i + by) % NZ) for i in range(NZ)])  19.2 us
    ppermute x17, waiting for transfers between devices, swap(): return lax.ppermute(value, axis, [(0, 1), (1, 0)])  16.9 us
    ppermute x12, starting transfers between devices, shift_x(): return lax.ppermute(value, 'x', [(i, (i + by) % NX) for i in range(NX)])  15.6 us
    ppermute x17, starting transfers between devices, swap(): return lax.ppermute(value, axis, [(0, 1), (1, 0)])  10.6 us
  transfers between devices with their start and end apart: 46, of which 25 were waited for; matrix products, arithmetic and copies ran while one was open for 0% of the time, Pallas kernels for 7%

profile of v4, /device:TPU:8, one launch (start us, length us, event | category | flops | bytes accessed | tf_op | source)
XLA Modules:
  0.0 147.3 jit_solution(10893678292994500065)
XLA Ops:
  2.2 2.2 %collective-permute-start.1 = (bf16[320,128]{1,0:T(8,128)(2,1)S(1)}, bf16[320,128]{1,0:T(8,128)(2,1)S(1)}, u32[]{:S(2)}, u32[]{:S(2)}) collective-permute-start(bf16[320,128]{1,0:T(8,128)(2,1)S(1)} %pad_maximum_fusion), channel_id=1, source_target_pairs={{0,128},{1,132},{2,0},{3,4},{4,160},{5,164},{6,32},{7,36},{8,136},... | collective-permute-start | bytes 245768 | tf_op jit(solution)/shard_map/ppermute | solution.py:403
  4.3 2.6 %collective-permute-start = (bf16[320,128]{1,0:T(8,128)(2,1)S(1)}, bf16[320,128]{1,0:T(8,128)(2,1)S(1)}, u32[]{:S(2)}, u32[]{:S(2)}) collective-permute-start(bf16[320,128]{1,0:T(8,128)(2,1)S(1)} %pad_maximum_fusion), channel_id=1, source_target_pairs={{0,0},{1,4},{2,128},{3,132},{4,32},{5,36},{6,160},{7,164},{8,8},{9... | collective-permute-start | bytes 245768 | tf_op jit(solution)/shard_map/ppermute | solution.py:402
  10.0 2.0 %collective-permute-start.2 = (f32[1,128]{1,0:T(1,128)S(1)}, f32[1,128]{1,0:T(1,128)S(1)}, u32[]{:S(2)}, u32[]{:S(2)}) collective-permute-start(f32[1,128]{1,0:T(1,128)S(1)} %get-tuple-element.72), channel_id=1, source_target_pairs={{0,1},{1,0},{2,3},{3,2},{4,5},{5,4},{6,7},{7,6},{8,9},{9,8},{10,11... | collective-permute-start | bytes 1544 | tf_op jit(solution)/shard_map/ppermute | solution.py:56
  12.9 6.4 %collective-permute-start.8 = (bf16[640,128]{1,0:T(8,128)(2,1)S(1)}, bf16[640,128]{1,0:T(8,128)(2,1)S(1)}, u32[]{:S(2)}, u32[]{:S(2)}) collective-permute-start(bf16[640,128]{1,0:T(8,128)(2,1)S(1)} %maximum_select_fusion.both), channel_id=1, source_target_pairs={{0,24},{4,28},{8,0},{12,4},{16,8},{20,12},{24,16},{28,20},{1,25},{... | collective-permute-start | bytes 491528 | tf_op jit(solution)/shard_map/ppermute | solution.py:52
  20.7 2.2 %collective-permute-done.3 = f32[1,128]{1,0:T(1,128)S(1)} collective-permute-done((f32[1,128]{1,0:T(1,128)S(1)}, f32[1,128]{1,0:T(1,128)S(1)}, u32[]{:S(2)}, u32[]{:S(2)}) %collective-permute-start.3) | collective-permute-done | bytes 544 | tf_op jit(solution)/shard_map/ppermute | solution.py:56
  24.5 3.0 %collective-permute-start.5 = (bf16[272,512]{1,0:T(8,128)(2,1)S(1)}, bf16[272,512]{1,0:T(8,128)(2,1)S(1)}, u32[]{:S(2)}, u32[]{:S(2)}) collective-permute-start(bf16[272,512]{1,0:T(8,128)(2,1)S(1)} %get-tuple-element.80), channel_id=1, source_target_pairs={{0,64},{32,96},{64,0},{96,32},{1,65},{33,97},{65,1},{97,33},{2,66}... | collective-permute-start | bytes 835592 | tf_op jit(solution)/shard_map/ppermute | solution.py:48
  27.5 3.6 %collective-permute-done.7.prev.prev2 = bf16[640,128]{1,0:T(8,128)(2,1)S(1)} collective-permute-done((bf16[640,128]{1,0:T(8,128)(2,1)S(1)}, bf16[640,128]{1,0:T(8,128)(2,1)S(1)}, u32[]{:S(2)}, u32[]{:S(2)}) %collective-permute-start.7) | collective-permute-done | bytes 163872 | tf_op jit(solution)/shard_map/ppermute | solution.py:52
  33.1 2.0 %collective-permute-start.10 = (bf16[1280,128]{1,0:T(8,128)(2,1)S(1)}, bf16[1280,128]{1,0:T(8,128)(2,1)S(1)}, u32[]{:S(2)}, u32[]{:S(2)}) collective-permute-start(bf16[1280,128]{1,0:T(8,128)(2,1)S(1)} %get-tuple-element.87), channel_id=1, source_target_pairs={{0,28},{4,0},{8,4},{12,8},{16,12},{20,16},{24,20},{28,24},{1,29},{... | collective-permute-start | bytes 983048 | tf_op jit(solution)/shard_map/ppermute | solution.py:52
  35.9 2.5 %collective-permute-done.4.refs_1_ = bf16[272,512]{1,0:T(8,128)(2,1)S(1)} collective-permute-done((bf16[272,512]{1,0:T(8,128)(2,1)S(1)}, bf16[272,512]{1,0:T(8,128)(2,1)S(1)}, u32[]{:S(2)}, u32[]{:S(2)}) %collective-permute-start.4) | collective-permute-done | bytes 278560 | tf_op jit(solution)/shard_map/ppermute | solution.py:48
  40.0 2.6 %collective-permute-start.12 = (bf16[320,128]{1,0:T(8,128)(2,1)S(1)}, bf16[320,128]{1,0:T(8,128)(2,1)S(1)}, u32[]{:S(2)}, u32[]{:S(2)}) collective-permute-start(bf16[320,128]{1,0:T(8,128)(2,1)S(1)} %get-tuple-element.89), channel_id=1, source_target_pairs={{0,24},{4,28},{8,0},{12,4},{16,8},{20,12},{24,16},{28,20},{1,25},{... | collective-permute-start | bytes 245768 | tf_op jit(solution)/shard_map/ppermute | solution.py:52
  51.7 2.2 %collective-permute-start.17 = (bf16[128,1024]{1,0:T(8,128)(2,1)S(1)}, bf16[128,1024]{1,0:T(8,128)(2,1)S(1)}, u32[]{:S(2)}, u32[]{:S(2)}) collective-permute-start(bf16[128,1024]{1,0:T(8,128)(2,1)S(1)} %shard_map.126), channel_id=1, source_target_pairs={{0,64},{32,96},{64,0},{96,32},{1,65},{33,97},{65,1},{97,33},{2,66}... | collective-permute-start | bytes 786440 | tf_op jit(solution)/shard_map/ppermute | solution.py:48
  55.8 3.0 %collective-permute-done.15.a = bf16[128,1024]{1,0:T(8,128)(2,1)S(1)} collective-permute-done((bf16[128,1024]{1,0:T(8,128)(2,1)S(1)}, bf16[128,1024]{1,0:T(8,128)(2,1)S(1)}, u32[]{:S(2)}, u32[]{:S(2)}) %collective-permute-start.15) | collective-permute-done | bytes 262176 | tf_op jit(solution)/shard_map/ppermute | solution.py:48
  58.8 3.7 %collective-permute-done.17.b = bf16[128,1024]{1,0:T(8,128)(2,1)S(1)} collective-permute-done((bf16[128,1024]{1,0:T(8,128)(2,1)S(1)}, bf16[128,1024]{1,0:T(8,128)(2,1)S(1)}, u32[]{:S(2)}, u32[]{:S(2)}) %collective-permute-start.17) | collective-permute-done | bytes 262176 | tf_op jit(solution)/shard_map/ppermute | solution.py:48
  62.5 4.4 %collective-permute-done.19.c = bf16[128,1024]{1,0:T(8,128)(2,1)S(1)} collective-permute-done((bf16[128,1024]{1,0:T(8,128)(2,1)S(1)}, bf16[128,1024]{1,0:T(8,128)(2,1)S(1)}, u32[]{:S(2)}, u32[]{:S(2)}) %collective-permute-start.19) | collective-permute-done | bytes 262176 | tf_op jit(solution)/shard_map/ppermute | solution.py:48
  69.0 6.9 %collective-permute-done.20.got = bf16[128,1024]{1,0:T(8,128)(2,1)S(1)} collective-permute-done((bf16[128,1024]{1,0:T(8,128)(2,1)S(1)}, bf16[128,1024]{1,0:T(8,128)(2,1)S(1)}, u32[]{:S(2)}, u32[]{:S(2)}) %collective-permute-start.20) | collective-permute-done | bytes 262176 | tf_op jit(solution)/shard_map/ppermute | solution.py:56
  79.6 2.2 %collective-permute-start.23 = (bf16[128,768]{1,0:T(8,128)(2,1)S(1)}, bf16[128,768]{1,0:T(8,128)(2,1)S(1)}, u32[]{:S(2)}, u32[]{:S(2)}) collective-permute-start(bf16[128,768]{1,0:T(8,128)(2,1)S(1)} %get-tuple-element.102.refs_0_), channel_id=1, source_target_pairs={{0,64},{32,96},{64,0},{96,32},{1,65},{33,97},{65,1},{97,33},{2,66}... | collective-permute-start | bytes 589832 | tf_op jit(solution)/shard_map/ppermute | solution.py:48
  83.1 4.2 %collective-permute-done.24.refs_3_ = bf16[128,768]{1,0:T(8,128)(2,1)S(1)} collective-permute-done((bf16[128,768]{1,0:T(8,128)(2,1)S(1)}, bf16[128,768]{1,0:T(8,128)(2,1)S(1)}, u32[]{:S(2)}, u32[]{:S(2)}) %collective-permute-start.24) | collective-permute-done | bytes 196640 | tf_op jit(solution)/shard_map/ppermute | solution.py:48
  89.0 3.4 %collective-permute-done.22.refs_1_ = bf16[128,768]{1,0:T(8,128)(2,1)S(1)} collective-permute-done((bf16[128,768]{1,0:T(8,128)(2,1)S(1)}, bf16[128,768]{1,0:T(8,128)(2,1)S(1)}, u32[]{:S(2)}, u32[]{:S(2)}) %collective-permute-start.22) | collective-permute-done | bytes 196640 | tf_op jit(solution)/shard_map/ppermute | solution.py:48
  93.8 2.8 %shard_map.131 = (bf16[656,128]{1,0:T(8,128)(2,1)S(1)}, bf16[1296,128]{1,0:T(8,128)(2,1)S(1)}, bf16[1296,128]{1,0:T(8,128)(2,1)S(1)}, bf16[640,128]{1,0:T(8,128)...) custom-call(s32[5]{0:T(128)S(1)} %stack.23.ids, ...), custom_call_target="tpu_custom_call" | custom-call | tf_op jit(solution)/shard_map/pallas_call | solution.py:73
  97.7 2.7 %collective-permute-start.31 = (bf16[1296,128]{1,0:T(8,128)(2,1)S(1)}, bf16[1296,128]{1,0:T(8,128)(2,1)S(1)}, u32[]{:S(2)}, u32[]{:S(2)}) collective-permute-start(bf16[1296,128]{1,0:T(8,128)(2,1)S(1)} %get-tuple-element.109), channel_id=1, source_target_pairs={{0,28},{4,0},{8,4},{12,8},{16,12},{20,16},{24,20},{28,24},{1,29},{... | collective-permute-start | bytes 995336 | tf_op jit(solution)/shard_map/ppermute | solution.py:52
  101.7 2.8 %collective-permute-start.33 = (bf16[336,128]{1,0:T(8,128)(2,1)S(1)}, bf16[336,128]{1,0:T(8,128)(2,1)S(1)}, u32[]{:S(2)}, u32[]{:S(2)}) collective-permute-start(bf16[336,128]{1,0:T(8,128)(2,1)S(1)} %get-tuple-element.113), channel_id=1, source_target_pairs={{0,24},{4,28},{8,0},{12,4},{16,8},{20,12},{24,16},{28,20},{1,25},{... | collective-permute-start | bytes 258056 | tf_op jit(solution)/shard_map/ppermute | solution.py:52
  105.6 3.1 %collective-permute-done.29.a = bf16[1296,128]{1,0:T(8,128)(2,1)S(1)} collective-permute-done((bf16[1296,128]{1,0:T(8,128)(2,1)S(1)}, bf16[1296,128]{1,0:T(8,128)(2,1)S(1)}, u32[]{:S(2)}, u32[]{:S(2)}) %collective-permute-start.29) | collective-permute-done | bytes 331808 | tf_op jit(solution)/shard_map/ppermute | solution.py:52
  108.7 4.3 %collective-permute-done.32.c = bf16[336,128]{1,0:T(8,128)(2,1)S(1)} collective-permute-done((bf16[336,128]{1,0:T(8,128)(2,1)S(1)}, bf16[336,128]{1,0:T(8,128)(2,1)S(1)}, u32[]{:S(2)}, u32[]{:S(2)}) %collective-permute-start.32) | collective-permute-done | bytes 86048 | tf_op jit(solution)/shard_map/ppermute | solution.py:52
  113.8 3.1 %collective-permute-start.34 = (bf16[640,128]{1,0:T(8,128)(2,1)S(1)}, bf16[640,128]{1,0:T(8,128)(2,1)S(1)}, u32[]{:S(2)}, u32[]{:S(2)}) collective-permute-start(bf16[640,128]{1,0:T(8,128)(2,1)S(1)} %get-tuple-element.118), channel_id=1, source_target_pairs={{0,8},{4,12},{8,16},{12,20},{16,24},{20,28},{24,0},{28,4},{1,9},{5... | collective-permute-start | bytes 491528 | tf_op jit(solution)/shard_map/ppermute | solution.py:52
  120.8 2.3 %collective-permute-done.34.up = bf16[640,128]{1,0:T(8,128)(2,1)S(1)} collective-permute-done((bf16[640,128]{1,0:T(8,128)(2,1)S(1)}, bf16[640,128]{1,0:T(8,128)(2,1)S(1)}, u32[]{:S(2)}, u32[]{:S(2)}) %collective-permute-start.34) | collective-permute-done | bytes 163872 | tf_op jit(solution)/shard_map/ppermute | solution.py:52
  125.3 2.6 %collective-permute-start.36 = (bf16[320,128]{1,0:T(8,128)(2,1)S(1)}, bf16[320,128]{1,0:T(8,128)(2,1)S(1)}, u32[]{:S(2)}, u32[]{:S(2)}) collective-permute-start(bf16[320,128]{1,0:T(8,128)(2,1)S(1)} %get-tuple-element.120), channel_id=1, source_target_pairs={{0,0},{4,1},{128,2},{132,3},{32,4},{36,5},{160,6},{164,7},{8,8},{1... | collective-permute-start | bytes 245768 | tf_op jit(solution)/shard_map/ppermute | solution.py:506
  128.8 3.6 %collective-permute-start.41 = (f32[16,128]{1,0:T(8,128)S(1)}, f32[16,128]{1,0:T(8,128)S(1)}, u32[]{:S(2)}, u32[]{:S(2)}) collective-permute-start(f32[16,128]{1,0:T(8,128)S(1)} %get-tuple-element.128), channel_id=1, source_target_pairs={{0,16},{4,20},{8,24},{12,28},{16,0},{20,4},{24,8},{28,12},{1,17},{... | collective-permute-start | bytes 24584 | tf_op jit(solution)/shard_map/ppermute | solution.py:52
  132.4 1.9 %shard_map.134 = f32[128,2048]{1,0:T(8,128)} custom-call(s32[5]{0:T(128)S(1)} %stack.23.ids, bf16[144,512]{1,0:T(8,128)(2,1)S(1)} %get-tuple-element.122.a.refs_0_, bf16[144,512]{1,0:T(8,128)(2,1)S(1)} %collective-permute-done.38.b.refs_1_, bf16[144,512]{1,0:T(8,128)(2,1)S(1)} %collective-permute-done.39.c.refs_2_, ...), custom_call_target="tpu_custom_call" | custom-call | tf_op jit(solution)/shard_map/pallas_call | solution.py:73
  134.3 2.2 %collective-permute-done.41 = f32[16,128]{1,0:T(8,128)S(1)} collective-permute-done((f32[16,128]{1,0:T(8,128)S(1)}, f32[16,128]{1,0:T(8,128)S(1)}, u32[]{:S(2)}, u32[]{:S(2)}) %collective-permute-start.41) | collective-permute-done | bytes 8224 | tf_op jit(solution)/shard_map/ppermute | solution.py:52
  137.1 1.8 %collective-permute-start.43 = (bf16[64,128]{1,0:T(8,128)(2,1)S(1)}, bf16[64,128]{1,0:T(8,128)(2,1)S(1)}, u32[]{:S(2)}, u32[]{:S(2)}) collective-permute-start(bf16[64,128]{1,0:T(8,128)(2,1)S(1)} %shard_map.136.own), channel_id=1, source_target_pairs={{0,2},{2,0},{1,3},{3,1},{4,6},{6,4},{5,7},{7,5},{8,10},{10,8},{9,1... | collective-permute-start | bytes 49160 | tf_op jit(solution)/shard_map/ppermute | solution.py:56
  138.9 2.0 %collective-permute-done.43.by_yl = bf16[64,128]{1,0:T(8,128)(2,1)S(1)} collective-permute-done((bf16[64,128]{1,0:T(8,128)(2,1)S(1)}, bf16[64,128]{1,0:T(8,128)(2,1)S(1)}, u32[]{:S(2)}, u32[]{:S(2)}) %collective-permute-start.43) | collective-permute-done | bytes 16416 | tf_op jit(solution)/shard_map/ppermute | solution.py:56
  140.9 2.7 %collective-permute-start.45 = (f32[16,128]{1,0:T(8,128)S(1)}, f32[16,128]{1,0:T(8,128)S(1)}, u32[]{:S(2)}, u32[]{:S(2)}) collective-permute-start(f32[16,128]{1,0:T(8,128)S(1)} %add.27), channel_id=1, source_target_pairs={{0,128},{128,0},{1,129},{129,1},{2,130},{130,2},{3,131},{131,3},{4... | collective-permute-start | bytes 24584 | tf_op jit(solution)/shard_map/ppermute | solution.py:56
  (101 shorter events, 49.7 us)
Async XLA Ops:
  2.2 10.7 %collective-permute-start.1 = (bf16[320,128]{1,0:T(8,128)(2,1)S(1)}, bf16[320,128]{1,0:T(8,128)(2,1)S(1)}, u32[]{:S(2)}, u32[]{:S(2)}) collective-permute-start(bf16[320,128]{1,0:T(8,128)(2,1)S(1)} %pad_maximum_fusion), channel_id=1, source_target_pairs={{0,128},{1,132},{2,0},{3,4},{4,160},{5,164},{6,32},{7,36},{8,136},... | collective-permute-start | bytes 245768 | tf_op jit(solution)/shard_map/ppermute | solution.py:403
  4.3 8.6 %collective-permute-start = (bf16[320,128]{1,0:T(8,128)(2,1)S(1)}, bf16[320,128]{1,0:T(8,128)(2,1)S(1)}, u32[]{:S(2)}, u32[]{:S(2)}) collective-permute-start(bf16[320,128]{1,0:T(8,128)(2,1)S(1)} %pad_maximum_fusion), channel_id=1, source_target_pairs={{0,0},{1,4},{2,128},{3,132},{4,32},{5,36},{6,160},{7,164},{8,8},{9... | collective-permute-start | bytes 245768 | tf_op jit(solution)/shard_map/ppermute | solution.py:402
  12.9 14.5 %collective-permute-start.8 = (bf16[640,128]{1,0:T(8,128)(2,1)S(1)}, bf16[640,128]{1,0:T(8,128)(2,1)S(1)}, u32[]{:S(2)}, u32[]{:S(2)}) collective-permute-start(bf16[640,128]{1,0:T(8,128)(2,1)S(1)} %maximum_select_fusion.both), channel_id=1, source_target_pairs={{0,24},{4,28},{8,0},{12,4},{16,8},{20,12},{24,16},{28,20},{1,25},{... | collective-permute-start | bytes 491528 | tf_op jit(solution)/shard_map/ppermute | solution.py:52
  19.3 11.8 %collective-permute-start.7 = (bf16[640,128]{1,0:T(8,128)(2,1)S(1)}, bf16[640,128]{1,0:T(8,128)(2,1)S(1)}, u32[]{:S(2)}, u32[]{:S(2)}) collective-permute-start(bf16[640,128]{1,0:T(8,128)(2,1)S(1)} %maximum_select_fusion.both), channel_id=1, source_target_pairs={{0,8},{4,12},{8,16},{12,20},{16,24},{20,28},{24,0},{28,4},{1,9},{5... | collective-permute-start | bytes 491528 | tf_op jit(solution)/shard_map/ppermute | solution.py:52
  23.4 15.0 %collective-permute-start.4 = (bf16[272,512]{1,0:T(8,128)(2,1)S(1)}, bf16[272,512]{1,0:T(8,128)(2,1)S(1)}, u32[]{:S(2)}, u32[]{:S(2)}) collective-permute-start(bf16[272,512]{1,0:T(8,128)(2,1)S(1)} %get-tuple-element.79), channel_id=1, source_target_pairs={{0,32},{32,64},{64,96},{96,0},{1,33},{33,65},{65,97},{97,1},{2,34}... | collective-permute-start | bytes 835592 | tf_op jit(solution)/shard_map/ppermute | solution.py:48
  24.5 15.5 %collective-permute-start.5 = (bf16[272,512]{1,0:T(8,128)(2,1)S(1)}, bf16[272,512]{1,0:T(8,128)(2,1)S(1)}, u32[]{:S(2)}, u32[]{:S(2)}) collective-permute-start(bf16[272,512]{1,0:T(8,128)(2,1)S(1)} %get-tuple-element.80), channel_id=1, source_target_pairs={{0,64},{32,96},{64,0},{96,32},{1,65},{33,97},{65,1},{97,33},{2,66}... | collective-permute-start | bytes 835592 | tf_op jit(solution)/shard_map/ppermute | solution.py:48
  31.8 13.6 %collective-permute-start.9 = (bf16[1280,128]{1,0:T(8,128)(2,1)S(1)}, bf16[1280,128]{1,0:T(8,128)(2,1)S(1)}, u32[]{:S(2)}, u32[]{:S(2)}) collective-permute-start(bf16[1280,128]{1,0:T(8,128)(2,1)S(1)} %get-tuple-element.86), channel_id=1, source_target_pairs={{0,4},{4,8},{8,12},{12,16},{16,20},{20,24},{24,28},{28,0},{1,5},{5... | collective-permute-start | bytes 983048 | tf_op jit(solution)/shard_map/ppermute | solution.py:52
  33.1 12.2 %collective-permute-start.10 = (bf16[1280,128]{1,0:T(8,128)(2,1)S(1)}, bf16[1280,128]{1,0:T(8,128)(2,1)S(1)}, u32[]{:S(2)}, u32[]{:S(2)}) collective-permute-start(bf16[1280,128]{1,0:T(8,128)(2,1)S(1)} %get-tuple-element.87), channel_id=1, source_target_pairs={{0,28},{4,0},{8,4},{12,8},{16,12},{20,16},{24,20},{28,24},{1,29},{... | collective-permute-start | bytes 983048 | tf_op jit(solution)/shard_map/ppermute | solution.py:52
  35.1 7.5 %collective-permute-start.6 = (bf16[272,512]{1,0:T(8,128)(2,1)S(1)}, bf16[272,512]{1,0:T(8,128)(2,1)S(1)}, u32[]{:S(2)}, u32[]{:S(2)}) collective-permute-start(bf16[272,512]{1,0:T(8,128)(2,1)S(1)} %get-tuple-element.81), channel_id=1, source_target_pairs={{0,96},{32,0},{64,32},{96,64},{1,97},{33,1},{65,33},{97,65},{2,98}... | collective-permute-start | bytes 835592 | tf_op jit(solution)/shard_map/ppermute | solution.py:48
  38.4 6.6 %collective-permute-start.11 = (bf16[320,128]{1,0:T(8,128)(2,1)S(1)}, bf16[320,128]{1,0:T(8,128)(2,1)S(1)}, u32[]{:S(2)}, u32[]{:S(2)}) collective-permute-start(bf16[320,128]{1,0:T(8,128)(2,1)S(1)} %get-tuple-element.88), channel_id=1, source_target_pairs={{0,8},{4,12},{8,16},{12,20},{16,24},{20,28},{24,0},{28,4},{1,9},{5... | collective-permute-start | bytes 245768 | tf_op jit(solution)/shard_map/ppermute | solution.py:52
  47.4 7.8 %collective-permute-start.13 = (f32[128,640]{1,0:T(8,128)S(1)}, f32[128,640]{1,0:T(8,128)S(1)}, u32[]{:S(2)}, u32[]{:S(2)}) collective-permute-start(f32[128,640]{1,0:T(8,128)S(1)} %get-tuple-element.93), channel_id=1, source_target_pairs={{0,1},{1,0},{2,3},{3,2},{4,5},{5,4},{6,7},{7,6},{8,9},{9,8},{10,11... | collective-permute-start | bytes 983048 | tf_op jit(solution)/shard_map/ppermute | solution.py:56
  49.6 9.2 %collective-permute-start.15 = (bf16[128,1024]{1,0:T(8,128)(2,1)S(1)}, bf16[128,1024]{1,0:T(8,128)(2,1)S(1)}, u32[]{:S(2)}, u32[]{:S(2)}) collective-permute-start(bf16[128,1024]{1,0:T(8,128)(2,1)S(1)} %shard_map.125), channel_id=1, source_target_pairs={{0,96},{32,0},{64,32},{96,64},{1,97},{33,1},{65,33},{97,65},{2,98}... | collective-permute-start | bytes 786440 | tf_op jit(solution)/shard_map/ppermute | solution.py:48
  51.7 10.8 %collective-permute-start.17 = (bf16[128,1024]{1,0:T(8,128)(2,1)S(1)}, bf16[128,1024]{1,0:T(8,128)(2,1)S(1)}, u32[]{:S(2)}, u32[]{:S(2)}) collective-permute-start(bf16[128,1024]{1,0:T(8,128)(2,1)S(1)} %shard_map.126), channel_id=1, source_target_pairs={{0,64},{32,96},{64,0},{96,32},{1,65},{33,97},{65,1},{97,33},{2,66}... | collective-permute-start | bytes 786440 | tf_op jit(solution)/shard_map/ppermute | solution.py:48
  54.5 12.4 %collective-permute-start.19 = (bf16[128,1024]{1,0:T(8,128)(2,1)S(1)}, bf16[128,1024]{1,0:T(8,128)(2,1)S(1)}, u32[]{:S(2)}, u32[]{:S(2)}) collective-permute-start(bf16[128,1024]{1,0:T(8,128)(2,1)S(1)} %shard_map.127), channel_id=1, source_target_pairs={{0,32},{32,64},{64,96},{96,0},{1,33},{33,65},{65,97},{97,1},{2,34}... | collective-permute-start | bytes 786440 | tf_op jit(solution)/shard_map/ppermute | solution.py:48
  67.6 8.3 %collective-permute-start.20 = (bf16[128,1024]{1,0:T(8,128)(2,1)S(1)}, bf16[128,1024]{1,0:T(8,128)(2,1)S(1)}, u32[]{:S(2)}, u32[]{:S(2)}) collective-permute-start(bf16[128,1024]{1,0:T(8,128)(2,1)S(1)} %shard_map.128.mine), channel_id=1, source_target_pairs={{0,2},{2,0},{1,3},{3,1},{4,6},{6,4},{5,7},{7,5},{8,10},{10,8},{9,1... | collective-permute-start | bytes 786440 | tf_op jit(solution)/shard_map/ppermute | solution.py:56
  79.5 7.8 %collective-permute-start.24 = (bf16[128,768]{1,0:T(8,128)(2,1)S(1)}, bf16[128,768]{1,0:T(8,128)(2,1)S(1)}, u32[]{:S(2)}, u32[]{:S(2)}) collective-permute-start(bf16[128,768]{1,0:T(8,128)(2,1)S(1)} %get-tuple-element.102.refs_0_), channel_id=1, source_target_pairs={{0,96},{32,0},{64,32},{96,64},{1,97},{33,1},{65,33},{97,65},{2,98}... | collective-permute-start | bytes 589832 | tf_op jit(solution)/shard_map/ppermute | solution.py:48
  79.6 9.4 %collective-permute-start.23 = (bf16[128,768]{1,0:T(8,128)(2,1)S(1)}, bf16[128,768]{1,0:T(8,128)(2,1)S(1)}, u32[]{:S(2)}, u32[]{:S(2)}) collective-permute-start(bf16[128,768]{1,0:T(8,128)(2,1)S(1)} %get-tuple-element.102.refs_0_), channel_id=1, source_target_pairs={{0,64},{32,96},{64,0},{96,32},{1,65},{33,97},{65,1},{97,33},{2,66}... | collective-permute-start | bytes 589832 | tf_op jit(solution)/shard_map/ppermute | solution.py:48
  81.8 10.6 %collective-permute-start.22 = (bf16[128,768]{1,0:T(8,128)(2,1)S(1)}, bf16[128,768]{1,0:T(8,128)(2,1)S(1)}, u32[]{:S(2)}, u32[]{:S(2)}) collective-permute-start(bf16[128,768]{1,0:T(8,128)(2,1)S(1)} %get-tuple-element.102.refs_0_), channel_id=1, source_target_pairs={{0,32},{32,64},{64,96},{96,0},{1,33},{33,65},{65,97},{97,1},{2,34}... | collective-permute-start | bytes 589832 | tf_op jit(solution)/shard_map/ppermute | solution.py:48
  83.1 9.3 %collective-permute-start.25 = (bf16[128,768]{1,0:T(8,128)(2,1)S(1)}, bf16[128,768]{1,0:T(8,128)(2,1)S(1)}, u32[]{:S(2)}, u32[]{:S(2)}) collective-permute-start(bf16[128,768]{1,0:T(8,128)(2,1)S(1)} %get-tuple-element.102.refs_0_), channel_id=1, source_target_pairs={{0,1},{1,0},{2,3},{3,2},{4,5},{5,4},{6,7},{7,6},{8,9},{9,8},{10,11... | collective-permute-start | bytes 589832 | tf_op jit(solution)/shard_map/ppermute | solution.py:56
  96.6 12.1 %collective-permute-start.29 = (bf16[1296,128]{1,0:T(8,128)(2,1)S(1)}, bf16[1296,128]{1,0:T(8,128)(2,1)S(1)}, u32[]{:S(2)}, u32[]{:S(2)}) collective-permute-start(bf16[1296,128]{1,0:T(8,128)(2,1)S(1)} %get-tuple-element.106), channel_id=1, source_target_pairs={{0,4},{4,8},{8,12},{12,16},{16,20},{20,24},{24,28},{28,0},{1,5},{5... | collective-permute-start | bytes 995336 | tf_op jit(solution)/shard_map/ppermute | solution.py:52
  97.7 15.5 %collective-permute-start.31 = (bf16[1296,128]{1,0:T(8,128)(2,1)S(1)}, bf16[1296,128]{1,0:T(8,128)(2,1)S(1)}, u32[]{:S(2)}, u32[]{:S(2)}) collective-permute-start(bf16[1296,128]{1,0:T(8,128)(2,1)S(1)} %get-tuple-element.109), channel_id=1, source_target_pairs={{0,28},{4,0},{8,4},{12,8},{16,12},{20,16},{24,20},{28,24},{1,29},{... | collective-permute-start | bytes 995336 | tf_op jit(solution)/shard_map/ppermute | solution.py:52
  100.3 12.7 %collective-permute-start.32 = (bf16[336,128]{1,0:T(8,128)(2,1)S(1)}, bf16[336,128]{1,0:T(8,128)(2,1)S(1)}, u32[]{:S(2)}, u32[]{:S(2)}) collective-permute-start(bf16[336,128]{1,0:T(8,128)(2,1)S(1)} %get-tuple-element.112), channel_id=1, source_target_pairs={{0,8},{4,12},{8,16},{12,20},{16,24},{20,28},{24,0},{28,4},{1,9},{5... | collective-permute-start | bytes 258056 | tf_op jit(solution)/shard_map/ppermute | solution.py:52
  101.7 11.5 %collective-permute-start.33 = (bf16[336,128]{1,0:T(8,128)(2,1)S(1)}, bf16[336,128]{1,0:T(8,128)(2,1)S(1)}, u32[]{:S(2)}, u32[]{:S(2)}) collective-permute-start(bf16[336,128]{1,0:T(8,128)(2,1)S(1)} %get-tuple-element.113), channel_id=1, source_target_pairs={{0,24},{4,28},{8,0},{12,4},{16,8},{20,12},{24,16},{28,20},{1,25},{... | collective-permute-start | bytes 258056 | tf_op jit(solution)/shard_map/ppermute | solution.py:52
  113.8 9.2 %collective-permute-start.34 = (bf16[640,128]{1,0:T(8,128)(2,1)S(1)}, bf16[640,128]{1,0:T(8,128)(2,1)S(1)}, u32[]{:S(2)}, u32[]{:S(2)}) collective-permute-start(bf16[640,128]{1,0:T(8,128)(2,1)S(1)} %get-tuple-element.118), channel_id=1, source_target_pairs={{0,8},{4,12},{8,16},{12,20},{16,24},{20,28},{24,0},{28,4},{1,9},{5... | collective-permute-start | bytes 491528 | tf_op jit(solution)/shard_map/ppermute | solution.py:52
  116.9 7.8 %collective-permute-start.35 = (bf16[640,128]{1,0:T(8,128)(2,1)S(1)}, bf16[640,128]{1,0:T(8,128)(2,1)S(1)}, u32[]{:S(2)}, u32[]{:S(2)}) collective-permute-start(bf16[640,128]{1,0:T(8,128)(2,1)S(1)} %get-tuple-element.119), channel_id=1, source_target_pairs={{0,24},{4,28},{8,0},{12,4},{16,8},{20,12},{24,16},{28,20},{1,25},{... | collective-permute-start | bytes 491528 | tf_op jit(solution)/shard_map/ppermute | solution.py:52
  118.0 10.0 %collective-permute-start.38 = (bf16[144,512]{1,0:T(8,128)(2,1)S(1)}, bf16[144,512]{1,0:T(8,128)(2,1)S(1)}, u32[]{:S(2)}, u32[]{:S(2)}) collective-permute-start(bf16[144,512]{1,0:T(8,128)(2,1)S(1)} %get-tuple-element.123), channel_id=1, source_target_pairs={{0,96},{32,0},{64,32},{96,64},{1,97},{33,1},{65,33},{97,65},{2,98}... | collective-permute-start | bytes 442376 | tf_op jit(solution)/shard_map/ppermute | solution.py:48
  119.5 8.5 %collective-permute-start.39 = (bf16[144,512]{1,0:T(8,128)(2,1)S(1)}, bf16[144,512]{1,0:T(8,128)(2,1)S(1)}, u32[]{:S(2)}, u32[]{:S(2)}) collective-permute-start(bf16[144,512]{1,0:T(8,128)(2,1)S(1)} %get-tuple-element.124), channel_id=1, source_target_pairs={{0,64},{32,96},{64,0},{96,32},{1,65},{33,97},{65,1},{97,33},{2,66}... | collective-permute-start | bytes 442376 | tf_op jit(solution)/shard_map/ppermute | solution.py:48
  120.0 8.3 %collective-permute-start.40 = (bf16[144,512]{1,0:T(8,128)(2,1)S(1)}, bf16[144,512]{1,0:T(8,128)(2,1)S(1)}, u32[]{:S(2)}, u32[]{:S(2)}) collective-permute-start(bf16[144,512]{1,0:T(8,128)(2,1)S(1)} %get-tuple-element.125), channel_id=1, source_target_pairs={{0,32},{32,64},{64,96},{96,0},{1,33},{33,65},{65,97},{97,1},{2,34}... | collective-permute-start | bytes 442376 | tf_op jit(solution)/shard_map/ppermute | solution.py:48
  125.3 11.2 %collective-permute-start.36 = (bf16[320,128]{1,0:T(8,128)(2,1)S(1)}, bf16[320,128]{1,0:T(8,128)(2,1)S(1)}, u32[]{:S(2)}, u32[]{:S(2)}) collective-permute-start(bf16[320,128]{1,0:T(8,128)(2,1)S(1)} %get-tuple-element.120), channel_id=1, source_target_pairs={{0,0},{4,1},{128,2},{132,3},{32,4},{36,5},{160,6},{164,7},{8,8},{1... | collective-permute-start | bytes 245768 | tf_op jit(solution)/shard_map/ppermute | solution.py:506
  127.9 8.6 %collective-permute-start.37 = (bf16[320,128]{1,0:T(8,128)(2,1)S(1)}, bf16[320,128]{1,0:T(8,128)(2,1)S(1)}, u32[]{:S(2)}, u32[]{:S(2)}) collective-permute-start(bf16[320,128]{1,0:T(8,128)(2,1)S(1)} %get-tuple-element.121), channel_id=1, source_target_pairs={{128,0},{132,1},{0,2},{4,3},{160,4},{164,5},{32,6},{36,7},{136,8},... | collective-permute-start | bytes 245768 | tf_op jit(solution)/shard_map/ppermute | solution.py:506
  128.8 7.7 %collective-permute-start.41 = (f32[16,128]{1,0:T(8,128)S(1)}, f32[16,128]{1,0:T(8,128)S(1)}, u32[]{:S(2)}, u32[]{:S(2)}) collective-permute-start(f32[16,128]{1,0:T(8,128)S(1)} %get-tuple-element.128), channel_id=1, source_target_pairs={{0,16},{4,20},{8,24},{12,28},{16,0},{20,4},{24,8},{28,12},{1,17},{... | collective-permute-start | bytes 24584 | tf_op jit(solution)/shard_map/ppermute | solution.py:52
  138.9 7.2 %collective-permute-start.42 = (bf16[64,128]{1,0:T(8,128)(2,1)S(1)}, bf16[64,128]{1,0:T(8,128)(2,1)S(1)}, u32[]{:S(2)}, u32[]{:S(2)}) collective-permute-start(bf16[64,128]{1,0:T(8,128)(2,1)S(1)} %shard_map.136.own), channel_id=1, source_target_pairs={{0,1},{1,0},{2,3},{3,2},{4,5},{5,4},{6,7},{7,6},{8,9},{9,8},{10,11... | collective-permute-start | bytes 49160 | tf_op jit(solution)/shard_map/ppermute | solution.py:56
  (19 other events, 71.9 us)

commit v5 on v4

--- a/solution.py
+++ b/solution.py
@@ -257,9 +257,8 @@
 
 def gradient_kernel(ids, *refs):
     mine, theirs, (normed_t, cot, unit, w_all) = refs[:4], refs[4:8], refs[8:12]
-    (t0, up, down, t2, m2, t4a, t4b), back = refs[12:19], refs[19:23]
-    heads, attended, shared = refs[23:]
-    z, c = ids[0], ids[2]
+    (up, down, t4a, t4b), back, (gain_out, heads, attended, shared) = refs[12:16], refs[16:20], refs[20:]
+    c = ids[2]
     for s in range(NX):
         rows = slice(s * HD, (s + 1) * HD)
         for ref, side in ((mine[s], c), (theirs[s], 1 - c)):
@@ -282,22 +281,35 @@
 
     shared[...] = dot(normed_t[...], heads[:, 4 * HD :], 1, 0)
     g, n = GROWS, BLOCK
-    for ref in (t0, up, down, t4a, t4b):
+    for ref in (up, down, t4a, t4b):
         ref[:g] = gain_rows
-    for d, out_first, out_second in (
-        (0, t0.at[g : g + n], t0.at[g + n :]),
-        (1, up.at[g : g + n], up.at[g + n : g + 2 * n]),
-        (3, up.at[g + 2 * n : g + 3 * n], up.at[g + 3 * n :]),
-        (-1, down.at[g : g + n], down.at[g + n : g + 2 * n]),
-        (-3, down.at[g + 2 * n : g + 3 * n], down.at[g + 3 * n :]),
-        (2, t2.at[:n], t2.at[n:]),
-        (-2, m2.at[:n], m2.at[n:]),
-        (4, t4a.at[g:], t4b.at[g:]),
-    ):
+    terms(
+        ids,
+        normed_t,
+        cot,
+        heads,
+        attended,
+        shared,
+        (
+            (1, up.at[g : g + n], up.at[g + n : g + 2 * n]),
+            (3, up.at[g + 2 * n : g + 3 * n], up.at[g + 3 * n :]),
+            (-1, down.at[g : g + n], down.at[g + n : g + 2 * n]),
+            (-3, down.at[g + 2 * n : g + 3 * n], down.at[g + 3 * n :]),
+            (4, t4a.at[g:], t4b.at[g:]),
+        ),
+    )
+    gain_out[...] = gain_rows
+
+
+def terms(ids, normed_t, cot, heads, attended, shared, places):
+    z = ids[0]
+    for d, out_first, out_second in places:
         zt = (z + d + NZ) % NZ
         side, j = zt % 2, zt // 2
-        g_q = dot(normed_t[pl.ds(pl.multiple_of(j * HD, HD), HD)], heads[:, lanes(side * 2 * HD, 2 * HD)], 1, 0).astype(BF16)
-        g_o = dot(attended[pl.ds(pl.multiple_of(side * 2 * HD, 2 * HD), 2 * HD)], cot[:, lanes(j * HD)], 1, 0).astype(BF16)
+        rows = pl.ds(pl.multiple_of(j * HD, HD), HD)
+        g_q = dot(normed_t[rows], heads[:, lanes(side * 2 * HD, 2 * HD)], 1, 0).astype(BF16)
+        rows = pl.ds(pl.multiple_of(side * 2 * HD, 2 * HD), 2 * HD)
+        g_o = dot(attended[rows], cot[:, lanes(j * HD)], 1, 0).astype(BF16)
         for half, out in enumerate((out_first, out_second)):
             out[:HD] = g_q[:, half * HD : (half + 1) * HD]
             out[HD : 2 * HD] = g_o[half * HD : (half + 1) * HD]
@@ -306,7 +318,12 @@
             out[2 * HD + PIECE :] = part[:, HD:]
 
 
-def relay_kernel(ids, t2, m2, a, b, c, d, t0, *refs):
+def near_kernel(ids, normed_t, cot, heads, attended, shared, t0, t2, m2):
+    n = BLOCK
+    terms(ids, normed_t, cot, heads, attended, shared, [(d, r.at[:n], r.at[n:]) for d, r in ((0, t0), (2, t2), (-2, m2))])
+
+
+def relay_kernel(ids, t2, m2, a, b, c, d, gain_own, *refs):
     up, down, *back = refs[NX:]
     g, n = GROWS, BLOCK
     total = t2[...].astype(F32) + a[g + 2 * n :].astype(F32)
@@ -315,7 +332,7 @@
     total = m2[...].astype(F32) + b[g + 2 * n :].astype(F32)
     down[:n] = total[:n].astype(BF16)
     down[n:] = (total[n:] + d[g:].astype(F32)).astype(BF16)
-    three = t0[:g].astype(F32) + a[:g].astype(F32) + b[:g].astype(F32)
+    three = gain_own[...].astype(F32) + a[:g].astype(F32) + b[:g].astype(F32)
     five = three + c[:g].astype(F32) + d[:g].astype(F32)
     terms = []
     for rows in (five, three):
@@ -332,20 +349,21 @@
     g, n = GROWS, BLOCK
     flip = ids[3]
     near = slice(g, g + 2 * n)
-    total = t0[near].astype(F32) + a[near].astype(F32) + b[near].astype(F32)
+    total = t0[...].astype(F32) + a[near].astype(F32) + b[near].astype(F32)
     total = total + up[...].astype(F32) + down[...].astype(F32)
     same[...] = jnp.where(flip == 0, total[:n], total[n:]).astype(BF16)
     other[...] = jnp.where(flip == 0, total[n:], total[:n]).astype(BF16)
 
 
 def gain_kernel(ids, *refs):
-    five, three = refs[NX:]
+    out = refs[NX]
     for s in range(NX):
         rows = refs[s][HD:].astype(F32)
-        for out, at in ((five, 0), (three, 2)):
+        for at in (0, 2):
             value = rows[at : at + 1] + rows[at + 1 : at + 2]
             for j in range(4):
-                out[4 * s + j : 4 * s + j + 1] = value[:, j * HD : (j + 1) * HD]
+                row = 2 * NX * at + 4 * s + j
+                out[row : row + 1] = value[:, j * HD : (j + 1) * HD]
 
 
 def input_kernel(width, ids, a, b, c, d, tokens, gain, total, row_sum, out):
@@ -460,19 +478,13 @@
     heads = [heads] + [shift_x(heads, s) for s in range(1, NX)]
 
     g, n = GROWS, BLOCK
-    t0, up, down, t2, m2, t4a, t4b, *back = call(
+    up, down, t4a, t4b, *back, gain_own, d_heads, attended_t, shared_terms = call(
         gradient_kernel,
-        [
-            ((g + 2 * n, HD), BF16),
-            ((g + 4 * n, HD), BF16),
-            ((g + 4 * n, HD), BF16),
-            ((2 * n, HD), BF16),
-            ((2 * n, HD), BF16),
-            ((g + n, HD), BF16),
-            ((g + n, HD), BF16),
-        ]
-        + [((rows + GROWS, sub), BF16)] * 4,
-        [((512, 6 * HD), BF16), ((512, 4 * HD), BF16), ((sub, 2 * HD), F32)],
+        [((g + 4 * n, HD), BF16)] * 2
+        + [((g + n, HD), BF16)] * 2
+        + [((rows + g, sub), BF16)] * 4
+        + [((g, HD), BF16), ((512, 6 * HD), BF16), ((4 * HD, 512), BF16), ((sub, 2 * HD), F32)],
+        [],
         ids,
         *heads,
         *[swap(h, "c") for h in heads],
@@ -481,6 +493,9 @@
         unit_sw,
         w_all,
     )
+    t0, t2, m2 = call(
+        near_kernel, [((2 * n, HD), BF16)] * 3, [], ids, normed_t, cot_sw, d_heads, attended_t, shared_terms
+    )
     c4, d4 = shift_z(t4a, 2), shift_z(t4b, -2)
     a, b = shift_z(up, 1), shift_z(down, -1)
     a, row_sum = lax.optimization_barrier((a, row_sum))
@@ -495,7 +510,7 @@
         b,
         c4,
         d4,
-        t0,
+        gain_own,
         *back,
         aliases={8 + s: 2 + s for s in range(NX)},
     )
@@ -504,8 +519,8 @@
     pieces = [back[0]] + [shift_x(back[s], -s) for s in range(1, NX)]
     to_same, to_other = call(finish_kernel, [((n, HD), BF16)] * 2, [], ids, t0, a, b, up, down)
     arrived = (lax.ppermute(to_same, AXES, inverse(owner_perm(0))), lax.ppermute(to_other, AXES, inverse(owner_perm(1))))
-    gain_five, gain_three = call(gain_kernel, [((4 * NX, HD), F32)] * 2, [], ids, *pieces)
-    gain_z = gain_five + shift_z(gain_three, 4)
+    (gain_z,) = call(gain_kernel, [((8 * NX, HD), F32)], [], ids, *pieces)
+    gain_z = gain_z + swap(gain_z, "yh")
     (grad_input,) = call(
         input_kernel,
         [((rows, quarter), F32)],
@@ -522,7 +537,7 @@
     (shared_own,) = call(shared_kernel, [((2 * PIECE, HD), BF16)], [], ids, *arrived)
     grad_query, grad_out = call(owner_kernel, [((HD, HD), F32)] * 2, [], ids, *arrived, static=loss_scale)
     shared_yl = swap(shared_own, "yl")
-    gain_z = gain_z + swap(gain_z, "yh")
+    gain_z = gain_z[: 4 * NX] + shift_z(gain_z[4 * NX :], 4)
     grad_key, grad_value, grad_gain = call(
         join_kernel,
         [((rows, HD), F32)] * 2 + [((4 * NX, 1, HD), F32)],

time: 149 us -> 148 us (level)
  waiting for transfers between devices: 59.2 us -> 56.5 us
    ppermute x17, waiting for transfers between devices: 16.9 us -> 14.6 us  [swap(): return lax.ppermute(value, axis, [(0, 1), (1, 0)])]
    pallas_call x21 -> x22, Pallas kernels: 20.3 us -> 21.1 us  [call(): pl.pallas_call(body, out_shape=[jax.ShapeDtypeStruct(s, d) for s, d in ou...]
  transfers between devices with their start and end apart: 46 -> 46, of which waited for: 25 -> 24; matrix products, arithmetic and copies ran while one was open for 0% -> 0% of each run, Pallas kernels for 7% -> 8%
where the time goes in v5:
time: 148 us; the launch traced here: 145 us
  starting transfers between devices  63 us (43%)
  waiting for transfers between devices  56.5 us (38%)
  Pallas kernels  21.1 us (14%)
  local copies, waits for them, and re-layouts  2.92 us (2%)
    ppermute x13, starting transfers between devices, shift_z(): return lax.ppermute(value, 'z', [(i, (i + by) % NZ) for i in range(NZ)])  29.1 us
    ppermute x12, waiting for transfers between devices, shift_x(): return lax.ppermute(value, 'x', [(i, (i + by) % NX) for i in range(NX)])  23.3 us
    pallas_call x22, Pallas kernels, call(): pl.pallas_call(body, out_shape=[jax.ShapeDtypeStruct(s, d) for s, d in ou...  21.1 us
    ppermute x13, waiting for transfers between devices, shift_z(): return lax.ppermute(value, 'z', [(i, (i + by) % NZ) for i in range(NZ)])  18.6 us
    ppermute x12, starting transfers between devices, shift_x(): return lax.ppermute(value, 'x', [(i, (i + by) % NX) for i in range(NX)])  15.7 us
    ppermute x17, waiting for transfers between devices, swap(): return lax.ppermute(value, axis, [(0, 1), (1, 0)])  14.6 us
    ppermute x17, starting transfers between devices, swap(): return lax.ppermute(value, axis, [(0, 1), (1, 0)])  10.9 us
  transfers between devices with their start and end apart: 46, of which 24 were waited for; matrix products, arithmetic and copies ran while one was open for 0% of the time, Pallas kernels for 8%

profile of v5, /device:TPU:8, one launch (start us, length us, event | category | flops | bytes accessed | tf_op | source)
XLA Modules:
  0.0 145.2 jit_solution(17140337996680843825)
XLA Ops:
  2.2 2.2 %collective-permute-start.1 = (bf16[320,128]{1,0:T(8,128)(2,1)S(1)}, bf16[320,128]{1,0:T(8,128)(2,1)S(1)}, u32[]{:S(2)}, u32[]{:S(2)}) collective-permute-start(bf16[320,128]{1,0:T(8,128)(2,1)S(1)} %pad_maximum_fusion), channel_id=1, source_target_pairs={{0,128},{1,132},{2,0},{3,4},{4,160},{5,164},{6,32},{7,36},{8,136},... | collective-permute-start | bytes 245768 | tf_op jit(solution)/shard_map/ppermute | solution.py:421
  4.3 2.6 %collective-permute-start = (bf16[320,128]{1,0:T(8,128)(2,1)S(1)}, bf16[320,128]{1,0:T(8,128)(2,1)S(1)}, u32[]{:S(2)}, u32[]{:S(2)}) collective-permute-start(bf16[320,128]{1,0:T(8,128)(2,1)S(1)} %pad_maximum_fusion), channel_id=1, source_target_pairs={{0,0},{1,4},{2,128},{3,132},{4,32},{5,36},{6,160},{7,164},{8,8},{9... | collective-permute-start | bytes 245768 | tf_op jit(solution)/shard_map/ppermute | solution.py:420
  10.0 2.0 %collective-permute-start.2 = (f32[1,128]{1,0:T(1,128)S(1)}, f32[1,128]{1,0:T(1,128)S(1)}, u32[]{:S(2)}, u32[]{:S(2)}) collective-permute-start(f32[1,128]{1,0:T(1,128)S(1)} %get-tuple-element.74), channel_id=1, source_target_pairs={{0,1},{1,0},{2,3},{3,2},{4,5},{5,4},{6,7},{7,6},{8,9},{9,8},{10,11... | collective-permute-start | bytes 1544 | tf_op jit(solution)/shard_map/ppermute | solution.py:56
  12.9 6.4 %collective-permute-start.8 = (bf16[640,128]{1,0:T(8,128)(2,1)S(1)}, bf16[640,128]{1,0:T(8,128)(2,1)S(1)}, u32[]{:S(2)}, u32[]{:S(2)}) collective-permute-start(bf16[640,128]{1,0:T(8,128)(2,1)S(1)} %maximum_select_fusion.both), channel_id=1, source_target_pairs={{0,24},{4,28},{8,0},{12,4},{16,8},{20,12},{24,16},{28,20},{1,25},{... | collective-permute-start | bytes 491528 | tf_op jit(solution)/shard_map/ppermute | solution.py:52
  20.7 2.2 %collective-permute-done.3 = f32[1,128]{1,0:T(1,128)S(1)} collective-permute-done((f32[1,128]{1,0:T(1,128)S(1)}, f32[1,128]{1,0:T(1,128)S(1)}, u32[]{:S(2)}, u32[]{:S(2)}) %collective-permute-start.3) | collective-permute-done | bytes 544 | tf_op jit(solution)/shard_map/ppermute | solution.py:56
  24.5 3.0 %collective-permute-start.5 = (bf16[272,512]{1,0:T(8,128)(2,1)S(1)}, bf16[272,512]{1,0:T(8,128)(2,1)S(1)}, u32[]{:S(2)}, u32[]{:S(2)}) collective-permute-start(bf16[272,512]{1,0:T(8,128)(2,1)S(1)} %get-tuple-element.82), channel_id=1, source_target_pairs={{0,64},{32,96},{64,0},{96,32},{1,65},{33,97},{65,1},{97,33},{2,66}... | collective-permute-start | bytes 835592 | tf_op jit(solution)/shard_map/ppermute | solution.py:48
  27.5 3.6 %collective-permute-done.7.prev.prev2 = bf16[640,128]{1,0:T(8,128)(2,1)S(1)} collective-permute-done((bf16[640,128]{1,0:T(8,128)(2,1)S(1)}, bf16[640,128]{1,0:T(8,128)(2,1)S(1)}, u32[]{:S(2)}, u32[]{:S(2)}) %collective-permute-start.7) | collective-permute-done | bytes 163872 | tf_op jit(solution)/shard_map/ppermute | solution.py:52
  33.1 2.0 %collective-permute-start.10 = (bf16[1280,128]{1,0:T(8,128)(2,1)S(1)}, bf16[1280,128]{1,0:T(8,128)(2,1)S(1)}, u32[]{:S(2)}, u32[]{:S(2)}) collective-permute-start(bf16[1280,128]{1,0:T(8,128)(2,1)S(1)} %get-tuple-element.89), channel_id=1, source_target_pairs={{0,28},{4,0},{8,4},{12,8},{16,12},{20,16},{24,20},{28,24},{1,29},{... | collective-permute-start | bytes 983048 | tf_op jit(solution)/shard_map/ppermute | solution.py:52
  35.9 2.5 %collective-permute-done.4.refs_1_ = bf16[272,512]{1,0:T(8,128)(2,1)S(1)} collective-permute-done((bf16[272,512]{1,0:T(8,128)(2,1)S(1)}, bf16[272,512]{1,0:T(8,128)(2,1)S(1)}, u32[]{:S(2)}, u32[]{:S(2)}) %collective-permute-start.4) | collective-permute-done | bytes 278560 | tf_op jit(solution)/shard_map/ppermute | solution.py:48
  40.0 2.6 %collective-permute-start.12 = (bf16[320,128]{1,0:T(8,128)(2,1)S(1)}, bf16[320,128]{1,0:T(8,128)(2,1)S(1)}, u32[]{:S(2)}, u32[]{:S(2)}) collective-permute-start(bf16[320,128]{1,0:T(8,128)(2,1)S(1)} %get-tuple-element.91), channel_id=1, source_target_pairs={{0,24},{4,28},{8,0},{12,4},{16,8},{20,12},{24,16},{28,20},{1,25},{... | collective-permute-start | bytes 245768 | tf_op jit(solution)/shard_map/ppermute | solution.py:52
  51.7 2.2 %collective-permute-start.17 = (bf16[128,1024]{1,0:T(8,128)(2,1)S(1)}, bf16[128,1024]{1,0:T(8,128)(2,1)S(1)}, u32[]{:S(2)}, u32[]{:S(2)}) collective-permute-start(bf16[128,1024]{1,0:T(8,128)(2,1)S(1)} %shard_map.126), channel_id=1, source_target_pairs={{0,64},{32,96},{64,0},{96,32},{1,65},{33,97},{65,1},{97,33},{2,66}... | collective-permute-start | bytes 786440 | tf_op jit(solution)/shard_map/ppermute | solution.py:48
  55.8 3.0 %collective-permute-done.15.a = bf16[128,1024]{1,0:T(8,128)(2,1)S(1)} collective-permute-done((bf16[128,1024]{1,0:T(8,128)(2,1)S(1)}, bf16[128,1024]{1,0:T(8,128)(2,1)S(1)}, u32[]{:S(2)}, u32[]{:S(2)}) %collective-permute-start.15) | collective-permute-done | bytes 262176 | tf_op jit(solution)/shard_map/ppermute | solution.py:48
  58.8 3.7 %collective-permute-done.17.b = bf16[128,1024]{1,0:T(8,128)(2,1)S(1)} collective-permute-done((bf16[128,1024]{1,0:T(8,128)(2,1)S(1)}, bf16[128,1024]{1,0:T(8,128)(2,1)S(1)}, u32[]{:S(2)}, u32[]{:S(2)}) %collective-permute-start.17) | collective-permute-done | bytes 262176 | tf_op jit(solution)/shard_map/ppermute | solution.py:48
  62.5 4.4 %collective-permute-done.19.c = bf16[128,1024]{1,0:T(8,128)(2,1)S(1)} collective-permute-done((bf16[128,1024]{1,0:T(8,128)(2,1)S(1)}, bf16[128,1024]{1,0:T(8,128)(2,1)S(1)}, u32[]{:S(2)}, u32[]{:S(2)}) %collective-permute-start.19) | collective-permute-done | bytes 262176 | tf_op jit(solution)/shard_map/ppermute | solution.py:48
  69.0 6.9 %collective-permute-done.20.got = bf16[128,1024]{1,0:T(8,128)(2,1)S(1)} collective-permute-done((bf16[128,1024]{1,0:T(8,128)(2,1)S(1)}, bf16[128,1024]{1,0:T(8,128)(2,1)S(1)}, u32[]{:S(2)}, u32[]{:S(2)}) %collective-permute-start.20) | collective-permute-done | bytes 262176 | tf_op jit(solution)/shard_map/ppermute | solution.py:56
  77.8 1.7 %shard_map.130 = (bf16[128,768]{1,0:T(8,128)(2,1)S(1)}, f32[1,128]{1,0:T(1,128)S(1)}) custom-call(s32[5]{0:T(128)S(1)} %stack.23.ids, bf16[128,512]{1,0:T(8,128)(2,1)S(1)} %get-tuple-element.103.qa, bf16[128,128]{1,0:T(8,128)(2,1)S(1)} %get-tuple-element.104.kv_mine, bf16[128,128]{1,0:T(8,128)(2,1)S(1)} %collective-permute-done.21.kv_theirs), custom_call_target="tpu_custom_call" | custom-call | tf_op jit(solution)/shard_map/pallas_call | solution.py:73
  79.6 2.2 %collective-permute-start.23 = (bf16[128,768]{1,0:T(8,128)(2,1)S(1)}, bf16[128,768]{1,0:T(8,128)(2,1)S(1)}, u32[]{:S(2)}, u32[]{:S(2)}) collective-permute-start(bf16[128,768]{1,0:T(8,128)(2,1)S(1)} %get-tuple-element.105.refs_0_), channel_id=1, source_target_pairs={{0,64},{32,96},{64,0},{96,32},{1,65},{33,97},{65,1},{97,33},{2,66}... | collective-permute-start | bytes 589832 | tf_op jit(solution)/shard_map/ppermute | solution.py:48
  83.1 4.2 %collective-permute-done.24.refs_3_ = bf16[128,768]{1,0:T(8,128)(2,1)S(1)} collective-permute-done((bf16[128,768]{1,0:T(8,128)(2,1)S(1)}, bf16[128,768]{1,0:T(8,128)(2,1)S(1)}, u32[]{:S(2)}, u32[]{:S(2)}) %collective-permute-start.24) | collective-permute-done | bytes 196640 | tf_op jit(solution)/shard_map/ppermute | solution.py:48
  87.3 1.6 %collective-permute-done.23.refs_2_ = bf16[128,768]{1,0:T(8,128)(2,1)S(1)} collective-permute-done((bf16[128,768]{1,0:T(8,128)(2,1)S(1)}, bf16[128,768]{1,0:T(8,128)(2,1)S(1)}, u32[]{:S(2)}, u32[]{:S(2)}) %collective-permute-start.23) | collective-permute-done | bytes 196640 | tf_op jit(solution)/shard_map/ppermute | solution.py:48
  89.0 3.4 %collective-permute-done.22.refs_1_ = bf16[128,768]{1,0:T(8,128)(2,1)S(1)} collective-permute-done((bf16[128,768]{1,0:T(8,128)(2,1)S(1)}, bf16[128,768]{1,0:T(8,128)(2,1)S(1)}, u32[]{:S(2)}, u32[]{:S(2)}) %collective-permute-start.22) | collective-permute-done | bytes 196640 | tf_op jit(solution)/shard_map/ppermute | solution.py:48
  93.8 2.5 %shard_map.131 = (bf16[1296,128]{1,0:T(8,128)(2,1)S(1)}, bf16[1296,128]{1,0:T(8,128)(2,1)S(1)}, bf16[336,128]{1,0:T(8,128)(2,1)S(1)}, bf16[336,128]{1,0:T(8,128)...) custom-call(s32[5]{0:T(128)S(1)} %stack.23.ids, ...), custom_call_target="tpu_custom_call" | custom-call | tf_op jit(solution)/shard_map/pallas_call | solution.py:73
  97.4 2.4 %collective-permute-start.31 = (bf16[1296,128]{1,0:T(8,128)(2,1)S(1)}, bf16[1296,128]{1,0:T(8,128)(2,1)S(1)}, u32[]{:S(2)}, u32[]{:S(2)}) collective-permute-start(bf16[1296,128]{1,0:T(8,128)(2,1)S(1)} %get-tuple-element.114), channel_id=1, source_target_pairs={{0,28},{4,0},{8,4},{12,8},{16,12},{20,16},{24,20},{28,24},{1,29},{... | collective-permute-start | bytes 995336 | tf_op jit(solution)/shard_map/ppermute | solution.py:52
  101.4 2.6 %collective-permute-start.33 = (bf16[336,128]{1,0:T(8,128)(2,1)S(1)}, bf16[336,128]{1,0:T(8,128)(2,1)S(1)}, u32[]{:S(2)}, u32[]{:S(2)}) collective-permute-start(bf16[336,128]{1,0:T(8,128)(2,1)S(1)} %get-tuple-element.118), channel_id=1, source_target_pairs={{0,24},{4,28},{8,0},{12,4},{16,8},{20,12},{24,16},{28,20},{1,25},{... | collective-permute-start | bytes 258056 | tf_op jit(solution)/shard_map/ppermute | solution.py:52
  106.1 2.3 %collective-permute-done.29.a = bf16[1296,128]{1,0:T(8,128)(2,1)S(1)} collective-permute-done((bf16[1296,128]{1,0:T(8,128)(2,1)S(1)}, bf16[1296,128]{1,0:T(8,128)(2,1)S(1)}, u32[]{:S(2)}, u32[]{:S(2)}) %collective-permute-start.29) | collective-permute-done | bytes 331808 | tf_op jit(solution)/shard_map/ppermute | solution.py:52
  108.4 4.3 %collective-permute-done.32.c = bf16[336,128]{1,0:T(8,128)(2,1)S(1)} collective-permute-done((bf16[336,128]{1,0:T(8,128)(2,1)S(1)}, bf16[336,128]{1,0:T(8,128)(2,1)S(1)}, u32[]{:S(2)}, u32[]{:S(2)}) %collective-permute-start.32) | collective-permute-done | bytes 86048 | tf_op jit(solution)/shard_map/ppermute | solution.py:52
  113.5 2.9 %collective-permute-start.34 = (bf16[640,128]{1,0:T(8,128)(2,1)S(1)}, bf16[640,128]{1,0:T(8,128)(2,1)S(1)}, u32[]{:S(2)}, u32[]{:S(2)}) collective-permute-start(bf16[640,128]{1,0:T(8,128)(2,1)S(1)} %get-tuple-element.124), channel_id=1, source_target_pairs={{0,8},{4,12},{8,16},{12,20},{16,24},{20,28},{24,0},{28,4},{1,9},{5... | collective-permute-start | bytes 491528 | tf_op jit(solution)/shard_map/ppermute | solution.py:52
  120.5 2.3 %collective-permute-done.34.up = bf16[640,128]{1,0:T(8,128)(2,1)S(1)} collective-permute-done((bf16[640,128]{1,0:T(8,128)(2,1)S(1)}, bf16[640,128]{1,0:T(8,128)(2,1)S(1)}, u32[]{:S(2)}, u32[]{:S(2)}) %collective-permute-start.34) | collective-permute-done | bytes 163872 | tf_op jit(solution)/shard_map/ppermute | solution.py:52
  125.0 2.5 %collective-permute-start.36 = (bf16[320,128]{1,0:T(8,128)(2,1)S(1)}, bf16[320,128]{1,0:T(8,128)(2,1)S(1)}, u32[]{:S(2)}, u32[]{:S(2)}) collective-permute-start(bf16[320,128]{1,0:T(8,128)(2,1)S(1)} %get-tuple-element.126), channel_id=1, source_target_pairs={{0,0},{4,1},{128,2},{132,3},{32,4},{36,5},{160,6},{164,7},{8,8},{1... | collective-permute-start | bytes 245768 | tf_op jit(solution)/shard_map/ppermute | solution.py:521
  128.5 2.7 %collective-permute-start.41 = (f32[32,128]{1,0:T(8,128)S(1)}, f32[32,128]{1,0:T(8,128)S(1)}, u32[]{:S(2)}, u32[]{:S(2)}) collective-permute-start(f32[32,128]{1,0:T(8,128)S(1)} %shard_map.136), channel_id=1, source_target_pairs={{0,128},{128,0},{1,129},{129,1},{2,130},{130,2},{3,131},{131,3},{4... | collective-permute-start | bytes 49160 | tf_op jit(solution)/shard_map/ppermute | solution.py:56
  131.3 1.9 %shard_map.135 = f32[128,2048]{1,0:T(8,128)} custom-call(s32[5]{0:T(128)S(1)} %stack.23.ids, bf16[144,512]{1,0:T(8,128)(2,1)S(1)} %get-tuple-element.128.a.refs_0_, bf16[144,512]{1,0:T(8,128)(2,1)S(1)} %collective-permute-done.38.b.refs_1_, bf16[144,512]{1,0:T(8,128)(2,1)S(1)} %collective-permute-done.39.c.refs_2_, ...), custom_call_target="tpu_custom_call" | custom-call | tf_op jit(solution)/shard_map/pallas_call | solution.py:73
  136.4 3.3 %collective-permute-start.45 = (f32[16,128]{1,0:T(8,128)S(1)}, f32[16,128]{1,0:T(8,128)S(1)}, u32[]{:S(2)}, u32[]{:S(2)}) collective-permute-start(f32[16,128]{1,0:T(8,128)S(1)} %slice.7), channel_id=1, source_target_pairs={{0,16},{4,20},{8,24},{12,28},{16,0},{20,4},{24,8},{28,12},{1,17},{... | collective-permute-start | bytes 24584 | tf_op jit(solution)/shard_map/ppermute | solution.py:52
  141.4 2.5 %collective-permute-done.45 = f32[16,128]{1,0:T(8,128)S(1)} collective-permute-done((f32[16,128]{1,0:T(8,128)S(1)}, f32[16,128]{1,0:T(8,128)S(1)}, u32[]{:S(2)}, u32[]{:S(2)}) %collective-permute-start.45) | collective-permute-done | bytes 8224 | tf_op jit(solution)/shard_map/ppermute | solution.py:52
  (103 shorter events, 49.7 us)
Async XLA Ops:
  2.2 10.7 %collective-permute-start.1 = (bf16[320,128]{1,0:T(8,128)(2,1)S(1)}, bf16[320,128]{1,0:T(8,128)(2,1)S(1)}, u32[]{:S(2)}, u32[]{:S(2)}) collective-permute-start(bf16[320,128]{1,0:T(8,128)(2,1)S(1)} %pad_maximum_fusion), channel_id=1, source_target_pairs={{0,128},{1,132},{2,0},{3,4},{4,160},{5,164},{6,32},{7,36},{8,136},... | collective-permute-start | bytes 245768 | tf_op jit(solution)/shard_map/ppermute | solution.py:421
  4.3 8.6 %collective-permute-start = (bf16[320,128]{1,0:T(8,128)(2,1)S(1)}, bf16[320,128]{1,0:T(8,128)(2,1)S(1)}, u32[]{:S(2)}, u32[]{:S(2)}) collective-permute-start(bf16[320,128]{1,0:T(8,128)(2,1)S(1)} %pad_maximum_fusion), channel_id=1, source_target_pairs={{0,0},{1,4},{2,128},{3,132},{4,32},{5,36},{6,160},{7,164},{8,8},{9... | collective-permute-start | bytes 245768 | tf_op jit(solution)/shard_map/ppermute | solution.py:420
  12.9 14.5 %collective-permute-start.8 = (bf16[640,128]{1,0:T(8,128)(2,1)S(1)}, bf16[640,128]{1,0:T(8,128)(2,1)S(1)}, u32[]{:S(2)}, u32[]{:S(2)}) collective-permute-start(bf16[640,128]{1,0:T(8,128)(2,1)S(1)} %maximum_select_fusion.both), channel_id=1, source_target_pairs={{0,24},{4,28},{8,0},{12,4},{16,8},{20,12},{24,16},{28,20},{1,25},{... | collective-permute-start | bytes 491528 | tf_op jit(solution)/shard_map/ppermute | solution.py:52
  19.3 11.8 %collective-permute-start.7 = (bf16[640,128]{1,0:T(8,128)(2,1)S(1)}, bf16[640,128]{1,0:T(8,128)(2,1)S(1)}, u32[]{:S(2)}, u32[]{:S(2)}) collective-permute-start(bf16[640,128]{1,0:T(8,128)(2,1)S(1)} %maximum_select_fusion.both), channel_id=1, source_target_pairs={{0,8},{4,12},{8,16},{12,20},{16,24},{20,28},{24,0},{28,4},{1,9},{5... | collective-permute-start | bytes 491528 | tf_op jit(solution)/shard_map/ppermute | solution.py:52
  23.4 15.0 %collective-permute-start.4 = (bf16[272,512]{1,0:T(8,128)(2,1)S(1)}, bf16[272,512]{1,0:T(8,128)(2,1)S(1)}, u32[]{:S(2)}, u32[]{:S(2)}) collective-permute-start(bf16[272,512]{1,0:T(8,128)(2,1)S(1)} %get-tuple-element.81), channel_id=1, source_target_pairs={{0,32},{32,64},{64,96},{96,0},{1,33},{33,65},{65,97},{97,1},{2,34}... | collective-permute-start | bytes 835592 | tf_op jit(solution)/shard_map/ppermute | solution.py:48
  24.5 15.5 %collective-permute-start.5 = (bf16[272,512]{1,0:T(8,128)(2,1)S(1)}, bf16[272,512]{1,0:T(8,128)(2,1)S(1)}, u32[]{:S(2)}, u32[]{:S(2)}) collective-permute-start(bf16[272,512]{1,0:T(8,128)(2,1)S(1)} %get-tuple-element.82), channel_id=1, source_target_pairs={{0,64},{32,96},{64,0},{96,32},{1,65},{33,97},{65,1},{97,33},{2,66}... | collective-permute-start | bytes 835592 | tf_op jit(solution)/shard_map/ppermute | solution.py:48
  31.8 13.6 %collective-permute-start.9 = (bf16[1280,128]{1,0:T(8,128)(2,1)S(1)}, bf16[1280,128]{1,0:T(8,128)(2,1)S(1)}, u32[]{:S(2)}, u32[]{:S(2)}) collective-permute-start(bf16[1280,128]{1,0:T(8,128)(2,1)S(1)} %get-tuple-element.88), channel_id=1, source_target_pairs={{0,4},{4,8},{8,12},{12,16},{16,20},{20,24},{24,28},{28,0},{1,5},{5... | collective-permute-start | bytes 983048 | tf_op jit(solution)/shard_map/ppermute | solution.py:52
  33.1 12.2 %collective-permute-start.10 = (bf16[1280,128]{1,0:T(8,128)(2,1)S(1)}, bf16[1280,128]{1,0:T(8,128)(2,1)S(1)}, u32[]{:S(2)}, u32[]{:S(2)}) collective-permute-start(bf16[1280,128]{1,0:T(8,128)(2,1)S(1)} %get-tuple-element.89), channel_id=1, source_target_pairs={{0,28},{4,0},{8,4},{12,8},{16,12},{20,16},{24,20},{28,24},{1,29},{... | collective-permute-start | bytes 983048 | tf_op jit(solution)/shard_map/ppermute | solution.py:52
  35.1 7.5 %collective-permute-start.6 = (bf16[272,512]{1,0:T(8,128)(2,1)S(1)}, bf16[272,512]{1,0:T(8,128)(2,1)S(1)}, u32[]{:S(2)}, u32[]{:S(2)}) collective-permute-start(bf16[272,512]{1,0:T(8,128)(2,1)S(1)} %get-tuple-element.83), channel_id=1, source_target_pairs={{0,96},{32,0},{64,32},{96,64},{1,97},{33,1},{65,33},{97,65},{2,98}... | collective-permute-start | bytes 835592 | tf_op jit(solution)/shard_map/ppermute | solution.py:48
  38.4 6.6 %collective-permute-start.11 = (bf16[320,128]{1,0:T(8,128)(2,1)S(1)}, bf16[320,128]{1,0:T(8,128)(2,1)S(1)}, u32[]{:S(2)}, u32[]{:S(2)}) collective-permute-start(bf16[320,128]{1,0:T(8,128)(2,1)S(1)} %get-tuple-element.90), channel_id=1, source_target_pairs={{0,8},{4,12},{8,16},{12,20},{16,24},{20,28},{24,0},{28,4},{1,9},{5... | collective-permute-start | bytes 245768 | tf_op jit(solution)/shard_map/ppermute | solution.py:52
  47.3 6.5 %collective-permute-start.18 = (f32[128,640]{1,0:T(8,128)S(1)}, f32[128,640]{1,0:T(8,128)S(1)}, u32[]{:S(2)}, u32[]{:S(2)}) collective-permute-start(f32[128,640]{1,0:T(8,128)S(1)} %get-tuple-element.102), channel_id=1, source_target_pairs={{0,1},{1,0},{2,3},{3,2},{4,5},{5,4},{6,7},{7,6},{8,9},{9,8},{10,11... | collective-permute-start | bytes 983048 | tf_op jit(solution)/shard_map/ppermute | solution.py:56
  47.4 7.8 %collective-permute-start.13 = (f32[128,640]{1,0:T(8,128)S(1)}, f32[128,640]{1,0:T(8,128)S(1)}, u32[]{:S(2)}, u32[]{:S(2)}) collective-permute-start(f32[128,640]{1,0:T(8,128)S(1)} %get-tuple-element.96), channel_id=1, source_target_pairs={{0,1},{1,0},{2,3},{3,2},{4,5},{5,4},{6,7},{7,6},{8,9},{9,8},{10,11... | collective-permute-start | bytes 983048 | tf_op jit(solution)/shard_map/ppermute | solution.py:56
  49.6 9.2 %collective-permute-start.15 = (bf16[128,1024]{1,0:T(8,128)(2,1)S(1)}, bf16[128,1024]{1,0:T(8,128)(2,1)S(1)}, u32[]{:S(2)}, u32[]{:S(2)}) collective-permute-start(bf16[128,1024]{1,0:T(8,128)(2,1)S(1)} %shard_map.125), channel_id=1, source_target_pairs={{0,96},{32,0},{64,32},{96,64},{1,97},{33,1},{65,33},{97,65},{2,98}... | collective-permute-start | bytes 786440 | tf_op jit(solution)/shard_map/ppermute | solution.py:48
  51.7 10.8 %collective-permute-start.17 = (bf16[128,1024]{1,0:T(8,128)(2,1)S(1)}, bf16[128,1024]{1,0:T(8,128)(2,1)S(1)}, u32[]{:S(2)}, u32[]{:S(2)}) collective-permute-start(bf16[128,1024]{1,0:T(8,128)(2,1)S(1)} %shard_map.126), channel_id=1, source_target_pairs={{0,64},{32,96},{64,0},{96,32},{1,65},{33,97},{65,1},{97,33},{2,66}... | collective-permute-start | bytes 786440 | tf_op jit(solution)/shard_map/ppermute | solution.py:48
  54.5 12.4 %collective-permute-start.19 = (bf16[128,1024]{1,0:T(8,128)(2,1)S(1)}, bf16[128,1024]{1,0:T(8,128)(2,1)S(1)}, u32[]{:S(2)}, u32[]{:S(2)}) collective-permute-start(bf16[128,1024]{1,0:T(8,128)(2,1)S(1)} %shard_map.127), channel_id=1, source_target_pairs={{0,32},{32,64},{64,96},{96,0},{1,33},{33,65},{65,97},{97,1},{2,34}... | collective-permute-start | bytes 786440 | tf_op jit(solution)/shard_map/ppermute | solution.py:48
  67.6 8.3 %collective-permute-start.20 = (bf16[128,1024]{1,0:T(8,128)(2,1)S(1)}, bf16[128,1024]{1,0:T(8,128)(2,1)S(1)}, u32[]{:S(2)}, u32[]{:S(2)}) collective-permute-start(bf16[128,1024]{1,0:T(8,128)(2,1)S(1)} %shard_map.128.mine), channel_id=1, source_target_pairs={{0,2},{2,0},{1,3},{3,1},{4,6},{6,4},{5,7},{7,5},{8,10},{10,8},{9,1... | collective-permute-start | bytes 786440 | tf_op jit(solution)/shard_map/ppermute | solution.py:56
  79.5 7.8 %collective-permute-start.24 = (bf16[128,768]{1,0:T(8,128)(2,1)S(1)}, bf16[128,768]{1,0:T(8,128)(2,1)S(1)}, u32[]{:S(2)}, u32[]{:S(2)}) collective-permute-start(bf16[128,768]{1,0:T(8,128)(2,1)S(1)} %get-tuple-element.105.refs_0_), channel_id=1, source_target_pairs={{0,96},{32,0},{64,32},{96,64},{1,97},{33,1},{65,33},{97,65},{2,98}... | collective-permute-start | bytes 589832 | tf_op jit(solution)/shard_map/ppermute | solution.py:48
  79.6 9.4 %collective-permute-start.23 = (bf16[128,768]{1,0:T(8,128)(2,1)S(1)}, bf16[128,768]{1,0:T(8,128)(2,1)S(1)}, u32[]{:S(2)}, u32[]{:S(2)}) collective-permute-start(bf16[128,768]{1,0:T(8,128)(2,1)S(1)} %get-tuple-element.105.refs_0_), channel_id=1, source_target_pairs={{0,64},{32,96},{64,0},{96,32},{1,65},{33,97},{65,1},{97,33},{2,66}... | collective-permute-start | bytes 589832 | tf_op jit(solution)/shard_map/ppermute | solution.py:48
  81.8 10.6 %collective-permute-start.22 = (bf16[128,768]{1,0:T(8,128)(2,1)S(1)}, bf16[128,768]{1,0:T(8,128)(2,1)S(1)}, u32[]{:S(2)}, u32[]{:S(2)}) collective-permute-start(bf16[128,768]{1,0:T(8,128)(2,1)S(1)} %get-tuple-element.105.refs_0_), channel_id=1, source_target_pairs={{0,32},{32,64},{64,96},{96,0},{1,33},{33,65},{65,97},{97,1},{2,34}... | collective-permute-start | bytes 589832 | tf_op jit(solution)/shard_map/ppermute | solution.py:48
  83.1 9.3 %collective-permute-start.25 = (bf16[128,768]{1,0:T(8,128)(2,1)S(1)}, bf16[128,768]{1,0:T(8,128)(2,1)S(1)}, u32[]{:S(2)}, u32[]{:S(2)}) collective-permute-start(bf16[128,768]{1,0:T(8,128)(2,1)S(1)} %get-tuple-element.105.refs_0_), channel_id=1, source_target_pairs={{0,1},{1,0},{2,3},{3,2},{4,5},{5,4},{6,7},{7,6},{8,9},{9,8},{10,11... | collective-permute-start | bytes 589832 | tf_op jit(solution)/shard_map/ppermute | solution.py:56
  96.3 12.1 %collective-permute-start.29 = (bf16[1296,128]{1,0:T(8,128)(2,1)S(1)}, bf16[1296,128]{1,0:T(8,128)(2,1)S(1)}, u32[]{:S(2)}, u32[]{:S(2)}) collective-permute-start(bf16[1296,128]{1,0:T(8,128)(2,1)S(1)} %get-tuple-element.111), channel_id=1, source_target_pairs={{0,4},{4,8},{8,12},{12,16},{16,20},{20,24},{24,28},{28,0},{1,5},{5... | collective-permute-start | bytes 995336 | tf_op jit(solution)/shard_map/ppermute | solution.py:52
  97.4 15.5 %collective-permute-start.31 = (bf16[1296,128]{1,0:T(8,128)(2,1)S(1)}, bf16[1296,128]{1,0:T(8,128)(2,1)S(1)}, u32[]{:S(2)}, u32[]{:S(2)}) collective-permute-start(bf16[1296,128]{1,0:T(8,128)(2,1)S(1)} %get-tuple-element.114), channel_id=1, source_target_pairs={{0,28},{4,0},{8,4},{12,8},{16,12},{20,16},{24,20},{28,24},{1,29},{... | collective-permute-start | bytes 995336 | tf_op jit(solution)/shard_map/ppermute | solution.py:52
  99.8 12.9 %collective-permute-start.32 = (bf16[336,128]{1,0:T(8,128)(2,1)S(1)}, bf16[336,128]{1,0:T(8,128)(2,1)S(1)}, u32[]{:S(2)}, u32[]{:S(2)}) collective-permute-start(bf16[336,128]{1,0:T(8,128)(2,1)S(1)} %get-tuple-element.117), channel_id=1, source_target_pairs={{0,8},{4,12},{8,16},{12,20},{16,24},{20,28},{24,0},{28,4},{1,9},{5... | collective-permute-start | bytes 258056 | tf_op jit(solution)/shard_map/ppermute | solution.py:52
  101.4 11.5 %collective-permute-start.33 = (bf16[336,128]{1,0:T(8,128)(2,1)S(1)}, bf16[336,128]{1,0:T(8,128)(2,1)S(1)}, u32[]{:S(2)}, u32[]{:S(2)}) collective-permute-start(bf16[336,128]{1,0:T(8,128)(2,1)S(1)} %get-tuple-element.118), channel_id=1, source_target_pairs={{0,24},{4,28},{8,0},{12,4},{16,8},{20,12},{24,16},{28,20},{1,25},{... | collective-permute-start | bytes 258056 | tf_op jit(solution)/shard_map/ppermute | solution.py:52
  113.5 9.3 %collective-permute-start.34 = (bf16[640,128]{1,0:T(8,128)(2,1)S(1)}, bf16[640,128]{1,0:T(8,128)(2,1)S(1)}, u32[]{:S(2)}, u32[]{:S(2)}) collective-permute-start(bf16[640,128]{1,0:T(8,128)(2,1)S(1)} %get-tuple-element.124), channel_id=1, source_target_pairs={{0,8},{4,12},{8,16},{12,20},{16,24},{20,28},{24,0},{28,4},{1,9},{5... | collective-permute-start | bytes 491528 | tf_op jit(solution)/shard_map/ppermute | solution.py:52
  116.4 7.9 %collective-permute-start.35 = (bf16[640,128]{1,0:T(8,128)(2,1)S(1)}, bf16[640,128]{1,0:T(8,128)(2,1)S(1)}, u32[]{:S(2)}, u32[]{:S(2)}) collective-permute-start(bf16[640,128]{1,0:T(8,128)(2,1)S(1)} %get-tuple-element.125), channel_id=1, source_target_pairs={{0,24},{4,28},{8,0},{12,4},{16,8},{20,12},{24,16},{28,20},{1,25},{... | collective-permute-start | bytes 491528 | tf_op jit(solution)/shard_map/ppermute | solution.py:52
  117.7 9.8 %collective-permute-start.38 = (bf16[144,512]{1,0:T(8,128)(2,1)S(1)}, bf16[144,512]{1,0:T(8,128)(2,1)S(1)}, u32[]{:S(2)}, u32[]{:S(2)}) collective-permute-start(bf16[144,512]{1,0:T(8,128)(2,1)S(1)} %get-tuple-element.129), channel_id=1, source_target_pairs={{0,96},{32,0},{64,32},{96,64},{1,97},{33,1},{65,33},{97,65},{2,98}... | collective-permute-start | bytes 442376 | tf_op jit(solution)/shard_map/ppermute | solution.py:48
  119.2 8.4 %collective-permute-start.39 = (bf16[144,512]{1,0:T(8,128)(2,1)S(1)}, bf16[144,512]{1,0:T(8,128)(2,1)S(1)}, u32[]{:S(2)}, u32[]{:S(2)}) collective-permute-start(bf16[144,512]{1,0:T(8,128)(2,1)S(1)} %get-tuple-element.130), channel_id=1, source_target_pairs={{0,64},{32,96},{64,0},{96,32},{1,65},{33,97},{65,1},{97,33},{2,66}... | collective-permute-start | bytes 442376 | tf_op jit(solution)/shard_map/ppermute | solution.py:48
  119.7 8.3 %collective-permute-start.40 = (bf16[144,512]{1,0:T(8,128)(2,1)S(1)}, bf16[144,512]{1,0:T(8,128)(2,1)S(1)}, u32[]{:S(2)}, u32[]{:S(2)}) collective-permute-start(bf16[144,512]{1,0:T(8,128)(2,1)S(1)} %get-tuple-element.131), channel_id=1, source_target_pairs={{0,32},{32,64},{64,96},{96,0},{1,33},{33,65},{65,97},{97,1},{2,34}... | collective-permute-start | bytes 442376 | tf_op jit(solution)/shard_map/ppermute | solution.py:48
  125.0 9.2 %collective-permute-start.36 = (bf16[320,128]{1,0:T(8,128)(2,1)S(1)}, bf16[320,128]{1,0:T(8,128)(2,1)S(1)}, u32[]{:S(2)}, u32[]{:S(2)}) collective-permute-start(bf16[320,128]{1,0:T(8,128)(2,1)S(1)} %get-tuple-element.126), channel_id=1, source_target_pairs={{0,0},{4,1},{128,2},{132,3},{32,4},{36,5},{160,6},{164,7},{8,8},{1... | collective-permute-start | bytes 245768 | tf_op jit(solution)/shard_map/ppermute | solution.py:521
  127.5 6.7 %collective-permute-start.37 = (bf16[320,128]{1,0:T(8,128)(2,1)S(1)}, bf16[320,128]{1,0:T(8,128)(2,1)S(1)}, u32[]{:S(2)}, u32[]{:S(2)}) collective-permute-start(bf16[320,128]{1,0:T(8,128)(2,1)S(1)} %get-tuple-element.127), channel_id=1, source_target_pairs={{128,0},{132,1},{0,2},{4,3},{160,4},{164,5},{32,6},{36,7},{136,8},... | collective-permute-start | bytes 245768 | tf_op jit(solution)/shard_map/ppermute | solution.py:521
  136.4 7.6 %collective-permute-start.45 = (f32[16,128]{1,0:T(8,128)S(1)}, f32[16,128]{1,0:T(8,128)S(1)}, u32[]{:S(2)}, u32[]{:S(2)}) collective-permute-start(f32[16,128]{1,0:T(8,128)S(1)} %slice.7), channel_id=1, source_target_pairs={{0,16},{4,20},{8,24},{12,28},{16,0},{20,4},{24,8},{28,12},{1,17},{... | collective-permute-start | bytes 24584 | tf_op jit(solution)/shard_map/ppermute | solution.py:52
  (19 other events, 68.3 us)

commit v6 on v5

--- a/solution.py
+++ b/solution.py
@@ -21,6 +21,7 @@
 GROWS = 16
 VMEM = pl.BlockSpec(memory_space=pltpu.VMEM)
 SMEM = pl.BlockSpec(memory_space=pltpu.SMEM)
+ANY = pl.BlockSpec(memory_space=pl.ANY)
 
 
 def flat(yh, x, z, yl, c):
@@ -68,20 +69,46 @@
     return ((at // 2) * 8 + 2 * j + at % 2) * HD
 
 
-def call(body, outs, scratch, ids, *args, static=None, aliases={}):
+def call(body, outs, scratch, ids, *args, static=None, aliases={}, after=None, copies=0):
     body = body if static is None else functools.partial(body, static)
     return pl.pallas_call(
         body,
         out_shape=[jax.ShapeDtypeStruct(s, d) for s, d in outs],
-        in_specs=[SMEM] + [VMEM] * len(args),
+        in_specs=[SMEM] + [ANY if copies else VMEM] * len(args) + [ANY] * (after is not None),
         out_specs=[VMEM] * len(outs),
         input_output_aliases=aliases,
-        scratch_shapes=[pltpu.VMEM(s, d) for s, d in scratch],
+        scratch_shapes=[pltpu.VMEM(s, d) for s, d in scratch]
+        + [pltpu.SemaphoreType.DMA((copies,))] * (copies > 0),
         compiler_params=pltpu.CompilerParams(vmem_limit_bytes=16 * 2**20),
-    )(ids, *args)
-
-
-def spread_kernel(ids, tokens, cot, total_out, *outs):
+    )(ids, *args, *(() if after is None else (after,)))
+
+
+def pack_kernel(ids, w_query, w_key, w_value, w_out, out, sems):
+    part = pl.ds(pl.multiple_of((2 * ids[1] + ids[2]) * PIECE, PIECE), PIECE)
+    copies = [
+        pltpu.make_async_copy(src, dst, sems.at[k])
+        for k, (src, dst) in enumerate(
+            (
+                (w_query, out.at[:HD]),
+                (w_out, out.at[HD : 2 * HD]),
+                (w_key.at[part], out.at[2 * HD : 2 * HD + PIECE]),
+                (w_value.at[part], out.at[2 * HD + PIECE :]),
+            )
+        )
+    ]
+    for copy in copies:
+        copy.start()
+    for copy in copies:
+        copy.wait()
+
+
+def spread_kernel(ids, tokens_in, cot_in, total_out, *refs):
+    outs, tokens, cot, sems = refs[:NX], refs[NX], refs[NX + 1], refs[NX + 2]
+    copies = [pltpu.make_async_copy(tokens_in, tokens, sems.at[0]), pltpu.make_async_copy(cot_in, cot, sems.at[1])]
+    for copy in copies:
+        copy.start()
+    for copy in copies:
+        copy.wait()
     rows = tokens.shape[0]
     squares = jnp.zeros((rows, HD), F32)
     for s in range(NX):
@@ -366,7 +393,10 @@
                 out[row : row + 1] = value[:, j * HD : (j + 1) * HD]
 
 
-def input_kernel(width, ids, a, b, c, d, tokens, gain, total, row_sum, out):
+def input_kernel(sizes, ids, a, b, c, d, tokens, gain, total, row_sum, same, other, later, out, grad_query, grad_out):
+    width, scale = sizes
+    for grad, at in ((grad_query, slice(0, HD)), (grad_out, slice(HD, 2 * HD))):
+        grad[...] = (same[at].astype(F32) + other[at].astype(F32)) * scale
     inv = lax.rsqrt(jnp.transpose(jnp.broadcast_to(total[...], (HD, HD))) / width + 1e-05)
     row_mean = jnp.transpose(jnp.broadcast_to(row_sum[...], (HD, HD))) / width
     for s, ref in enumerate((a, b, c, d)):
@@ -378,11 +408,6 @@
             out[:, cols] = inv * (scaled - unit * row_mean)
 
 
-def owner_kernel(scale, ids, same, other, grad_query, grad_out):
-    for grad, at in ((grad_query, slice(0, HD)), (grad_out, slice(HD, 2 * HD))):
-        grad[...] = (same[at].astype(F32) + other[at].astype(F32)) * scale
-
-
 def shared_kernel(ids, a, b, shared):
     shared[...] = (a[2 * HD :].astype(F32) + b[2 * HD :].astype(F32)).astype(BF16)
 
@@ -396,7 +421,7 @@
     for s in range(NX):
         at = (x + s) % NX
         for j in range(4):
-            grad_gain[(at // 2) * 8 + 2 * j + at % 2] = gains[4 * s + j : 4 * s + j + 1] * scale
+            grad_gain[pl.ds((at // 2) * 8 + 2 * j + at % 2, 1)] = gains[4 * s + j : 4 * s + j + 1] * scale
 
 
 def local(tokens, gain, w_query, w_key, w_value, w_out, cotangent):
@@ -405,22 +430,21 @@
     width = quarter * 4
     yh, x, z, yl, c = (lax.axis_index(a) for a in AXES)
     ids = jnp.stack([z, yl, c, yh, x]).astype(jnp.int32)
-    head = yl * 2 + c
     loss_scale = 1.0 / math.sqrt(rows * 64)
 
-    pack = jnp.concatenate(
-        [
-            w_query,
-            w_out,
-            lax.dynamic_slice_in_dim(w_key, head * PIECE, PIECE, 0),
-            lax.dynamic_slice_in_dim(w_value, head * PIECE, PIECE, 0),
-        ],
-        axis=0,
-    )
+    (pack,) = call(pack_kernel, [((BLOCK, HD), BF16)], [], ids, w_query, w_key, w_value, w_out, copies=4)
     same = lax.ppermute(pack, AXES, owner_perm(0))
     other = lax.ppermute(pack, AXES, owner_perm(1))
     part_shape = ((2 * rows + GROWS, sub), BF16)
-    total, *parts = call(spread_kernel, [((1, rows), F32)] + [part_shape] * 4, [], ids, tokens, cotangent)
+    total, *parts = call(
+        spread_kernel,
+        [((1, rows), F32)] + [part_shape] * 4,
+        [(tokens.shape, BF16)] * 2,
+        ids,
+        tokens,
+        cotangent,
+        copies=2,
+    )
     total = total + swap(total, "c")
     same, other, total = lax.optimization_barrier((same, other, total))
     total = total + swap(total, "yl")
@@ -521,9 +545,12 @@
     arrived = (lax.ppermute(to_same, AXES, inverse(owner_perm(0))), lax.ppermute(to_other, AXES, inverse(owner_perm(1))))
     (gain_z,) = call(gain_kernel, [((8 * NX, HD), F32)], [], ids, *pieces)
     gain_z = gain_z + swap(gain_z, "yh")
-    (grad_input,) = call(
+    *arrived, gain_z = lax.optimization_barrier((*arrived, gain_z))
+    (shared_own,) = call(shared_kernel, [((2 * PIECE, HD), BF16)], [], ids, *arrived)
+    shared_yl = swap(shared_own, "yl")
+    grad_input, grad_query, grad_out = call(
         input_kernel,
-        [((rows, quarter), F32)],
+        [((rows, quarter), F32)] + [((HD, HD), F32)] * 2,
         [],
         ids,
         *pieces,
@@ -531,16 +558,14 @@
         gain_f,
         total,
         row_sum,
-        static=width,
-    )
-    *arrived, grad_input, gain_z = lax.optimization_barrier((*arrived, grad_input, gain_z))
-    (shared_own,) = call(shared_kernel, [((2 * PIECE, HD), BF16)], [], ids, *arrived)
-    grad_query, grad_out = call(owner_kernel, [((HD, HD), F32)] * 2, [], ids, *arrived, static=loss_scale)
-    shared_yl = swap(shared_own, "yl")
+        *arrived,
+        static=(width, loss_scale),
+        after=shared_own,
+    )
     gain_z = gain_z[: 4 * NX] + shift_z(gain_z[4 * NX :], 4)
     grad_key, grad_value, grad_gain = call(
         join_kernel,
-        [((rows, HD), F32)] * 2 + [((4 * NX, 1, HD), F32)],
+        [((rows, HD), F32)] * 2 + [((4 * NX, HD), F32)],
         [],
         ids,
         shared_own,

time: 148 us -> 148 us (level); the launches traced: 145 us -> 148 us
  local copies, waits for them, and re-layouts: 2.92 us -> 5.11 us
    unnamed x10 -> x16, local copies, waits for them, and re-layouts: 2.12 us -> 5.02 us
    ppermute x17, waiting for transfers between devices: 14.6 us -> 16.6 us  [swap(): return lax.ppermute(value, axis, [(0, 1), (1, 0)])]
  transfers between devices with their start and end apart: 46 -> 46, of which waited for: 24 -> 24; matrix products, arithmetic and copies ran while one was open for 0% -> 0% of each run, Pallas kernels for 8% -> 7%
where the time goes in v6:
time: 148 us
  starting transfers between devices  63.3 us (43%)
  waiting for transfers between devices  57.5 us (39%)
  Pallas kernels  20.6 us (14%)
  local copies, waits for them, and re-layouts  5.11 us (3%)
    ppermute x13, starting transfers between devices, shift_z(): return lax.ppermute(value, 'z', [(i, (i + by) % NZ) for i in range(NZ)])  29.2 us
    ppermute x12, waiting for transfers between devices, shift_x(): return lax.ppermute(value, 'x', [(i, (i + by) % NX) for i in range(NX)])  23.1 us
    pallas_call x22, Pallas kernels, call(): pl.pallas_call(body, out_shape=[jax.ShapeDtypeStruct(s, d) for s, d in ou...  20.6 us
    ppermute x13, waiting for transfers between devices, shift_z(): return lax.ppermute(value, 'z', [(i, (i + by) % NZ) for i in range(NZ)])  17.8 us
    ppermute x17, waiting for transfers between devices, swap(): return lax.ppermute(value, axis, [(0, 1), (1, 0)])  16.6 us
    ppermute x12, starting transfers between devices, shift_x(): return lax.ppermute(value, 'x', [(i, (i + by) % NX) for i in range(NX)])  15.7 us
    ppermute x17, starting transfers between devices, swap(): return lax.ppermute(value, axis, [(0, 1), (1, 0)])  10.9 us
    unnamed x16, local copies, waits for them, and re-layouts  5.02 us
  transfers between devices with their start and end apart: 46, of which 24 were waited for; matrix products, arithmetic and copies ran while one was open for 0% of the time, Pallas kernels for 7%

profile of v6, /device:TPU:8, one launch (start us, length us, event | category | flops | bytes accessed | tf_op | source)
XLA Modules:
  0.0 147.5 jit_solution(13590083584246148542)
XLA Ops:
  4.4 2.3 %collective-permute-start.1 = (bf16[320,128]{1,0:T(8,128)(2,1)S(1)}, bf16[320,128]{1,0:T(8,128)(2,1)S(1)}, u32[]{:S(2)}, u32[]{:S(2)}) collective-permute-start(bf16[320,128]{1,0:T(8,128)(2,1)S(1)} %shard_map.118), channel_id=1, source_target_pairs={{0,128},{1,132},{2,0},{3,4},{4,160},{5,164},{6,32},{7,36},{8,136},... | collective-permute-start | bytes 245768 | tf_op jit(solution)/shard_map/ppermute | solution.py:437
  6.6 2.6 %collective-permute-start = (bf16[320,128]{1,0:T(8,128)(2,1)S(1)}, bf16[320,128]{1,0:T(8,128)(2,1)S(1)}, u32[]{:S(2)}, u32[]{:S(2)}) collective-permute-start(bf16[320,128]{1,0:T(8,128)(2,1)S(1)} %shard_map.118), channel_id=1, source_target_pairs={{0,0},{1,4},{2,128},{3,132},{4,32},{5,36},{6,160},{7,164},{8,8},{9... | collective-permute-start | bytes 245768 | tf_op jit(solution)/shard_map/ppermute | solution.py:436
  12.3 2.0 %collective-permute-start.2 = (f32[1,128]{1,0:T(1,128)S(1)}, f32[1,128]{1,0:T(1,128)S(1)}, u32[]{:S(2)}, u32[]{:S(2)}) collective-permute-start(f32[1,128]{1,0:T(1,128)S(1)} %get-tuple-element.74), channel_id=1, source_target_pairs={{0,1},{1,0},{2,3},{3,2},{4,5},{5,4},{6,7},{7,6},{8,9},{9,8},{10,11... | collective-permute-start | bytes 1544 | tf_op jit(solution)/shard_map/ppermute | solution.py:57
  15.2 6.4 %collective-permute-start.8 = (bf16[640,128]{1,0:T(8,128)(2,1)S(1)}, bf16[640,128]{1,0:T(8,128)(2,1)S(1)}, u32[]{:S(2)}, u32[]{:S(2)}) collective-permute-start(bf16[640,128]{1,0:T(8,128)(2,1)S(1)} %maximum_select_fusion.both), channel_id=1, source_target_pairs={{0,24},{4,28},{8,0},{12,4},{16,8},{20,12},{24,16},{28,20},{1,25},{... | collective-permute-start | bytes 491528 | tf_op jit(solution)/shard_map/ppermute | solution.py:53
  23.0 2.2 %collective-permute-done.3 = f32[1,128]{1,0:T(1,128)S(1)} collective-permute-done((f32[1,128]{1,0:T(1,128)S(1)}, f32[1,128]{1,0:T(1,128)S(1)}, u32[]{:S(2)}, u32[]{:S(2)}) %collective-permute-start.3) | collective-permute-done | bytes 544 | tf_op jit(solution)/shard_map/ppermute | solution.py:57
  26.7 3.0 %collective-permute-start.5 = (bf16[272,512]{1,0:T(8,128)(2,1)S(1)}, bf16[272,512]{1,0:T(8,128)(2,1)S(1)}, u32[]{:S(2)}, u32[]{:S(2)}) collective-permute-start(bf16[272,512]{1,0:T(8,128)(2,1)S(1)} %get-tuple-element.82), channel_id=1, source_target_pairs={{0,64},{32,96},{64,0},{96,32},{1,65},{33,97},{65,1},{97,33},{2,66}... | collective-permute-start | bytes 835592 | tf_op jit(solution)/shard_map/ppermute | solution.py:49
  29.8 3.6 %collective-permute-done.7.prev.prev2 = bf16[640,128]{1,0:T(8,128)(2,1)S(1)} collective-permute-done((bf16[640,128]{1,0:T(8,128)(2,1)S(1)}, bf16[640,128]{1,0:T(8,128)(2,1)S(1)}, u32[]{:S(2)}, u32[]{:S(2)}) %collective-permute-start.7) | collective-permute-done | bytes 163872 | tf_op jit(solution)/shard_map/ppermute | solution.py:53
  35.4 2.0 %collective-permute-start.10 = (bf16[1280,128]{1,0:T(8,128)(2,1)S(1)}, bf16[1280,128]{1,0:T(8,128)(2,1)S(1)}, u32[]{:S(2)}, u32[]{:S(2)}) collective-permute-start(bf16[1280,128]{1,0:T(8,128)(2,1)S(1)} %get-tuple-element.89), channel_id=1, source_target_pairs={{0,28},{4,0},{8,4},{12,8},{16,12},{20,16},{24,20},{28,24},{1,29},{... | collective-permute-start | bytes 983048 | tf_op jit(solution)/shard_map/ppermute | solution.py:53
  38.2 2.5 %collective-permute-done.4.refs_1_ = bf16[272,512]{1,0:T(8,128)(2,1)S(1)} collective-permute-done((bf16[272,512]{1,0:T(8,128)(2,1)S(1)}, bf16[272,512]{1,0:T(8,128)(2,1)S(1)}, u32[]{:S(2)}, u32[]{:S(2)}) %collective-permute-start.4) | collective-permute-done | bytes 278560 | tf_op jit(solution)/shard_map/ppermute | solution.py:49
  42.3 2.6 %collective-permute-start.12 = (bf16[320,128]{1,0:T(8,128)(2,1)S(1)}, bf16[320,128]{1,0:T(8,128)(2,1)S(1)}, u32[]{:S(2)}, u32[]{:S(2)}) collective-permute-start(bf16[320,128]{1,0:T(8,128)(2,1)S(1)} %get-tuple-element.91), channel_id=1, source_target_pairs={{0,24},{4,28},{8,0},{12,4},{16,8},{20,12},{24,16},{28,20},{1,25},{... | collective-permute-start | bytes 245768 | tf_op jit(solution)/shard_map/ppermute | solution.py:53
  53.9 2.2 %collective-permute-start.17 = (bf16[128,1024]{1,0:T(8,128)(2,1)S(1)}, bf16[128,1024]{1,0:T(8,128)(2,1)S(1)}, u32[]{:S(2)}, u32[]{:S(2)}) collective-permute-start(bf16[128,1024]{1,0:T(8,128)(2,1)S(1)} %shard_map.127), channel_id=1, source_target_pairs={{0,64},{32,96},{64,0},{96,32},{1,65},{33,97},{65,1},{97,33},{2,66}... | collective-permute-start | bytes 786440 | tf_op jit(solution)/shard_map/ppermute | solution.py:49
  58.1 3.0 %collective-permute-done.15.a = bf16[128,1024]{1,0:T(8,128)(2,1)S(1)} collective-permute-done((bf16[128,1024]{1,0:T(8,128)(2,1)S(1)}, bf16[128,1024]{1,0:T(8,128)(2,1)S(1)}, u32[]{:S(2)}, u32[]{:S(2)}) %collective-permute-start.15) | collective-permute-done | bytes 262176 | tf_op jit(solution)/shard_map/ppermute | solution.py:49
  61.1 3.7 %collective-permute-done.17.b = bf16[128,1024]{1,0:T(8,128)(2,1)S(1)} collective-permute-done((bf16[128,1024]{1,0:T(8,128)(2,1)S(1)}, bf16[128,1024]{1,0:T(8,128)(2,1)S(1)}, u32[]{:S(2)}, u32[]{:S(2)}) %collective-permute-start.17) | collective-permute-done | bytes 262176 | tf_op jit(solution)/shard_map/ppermute | solution.py:49
  64.8 4.4 %collective-permute-done.19.c = bf16[128,1024]{1,0:T(8,128)(2,1)S(1)} collective-permute-done((bf16[128,1024]{1,0:T(8,128)(2,1)S(1)}, bf16[128,1024]{1,0:T(8,128)(2,1)S(1)}, u32[]{:S(2)}, u32[]{:S(2)}) %collective-permute-start.19) | collective-permute-done | bytes 262176 | tf_op jit(solution)/shard_map/ppermute | solution.py:49
  71.3 6.9 %collective-permute-done.20.got = bf16[128,1024]{1,0:T(8,128)(2,1)S(1)} collective-permute-done((bf16[128,1024]{1,0:T(8,128)(2,1)S(1)}, bf16[128,1024]{1,0:T(8,128)(2,1)S(1)}, u32[]{:S(2)}, u32[]{:S(2)}) %collective-permute-start.20) | collective-permute-done | bytes 262176 | tf_op jit(solution)/shard_map/ppermute | solution.py:57
  80.1 1.7 %shard_map.131 = (bf16[128,768]{1,0:T(8,128)(2,1)S(1)}, f32[1,128]{1,0:T(1,128)S(1)}) custom-call(s32[5]{0:T(128)S(1)} %stack.23.ids, bf16[128,512]{1,0:T(8,128)(2,1)S(1)} %get-tuple-element.103.qa, bf16[128,128]{1,0:T(8,128)(2,1)S(1)} %get-tuple-element.104.kv_mine, bf16[128,128]{1,0:T(8,128)(2,1)S(1)} %collective-permute-done.21.kv_theirs), custom_call_target="tpu_custom_call" | custom-call | tf_op jit(solution)/shard_map/pallas_call | solution.py:74
  81.9 2.2 %collective-permute-start.23 = (bf16[128,768]{1,0:T(8,128)(2,1)S(1)}, bf16[128,768]{1,0:T(8,128)(2,1)S(1)}, u32[]{:S(2)}, u32[]{:S(2)}) collective-permute-start(bf16[128,768]{1,0:T(8,128)(2,1)S(1)} %get-tuple-element.105.refs_0_), channel_id=1, source_target_pairs={{0,64},{32,96},{64,0},{96,32},{1,65},{33,97},{65,1},{97,33},{2,66}... | collective-permute-start | bytes 589832 | tf_op jit(solution)/shard_map/ppermute | solution.py:49
  85.4 4.2 %collective-permute-done.24.refs_3_ = bf16[128,768]{1,0:T(8,128)(2,1)S(1)} collective-permute-done((bf16[128,768]{1,0:T(8,128)(2,1)S(1)}, bf16[128,768]{1,0:T(8,128)(2,1)S(1)}, u32[]{:S(2)}, u32[]{:S(2)}) %collective-permute-start.24) | collective-permute-done | bytes 196640 | tf_op jit(solution)/shard_map/ppermute | solution.py:49
  91.2 3.4 %collective-permute-done.22.refs_1_ = bf16[128,768]{1,0:T(8,128)(2,1)S(1)} collective-permute-done((bf16[128,768]{1,0:T(8,128)(2,1)S(1)}, bf16[128,768]{1,0:T(8,128)(2,1)S(1)}, u32[]{:S(2)}, u32[]{:S(2)}) %collective-permute-start.22) | collective-permute-done | bytes 196640 | tf_op jit(solution)/shard_map/ppermute | solution.py:49
  96.1 2.5 %shard_map.132 = (bf16[1296,128]{1,0:T(8,128)(2,1)S(1)}, bf16[1296,128]{1,0:T(8,128)(2,1)S(1)}, bf16[336,128]{1,0:T(8,128)(2,1)S(1)}, bf16[336,128]{1,0:T(8,128)...) custom-call(s32[5]{0:T(128)S(1)} %stack.23.ids, ...), custom_call_target="tpu_custom_call" | custom-call | tf_op jit(solution)/shard_map/pallas_call | solution.py:74
  99.7 2.6 %collective-permute-start.31 = (bf16[1296,128]{1,0:T(8,128)(2,1)S(1)}, bf16[1296,128]{1,0:T(8,128)(2,1)S(1)}, u32[]{:S(2)}, u32[]{:S(2)}) collective-permute-start(bf16[1296,128]{1,0:T(8,128)(2,1)S(1)} %get-tuple-element.115), channel_id=1, source_target_pairs={{0,28},{4,0},{8,4},{12,8},{16,12},{20,16},{24,20},{28,24},{1,29},{... | collective-permute-start | bytes 995336 | tf_op jit(solution)/shard_map/ppermute | solution.py:53
  103.6 2.8 %collective-permute-start.33 = (bf16[336,128]{1,0:T(8,128)(2,1)S(1)}, bf16[336,128]{1,0:T(8,128)(2,1)S(1)}, u32[]{:S(2)}, u32[]{:S(2)}) collective-permute-start(bf16[336,128]{1,0:T(8,128)(2,1)S(1)} %get-tuple-element.117), channel_id=1, source_target_pairs={{0,24},{4,28},{8,0},{12,4},{16,8},{20,12},{24,16},{28,20},{1,25},{... | collective-permute-start | bytes 258056 | tf_op jit(solution)/shard_map/ppermute | solution.py:53
  108.6 2.1 %collective-permute-done.29.a = bf16[1296,128]{1,0:T(8,128)(2,1)S(1)} collective-permute-done((bf16[1296,128]{1,0:T(8,128)(2,1)S(1)}, bf16[1296,128]{1,0:T(8,128)(2,1)S(1)}, u32[]{:S(2)}, u32[]{:S(2)}) %collective-permute-start.29) | collective-permute-done | bytes 331808 | tf_op jit(solution)/shard_map/ppermute | solution.py:53
  110.7 4.3 %collective-permute-done.32.c = bf16[336,128]{1,0:T(8,128)(2,1)S(1)} collective-permute-done((bf16[336,128]{1,0:T(8,128)(2,1)S(1)}, bf16[336,128]{1,0:T(8,128)(2,1)S(1)}, u32[]{:S(2)}, u32[]{:S(2)}) %collective-permute-start.32) | collective-permute-done | bytes 86048 | tf_op jit(solution)/shard_map/ppermute | solution.py:53
  115.8 3.1 %collective-permute-start.37 = (bf16[640,128]{1,0:T(8,128)(2,1)S(1)}, bf16[640,128]{1,0:T(8,128)(2,1)S(1)}, u32[]{:S(2)}, u32[]{:S(2)}) collective-permute-start(bf16[640,128]{1,0:T(8,128)(2,1)S(1)} %get-tuple-element.129), channel_id=1, source_target_pairs={{0,8},{4,12},{8,16},{12,20},{16,24},{20,28},{24,0},{28,4},{1,9},{5... | collective-permute-start | bytes 491528 | tf_op jit(solution)/shard_map/ppermute | solution.py:53
  122.8 2.3 %collective-permute-done.37.up = bf16[640,128]{1,0:T(8,128)(2,1)S(1)} collective-permute-done((bf16[640,128]{1,0:T(8,128)(2,1)S(1)}, bf16[640,128]{1,0:T(8,128)(2,1)S(1)}, u32[]{:S(2)}, u32[]{:S(2)}) %collective-permute-start.37) | collective-permute-done | bytes 163872 | tf_op jit(solution)/shard_map/ppermute | solution.py:53
  127.3 2.6 %collective-permute-start.39 = (bf16[320,128]{1,0:T(8,128)(2,1)S(1)}, bf16[320,128]{1,0:T(8,128)(2,1)S(1)}, u32[]{:S(2)}, u32[]{:S(2)}) collective-permute-start(bf16[320,128]{1,0:T(8,128)(2,1)S(1)} %get-tuple-element.131), channel_id=1, source_target_pairs={{0,0},{4,1},{128,2},{132,3},{32,4},{36,5},{160,6},{164,7},{8,8},{1... | collective-permute-start | bytes 245768 | tf_op jit(solution)/shard_map/ppermute | solution.py:545
  130.8 2.8 %collective-permute-start.41 = (f32[32,128]{1,0:T(8,128)S(1)}, f32[32,128]{1,0:T(8,128)S(1)}, u32[]{:S(2)}, u32[]{:S(2)}) collective-permute-start(f32[32,128]{1,0:T(8,128)S(1)} %shard_map.136), channel_id=1, source_target_pairs={{0,128},{128,0},{1,129},{129,1},{2,130},{130,2},{3,131},{131,3},{4... | collective-permute-start | bytes 49160 | tf_op jit(solution)/shard_map/ppermute | solution.py:57
  133.6 3.0 %collective-permute-done.41 = f32[32,128]{1,0:T(8,128)S(1)} collective-permute-done((f32[32,128]{1,0:T(8,128)S(1)}, f32[32,128]{1,0:T(8,128)S(1)}, u32[]{:S(2)}, u32[]{:S(2)}) %collective-permute-start.41) | collective-permute-done | bytes 16416 | tf_op jit(solution)/shard_map/ppermute | solution.py:57
  138.7 3.3 %collective-permute-start.45 = (f32[16,128]{1,0:T(8,128)S(1)}, f32[16,128]{1,0:T(8,128)S(1)}, u32[]{:S(2)}, u32[]{:S(2)}) collective-permute-start(f32[16,128]{1,0:T(8,128)S(1)} %slice.7), channel_id=1, source_target_pairs={{0,16},{4,20},{8,24},{12,28},{16,0},{20,4},{24,8},{28,12},{1,17},{... | collective-permute-start | bytes 24584 | tf_op jit(solution)/shard_map/ppermute | solution.py:53
  142.0 2.0 %shard_map.138 = (f32[128,2048]{1,0:T(8,128)}, f32[128,128]{1,0:T(8,128)}, f32[128,128]{1,0:T(8,128)}) custom-call(s32[5]{0:T(128)S(1)} %stack.23.ids, bf16[144,512]{1,0:T(8,128)(2,1)S(1)} %get-tuple-element.123.refs_0_.a, bf16[144,512]{1,0:T(8,128)(2,1)S(1)} %collective-permute-done.34.refs_1_.b, bf16[144,512]{1,0:T(8,128)(2,1)S(1)} %collective-permute-done.35.refs_2_.c, ...), custom_call_target="tpu_custom_call" | custom-call | tf_op jit(solution)/shard_map/pallas_call | solution.py:74
  144.5 1.8 %collective-permute-done.45 = f32[16,128]{1,0:T(8,128)S(1)} collective-permute-done((f32[16,128]{1,0:T(8,128)S(1)}, f32[16,128]{1,0:T(8,128)S(1)}, u32[]{:S(2)}, u32[]{:S(2)}) %collective-permute-start.45) | collective-permute-done | bytes 8224 | tf_op jit(solution)/shard_map/ppermute | solution.py:53
  (107 shorter events, 50.8 us)
Async XLA Ops:
  4.4 10.8 %collective-permute-start.1 = (bf16[320,128]{1,0:T(8,128)(2,1)S(1)}, bf16[320,128]{1,0:T(8,128)(2,1)S(1)}, u32[]{:S(2)}, u32[]{:S(2)}) collective-permute-start(bf16[320,128]{1,0:T(8,128)(2,1)S(1)} %shard_map.118), channel_id=1, source_target_pairs={{0,128},{1,132},{2,0},{3,4},{4,160},{5,164},{6,32},{7,36},{8,136},... | collective-permute-start | bytes 245768 | tf_op jit(solution)/shard_map/ppermute | solution.py:437
  6.6 8.5 %collective-permute-start = (bf16[320,128]{1,0:T(8,128)(2,1)S(1)}, bf16[320,128]{1,0:T(8,128)(2,1)S(1)}, u32[]{:S(2)}, u32[]{:S(2)}) collective-permute-start(bf16[320,128]{1,0:T(8,128)(2,1)S(1)} %shard_map.118), channel_id=1, source_target_pairs={{0,0},{1,4},{2,128},{3,132},{4,32},{5,36},{6,160},{7,164},{8,8},{9... | collective-permute-start | bytes 245768 | tf_op jit(solution)/shard_map/ppermute | solution.py:436
  15.2 14.5 %collective-permute-start.8 = (bf16[640,128]{1,0:T(8,128)(2,1)S(1)}, bf16[640,128]{1,0:T(8,128)(2,1)S(1)}, u32[]{:S(2)}, u32[]{:S(2)}) collective-permute-start(bf16[640,128]{1,0:T(8,128)(2,1)S(1)} %maximum_select_fusion.both), channel_id=1, source_target_pairs={{0,24},{4,28},{8,0},{12,4},{16,8},{20,12},{24,16},{28,20},{1,25},{... | collective-permute-start | bytes 491528 | tf_op jit(solution)/shard_map/ppermute | solution.py:53
  21.6 11.8 %collective-permute-start.7 = (bf16[640,128]{1,0:T(8,128)(2,1)S(1)}, bf16[640,128]{1,0:T(8,128)(2,1)S(1)}, u32[]{:S(2)}, u32[]{:S(2)}) collective-permute-start(bf16[640,128]{1,0:T(8,128)(2,1)S(1)} %maximum_select_fusion.both), channel_id=1, source_target_pairs={{0,8},{4,12},{8,16},{12,20},{16,24},{20,28},{24,0},{28,4},{1,9},{5... | collective-permute-start | bytes 491528 | tf_op jit(solution)/shard_map/ppermute | solution.py:53
  25.7 15.0 %collective-permute-start.4 = (bf16[272,512]{1,0:T(8,128)(2,1)S(1)}, bf16[272,512]{1,0:T(8,128)(2,1)S(1)}, u32[]{:S(2)}, u32[]{:S(2)}) collective-permute-start(bf16[272,512]{1,0:T(8,128)(2,1)S(1)} %get-tuple-element.81), channel_id=1, source_target_pairs={{0,32},{32,64},{64,96},{96,0},{1,33},{33,65},{65,97},{97,1},{2,34}... | collective-permute-start | bytes 835592 | tf_op jit(solution)/shard_map/ppermute | solution.py:49
  26.7 15.5 %collective-permute-start.5 = (bf16[272,512]{1,0:T(8,128)(2,1)S(1)}, bf16[272,512]{1,0:T(8,128)(2,1)S(1)}, u32[]{:S(2)}, u32[]{:S(2)}) collective-permute-start(bf16[272,512]{1,0:T(8,128)(2,1)S(1)} %get-tuple-element.82), channel_id=1, source_target_pairs={{0,64},{32,96},{64,0},{96,32},{1,65},{33,97},{65,1},{97,33},{2,66}... | collective-permute-start | bytes 835592 | tf_op jit(solution)/shard_map/ppermute | solution.py:49
  34.1 13.6 %collective-permute-start.9 = (bf16[1280,128]{1,0:T(8,128)(2,1)S(1)}, bf16[1280,128]{1,0:T(8,128)(2,1)S(1)}, u32[]{:S(2)}, u32[]{:S(2)}) collective-permute-start(bf16[1280,128]{1,0:T(8,128)(2,1)S(1)} %get-tuple-element.88), channel_id=1, source_target_pairs={{0,4},{4,8},{8,12},{12,16},{16,20},{20,24},{24,28},{28,0},{1,5},{5... | collective-permute-start | bytes 983048 | tf_op jit(solution)/shard_map/ppermute | solution.py:53
  35.4 12.2 %collective-permute-start.10 = (bf16[1280,128]{1,0:T(8,128)(2,1)S(1)}, bf16[1280,128]{1,0:T(8,128)(2,1)S(1)}, u32[]{:S(2)}, u32[]{:S(2)}) collective-permute-start(bf16[1280,128]{1,0:T(8,128)(2,1)S(1)} %get-tuple-element.89), channel_id=1, source_target_pairs={{0,28},{4,0},{8,4},{12,8},{16,12},{20,16},{24,20},{28,24},{1,29},{... | collective-permute-start | bytes 983048 | tf_op jit(solution)/shard_map/ppermute | solution.py:53
  37.4 7.5 %collective-permute-start.6 = (bf16[272,512]{1,0:T(8,128)(2,1)S(1)}, bf16[272,512]{1,0:T(8,128)(2,1)S(1)}, u32[]{:S(2)}, u32[]{:S(2)}) collective-permute-start(bf16[272,512]{1,0:T(8,128)(2,1)S(1)} %get-tuple-element.83), channel_id=1, source_target_pairs={{0,96},{32,0},{64,32},{96,64},{1,97},{33,1},{65,33},{97,65},{2,98}... | collective-permute-start | bytes 835592 | tf_op jit(solution)/shard_map/ppermute | solution.py:49
  40.7 6.6 %collective-permute-start.11 = (bf16[320,128]{1,0:T(8,128)(2,1)S(1)}, bf16[320,128]{1,0:T(8,128)(2,1)S(1)}, u32[]{:S(2)}, u32[]{:S(2)}) collective-permute-start(bf16[320,128]{1,0:T(8,128)(2,1)S(1)} %get-tuple-element.90), channel_id=1, source_target_pairs={{0,8},{4,12},{8,16},{12,20},{16,24},{20,28},{24,0},{28,4},{1,9},{5... | collective-permute-start | bytes 245768 | tf_op jit(solution)/shard_map/ppermute | solution.py:53
  49.7 7.8 %collective-permute-start.13 = (f32[128,640]{1,0:T(8,128)S(1)}, f32[128,640]{1,0:T(8,128)S(1)}, u32[]{:S(2)}, u32[]{:S(2)}) collective-permute-start(f32[128,640]{1,0:T(8,128)S(1)} %get-tuple-element.96), channel_id=1, source_target_pairs={{0,1},{1,0},{2,3},{3,2},{4,5},{5,4},{6,7},{7,6},{8,9},{9,8},{10,11... | collective-permute-start | bytes 983048 | tf_op jit(solution)/shard_map/ppermute | solution.py:57
  51.9 9.2 %collective-permute-start.15 = (bf16[128,1024]{1,0:T(8,128)(2,1)S(1)}, bf16[128,1024]{1,0:T(8,128)(2,1)S(1)}, u32[]{:S(2)}, u32[]{:S(2)}) collective-permute-start(bf16[128,1024]{1,0:T(8,128)(2,1)S(1)} %shard_map.126), channel_id=1, source_target_pairs={{0,96},{32,0},{64,32},{96,64},{1,97},{33,1},{65,33},{97,65},{2,98}... | collective-permute-start | bytes 786440 | tf_op jit(solution)/shard_map/ppermute | solution.py:49
  53.9 10.8 %collective-permute-start.17 = (bf16[128,1024]{1,0:T(8,128)(2,1)S(1)}, bf16[128,1024]{1,0:T(8,128)(2,1)S(1)}, u32[]{:S(2)}, u32[]{:S(2)}) collective-permute-start(bf16[128,1024]{1,0:T(8,128)(2,1)S(1)} %shard_map.127), channel_id=1, source_target_pairs={{0,64},{32,96},{64,0},{96,32},{1,65},{33,97},{65,1},{97,33},{2,66}... | collective-permute-start | bytes 786440 | tf_op jit(solution)/shard_map/ppermute | solution.py:49
  56.7 12.4 %collective-permute-start.19 = (bf16[128,1024]{1,0:T(8,128)(2,1)S(1)}, bf16[128,1024]{1,0:T(8,128)(2,1)S(1)}, u32[]{:S(2)}, u32[]{:S(2)}) collective-permute-start(bf16[128,1024]{1,0:T(8,128)(2,1)S(1)} %shard_map.128), channel_id=1, source_target_pairs={{0,32},{32,64},{64,96},{96,0},{1,33},{33,65},{65,97},{97,1},{2,34}... | collective-permute-start | bytes 786440 | tf_op jit(solution)/shard_map/ppermute | solution.py:49
  69.9 8.3 %collective-permute-start.20 = (bf16[128,1024]{1,0:T(8,128)(2,1)S(1)}, bf16[128,1024]{1,0:T(8,128)(2,1)S(1)}, u32[]{:S(2)}, u32[]{:S(2)}) collective-permute-start(bf16[128,1024]{1,0:T(8,128)(2,1)S(1)} %shard_map.129.mine), channel_id=1, source_target_pairs={{0,2},{2,0},{1,3},{3,1},{4,6},{6,4},{5,7},{7,5},{8,10},{10,8},{9,1... | collective-permute-start | bytes 786440 | tf_op jit(solution)/shard_map/ppermute | solution.py:57
  81.8 7.8 %collective-permute-start.24 = (bf16[128,768]{1,0:T(8,128)(2,1)S(1)}, bf16[128,768]{1,0:T(8,128)(2,1)S(1)}, u32[]{:S(2)}, u32[]{:S(2)}) collective-permute-start(bf16[128,768]{1,0:T(8,128)(2,1)S(1)} %get-tuple-element.105.refs_0_), channel_id=1, source_target_pairs={{0,96},{32,0},{64,32},{96,64},{1,97},{33,1},{65,33},{97,65},{2,98}... | collective-permute-start | bytes 589832 | tf_op jit(solution)/shard_map/ppermute | solution.py:49
  81.9 9.4 %collective-permute-start.23 = (bf16[128,768]{1,0:T(8,128)(2,1)S(1)}, bf16[128,768]{1,0:T(8,128)(2,1)S(1)}, u32[]{:S(2)}, u32[]{:S(2)}) collective-permute-start(bf16[128,768]{1,0:T(8,128)(2,1)S(1)} %get-tuple-element.105.refs_0_), channel_id=1, source_target_pairs={{0,64},{32,96},{64,0},{96,32},{1,65},{33,97},{65,1},{97,33},{2,66}... | collective-permute-start | bytes 589832 | tf_op jit(solution)/shard_map/ppermute | solution.py:49
  84.1 10.6 %collective-permute-start.22 = (bf16[128,768]{1,0:T(8,128)(2,1)S(1)}, bf16[128,768]{1,0:T(8,128)(2,1)S(1)}, u32[]{:S(2)}, u32[]{:S(2)}) collective-permute-start(bf16[128,768]{1,0:T(8,128)(2,1)S(1)} %get-tuple-element.105.refs_0_), channel_id=1, source_target_pairs={{0,32},{32,64},{64,96},{96,0},{1,33},{33,65},{65,97},{97,1},{2,34}... | collective-permute-start | bytes 589832 | tf_op jit(solution)/shard_map/ppermute | solution.py:49
  85.4 9.3 %collective-permute-start.25 = (bf16[128,768]{1,0:T(8,128)(2,1)S(1)}, bf16[128,768]{1,0:T(8,128)(2,1)S(1)}, u32[]{:S(2)}, u32[]{:S(2)}) collective-permute-start(bf16[128,768]{1,0:T(8,128)(2,1)S(1)} %get-tuple-element.105.refs_0_), channel_id=1, source_target_pairs={{0,1},{1,0},{2,3},{3,2},{4,5},{5,4},{6,7},{7,6},{8,9},{9,8},{10,11... | collective-permute-start | bytes 589832 | tf_op jit(solution)/shard_map/ppermute | solution.py:57
  98.5 12.1 %collective-permute-start.29 = (bf16[1296,128]{1,0:T(8,128)(2,1)S(1)}, bf16[1296,128]{1,0:T(8,128)(2,1)S(1)}, u32[]{:S(2)}, u32[]{:S(2)}) collective-permute-start(bf16[1296,128]{1,0:T(8,128)(2,1)S(1)} %get-tuple-element.112), channel_id=1, source_target_pairs={{0,4},{4,8},{8,12},{12,16},{16,20},{20,24},{24,28},{28,0},{1,5},{5... | collective-permute-start | bytes 995336 | tf_op jit(solution)/shard_map/ppermute | solution.py:53
  99.7 15.5 %collective-permute-start.31 = (bf16[1296,128]{1,0:T(8,128)(2,1)S(1)}, bf16[1296,128]{1,0:T(8,128)(2,1)S(1)}, u32[]{:S(2)}, u32[]{:S(2)}) collective-permute-start(bf16[1296,128]{1,0:T(8,128)(2,1)S(1)} %get-tuple-element.115), channel_id=1, source_target_pairs={{0,28},{4,0},{8,4},{12,8},{16,12},{20,16},{24,20},{28,24},{1,29},{... | collective-permute-start | bytes 995336 | tf_op jit(solution)/shard_map/ppermute | solution.py:53
  102.3 12.7 %collective-permute-start.32 = (bf16[336,128]{1,0:T(8,128)(2,1)S(1)}, bf16[336,128]{1,0:T(8,128)(2,1)S(1)}, u32[]{:S(2)}, u32[]{:S(2)}) collective-permute-start(bf16[336,128]{1,0:T(8,128)(2,1)S(1)} %get-tuple-element.116), channel_id=1, source_target_pairs={{0,8},{4,12},{8,16},{12,20},{16,24},{20,28},{24,0},{28,4},{1,9},{5... | collective-permute-start | bytes 258056 | tf_op jit(solution)/shard_map/ppermute | solution.py:53
  103.6 11.5 %collective-permute-start.33 = (bf16[336,128]{1,0:T(8,128)(2,1)S(1)}, bf16[336,128]{1,0:T(8,128)(2,1)S(1)}, u32[]{:S(2)}, u32[]{:S(2)}) collective-permute-start(bf16[336,128]{1,0:T(8,128)(2,1)S(1)} %get-tuple-element.117), channel_id=1, source_target_pairs={{0,24},{4,28},{8,0},{12,4},{16,8},{20,12},{24,16},{28,20},{1,25},{... | collective-permute-start | bytes 258056 | tf_op jit(solution)/shard_map/ppermute | solution.py:53
  115.8 9.2 %collective-permute-start.37 = (bf16[640,128]{1,0:T(8,128)(2,1)S(1)}, bf16[640,128]{1,0:T(8,128)(2,1)S(1)}, u32[]{:S(2)}, u32[]{:S(2)}) collective-permute-start(bf16[640,128]{1,0:T(8,128)(2,1)S(1)} %get-tuple-element.129), channel_id=1, source_target_pairs={{0,8},{4,12},{8,16},{12,20},{16,24},{20,28},{24,0},{28,4},{1,9},{5... | collective-permute-start | bytes 491528 | tf_op jit(solution)/shard_map/ppermute | solution.py:53
  118.9 7.8 %collective-permute-start.38 = (bf16[640,128]{1,0:T(8,128)(2,1)S(1)}, bf16[640,128]{1,0:T(8,128)(2,1)S(1)}, u32[]{:S(2)}, u32[]{:S(2)}) collective-permute-start(bf16[640,128]{1,0:T(8,128)(2,1)S(1)} %get-tuple-element.130), channel_id=1, source_target_pairs={{0,24},{4,28},{8,0},{12,4},{16,8},{20,12},{24,16},{28,20},{1,25},{... | collective-permute-start | bytes 491528 | tf_op jit(solution)/shard_map/ppermute | solution.py:53
  120.0 10.0 %collective-permute-start.34 = (bf16[144,512]{1,0:T(8,128)(2,1)S(1)}, bf16[144,512]{1,0:T(8,128)(2,1)S(1)}, u32[]{:S(2)}, u32[]{:S(2)}) collective-permute-start(bf16[144,512]{1,0:T(8,128)(2,1)S(1)} %get-tuple-element.124), channel_id=1, source_target_pairs={{0,96},{32,0},{64,32},{96,64},{1,97},{33,1},{65,33},{97,65},{2,98}... | collective-permute-start | bytes 442376 | tf_op jit(solution)/shard_map/ppermute | solution.py:49
  121.5 8.6 %collective-permute-start.35 = (bf16[144,512]{1,0:T(8,128)(2,1)S(1)}, bf16[144,512]{1,0:T(8,128)(2,1)S(1)}, u32[]{:S(2)}, u32[]{:S(2)}) collective-permute-start(bf16[144,512]{1,0:T(8,128)(2,1)S(1)} %get-tuple-element.125), channel_id=1, source_target_pairs={{0,64},{32,96},{64,0},{96,32},{1,65},{33,97},{65,1},{97,33},{2,66}... | collective-permute-start | bytes 442376 | tf_op jit(solution)/shard_map/ppermute | solution.py:49
  122.0 8.3 %collective-permute-start.36 = (bf16[144,512]{1,0:T(8,128)(2,1)S(1)}, bf16[144,512]{1,0:T(8,128)(2,1)S(1)}, u32[]{:S(2)}, u32[]{:S(2)}) collective-permute-start(bf16[144,512]{1,0:T(8,128)(2,1)S(1)} %get-tuple-element.126), channel_id=1, source_target_pairs={{0,32},{32,64},{64,96},{96,0},{1,33},{33,65},{65,97},{97,1},{2,34}... | collective-permute-start | bytes 442376 | tf_op jit(solution)/shard_map/ppermute | solution.py:49
  127.3 9.3 %collective-permute-start.39 = (bf16[320,128]{1,0:T(8,128)(2,1)S(1)}, bf16[320,128]{1,0:T(8,128)(2,1)S(1)}, u32[]{:S(2)}, u32[]{:S(2)}) collective-permute-start(bf16[320,128]{1,0:T(8,128)(2,1)S(1)} %get-tuple-element.131), channel_id=1, source_target_pairs={{0,0},{4,1},{128,2},{132,3},{32,4},{36,5},{160,6},{164,7},{8,8},{1... | collective-permute-start | bytes 245768 | tf_op jit(solution)/shard_map/ppermute | solution.py:545
  129.9 6.7 %collective-permute-start.40 = (bf16[320,128]{1,0:T(8,128)(2,1)S(1)}, bf16[320,128]{1,0:T(8,128)(2,1)S(1)}, u32[]{:S(2)}, u32[]{:S(2)}) collective-permute-start(bf16[320,128]{1,0:T(8,128)(2,1)S(1)} %get-tuple-element.132), channel_id=1, source_target_pairs={{128,0},{132,1},{0,2},{4,3},{160,4},{164,5},{32,6},{36,7},{136,8},... | collective-permute-start | bytes 245768 | tf_op jit(solution)/shard_map/ppermute | solution.py:545
  137.2 6.8 %collective-permute-start.43 = (bf16[64,128]{1,0:T(8,128)(2,1)S(1)}, bf16[64,128]{1,0:T(8,128)(2,1)S(1)}, u32[]{:S(2)}, u32[]{:S(2)}) collective-permute-start(bf16[64,128]{1,0:T(8,128)(2,1)S(1)} %shard_map.137.later.own), channel_id=1, source_target_pairs={{0,2},{2,0},{1,3},{3,1},{4,6},{6,4},{5,7},{7,5},{8,10},{10,8},{9,1... | collective-permute-start | bytes 49160 | tf_op jit(solution)/shard_map/ppermute | solution.py:57
  138.7 7.6 %collective-permute-start.45 = (f32[16,128]{1,0:T(8,128)S(1)}, f32[16,128]{1,0:T(8,128)S(1)}, u32[]{:S(2)}, u32[]{:S(2)}) collective-permute-start(f32[16,128]{1,0:T(8,128)S(1)} %slice.7), channel_id=1, source_target_pairs={{0,16},{4,20},{8,24},{12,28},{16,0},{20,4},{24,8},{28,12},{1,17},{... | collective-permute-start | bytes 24584 | tf_op jit(solution)/shard_map/ppermute | solution.py:53
  (22 other events, 80.0 us)

commit v7 on v5

--- a/solution.py
+++ b/solution.py
@@ -34,7 +34,7 @@
             for z in range(NZ):
                 for yl in range(2):
                     for c in range(2):
-                        dest_x = (x % 2) * 2 + z % 2
+                        dest_x = (z % 2) * 2 + 1 - x % 2
                         dest_z = (z // 2) * 2 + c
                         pairs.append((flat(yh, x, z, yl, c), flat(yl ^ flip, dest_x, dest_z, yh, x // 2)))
     return pairs
@@ -65,7 +65,7 @@
 
 
 def feature(at, j):
-    return ((at // 2) * 8 + 2 * j + at % 2) * HD
+    return ((1 - at % 2) * 8 + 2 * j + at // 2) * HD
 
 
 def call(body, outs, scratch, ids, *args, static=None, aliases={}):
@@ -86,12 +86,15 @@
     squares = jnp.zeros((rows, HD), F32)
     for s in range(NX):
         at = (ids[4] + s) % NX
-        for j in range(4):
-            block, cols = lanes(feature(at, j)), slice(j * HD, (j + 1) * HD)
+
+        def cut(j, squares, s=s, at=at):
+            block, cols = lanes(feature(at, j)), lanes(j * HD)
             value = tokens[:, block]
-            squares = squares + value.astype(F32) * value.astype(F32)
             outs[s][:rows, cols] = value
             outs[s][rows : 2 * rows, cols] = cot[:, block]
+            return squares + value.astype(F32) * value.astype(F32)
+
+        squares = lax.fori_loop(0, 4, cut, squares)
     total_out[...] = jnp.sum(jnp.transpose(squares), axis=0, keepdims=True)
 
 
@@ -113,11 +116,14 @@
         total = (terms[2:3] + terms[1:2]) + terms[0:1]
         column = jnp.transpose(jnp.broadcast_to(total, (HD, HD)))
         inv = lax.rsqrt(column / width + 1e-05)
-        for j in range(4):
-            cols = slice(j * HD, (j + 1) * HD)
+
+        @pl.loop(0, 4)
+        def scale(j, s=s, rows=rows, inv=inv):
+            cols = lanes(j * HD)
             value = parts[s][:HD, cols].astype(F32) * inv
             unit[rows, cols] = value
             normed[rows, cols] = (value * gain[:, lanes(feature(ids[4], j))]).astype(BF16)
+
         cot[rows] = parts[s][HD : 2 * HD]
 
 
@@ -152,12 +158,15 @@
     def place(ref, base, d, half):
         zt = (z + d + NZ) % NZ
         side, j = zt % 2, zt // 2
-        rows = pl.ds(pl.multiple_of(j * HD, HD), HD)
-        w_all[rows, lanes(side * 2 * HD + half * HD)] = ref[base : base + HD]
-        w_out[side, half * HD : (half + 1) * HD, lanes(j * HD)] = ref[base + HD : base + 2 * HD]
-        part = pl.ds(pl.multiple_of(j * HD + (2 * half + side) * PIECE, PIECE), PIECE)
-        w_all[part, 4 * HD : 5 * HD] = ref[base + 2 * HD : base + 2 * HD + PIECE]
-        w_all[part, 5 * HD : 6 * HD] = ref[base + 2 * HD + PIECE : base + BLOCK]
+
+        def block(start, size, unit=PIECE):
+            return pl.ds(pl.multiple_of(start, unit), size)
+
+        w_all[block(j * HD, HD), lanes(side * 2 * HD + half * HD)] = ref[block(base, HD)]
+        w_out[side, block(half * HD, HD, HD), lanes(j * HD)] = ref[block(base + HD, HD)]
+        part = block(j * HD + (2 * half + side) * PIECE, PIECE)
+        w_all[part, 4 * HD : 5 * HD] = ref[block(base + 2 * HD, PIECE)]
+        w_all[part, 5 * HD : 6 * HD] = ref[block(base + 2 * HD + PIECE, PIECE)]
 
     for ref, base, d in (
         (both, 0, 0),
@@ -168,8 +177,12 @@
         (prev2, 0, -2),
         (next2, 0, 2),
     ):
-        place(ref, base, d, 0)
-        place(ref, base + BLOCK, d, 1)
+
+
+        @pl.loop(0, 2)
+        def both_halves(half, ref=ref, base=base, d=d):
+            place(ref, base + half * BLOCK, d, half)
+
     place(far_first, 0, 4, 0)
     place(far_second, 0, 4, 1)
     product(outs, 1 - c, normed, cot, w_all, w_out)
@@ -371,10 +384,12 @@
     row_mean = jnp.transpose(jnp.broadcast_to(row_sum[...], (HD, HD))) / width
     for s, ref in enumerate((a, b, c, d)):
         at = (ids[4] + s) % NX
-        for j in range(4):
+
+        @pl.loop(0, 4)
+        def place(j, ref=ref, at=at):
             cols = lanes(feature(at, j))
             unit = tokens[:, cols].astype(F32) * inv
-            scaled = ref[:HD, j * HD : (j + 1) * HD].astype(F32) * gain[:, cols]
+            scaled = ref[:HD, lanes(j * HD)].astype(F32) * gain[:, cols]
             out[:, cols] = inv * (scaled - unit * row_mean)
 
 
@@ -396,7 +411,7 @@
     for s in range(NX):
         at = (x + s) % NX
         for j in range(4):
-            grad_gain[(at // 2) * 8 + 2 * j + at % 2] = gains[4 * s + j : 4 * s + j + 1] * scale
+            grad_gain[(1 - at % 2) * 8 + 2 * j + at // 2] = gains[4 * s + j : 4 * s + j + 1] * scale
 
 
 def local(tokens, gain, w_query, w_key, w_value, w_out, cotangent):

time: 148 us -> 144 us (0.973); the launches traced: 145 us -> 144 us
  starting transfers between devices: 63 us -> 58 us
  waiting for transfers between devices: 56.5 us -> 59.1 us
    ppermute x1, starting transfers between devices: 0.09 us -> 2.72 us  [local(): lax.ppermute(to_other, AXES, inverse(owner_perm(1)))]
    ppermute x12, starting transfers between devices: 15.7 us -> 13.1 us  [shift_x(): return lax.ppermute(value, 'x', [(i, (i + by) % NX) for i in range(NX)])]
    ppermute x12, waiting for transfers between devices: 23.3 us -> 25.5 us  [shift_x(): return lax.ppermute(value, 'x', [(i, (i + by) % NX) for i in range(NX)])]
    ppermute x1, starting transfers between devices: 2.48 us -> 0.78 us  [local(): lax.ppermute(to_same, AXES, inverse(owner_perm(0)))]
  transfers between devices with their start and end apart: 46 -> 46, of which waited for: 24 -> 22; matrix products, arithmetic and copies ran while one was open for 0% -> 0% of each run, Pallas kernels for 8% -> 9%
where the time goes in v7:
time: 144 us
  waiting for transfers between devices  59.1 us (41%)
  starting transfers between devices  58 us (40%)
  Pallas kernels  22 us (15%)
  local copies, waits for them, and re-layouts  2.92 us (2%)
    ppermute x13, starting transfers between devices, shift_z(): return lax.ppermute(value, 'z', [(i, (i + by) % NZ) for i in range(NZ)])  28.2 us
    ppermute x12, waiting for transfers between devices, shift_x(): return lax.ppermute(value, 'x', [(i, (i + by) % NX) for i in range(NX)])  25.5 us
    pallas_call x22, Pallas kernels, call(): pl.pallas_call(body, out_shape=[jax.ShapeDtypeStruct(s, d) for s, d in ou...  22 us
    ppermute x13, waiting for transfers between devices, shift_z(): return lax.ppermute(value, 'z', [(i, (i + by) % NZ) for i in range(NZ)])  17.8 us
    ppermute x17, waiting for transfers between devices, swap(): return lax.ppermute(value, axis, [(0, 1), (1, 0)])  15.7 us
    ppermute x12, starting transfers between devices, shift_x(): return lax.ppermute(value, 'x', [(i, (i + by) % NX) for i in range(NX)])  13.1 us
    ppermute x17, starting transfers between devices, swap(): return lax.ppermute(value, axis, [(0, 1), (1, 0)])  9.52 us
  transfers between devices with their start and end apart: 46, of which 22 were waited for; matrix products, arithmetic and copies ran while one was open for 0% of the time, Pallas kernels for 9%

profile of v7, /device:TPU:8, one launch (start us, length us, event | category | flops | bytes accessed | tf_op | source)
XLA Modules:
  0.0 143.7 jit_solution(16407191320021365874)
XLA Ops:
  3.5 2.4 %collective-permute-start = (bf16[320,128]{1,0:T(8,128)(2,1)S(1)}, bf16[320,128]{1,0:T(8,128)(2,1)S(1)}, u32[]{:S(2)}, u32[]{:S(2)}) collective-permute-start(bf16[320,128]{1,0:T(8,128)(2,1)S(1)} %pad_maximum_fusion), channel_id=1, source_target_pairs={{0,32},{1,36},{2,160},{3,164},{4,96},{5,100},{6,224},{7,228},{8,40... | collective-permute-start | bytes 245768 | tf_op jit(solution)/shard_map/ppermute | solution.py:435
  9.2 2.1 %collective-permute-start.2 = (f32[1,128]{1,0:T(1,128)S(1)}, f32[1,128]{1,0:T(1,128)S(1)}, u32[]{:S(2)}, u32[]{:S(2)}) collective-permute-start(f32[1,128]{1,0:T(1,128)S(1)} %get-tuple-element.74), channel_id=1, source_target_pairs={{0,1},{1,0},{2,3},{3,2},{4,5},{5,4},{6,7},{7,6},{8,9},{9,8},{10,11... | collective-permute-start | bytes 1544 | tf_op jit(solution)/shard_map/ppermute | solution.py:56
  12.1 6.4 %collective-permute-start.8 = (bf16[640,128]{1,0:T(8,128)(2,1)S(1)}, bf16[640,128]{1,0:T(8,128)(2,1)S(1)}, u32[]{:S(2)}, u32[]{:S(2)}) collective-permute-start(bf16[640,128]{1,0:T(8,128)(2,1)S(1)} %maximum_select_fusion.both), channel_id=1, source_target_pairs={{0,24},{4,28},{8,0},{12,4},{16,8},{20,12},{24,16},{28,20},{1,25},{... | collective-permute-start | bytes 491528 | tf_op jit(solution)/shard_map/ppermute | solution.py:52
  19.8 2.2 %collective-permute-done.3 = f32[1,128]{1,0:T(1,128)S(1)} collective-permute-done((f32[1,128]{1,0:T(1,128)S(1)}, f32[1,128]{1,0:T(1,128)S(1)}, u32[]{:S(2)}, u32[]{:S(2)}) %collective-permute-start.3) | collective-permute-done | bytes 544 | tf_op jit(solution)/shard_map/ppermute | solution.py:56
  22.6 1.9 %collective-permute-start.4 = (bf16[272,512]{1,0:T(8,128)(2,1)S(1)}, bf16[272,512]{1,0:T(8,128)(2,1)S(1)}, u32[]{:S(2)}, u32[]{:S(2)}) collective-permute-start(bf16[272,512]{1,0:T(8,128)(2,1)S(1)} %get-tuple-element.81), channel_id=1, source_target_pairs={{0,32},{32,64},{64,96},{96,0},{1,33},{33,65},{65,97},{97,1},{2,34}... | collective-permute-start | bytes 835592 | tf_op jit(solution)/shard_map/ppermute | solution.py:48
  24.5 2.3 %collective-permute-start.5 = (bf16[272,512]{1,0:T(8,128)(2,1)S(1)}, bf16[272,512]{1,0:T(8,128)(2,1)S(1)}, u32[]{:S(2)}, u32[]{:S(2)}) collective-permute-start(bf16[272,512]{1,0:T(8,128)(2,1)S(1)} %get-tuple-element.82), channel_id=1, source_target_pairs={{0,64},{32,96},{64,0},{96,32},{1,65},{33,97},{65,1},{97,33},{2,66}... | collective-permute-start | bytes 835592 | tf_op jit(solution)/shard_map/ppermute | solution.py:48
  26.8 2.5 %collective-permute-done.7.prev.prev2 = bf16[640,128]{1,0:T(8,128)(2,1)S(1)} collective-permute-done((bf16[640,128]{1,0:T(8,128)(2,1)S(1)}, bf16[640,128]{1,0:T(8,128)(2,1)S(1)}, u32[]{:S(2)}, u32[]{:S(2)}) %collective-permute-start.7) | collective-permute-done | bytes 163872 | tf_op jit(solution)/shard_map/ppermute | solution.py:52
  31.6 1.7 %collective-permute-start.10 = (bf16[1280,128]{1,0:T(8,128)(2,1)S(1)}, bf16[1280,128]{1,0:T(8,128)(2,1)S(1)}, u32[]{:S(2)}, u32[]{:S(2)}) collective-permute-start(bf16[1280,128]{1,0:T(8,128)(2,1)S(1)} %get-tuple-element.89), channel_id=1, source_target_pairs={{0,28},{4,0},{8,4},{12,8},{16,12},{20,16},{24,20},{28,24},{1,29},{... | collective-permute-start | bytes 983048 | tf_op jit(solution)/shard_map/ppermute | solution.py:52
  34.1 4.0 %collective-permute-done.5.refs_2_ = bf16[272,512]{1,0:T(8,128)(2,1)S(1)} collective-permute-done((bf16[272,512]{1,0:T(8,128)(2,1)S(1)}, bf16[272,512]{1,0:T(8,128)(2,1)S(1)}, u32[]{:S(2)}, u32[]{:S(2)}) %collective-permute-start.5) | collective-permute-done | bytes 278560 | tf_op jit(solution)/shard_map/ppermute | solution.py:48
  38.1 3.9 %collective-permute-start.12 = (bf16[320,128]{1,0:T(8,128)(2,1)S(1)}, bf16[320,128]{1,0:T(8,128)(2,1)S(1)}, u32[]{:S(2)}, u32[]{:S(2)}) collective-permute-start(bf16[320,128]{1,0:T(8,128)(2,1)S(1)} %get-tuple-element.91), channel_id=1, source_target_pairs={{0,24},{4,28},{8,0},{12,4},{16,8},{20,12},{24,16},{28,20},{1,25},{... | collective-permute-start | bytes 245768 | tf_op jit(solution)/shard_map/ppermute | solution.py:52
  49.6 1.7 %collective-permute-start.17 = (bf16[128,1024]{1,0:T(8,128)(2,1)S(1)}, bf16[128,1024]{1,0:T(8,128)(2,1)S(1)}, u32[]{:S(2)}, u32[]{:S(2)}) collective-permute-start(bf16[128,1024]{1,0:T(8,128)(2,1)S(1)} %shard_map.126), channel_id=1, source_target_pairs={{0,64},{32,96},{64,0},{96,32},{1,65},{33,97},{65,1},{97,33},{2,66}... | collective-permute-start | bytes 786440 | tf_op jit(solution)/shard_map/ppermute | solution.py:48
  53.6 4.5 %collective-permute-done.15.a = bf16[128,1024]{1,0:T(8,128)(2,1)S(1)} collective-permute-done((bf16[128,1024]{1,0:T(8,128)(2,1)S(1)}, bf16[128,1024]{1,0:T(8,128)(2,1)S(1)}, u32[]{:S(2)}, u32[]{:S(2)}) %collective-permute-start.15) | collective-permute-done | bytes 262176 | tf_op jit(solution)/shard_map/ppermute | solution.py:48
  58.1 2.3 %collective-permute-done.17.b = bf16[128,1024]{1,0:T(8,128)(2,1)S(1)} collective-permute-done((bf16[128,1024]{1,0:T(8,128)(2,1)S(1)}, bf16[128,1024]{1,0:T(8,128)(2,1)S(1)}, u32[]{:S(2)}, u32[]{:S(2)}) %collective-permute-start.17) | collective-permute-done | bytes 262176 | tf_op jit(solution)/shard_map/ppermute | solution.py:48
  60.4 4.7 %collective-permute-done.19.c = bf16[128,1024]{1,0:T(8,128)(2,1)S(1)} collective-permute-done((bf16[128,1024]{1,0:T(8,128)(2,1)S(1)}, bf16[128,1024]{1,0:T(8,128)(2,1)S(1)}, u32[]{:S(2)}, u32[]{:S(2)}) %collective-permute-start.19) | collective-permute-done | bytes 262176 | tf_op jit(solution)/shard_map/ppermute | solution.py:48
  67.3 6.8 %collective-permute-done.20.got = bf16[128,1024]{1,0:T(8,128)(2,1)S(1)} collective-permute-done((bf16[128,1024]{1,0:T(8,128)(2,1)S(1)}, bf16[128,1024]{1,0:T(8,128)(2,1)S(1)}, u32[]{:S(2)}, u32[]{:S(2)}) %collective-permute-start.20) | collective-permute-done | bytes 262176 | tf_op jit(solution)/shard_map/ppermute | solution.py:56
  76.0 1.7 %shard_map.130 = (bf16[128,768]{1,0:T(8,128)(2,1)S(1)}, f32[1,128]{1,0:T(1,128)S(1)}) custom-call(s32[5]{0:T(128)S(1)} %stack.23.ids, bf16[128,512]{1,0:T(8,128)(2,1)S(1)} %get-tuple-element.103.qa, bf16[128,128]{1,0:T(8,128)(2,1)S(1)} %get-tuple-element.104.kv_mine, bf16[128,128]{1,0:T(8,128)(2,1)S(1)} %collective-permute-done.21.kv_theirs), custom_call_target="tpu_custom_call" | custom-call | tf_op jit(solution)/shard_map/pallas_call | solution.py:73
  80.5 5.0 %collective-permute-done.24.refs_3_ = bf16[128,768]{1,0:T(8,128)(2,1)S(1)} collective-permute-done((bf16[128,768]{1,0:T(8,128)(2,1)S(1)}, bf16[128,768]{1,0:T(8,128)(2,1)S(1)}, u32[]{:S(2)}, u32[]{:S(2)}) %collective-permute-start.24) | collective-permute-done | bytes 196640 | tf_op jit(solution)/shard_map/ppermute | solution.py:48
  85.5 1.6 %collective-permute-done.23.refs_2_ = bf16[128,768]{1,0:T(8,128)(2,1)S(1)} collective-permute-done((bf16[128,768]{1,0:T(8,128)(2,1)S(1)}, bf16[128,768]{1,0:T(8,128)(2,1)S(1)}, u32[]{:S(2)}, u32[]{:S(2)}) %collective-permute-start.23) | collective-permute-done | bytes 196640 | tf_op jit(solution)/shard_map/ppermute | solution.py:48
  87.2 3.4 %collective-permute-done.22.refs_1_ = bf16[128,768]{1,0:T(8,128)(2,1)S(1)} collective-permute-done((bf16[128,768]{1,0:T(8,128)(2,1)S(1)}, bf16[128,768]{1,0:T(8,128)(2,1)S(1)}, u32[]{:S(2)}, u32[]{:S(2)}) %collective-permute-start.22) | collective-permute-done | bytes 196640 | tf_op jit(solution)/shard_map/ppermute | solution.py:48
  92.0 2.5 %shard_map.131 = (bf16[1296,128]{1,0:T(8,128)(2,1)S(1)}, bf16[1296,128]{1,0:T(8,128)(2,1)S(1)}, bf16[336,128]{1,0:T(8,128)(2,1)S(1)}, bf16[336,128]{1,0:T(8,128)...) custom-call(s32[5]{0:T(128)S(1)} %stack.23.ids, ...), custom_call_target="tpu_custom_call" | custom-call | tf_op jit(solution)/shard_map/pallas_call | solution.py:73
  95.9 1.9 %collective-permute-start.31 = (bf16[1296,128]{1,0:T(8,128)(2,1)S(1)}, bf16[1296,128]{1,0:T(8,128)(2,1)S(1)}, u32[]{:S(2)}, u32[]{:S(2)}) collective-permute-start(bf16[1296,128]{1,0:T(8,128)(2,1)S(1)} %get-tuple-element.114), channel_id=1, source_target_pairs={{0,28},{4,0},{8,4},{12,8},{16,12},{20,16},{24,20},{28,24},{1,29},{... | collective-permute-start | bytes 995336 | tf_op jit(solution)/shard_map/ppermute | solution.py:52
  98.9 3.0 %collective-permute-start.33 = (bf16[336,128]{1,0:T(8,128)(2,1)S(1)}, bf16[336,128]{1,0:T(8,128)(2,1)S(1)}, u32[]{:S(2)}, u32[]{:S(2)}) collective-permute-start(bf16[336,128]{1,0:T(8,128)(2,1)S(1)} %get-tuple-element.118), channel_id=1, source_target_pairs={{0,24},{4,28},{8,0},{12,4},{16,8},{20,12},{24,16},{28,20},{1,25},{... | collective-permute-start | bytes 258056 | tf_op jit(solution)/shard_map/ppermute | solution.py:52
  104.1 2.3 %collective-permute-done.29.a = bf16[1296,128]{1,0:T(8,128)(2,1)S(1)} collective-permute-done((bf16[1296,128]{1,0:T(8,128)(2,1)S(1)}, bf16[1296,128]{1,0:T(8,128)(2,1)S(1)}, u32[]{:S(2)}, u32[]{:S(2)}) %collective-permute-start.29) | collective-permute-done | bytes 331808 | tf_op jit(solution)/shard_map/ppermute | solution.py:52
  106.4 3.1 %collective-permute-done.32.c = bf16[336,128]{1,0:T(8,128)(2,1)S(1)} collective-permute-done((bf16[336,128]{1,0:T(8,128)(2,1)S(1)}, bf16[336,128]{1,0:T(8,128)(2,1)S(1)}, u32[]{:S(2)}, u32[]{:S(2)}) %collective-permute-start.32) | collective-permute-done | bytes 86048 | tf_op jit(solution)/shard_map/ppermute | solution.py:52
  111.1 3.1 %collective-permute-start.34 = (bf16[640,128]{1,0:T(8,128)(2,1)S(1)}, bf16[640,128]{1,0:T(8,128)(2,1)S(1)}, u32[]{:S(2)}, u32[]{:S(2)}) collective-permute-start(bf16[640,128]{1,0:T(8,128)(2,1)S(1)} %get-tuple-element.124), channel_id=1, source_target_pairs={{0,8},{4,12},{8,16},{12,20},{16,24},{20,28},{24,0},{28,4},{1,9},{5... | collective-permute-start | bytes 491528 | tf_op jit(solution)/shard_map/ppermute | solution.py:52
  117.7 3.6 %collective-permute-done.34.up = bf16[640,128]{1,0:T(8,128)(2,1)S(1)} collective-permute-done((bf16[640,128]{1,0:T(8,128)(2,1)S(1)}, bf16[640,128]{1,0:T(8,128)(2,1)S(1)}, u32[]{:S(2)}, u32[]{:S(2)}) %collective-permute-start.34) | collective-permute-done | bytes 163872 | tf_op jit(solution)/shard_map/ppermute | solution.py:52
  123.9 2.7 %collective-permute-start.37 = (bf16[320,128]{1,0:T(8,128)(2,1)S(1)}, bf16[320,128]{1,0:T(8,128)(2,1)S(1)}, u32[]{:S(2)}, u32[]{:S(2)}) collective-permute-start(bf16[320,128]{1,0:T(8,128)(2,1)S(1)} %get-tuple-element.127), channel_id=1, source_target_pairs={{160,0},{164,1},{32,2},{36,3},{224,4},{228,5},{96,6},{100,7},{168,... | collective-permute-start | bytes 245768 | tf_op jit(solution)/shard_map/ppermute | solution.py:536
  128.3 2.1 %shard_map.135 = f32[128,2048]{1,0:T(8,128)} custom-call(s32[5]{0:T(128)S(1)} %stack.23.ids, bf16[144,512]{1,0:T(8,128)(2,1)S(1)} %get-tuple-element.128.a.refs_0_, bf16[144,512]{1,0:T(8,128)(2,1)S(1)} %collective-permute-done.38.b.refs_1_, bf16[144,512]{1,0:T(8,128)(2,1)S(1)} %collective-permute-done.39.c.refs_2_, ...), custom_call_target="tpu_custom_call" | custom-call | tf_op jit(solution)/shard_map/pallas_call | solution.py:73
  130.4 2.1 %collective-permute-done.41 = f32[32,128]{1,0:T(8,128)S(1)} collective-permute-done((f32[32,128]{1,0:T(8,128)S(1)}, f32[32,128]{1,0:T(8,128)S(1)}, u32[]{:S(2)}, u32[]{:S(2)}) %collective-permute-start.41) | collective-permute-done | bytes 16416 | tf_op jit(solution)/shard_map/ppermute | solution.py:56
  133.1 1.8 %collective-permute-start.43 = (bf16[64,128]{1,0:T(8,128)(2,1)S(1)}, bf16[64,128]{1,0:T(8,128)(2,1)S(1)}, u32[]{:S(2)}, u32[]{:S(2)}) collective-permute-start(bf16[64,128]{1,0:T(8,128)(2,1)S(1)} %shard_map.137.own), channel_id=1, source_target_pairs={{0,2},{2,0},{1,3},{3,1},{4,6},{6,4},{5,7},{7,5},{8,10},{10,8},{9,1... | collective-permute-start | bytes 49160 | tf_op jit(solution)/shard_map/ppermute | solution.py:56
  134.9 2.8 %collective-permute-start.45 = (f32[16,128]{1,0:T(8,128)S(1)}, f32[16,128]{1,0:T(8,128)S(1)}, u32[]{:S(2)}, u32[]{:S(2)}) collective-permute-start(f32[16,128]{1,0:T(8,128)S(1)} %slice.7), channel_id=1, source_target_pairs={{0,16},{4,20},{8,24},{12,28},{16,0},{20,4},{24,8},{28,12},{1,17},{... | collective-permute-start | bytes 24584 | tf_op jit(solution)/shard_map/ppermute | solution.py:52
  139.4 3.0 %collective-permute-done.45 = f32[16,128]{1,0:T(8,128)S(1)} collective-permute-done((f32[16,128]{1,0:T(8,128)S(1)}, f32[16,128]{1,0:T(8,128)S(1)}, u32[]{:S(2)}, u32[]{:S(2)}) %collective-permute-start.45) | collective-permute-done | bytes 8224 | tf_op jit(solution)/shard_map/ppermute | solution.py:52
  (103 shorter events, 47.7 us)
Async XLA Ops:
  2.2 9.9 %collective-permute-start.1 = (bf16[320,128]{1,0:T(8,128)(2,1)S(1)}, bf16[320,128]{1,0:T(8,128)(2,1)S(1)}, u32[]{:S(2)}, u32[]{:S(2)}) collective-permute-start(bf16[320,128]{1,0:T(8,128)(2,1)S(1)} %pad_maximum_fusion), channel_id=1, source_target_pairs={{0,160},{1,164},{2,32},{3,36},{4,224},{5,228},{6,96},{7,100},{8,16... | collective-permute-start | bytes 245768 | tf_op jit(solution)/shard_map/ppermute | solution.py:436
  3.5 8.5 %collective-permute-start = (bf16[320,128]{1,0:T(8,128)(2,1)S(1)}, bf16[320,128]{1,0:T(8,128)(2,1)S(1)}, u32[]{:S(2)}, u32[]{:S(2)}) collective-permute-start(bf16[320,128]{1,0:T(8,128)(2,1)S(1)} %pad_maximum_fusion), channel_id=1, source_target_pairs={{0,32},{1,36},{2,160},{3,164},{4,96},{5,100},{6,224},{7,228},{8,40... | collective-permute-start | bytes 245768 | tf_op jit(solution)/shard_map/ppermute | solution.py:435
  12.1 14.7 %collective-permute-start.8 = (bf16[640,128]{1,0:T(8,128)(2,1)S(1)}, bf16[640,128]{1,0:T(8,128)(2,1)S(1)}, u32[]{:S(2)}, u32[]{:S(2)}) collective-permute-start(bf16[640,128]{1,0:T(8,128)(2,1)S(1)} %maximum_select_fusion.both), channel_id=1, source_target_pairs={{0,24},{4,28},{8,0},{12,4},{16,8},{20,12},{24,16},{28,20},{1,25},{... | collective-permute-start | bytes 491528 | tf_op jit(solution)/shard_map/ppermute | solution.py:52
  18.5 10.8 %collective-permute-start.7 = (bf16[640,128]{1,0:T(8,128)(2,1)S(1)}, bf16[640,128]{1,0:T(8,128)(2,1)S(1)}, u32[]{:S(2)}, u32[]{:S(2)}) collective-permute-start(bf16[640,128]{1,0:T(8,128)(2,1)S(1)} %maximum_select_fusion.both), channel_id=1, source_target_pairs={{0,8},{4,12},{8,16},{12,20},{16,24},{20,28},{24,0},{28,4},{1,9},{5... | collective-permute-start | bytes 491528 | tf_op jit(solution)/shard_map/ppermute | solution.py:52
  22.6 11.4 %collective-permute-start.4 = (bf16[272,512]{1,0:T(8,128)(2,1)S(1)}, bf16[272,512]{1,0:T(8,128)(2,1)S(1)}, u32[]{:S(2)}, u32[]{:S(2)}) collective-permute-start(bf16[272,512]{1,0:T(8,128)(2,1)S(1)} %get-tuple-element.81), channel_id=1, source_target_pairs={{0,32},{32,64},{64,96},{96,0},{1,33},{33,65},{65,97},{97,1},{2,34}... | collective-permute-start | bytes 835592 | tf_op jit(solution)/shard_map/ppermute | solution.py:48
  24.5 13.6 %collective-permute-start.5 = (bf16[272,512]{1,0:T(8,128)(2,1)S(1)}, bf16[272,512]{1,0:T(8,128)(2,1)S(1)}, u32[]{:S(2)}, u32[]{:S(2)}) collective-permute-start(bf16[272,512]{1,0:T(8,128)(2,1)S(1)} %get-tuple-element.82), channel_id=1, source_target_pairs={{0,64},{32,96},{64,0},{96,32},{1,65},{33,97},{65,1},{97,33},{2,66}... | collective-permute-start | bytes 835592 | tf_op jit(solution)/shard_map/ppermute | solution.py:48
  30.0 14.5 %collective-permute-start.9 = (bf16[1280,128]{1,0:T(8,128)(2,1)S(1)}, bf16[1280,128]{1,0:T(8,128)(2,1)S(1)}, u32[]{:S(2)}, u32[]{:S(2)}) collective-permute-start(bf16[1280,128]{1,0:T(8,128)(2,1)S(1)} %get-tuple-element.88), channel_id=1, source_target_pairs={{0,4},{4,8},{8,12},{12,16},{16,20},{20,24},{24,28},{28,0},{1,5},{5... | collective-permute-start | bytes 983048 | tf_op jit(solution)/shard_map/ppermute | solution.py:52
  31.6 12.9 %collective-permute-start.10 = (bf16[1280,128]{1,0:T(8,128)(2,1)S(1)}, bf16[1280,128]{1,0:T(8,128)(2,1)S(1)}, u32[]{:S(2)}, u32[]{:S(2)}) collective-permute-start(bf16[1280,128]{1,0:T(8,128)(2,1)S(1)} %get-tuple-element.89), channel_id=1, source_target_pairs={{0,28},{4,0},{8,4},{12,8},{16,12},{20,16},{24,20},{28,24},{1,29},{... | collective-permute-start | bytes 983048 | tf_op jit(solution)/shard_map/ppermute | solution.py:52
  33.3 8.7 %collective-permute-start.6 = (bf16[272,512]{1,0:T(8,128)(2,1)S(1)}, bf16[272,512]{1,0:T(8,128)(2,1)S(1)}, u32[]{:S(2)}, u32[]{:S(2)}) collective-permute-start(bf16[272,512]{1,0:T(8,128)(2,1)S(1)} %get-tuple-element.83), channel_id=1, source_target_pairs={{0,96},{32,0},{64,32},{96,64},{1,97},{33,1},{65,33},{97,65},{2,98}... | collective-permute-start | bytes 835592 | tf_op jit(solution)/shard_map/ppermute | solution.py:48
  34.0 9.3 %collective-permute-start.11 = (bf16[320,128]{1,0:T(8,128)(2,1)S(1)}, bf16[320,128]{1,0:T(8,128)(2,1)S(1)}, u32[]{:S(2)}, u32[]{:S(2)}) collective-permute-start(bf16[320,128]{1,0:T(8,128)(2,1)S(1)} %get-tuple-element.90), channel_id=1, source_target_pairs={{0,8},{4,12},{8,16},{12,20},{16,24},{20,28},{24,0},{28,4},{1,9},{5... | collective-permute-start | bytes 245768 | tf_op jit(solution)/shard_map/ppermute | solution.py:52
  38.1 6.4 %collective-permute-start.12 = (bf16[320,128]{1,0:T(8,128)(2,1)S(1)}, bf16[320,128]{1,0:T(8,128)(2,1)S(1)}, u32[]{:S(2)}, u32[]{:S(2)}) collective-permute-start(bf16[320,128]{1,0:T(8,128)(2,1)S(1)} %get-tuple-element.91), channel_id=1, source_target_pairs={{0,24},{4,28},{8,0},{12,4},{16,8},{20,12},{24,16},{28,20},{1,25},{... | collective-permute-start | bytes 245768 | tf_op jit(solution)/shard_map/ppermute | solution.py:52
  46.8 6.3 %collective-permute-start.13 = (f32[128,640]{1,0:T(8,128)S(1)}, f32[128,640]{1,0:T(8,128)S(1)}, u32[]{:S(2)}, u32[]{:S(2)}) collective-permute-start(f32[128,640]{1,0:T(8,128)S(1)} %get-tuple-element.96), channel_id=1, source_target_pairs={{0,1},{1,0},{2,3},{3,2},{4,5},{5,4},{6,7},{7,6},{8,9},{9,8},{10,11... | collective-permute-start | bytes 983048 | tf_op jit(solution)/shard_map/ppermute | solution.py:56
  48.9 9.2 %collective-permute-start.15 = (bf16[128,1024]{1,0:T(8,128)(2,1)S(1)}, bf16[128,1024]{1,0:T(8,128)(2,1)S(1)}, u32[]{:S(2)}, u32[]{:S(2)}) collective-permute-start(bf16[128,1024]{1,0:T(8,128)(2,1)S(1)} %shard_map.125), channel_id=1, source_target_pairs={{0,96},{32,0},{64,32},{96,64},{1,97},{33,1},{65,33},{97,65},{2,98}... | collective-permute-start | bytes 786440 | tf_op jit(solution)/shard_map/ppermute | solution.py:48
  49.6 10.8 %collective-permute-start.17 = (bf16[128,1024]{1,0:T(8,128)(2,1)S(1)}, bf16[128,1024]{1,0:T(8,128)(2,1)S(1)}, u32[]{:S(2)}, u32[]{:S(2)}) collective-permute-start(bf16[128,1024]{1,0:T(8,128)(2,1)S(1)} %shard_map.126), channel_id=1, source_target_pairs={{0,64},{32,96},{64,0},{96,32},{1,65},{33,97},{65,1},{97,33},{2,66}... | collective-permute-start | bytes 786440 | tf_op jit(solution)/shard_map/ppermute | solution.py:48
  51.9 13.3 %collective-permute-start.19 = (bf16[128,1024]{1,0:T(8,128)(2,1)S(1)}, bf16[128,1024]{1,0:T(8,128)(2,1)S(1)}, u32[]{:S(2)}, u32[]{:S(2)}) collective-permute-start(bf16[128,1024]{1,0:T(8,128)(2,1)S(1)} %shard_map.127), channel_id=1, source_target_pairs={{0,32},{32,64},{64,96},{96,0},{1,33},{33,65},{65,97},{97,1},{2,34}... | collective-permute-start | bytes 786440 | tf_op jit(solution)/shard_map/ppermute | solution.py:48
  65.8 8.3 %collective-permute-start.20 = (bf16[128,1024]{1,0:T(8,128)(2,1)S(1)}, bf16[128,1024]{1,0:T(8,128)(2,1)S(1)}, u32[]{:S(2)}, u32[]{:S(2)}) collective-permute-start(bf16[128,1024]{1,0:T(8,128)(2,1)S(1)} %shard_map.128.mine), channel_id=1, source_target_pairs={{0,2},{2,0},{1,3},{3,1},{4,6},{6,4},{5,7},{7,5},{8,10},{10,8},{9,1... | collective-permute-start | bytes 786440 | tf_op jit(solution)/shard_map/ppermute | solution.py:56
  77.7 7.8 %collective-permute-start.24 = (bf16[128,768]{1,0:T(8,128)(2,1)S(1)}, bf16[128,768]{1,0:T(8,128)(2,1)S(1)}, u32[]{:S(2)}, u32[]{:S(2)}) collective-permute-start(bf16[128,768]{1,0:T(8,128)(2,1)S(1)} %get-tuple-element.105.refs_0_), channel_id=1, source_target_pairs={{0,96},{32,0},{64,32},{96,64},{1,97},{33,1},{65,33},{97,65},{2,98}... | collective-permute-start | bytes 589832 | tf_op jit(solution)/shard_map/ppermute | solution.py:48
  77.8 9.4 %collective-permute-start.23 = (bf16[128,768]{1,0:T(8,128)(2,1)S(1)}, bf16[128,768]{1,0:T(8,128)(2,1)S(1)}, u32[]{:S(2)}, u32[]{:S(2)}) collective-permute-start(bf16[128,768]{1,0:T(8,128)(2,1)S(1)} %get-tuple-element.105.refs_0_), channel_id=1, source_target_pairs={{0,64},{32,96},{64,0},{96,32},{1,65},{33,97},{65,1},{97,33},{2,66}... | collective-permute-start | bytes 589832 | tf_op jit(solution)/shard_map/ppermute | solution.py:48
  79.2 11.4 %collective-permute-start.22 = (bf16[128,768]{1,0:T(8,128)(2,1)S(1)}, bf16[128,768]{1,0:T(8,128)(2,1)S(1)}, u32[]{:S(2)}, u32[]{:S(2)}) collective-permute-start(bf16[128,768]{1,0:T(8,128)(2,1)S(1)} %get-tuple-element.105.refs_0_), channel_id=1, source_target_pairs={{0,32},{32,64},{64,96},{96,0},{1,33},{33,65},{65,97},{97,1},{2,34}... | collective-permute-start | bytes 589832 | tf_op jit(solution)/shard_map/ppermute | solution.py:48
  80.5 10.1 %collective-permute-start.25 = (bf16[128,768]{1,0:T(8,128)(2,1)S(1)}, bf16[128,768]{1,0:T(8,128)(2,1)S(1)}, u32[]{:S(2)}, u32[]{:S(2)}) collective-permute-start(bf16[128,768]{1,0:T(8,128)(2,1)S(1)} %get-tuple-element.105.refs_0_), channel_id=1, source_target_pairs={{0,1},{1,0},{2,3},{3,2},{4,5},{5,4},{6,7},{7,6},{8,9},{9,8},{10,11... | collective-permute-start | bytes 589832 | tf_op jit(solution)/shard_map/ppermute | solution.py:56
  94.5 11.9 %collective-permute-start.29 = (bf16[1296,128]{1,0:T(8,128)(2,1)S(1)}, bf16[1296,128]{1,0:T(8,128)(2,1)S(1)}, u32[]{:S(2)}, u32[]{:S(2)}) collective-permute-start(bf16[1296,128]{1,0:T(8,128)(2,1)S(1)} %get-tuple-element.111), channel_id=1, source_target_pairs={{0,4},{4,8},{8,12},{12,16},{16,20},{20,24},{24,28},{28,0},{1,5},{5... | collective-permute-start | bytes 995336 | tf_op jit(solution)/shard_map/ppermute | solution.py:52
  95.9 14.5 %collective-permute-start.31 = (bf16[1296,128]{1,0:T(8,128)(2,1)S(1)}, bf16[1296,128]{1,0:T(8,128)(2,1)S(1)}, u32[]{:S(2)}, u32[]{:S(2)}) collective-permute-start(bf16[1296,128]{1,0:T(8,128)(2,1)S(1)} %get-tuple-element.114), channel_id=1, source_target_pairs={{0,28},{4,0},{8,4},{12,8},{16,12},{20,16},{24,20},{28,24},{1,29},{... | collective-permute-start | bytes 995336 | tf_op jit(solution)/shard_map/ppermute | solution.py:52
  97.8 11.7 %collective-permute-start.32 = (bf16[336,128]{1,0:T(8,128)(2,1)S(1)}, bf16[336,128]{1,0:T(8,128)(2,1)S(1)}, u32[]{:S(2)}, u32[]{:S(2)}) collective-permute-start(bf16[336,128]{1,0:T(8,128)(2,1)S(1)} %get-tuple-element.117), channel_id=1, source_target_pairs={{0,8},{4,12},{8,16},{12,20},{16,24},{20,28},{24,0},{28,4},{1,9},{5... | collective-permute-start | bytes 258056 | tf_op jit(solution)/shard_map/ppermute | solution.py:52
  98.9 11.5 %collective-permute-start.33 = (bf16[336,128]{1,0:T(8,128)(2,1)S(1)}, bf16[336,128]{1,0:T(8,128)(2,1)S(1)}, u32[]{:S(2)}, u32[]{:S(2)}) collective-permute-start(bf16[336,128]{1,0:T(8,128)(2,1)S(1)} %get-tuple-element.118), channel_id=1, source_target_pairs={{0,24},{4,28},{8,0},{12,4},{16,8},{20,12},{24,16},{28,20},{1,25},{... | collective-permute-start | bytes 258056 | tf_op jit(solution)/shard_map/ppermute | solution.py:52
  111.1 10.3 %collective-permute-start.34 = (bf16[640,128]{1,0:T(8,128)(2,1)S(1)}, bf16[640,128]{1,0:T(8,128)(2,1)S(1)}, u32[]{:S(2)}, u32[]{:S(2)}) collective-permute-start(bf16[640,128]{1,0:T(8,128)(2,1)S(1)} %get-tuple-element.124), channel_id=1, source_target_pairs={{0,8},{4,12},{8,16},{12,20},{16,24},{20,28},{24,0},{28,4},{1,9},{5... | collective-permute-start | bytes 491528 | tf_op jit(solution)/shard_map/ppermute | solution.py:52
  114.1 8.3 %collective-permute-start.35 = (bf16[640,128]{1,0:T(8,128)(2,1)S(1)}, bf16[640,128]{1,0:T(8,128)(2,1)S(1)}, u32[]{:S(2)}, u32[]{:S(2)}) collective-permute-start(bf16[640,128]{1,0:T(8,128)(2,1)S(1)} %get-tuple-element.125), channel_id=1, source_target_pairs={{0,24},{4,28},{8,0},{12,4},{16,8},{20,12},{24,16},{28,20},{1,25},{... | collective-permute-start | bytes 491528 | tf_op jit(solution)/shard_map/ppermute | solution.py:52
  115.3 11.3 %collective-permute-start.38 = (bf16[144,512]{1,0:T(8,128)(2,1)S(1)}, bf16[144,512]{1,0:T(8,128)(2,1)S(1)}, u32[]{:S(2)}, u32[]{:S(2)}) collective-permute-start(bf16[144,512]{1,0:T(8,128)(2,1)S(1)} %get-tuple-element.129), channel_id=1, source_target_pairs={{0,96},{32,0},{64,32},{96,64},{1,97},{33,1},{65,33},{97,65},{2,98}... | collective-permute-start | bytes 442376 | tf_op jit(solution)/shard_map/ppermute | solution.py:48
  116.7 9.9 %collective-permute-start.39 = (bf16[144,512]{1,0:T(8,128)(2,1)S(1)}, bf16[144,512]{1,0:T(8,128)(2,1)S(1)}, u32[]{:S(2)}, u32[]{:S(2)}) collective-permute-start(bf16[144,512]{1,0:T(8,128)(2,1)S(1)} %get-tuple-element.130), channel_id=1, source_target_pairs={{0,64},{32,96},{64,0},{96,32},{1,65},{33,97},{65,1},{97,33},{2,66}... | collective-permute-start | bytes 442376 | tf_op jit(solution)/shard_map/ppermute | solution.py:48
  117.3 9.3 %collective-permute-start.40 = (bf16[144,512]{1,0:T(8,128)(2,1)S(1)}, bf16[144,512]{1,0:T(8,128)(2,1)S(1)}, u32[]{:S(2)}, u32[]{:S(2)}) collective-permute-start(bf16[144,512]{1,0:T(8,128)(2,1)S(1)} %get-tuple-element.131), channel_id=1, source_target_pairs={{0,32},{32,64},{64,96},{96,0},{1,33},{33,65},{65,97},{97,1},{2,34}... | collective-permute-start | bytes 442376 | tf_op jit(solution)/shard_map/ppermute | solution.py:48
  123.1 9.4 %collective-permute-start.36 = (bf16[320,128]{1,0:T(8,128)(2,1)S(1)}, bf16[320,128]{1,0:T(8,128)(2,1)S(1)}, u32[]{:S(2)}, u32[]{:S(2)}) collective-permute-start(bf16[320,128]{1,0:T(8,128)(2,1)S(1)} %get-tuple-element.126), channel_id=1, source_target_pairs={{32,0},{36,1},{160,2},{164,3},{96,4},{100,5},{224,6},{228,7},{40,8... | collective-permute-start | bytes 245768 | tf_op jit(solution)/shard_map/ppermute | solution.py:536
  123.9 8.6 %collective-permute-start.37 = (bf16[320,128]{1,0:T(8,128)(2,1)S(1)}, bf16[320,128]{1,0:T(8,128)(2,1)S(1)}, u32[]{:S(2)}, u32[]{:S(2)}) collective-permute-start(bf16[320,128]{1,0:T(8,128)(2,1)S(1)} %get-tuple-element.127), channel_id=1, source_target_pairs={{160,0},{164,1},{32,2},{36,3},{224,4},{228,5},{96,6},{100,7},{168,... | collective-permute-start | bytes 245768 | tf_op jit(solution)/shard_map/ppermute | solution.py:536
  134.9 7.6 %collective-permute-start.45 = (f32[16,128]{1,0:T(8,128)S(1)}, f32[16,128]{1,0:T(8,128)S(1)}, u32[]{:S(2)}, u32[]{:S(2)}) collective-permute-start(f32[16,128]{1,0:T(8,128)S(1)} %slice.7), channel_id=1, source_target_pairs={{0,16},{4,20},{8,24},{12,28},{16,0},{20,4},{24,8},{28,12},{1,17},{... | collective-permute-start | bytes 24584 | tf_op jit(solution)/shard_map/ppermute | solution.py:52
  (19 other events, 66.7 us)

commit v8 on v7

--- a/solution.py
+++ b/solution.py
@@ -548,10 +548,11 @@
         row_sum,
         static=width,
     )
-    *arrived, grad_input, gain_z = lax.optimization_barrier((*arrived, grad_input, gain_z))
+    *arrived, grad_input = lax.optimization_barrier((*arrived, grad_input))
     (shared_own,) = call(shared_kernel, [((2 * PIECE, HD), BF16)], [], ids, *arrived)
     grad_query, grad_out = call(owner_kernel, [((HD, HD), F32)] * 2, [], ids, *arrived, static=loss_scale)
     shared_yl = swap(shared_own, "yl")
+    shared_yl, grad_query, grad_out = lax.optimization_barrier((shared_yl, grad_query, grad_out))
     gain_z = gain_z[: 4 * NX] + shift_z(gain_z[4 * NX :], 4)
     grad_key, grad_value, grad_gain = call(
         join_kernel,

time: 144 us -> 143 us (level)
  waiting for transfers between devices: 59.1 us -> 55.5 us
  starting transfers between devices: 58 us -> 59.8 us
    ppermute x17, waiting for transfers between devices: 15.7 us -> 13.6 us  [swap(): return lax.ppermute(value, axis, [(0, 1), (1, 0)])]
    ppermute x13, starting transfers between devices: 28.2 us -> 29.6 us  [shift_z(): return lax.ppermute(value, 'z', [(i, (i + by) % NZ) for i in range(NZ)])]
  transfers between devices with their start and end apart: 46 -> 46, of which waited for: 22 -> 21; matrix products, arithmetic and copies ran while one was open for 0% -> 0% of each run, Pallas kernels for 9% -> 9%
where the time goes in v8:
time: 143 us; the launch traced here: 142 us
  starting transfers between devices  59.8 us (42%)
  waiting for transfers between devices  55.5 us (39%)
  Pallas kernels  22 us (15%)
  local copies, waits for them, and re-layouts  2.93 us (2%)
    ppermute x13, starting transfers between devices, shift_z(): return lax.ppermute(value, 'z', [(i, (i + by) % NZ) for i in range(NZ)])  29.6 us
    ppermute x12, waiting for transfers between devices, shift_x(): return lax.ppermute(value, 'x', [(i, (i + by) % NX) for i in range(NX)])  25.5 us
    pallas_call x22, Pallas kernels, call(): pl.pallas_call(body, out_shape=[jax.ShapeDtypeStruct(s, d) for s, d in ou...  22 us
    ppermute x13, waiting for transfers between devices, shift_z(): return lax.ppermute(value, 'z', [(i, (i + by) % NZ) for i in range(NZ)])  16.4 us
    ppermute x17, waiting for transfers between devices, swap(): return lax.ppermute(value, axis, [(0, 1), (1, 0)])  13.6 us
    ppermute x12, starting transfers between devices, shift_x(): return lax.ppermute(value, 'x', [(i, (i + by) % NX) for i in range(NX)])  13.1 us
    ppermute x17, starting transfers between devices, swap(): return lax.ppermute(value, axis, [(0, 1), (1, 0)])  9.82 us
  transfers between devices with their start and end apart: 46, of which 21 were waited for; matrix products, arithmetic and copies ran while one was open for 0% of the time, Pallas kernels for 9%

profile of v8, /device:TPU:8, one launch (start us, length us, event | category | flops | bytes accessed | tf_op | source)
XLA Modules:
  0.0 142.0 jit_solution(14622147391623394113)
XLA Ops:
  3.5 2.4 %collective-permute-start = (bf16[320,128]{1,0:T(8,128)(2,1)S(1)}, bf16[320,128]{1,0:T(8,128)(2,1)S(1)}, u32[]{:S(2)}, u32[]{:S(2)}) collective-permute-start(bf16[320,128]{1,0:T(8,128)(2,1)S(1)} %pad_maximum_fusion), channel_id=1, source_target_pairs={{0,32},{1,36},{2,160},{3,164},{4,96},{5,100},{6,224},{7,228},{8,40... | collective-permute-start | bytes 245768 | tf_op jit(solution)/shard_map/ppermute | solution.py:435
  9.2 2.1 %collective-permute-start.2 = (f32[1,128]{1,0:T(1,128)S(1)}, f32[1,128]{1,0:T(1,128)S(1)}, u32[]{:S(2)}, u32[]{:S(2)}) collective-permute-start(f32[1,128]{1,0:T(1,128)S(1)} %get-tuple-element.76), channel_id=1, source_target_pairs={{0,1},{1,0},{2,3},{3,2},{4,5},{5,4},{6,7},{7,6},{8,9},{9,8},{10,11... | collective-permute-start | bytes 1544 | tf_op jit(solution)/shard_map/ppermute | solution.py:56
  12.1 6.4 %collective-permute-start.8 = (bf16[640,128]{1,0:T(8,128)(2,1)S(1)}, bf16[640,128]{1,0:T(8,128)(2,1)S(1)}, u32[]{:S(2)}, u32[]{:S(2)}) collective-permute-start(bf16[640,128]{1,0:T(8,128)(2,1)S(1)} %maximum_select_fusion.both), channel_id=1, source_target_pairs={{0,24},{4,28},{8,0},{12,4},{16,8},{20,12},{24,16},{28,20},{1,25},{... | collective-permute-start | bytes 491528 | tf_op jit(solution)/shard_map/ppermute | solution.py:52
  19.8 2.2 %collective-permute-done.3 = f32[1,128]{1,0:T(1,128)S(1)} collective-permute-done((f32[1,128]{1,0:T(1,128)S(1)}, f32[1,128]{1,0:T(1,128)S(1)}, u32[]{:S(2)}, u32[]{:S(2)}) %collective-permute-start.3) | collective-permute-done | bytes 544 | tf_op jit(solution)/shard_map/ppermute | solution.py:56
  22.6 1.9 %collective-permute-start.4 = (bf16[272,512]{1,0:T(8,128)(2,1)S(1)}, bf16[272,512]{1,0:T(8,128)(2,1)S(1)}, u32[]{:S(2)}, u32[]{:S(2)}) collective-permute-start(bf16[272,512]{1,0:T(8,128)(2,1)S(1)} %get-tuple-element.83), channel_id=1, source_target_pairs={{0,32},{32,64},{64,96},{96,0},{1,33},{33,65},{65,97},{97,1},{2,34}... | collective-permute-start | bytes 835592 | tf_op jit(solution)/shard_map/ppermute | solution.py:48
  24.5 2.3 %collective-permute-start.5 = (bf16[272,512]{1,0:T(8,128)(2,1)S(1)}, bf16[272,512]{1,0:T(8,128)(2,1)S(1)}, u32[]{:S(2)}, u32[]{:S(2)}) collective-permute-start(bf16[272,512]{1,0:T(8,128)(2,1)S(1)} %get-tuple-element.84), channel_id=1, source_target_pairs={{0,64},{32,96},{64,0},{96,32},{1,65},{33,97},{65,1},{97,33},{2,66}... | collective-permute-start | bytes 835592 | tf_op jit(solution)/shard_map/ppermute | solution.py:48
  26.8 2.5 %collective-permute-done.7.prev.prev2 = bf16[640,128]{1,0:T(8,128)(2,1)S(1)} collective-permute-done((bf16[640,128]{1,0:T(8,128)(2,1)S(1)}, bf16[640,128]{1,0:T(8,128)(2,1)S(1)}, u32[]{:S(2)}, u32[]{:S(2)}) %collective-permute-start.7) | collective-permute-done | bytes 163872 | tf_op jit(solution)/shard_map/ppermute | solution.py:52
  30.0 1.6 %collective-permute-start.9 = (bf16[1280,128]{1,0:T(8,128)(2,1)S(1)}, bf16[1280,128]{1,0:T(8,128)(2,1)S(1)}, u32[]{:S(2)}, u32[]{:S(2)}) collective-permute-start(bf16[1280,128]{1,0:T(8,128)(2,1)S(1)} %get-tuple-element.90), channel_id=1, source_target_pairs={{0,4},{4,8},{8,12},{12,16},{16,20},{20,24},{24,28},{28,0},{1,5},{5... | collective-permute-start | bytes 983048 | tf_op jit(solution)/shard_map/ppermute | solution.py:52
  31.6 1.7 %collective-permute-start.10 = (bf16[1280,128]{1,0:T(8,128)(2,1)S(1)}, bf16[1280,128]{1,0:T(8,128)(2,1)S(1)}, u32[]{:S(2)}, u32[]{:S(2)}) collective-permute-start(bf16[1280,128]{1,0:T(8,128)(2,1)S(1)} %get-tuple-element.91), channel_id=1, source_target_pairs={{0,28},{4,0},{8,4},{12,8},{16,12},{20,16},{24,20},{28,24},{1,29},{... | collective-permute-start | bytes 983048 | tf_op jit(solution)/shard_map/ppermute | solution.py:52
  34.1 4.0 %collective-permute-done.5.refs_2_ = bf16[272,512]{1,0:T(8,128)(2,1)S(1)} collective-permute-done((bf16[272,512]{1,0:T(8,128)(2,1)S(1)}, bf16[272,512]{1,0:T(8,128)(2,1)S(1)}, u32[]{:S(2)}, u32[]{:S(2)}) %collective-permute-start.5) | collective-permute-done | bytes 278560 | tf_op jit(solution)/shard_map/ppermute | solution.py:48
  38.1 3.9 %collective-permute-start.12 = (bf16[320,128]{1,0:T(8,128)(2,1)S(1)}, bf16[320,128]{1,0:T(8,128)(2,1)S(1)}, u32[]{:S(2)}, u32[]{:S(2)}) collective-permute-start(bf16[320,128]{1,0:T(8,128)(2,1)S(1)} %get-tuple-element.93), channel_id=1, source_target_pairs={{0,24},{4,28},{8,0},{12,4},{16,8},{20,12},{24,16},{28,20},{1,25},{... | collective-permute-start | bytes 245768 | tf_op jit(solution)/shard_map/ppermute | solution.py:52
  49.6 1.7 %collective-permute-start.17 = (bf16[128,1024]{1,0:T(8,128)(2,1)S(1)}, bf16[128,1024]{1,0:T(8,128)(2,1)S(1)}, u32[]{:S(2)}, u32[]{:S(2)}) collective-permute-start(bf16[128,1024]{1,0:T(8,128)(2,1)S(1)} %shard_map.126), channel_id=1, source_target_pairs={{0,64},{32,96},{64,0},{96,32},{1,65},{33,97},{65,1},{97,33},{2,66}... | collective-permute-start | bytes 786440 | tf_op jit(solution)/shard_map/ppermute | solution.py:48
  53.6 4.5 %collective-permute-done.15.a = bf16[128,1024]{1,0:T(8,128)(2,1)S(1)} collective-permute-done((bf16[128,1024]{1,0:T(8,128)(2,1)S(1)}, bf16[128,1024]{1,0:T(8,128)(2,1)S(1)}, u32[]{:S(2)}, u32[]{:S(2)}) %collective-permute-start.15) | collective-permute-done | bytes 262176 | tf_op jit(solution)/shard_map/ppermute | solution.py:48
  58.1 2.3 %collective-permute-done.17.b = bf16[128,1024]{1,0:T(8,128)(2,1)S(1)} collective-permute-done((bf16[128,1024]{1,0:T(8,128)(2,1)S(1)}, bf16[128,1024]{1,0:T(8,128)(2,1)S(1)}, u32[]{:S(2)}, u32[]{:S(2)}) %collective-permute-start.17) | collective-permute-done | bytes 262176 | tf_op jit(solution)/shard_map/ppermute | solution.py:48
  60.4 4.7 %collective-permute-done.19.c = bf16[128,1024]{1,0:T(8,128)(2,1)S(1)} collective-permute-done((bf16[128,1024]{1,0:T(8,128)(2,1)S(1)}, bf16[128,1024]{1,0:T(8,128)(2,1)S(1)}, u32[]{:S(2)}, u32[]{:S(2)}) %collective-permute-start.19) | collective-permute-done | bytes 262176 | tf_op jit(solution)/shard_map/ppermute | solution.py:48
  67.3 6.8 %collective-permute-done.20.got = bf16[128,1024]{1,0:T(8,128)(2,1)S(1)} collective-permute-done((bf16[128,1024]{1,0:T(8,128)(2,1)S(1)}, bf16[128,1024]{1,0:T(8,128)(2,1)S(1)}, u32[]{:S(2)}, u32[]{:S(2)}) %collective-permute-start.20) | collective-permute-done | bytes 262176 | tf_op jit(solution)/shard_map/ppermute | solution.py:56
  76.0 1.7 %shard_map.130 = (bf16[128,768]{1,0:T(8,128)(2,1)S(1)}, f32[1,128]{1,0:T(1,128)S(1)}) custom-call(s32[5]{0:T(128)S(1)} %stack.23.ids, bf16[128,512]{1,0:T(8,128)(2,1)S(1)} %get-tuple-element.105.qa, bf16[128,128]{1,0:T(8,128)(2,1)S(1)} %get-tuple-element.106.kv_mine, bf16[128,128]{1,0:T(8,128)(2,1)S(1)} %collective-permute-done.21.kv_theirs), custom_call_target="tpu_custom_call" | custom-call | tf_op jit(solution)/shard_map/pallas_call | solution.py:73
  80.5 5.0 %collective-permute-done.24.refs_3_ = bf16[128,768]{1,0:T(8,128)(2,1)S(1)} collective-permute-done((bf16[128,768]{1,0:T(8,128)(2,1)S(1)}, bf16[128,768]{1,0:T(8,128)(2,1)S(1)}, u32[]{:S(2)}, u32[]{:S(2)}) %collective-permute-start.24) | collective-permute-done | bytes 196640 | tf_op jit(solution)/shard_map/ppermute | solution.py:48
  85.5 1.6 %collective-permute-done.23.refs_2_ = bf16[128,768]{1,0:T(8,128)(2,1)S(1)} collective-permute-done((bf16[128,768]{1,0:T(8,128)(2,1)S(1)}, bf16[128,768]{1,0:T(8,128)(2,1)S(1)}, u32[]{:S(2)}, u32[]{:S(2)}) %collective-permute-start.23) | collective-permute-done | bytes 196640 | tf_op jit(solution)/shard_map/ppermute | solution.py:48
  87.2 3.4 %collective-permute-done.22.refs_1_ = bf16[128,768]{1,0:T(8,128)(2,1)S(1)} collective-permute-done((bf16[128,768]{1,0:T(8,128)(2,1)S(1)}, bf16[128,768]{1,0:T(8,128)(2,1)S(1)}, u32[]{:S(2)}, u32[]{:S(2)}) %collective-permute-start.22) | collective-permute-done | bytes 196640 | tf_op jit(solution)/shard_map/ppermute | solution.py:48
  92.0 2.5 %shard_map.131 = (bf16[1296,128]{1,0:T(8,128)(2,1)S(1)}, bf16[1296,128]{1,0:T(8,128)(2,1)S(1)}, bf16[336,128]{1,0:T(8,128)(2,1)S(1)}, bf16[336,128]{1,0:T(8,128)...) custom-call(s32[5]{0:T(128)S(1)} %stack.23.ids, ...), custom_call_target="tpu_custom_call" | custom-call | tf_op jit(solution)/shard_map/pallas_call | solution.py:73
  95.9 1.9 %collective-permute-start.31 = (bf16[1296,128]{1,0:T(8,128)(2,1)S(1)}, bf16[1296,128]{1,0:T(8,128)(2,1)S(1)}, u32[]{:S(2)}, u32[]{:S(2)}) collective-permute-start(bf16[1296,128]{1,0:T(8,128)(2,1)S(1)} %get-tuple-element.116), channel_id=1, source_target_pairs={{0,28},{4,0},{8,4},{12,8},{16,12},{20,16},{24,20},{28,24},{1,29},{... | collective-permute-start | bytes 995336 | tf_op jit(solution)/shard_map/ppermute | solution.py:52
  98.9 3.0 %collective-permute-start.33 = (bf16[336,128]{1,0:T(8,128)(2,1)S(1)}, bf16[336,128]{1,0:T(8,128)(2,1)S(1)}, u32[]{:S(2)}, u32[]{:S(2)}) collective-permute-start(bf16[336,128]{1,0:T(8,128)(2,1)S(1)} %get-tuple-element.120), channel_id=1, source_target_pairs={{0,24},{4,28},{8,0},{12,4},{16,8},{20,12},{24,16},{28,20},{1,25},{... | collective-permute-start | bytes 258056 | tf_op jit(solution)/shard_map/ppermute | solution.py:52
  104.1 2.3 %collective-permute-done.29.a = bf16[1296,128]{1,0:T(8,128)(2,1)S(1)} collective-permute-done((bf16[1296,128]{1,0:T(8,128)(2,1)S(1)}, bf16[1296,128]{1,0:T(8,128)(2,1)S(1)}, u32[]{:S(2)}, u32[]{:S(2)}) %collective-permute-start.29) | collective-permute-done | bytes 331808 | tf_op jit(solution)/shard_map/ppermute | solution.py:52
  106.4 3.1 %collective-permute-done.32.c = bf16[336,128]{1,0:T(8,128)(2,1)S(1)} collective-permute-done((bf16[336,128]{1,0:T(8,128)(2,1)S(1)}, bf16[336,128]{1,0:T(8,128)(2,1)S(1)}, u32[]{:S(2)}, u32[]{:S(2)}) %collective-permute-start.32) | collective-permute-done | bytes 86048 | tf_op jit(solution)/shard_map/ppermute | solution.py:52
  111.1 3.1 %collective-permute-start.34 = (bf16[640,128]{1,0:T(8,128)(2,1)S(1)}, bf16[640,128]{1,0:T(8,128)(2,1)S(1)}, u32[]{:S(2)}, u32[]{:S(2)}) collective-permute-start(bf16[640,128]{1,0:T(8,128)(2,1)S(1)} %get-tuple-element.126), channel_id=1, source_target_pairs={{0,8},{4,12},{8,16},{12,20},{16,24},{20,28},{24,0},{28,4},{1,9},{5... | collective-permute-start | bytes 491528 | tf_op jit(solution)/shard_map/ppermute | solution.py:52
  117.7 3.6 %collective-permute-done.34.up = bf16[640,128]{1,0:T(8,128)(2,1)S(1)} collective-permute-done((bf16[640,128]{1,0:T(8,128)(2,1)S(1)}, bf16[640,128]{1,0:T(8,128)(2,1)S(1)}, u32[]{:S(2)}, u32[]{:S(2)}) %collective-permute-start.34) | collective-permute-done | bytes 163872 | tf_op jit(solution)/shard_map/ppermute | solution.py:52
  123.9 2.7 %collective-permute-start.37 = (bf16[320,128]{1,0:T(8,128)(2,1)S(1)}, bf16[320,128]{1,0:T(8,128)(2,1)S(1)}, u32[]{:S(2)}, u32[]{:S(2)}) collective-permute-start(bf16[320,128]{1,0:T(8,128)(2,1)S(1)} %get-tuple-element.129), channel_id=1, source_target_pairs={{160,0},{164,1},{32,2},{36,3},{224,4},{228,5},{96,6},{100,7},{168,... | collective-permute-start | bytes 245768 | tf_op jit(solution)/shard_map/ppermute | solution.py:536
  128.3 2.1 %shard_map.135 = f32[128,2048]{1,0:T(8,128)} custom-call(s32[5]{0:T(128)S(1)} %stack.23.ids, bf16[144,512]{1,0:T(8,128)(2,1)S(1)} %get-tuple-element.130.a.refs_0_, bf16[144,512]{1,0:T(8,128)(2,1)S(1)} %collective-permute-done.38.b.refs_1_, bf16[144,512]{1,0:T(8,128)(2,1)S(1)} %collective-permute-done.39.c.refs_2_, ...), custom_call_target="tpu_custom_call" | custom-call | tf_op jit(solution)/shard_map/pallas_call | solution.py:73
  130.9 2.1 %collective-permute-start.42 = (bf16[64,128]{1,0:T(8,128)(2,1)S(1)}, bf16[64,128]{1,0:T(8,128)(2,1)S(1)}, u32[]{:S(2)}, u32[]{:S(2)}) collective-permute-start(bf16[64,128]{1,0:T(8,128)(2,1)S(1)} %shard_map.136.own), channel_id=1, source_target_pairs={{0,2},{2,0},{1,3},{3,1},{4,6},{6,4},{5,7},{7,5},{8,10},{10,8},{9,1... | collective-permute-start | bytes 49160 | tf_op jit(solution)/shard_map/ppermute | solution.py:56
  133.1 4.3 %collective-permute-start.45 = (f32[16,128]{1,0:T(8,128)S(1)}, f32[16,128]{1,0:T(8,128)S(1)}, u32[]{:S(2)}, u32[]{:S(2)}) collective-permute-start(f32[16,128]{1,0:T(8,128)S(1)} %slice.9), channel_id=1, source_target_pairs={{0,16},{4,20},{8,24},{12,28},{16,0},{20,4},{24,8},{28,12},{1,17},{... | collective-permute-start | bytes 24584 | tf_op jit(solution)/shard_map/ppermute | solution.py:52
  139.1 1.7 %collective-permute-done.45 = f32[16,128]{1,0:T(8,128)S(1)} collective-permute-done((f32[16,128]{1,0:T(8,128)S(1)}, f32[16,128]{1,0:T(8,128)S(1)}, u32[]{:S(2)}, u32[]{:S(2)}) %collective-permute-start.45) | collective-permute-done | bytes 8224 | tf_op jit(solution)/shard_map/ppermute | solution.py:52
  (103 shorter events, 46.1 us)
Async XLA Ops:
  2.2 9.9 %collective-permute-start.1 = (bf16[320,128]{1,0:T(8,128)(2,1)S(1)}, bf16[320,128]{1,0:T(8,128)(2,1)S(1)}, u32[]{:S(2)}, u32[]{:S(2)}) collective-permute-start(bf16[320,128]{1,0:T(8,128)(2,1)S(1)} %pad_maximum_fusion), channel_id=1, source_target_pairs={{0,160},{1,164},{2,32},{3,36},{4,224},{5,228},{6,96},{7,100},{8,16... | collective-permute-start | bytes 245768 | tf_op jit(solution)/shard_map/ppermute | solution.py:436
  3.5 8.5 %collective-permute-start = (bf16[320,128]{1,0:T(8,128)(2,1)S(1)}, bf16[320,128]{1,0:T(8,128)(2,1)S(1)}, u32[]{:S(2)}, u32[]{:S(2)}) collective-permute-start(bf16[320,128]{1,0:T(8,128)(2,1)S(1)} %pad_maximum_fusion), channel_id=1, source_target_pairs={{0,32},{1,36},{2,160},{3,164},{4,96},{5,100},{6,224},{7,228},{8,40... | collective-permute-start | bytes 245768 | tf_op jit(solution)/shard_map/ppermute | solution.py:435
  12.1 14.7 %collective-permute-start.8 = (bf16[640,128]{1,0:T(8,128)(2,1)S(1)}, bf16[640,128]{1,0:T(8,128)(2,1)S(1)}, u32[]{:S(2)}, u32[]{:S(2)}) collective-permute-start(bf16[640,128]{1,0:T(8,128)(2,1)S(1)} %maximum_select_fusion.both), channel_id=1, source_target_pairs={{0,24},{4,28},{8,0},{12,4},{16,8},{20,12},{24,16},{28,20},{1,25},{... | collective-permute-start | bytes 491528 | tf_op jit(solution)/shard_map/ppermute | solution.py:52
  18.5 10.8 %collective-permute-start.7 = (bf16[640,128]{1,0:T(8,128)(2,1)S(1)}, bf16[640,128]{1,0:T(8,128)(2,1)S(1)}, u32[]{:S(2)}, u32[]{:S(2)}) collective-permute-start(bf16[640,128]{1,0:T(8,128)(2,1)S(1)} %maximum_select_fusion.both), channel_id=1, source_target_pairs={{0,8},{4,12},{8,16},{12,20},{16,24},{20,28},{24,0},{28,4},{1,9},{5... | collective-permute-start | bytes 491528 | tf_op jit(solution)/shard_map/ppermute | solution.py:52
  22.6 11.4 %collective-permute-start.4 = (bf16[272,512]{1,0:T(8,128)(2,1)S(1)}, bf16[272,512]{1,0:T(8,128)(2,1)S(1)}, u32[]{:S(2)}, u32[]{:S(2)}) collective-permute-start(bf16[272,512]{1,0:T(8,128)(2,1)S(1)} %get-tuple-element.83), channel_id=1, source_target_pairs={{0,32},{32,64},{64,96},{96,0},{1,33},{33,65},{65,97},{97,1},{2,34}... | collective-permute-start | bytes 835592 | tf_op jit(solution)/shard_map/ppermute | solution.py:48
  24.5 13.6 %collective-permute-start.5 = (bf16[272,512]{1,0:T(8,128)(2,1)S(1)}, bf16[272,512]{1,0:T(8,128)(2,1)S(1)}, u32[]{:S(2)}, u32[]{:S(2)}) collective-permute-start(bf16[272,512]{1,0:T(8,128)(2,1)S(1)} %get-tuple-element.84), channel_id=1, source_target_pairs={{0,64},{32,96},{64,0},{96,32},{1,65},{33,97},{65,1},{97,33},{2,66}... | collective-permute-start | bytes 835592 | tf_op jit(solution)/shard_map/ppermute | solution.py:48
  30.0 14.5 %collective-permute-start.9 = (bf16[1280,128]{1,0:T(8,128)(2,1)S(1)}, bf16[1280,128]{1,0:T(8,128)(2,1)S(1)}, u32[]{:S(2)}, u32[]{:S(2)}) collective-permute-start(bf16[1280,128]{1,0:T(8,128)(2,1)S(1)} %get-tuple-element.90), channel_id=1, source_target_pairs={{0,4},{4,8},{8,12},{12,16},{16,20},{20,24},{24,28},{28,0},{1,5},{5... | collective-permute-start | bytes 983048 | tf_op jit(solution)/shard_map/ppermute | solution.py:52
  31.6 12.9 %collective-permute-start.10 = (bf16[1280,128]{1,0:T(8,128)(2,1)S(1)}, bf16[1280,128]{1,0:T(8,128)(2,1)S(1)}, u32[]{:S(2)}, u32[]{:S(2)}) collective-permute-start(bf16[1280,128]{1,0:T(8,128)(2,1)S(1)} %get-tuple-element.91), channel_id=1, source_target_pairs={{0,28},{4,0},{8,4},{12,8},{16,12},{20,16},{24,20},{28,24},{1,29},{... | collective-permute-start | bytes 983048 | tf_op jit(solution)/shard_map/ppermute | solution.py:52
  33.3 8.7 %collective-permute-start.6 = (bf16[272,512]{1,0:T(8,128)(2,1)S(1)}, bf16[272,512]{1,0:T(8,128)(2,1)S(1)}, u32[]{:S(2)}, u32[]{:S(2)}) collective-permute-start(bf16[272,512]{1,0:T(8,128)(2,1)S(1)} %get-tuple-element.85), channel_id=1, source_target_pairs={{0,96},{32,0},{64,32},{96,64},{1,97},{33,1},{65,33},{97,65},{2,98}... | collective-permute-start | bytes 835592 | tf_op jit(solution)/shard_map/ppermute | solution.py:48
  34.0 9.3 %collective-permute-start.11 = (bf16[320,128]{1,0:T(8,128)(2,1)S(1)}, bf16[320,128]{1,0:T(8,128)(2,1)S(1)}, u32[]{:S(2)}, u32[]{:S(2)}) collective-permute-start(bf16[320,128]{1,0:T(8,128)(2,1)S(1)} %get-tuple-element.92), channel_id=1, source_target_pairs={{0,8},{4,12},{8,16},{12,20},{16,24},{20,28},{24,0},{28,4},{1,9},{5... | collective-permute-start | bytes 245768 | tf_op jit(solution)/shard_map/ppermute | solution.py:52
  38.1 6.4 %collective-permute-start.12 = (bf16[320,128]{1,0:T(8,128)(2,1)S(1)}, bf16[320,128]{1,0:T(8,128)(2,1)S(1)}, u32[]{:S(2)}, u32[]{:S(2)}) collective-permute-start(bf16[320,128]{1,0:T(8,128)(2,1)S(1)} %get-tuple-element.93), channel_id=1, source_target_pairs={{0,24},{4,28},{8,0},{12,4},{16,8},{20,12},{24,16},{28,20},{1,25},{... | collective-permute-start | bytes 245768 | tf_op jit(solution)/shard_map/ppermute | solution.py:52
  48.9 9.2 %collective-permute-start.15 = (bf16[128,1024]{1,0:T(8,128)(2,1)S(1)}, bf16[128,1024]{1,0:T(8,128)(2,1)S(1)}, u32[]{:S(2)}, u32[]{:S(2)}) collective-permute-start(bf16[128,1024]{1,0:T(8,128)(2,1)S(1)} %shard_map.125), channel_id=1, source_target_pairs={{0,96},{32,0},{64,32},{96,64},{1,97},{33,1},{65,33},{97,65},{2,98}... | collective-permute-start | bytes 786440 | tf_op jit(solution)/shard_map/ppermute | solution.py:48
  49.6 10.8 %collective-permute-start.17 = (bf16[128,1024]{1,0:T(8,128)(2,1)S(1)}, bf16[128,1024]{1,0:T(8,128)(2,1)S(1)}, u32[]{:S(2)}, u32[]{:S(2)}) collective-permute-start(bf16[128,1024]{1,0:T(8,128)(2,1)S(1)} %shard_map.126), channel_id=1, source_target_pairs={{0,64},{32,96},{64,0},{96,32},{1,65},{33,97},{65,1},{97,33},{2,66}... | collective-permute-start | bytes 786440 | tf_op jit(solution)/shard_map/ppermute | solution.py:48
  51.9 13.3 %collective-permute-start.19 = (bf16[128,1024]{1,0:T(8,128)(2,1)S(1)}, bf16[128,1024]{1,0:T(8,128)(2,1)S(1)}, u32[]{:S(2)}, u32[]{:S(2)}) collective-permute-start(bf16[128,1024]{1,0:T(8,128)(2,1)S(1)} %shard_map.127), channel_id=1, source_target_pairs={{0,32},{32,64},{64,96},{96,0},{1,33},{33,65},{65,97},{97,1},{2,34}... | collective-permute-start | bytes 786440 | tf_op jit(solution)/shard_map/ppermute | solution.py:48
  65.8 8.3 %collective-permute-start.20 = (bf16[128,1024]{1,0:T(8,128)(2,1)S(1)}, bf16[128,1024]{1,0:T(8,128)(2,1)S(1)}, u32[]{:S(2)}, u32[]{:S(2)}) collective-permute-start(bf16[128,1024]{1,0:T(8,128)(2,1)S(1)} %shard_map.128.mine), channel_id=1, source_target_pairs={{0,2},{2,0},{1,3},{3,1},{4,6},{6,4},{5,7},{7,5},{8,10},{10,8},{9,1... | collective-permute-start | bytes 786440 | tf_op jit(solution)/shard_map/ppermute | solution.py:56
  77.7 7.8 %collective-permute-start.24 = (bf16[128,768]{1,0:T(8,128)(2,1)S(1)}, bf16[128,768]{1,0:T(8,128)(2,1)S(1)}, u32[]{:S(2)}, u32[]{:S(2)}) collective-permute-start(bf16[128,768]{1,0:T(8,128)(2,1)S(1)} %get-tuple-element.107.refs_0_), channel_id=1, source_target_pairs={{0,96},{32,0},{64,32},{96,64},{1,97},{33,1},{65,33},{97,65},{2,98}... | collective-permute-start | bytes 589832 | tf_op jit(solution)/shard_map/ppermute | solution.py:48
  77.8 9.4 %collective-permute-start.23 = (bf16[128,768]{1,0:T(8,128)(2,1)S(1)}, bf16[128,768]{1,0:T(8,128)(2,1)S(1)}, u32[]{:S(2)}, u32[]{:S(2)}) collective-permute-start(bf16[128,768]{1,0:T(8,128)(2,1)S(1)} %get-tuple-element.107.refs_0_), channel_id=1, source_target_pairs={{0,64},{32,96},{64,0},{96,32},{1,65},{33,97},{65,1},{97,33},{2,66}... | collective-permute-start | bytes 589832 | tf_op jit(solution)/shard_map/ppermute | solution.py:48
  79.2 11.4 %collective-permute-start.22 = (bf16[128,768]{1,0:T(8,128)(2,1)S(1)}, bf16[128,768]{1,0:T(8,128)(2,1)S(1)}, u32[]{:S(2)}, u32[]{:S(2)}) collective-permute-start(bf16[128,768]{1,0:T(8,128)(2,1)S(1)} %get-tuple-element.107.refs_0_), channel_id=1, source_target_pairs={{0,32},{32,64},{64,96},{96,0},{1,33},{33,65},{65,97},{97,1},{2,34}... | collective-permute-start | bytes 589832 | tf_op jit(solution)/shard_map/ppermute | solution.py:48
  80.5 10.1 %collective-permute-start.25 = (bf16[128,768]{1,0:T(8,128)(2,1)S(1)}, bf16[128,768]{1,0:T(8,128)(2,1)S(1)}, u32[]{:S(2)}, u32[]{:S(2)}) collective-permute-start(bf16[128,768]{1,0:T(8,128)(2,1)S(1)} %get-tuple-element.107.refs_0_), channel_id=1, source_target_pairs={{0,1},{1,0},{2,3},{3,2},{4,5},{5,4},{6,7},{7,6},{8,9},{9,8},{10,11... | collective-permute-start | bytes 589832 | tf_op jit(solution)/shard_map/ppermute | solution.py:56
  94.5 11.9 %collective-permute-start.29 = (bf16[1296,128]{1,0:T(8,128)(2,1)S(1)}, bf16[1296,128]{1,0:T(8,128)(2,1)S(1)}, u32[]{:S(2)}, u32[]{:S(2)}) collective-permute-start(bf16[1296,128]{1,0:T(8,128)(2,1)S(1)} %get-tuple-element.113), channel_id=1, source_target_pairs={{0,4},{4,8},{8,12},{12,16},{16,20},{20,24},{24,28},{28,0},{1,5},{5... | collective-permute-start | bytes 995336 | tf_op jit(solution)/shard_map/ppermute | solution.py:52
  95.9 14.5 %collective-permute-start.31 = (bf16[1296,128]{1,0:T(8,128)(2,1)S(1)}, bf16[1296,128]{1,0:T(8,128)(2,1)S(1)}, u32[]{:S(2)}, u32[]{:S(2)}) collective-permute-start(bf16[1296,128]{1,0:T(8,128)(2,1)S(1)} %get-tuple-element.116), channel_id=1, source_target_pairs={{0,28},{4,0},{8,4},{12,8},{16,12},{20,16},{24,20},{28,24},{1,29},{... | collective-permute-start | bytes 995336 | tf_op jit(solution)/shard_map/ppermute | solution.py:52
  97.8 11.7 %collective-permute-start.32 = (bf16[336,128]{1,0:T(8,128)(2,1)S(1)}, bf16[336,128]{1,0:T(8,128)(2,1)S(1)}, u32[]{:S(2)}, u32[]{:S(2)}) collective-permute-start(bf16[336,128]{1,0:T(8,128)(2,1)S(1)} %get-tuple-element.119), channel_id=1, source_target_pairs={{0,8},{4,12},{8,16},{12,20},{16,24},{20,28},{24,0},{28,4},{1,9},{5... | collective-permute-start | bytes 258056 | tf_op jit(solution)/shard_map/ppermute | solution.py:52
  98.9 11.5 %collective-permute-start.33 = (bf16[336,128]{1,0:T(8,128)(2,1)S(1)}, bf16[336,128]{1,0:T(8,128)(2,1)S(1)}, u32[]{:S(2)}, u32[]{:S(2)}) collective-permute-start(bf16[336,128]{1,0:T(8,128)(2,1)S(1)} %get-tuple-element.120), channel_id=1, source_target_pairs={{0,24},{4,28},{8,0},{12,4},{16,8},{20,12},{24,16},{28,20},{1,25},{... | collective-permute-start | bytes 258056 | tf_op jit(solution)/shard_map/ppermute | solution.py:52
  111.1 10.3 %collective-permute-start.34 = (bf16[640,128]{1,0:T(8,128)(2,1)S(1)}, bf16[640,128]{1,0:T(8,128)(2,1)S(1)}, u32[]{:S(2)}, u32[]{:S(2)}) collective-permute-start(bf16[640,128]{1,0:T(8,128)(2,1)S(1)} %get-tuple-element.126), channel_id=1, source_target_pairs={{0,8},{4,12},{8,16},{12,20},{16,24},{20,28},{24,0},{28,4},{1,9},{5... | collective-permute-start | bytes 491528 | tf_op jit(solution)/shard_map/ppermute | solution.py:52
  114.1 8.3 %collective-permute-start.35 = (bf16[640,128]{1,0:T(8,128)(2,1)S(1)}, bf16[640,128]{1,0:T(8,128)(2,1)S(1)}, u32[]{:S(2)}, u32[]{:S(2)}) collective-permute-start(bf16[640,128]{1,0:T(8,128)(2,1)S(1)} %get-tuple-element.127), channel_id=1, source_target_pairs={{0,24},{4,28},{8,0},{12,4},{16,8},{20,12},{24,16},{28,20},{1,25},{... | collective-permute-start | bytes 491528 | tf_op jit(solution)/shard_map/ppermute | solution.py:52
  115.3 11.3 %collective-permute-start.38 = (bf16[144,512]{1,0:T(8,128)(2,1)S(1)}, bf16[144,512]{1,0:T(8,128)(2,1)S(1)}, u32[]{:S(2)}, u32[]{:S(2)}) collective-permute-start(bf16[144,512]{1,0:T(8,128)(2,1)S(1)} %get-tuple-element.131), channel_id=1, source_target_pairs={{0,96},{32,0},{64,32},{96,64},{1,97},{33,1},{65,33},{97,65},{2,98}... | collective-permute-start | bytes 442376 | tf_op jit(solution)/shard_map/ppermute | solution.py:48
  116.7 9.9 %collective-permute-start.39 = (bf16[144,512]{1,0:T(8,128)(2,1)S(1)}, bf16[144,512]{1,0:T(8,128)(2,1)S(1)}, u32[]{:S(2)}, u32[]{:S(2)}) collective-permute-start(bf16[144,512]{1,0:T(8,128)(2,1)S(1)} %get-tuple-element.132), channel_id=1, source_target_pairs={{0,64},{32,96},{64,0},{96,32},{1,65},{33,97},{65,1},{97,33},{2,66}... | collective-permute-start | bytes 442376 | tf_op jit(solution)/shard_map/ppermute | solution.py:48
  117.3 9.3 %collective-permute-start.40 = (bf16[144,512]{1,0:T(8,128)(2,1)S(1)}, bf16[144,512]{1,0:T(8,128)(2,1)S(1)}, u32[]{:S(2)}, u32[]{:S(2)}) collective-permute-start(bf16[144,512]{1,0:T(8,128)(2,1)S(1)} %get-tuple-element.133), channel_id=1, source_target_pairs={{0,32},{32,64},{64,96},{96,0},{1,33},{33,65},{65,97},{97,1},{2,34}... | collective-permute-start | bytes 442376 | tf_op jit(solution)/shard_map/ppermute | solution.py:48
  123.1 7.3 %collective-permute-start.36 = (bf16[320,128]{1,0:T(8,128)(2,1)S(1)}, bf16[320,128]{1,0:T(8,128)(2,1)S(1)}, u32[]{:S(2)}, u32[]{:S(2)}) collective-permute-start(bf16[320,128]{1,0:T(8,128)(2,1)S(1)} %get-tuple-element.128), channel_id=1, source_target_pairs={{32,0},{36,1},{160,2},{164,3},{96,4},{100,5},{224,6},{228,7},{40,8... | collective-permute-start | bytes 245768 | tf_op jit(solution)/shard_map/ppermute | solution.py:536
  123.9 6.5 %collective-permute-start.37 = (bf16[320,128]{1,0:T(8,128)(2,1)S(1)}, bf16[320,128]{1,0:T(8,128)(2,1)S(1)}, u32[]{:S(2)}, u32[]{:S(2)}) collective-permute-start(bf16[320,128]{1,0:T(8,128)(2,1)S(1)} %get-tuple-element.129), channel_id=1, source_target_pairs={{160,0},{164,1},{32,2},{36,3},{224,4},{228,5},{96,6},{100,7},{168,... | collective-permute-start | bytes 245768 | tf_op jit(solution)/shard_map/ppermute | solution.py:536
  130.9 7.6 %collective-permute-start.42 = (bf16[64,128]{1,0:T(8,128)(2,1)S(1)}, bf16[64,128]{1,0:T(8,128)(2,1)S(1)}, u32[]{:S(2)}, u32[]{:S(2)}) collective-permute-start(bf16[64,128]{1,0:T(8,128)(2,1)S(1)} %shard_map.136.own), channel_id=1, source_target_pairs={{0,2},{2,0},{1,3},{3,1},{4,6},{6,4},{5,7},{7,5},{8,10},{10,8},{9,1... | collective-permute-start | bytes 49160 | tf_op jit(solution)/shard_map/ppermute | solution.py:56
  133.1 7.6 %collective-permute-start.45 = (f32[16,128]{1,0:T(8,128)S(1)}, f32[16,128]{1,0:T(8,128)S(1)}, u32[]{:S(2)}, u32[]{:S(2)}) collective-permute-start(f32[16,128]{1,0:T(8,128)S(1)} %slice.9), channel_id=1, source_target_pairs={{0,16},{4,20},{8,24},{12,28},{16,0},{20,4},{24,8},{28,12},{1,17},{... | collective-permute-start | bytes 24584 | tf_op jit(solution)/shard_map/ppermute | solution.py:52
  (19 other events, 65.0 us)

commit v9 on v7

--- a/solution.py
+++ b/solution.py
@@ -548,10 +548,12 @@
         row_sum,
         static=width,
     )
-    *arrived, grad_input, gain_z = lax.optimization_barrier((*arrived, grad_input, gain_z))
     (shared_own,) = call(shared_kernel, [((2 * PIECE, HD), BF16)], [], ids, *arrived)
     grad_query, grad_out = call(owner_kernel, [((HD, HD), F32)] * 2, [], ids, *arrived, static=loss_scale)
     shared_yl = swap(shared_own, "yl")
+    shared_yl, grad_input, grad_query, grad_out = lax.optimization_barrier(
+        (shared_yl, grad_input, grad_query, grad_out)
+    )
     gain_z = gain_z[: 4 * NX] + shift_z(gain_z[4 * NX :], 4)
     grad_key, grad_value, grad_gain = call(
         join_kernel,

time: 144 us -> 144 us (level)
  waiting for transfers between devices: 59.1 us -> 56.7 us
    ppermute x13, waiting for transfers between devices: 17.8 us -> 15.1 us  [shift_z(): return lax.ppermute(value, 'z', [(i, (i + by) % NZ) for i in range(NZ)])]
    ppermute x17, waiting for transfers between devices: 15.7 us -> 14.2 us  [swap(): return lax.ppermute(value, axis, [(0, 1), (1, 0)])]
  transfers between devices with their start and end apart: 46 -> 46, of which waited for: 22 -> 24; matrix products, arithmetic and copies ran while one was open for 0% -> 0% of each run, Pallas kernels for 9% -> 9%
where the time goes in v9:
time: 144 us; the launch traced here: 142 us
  starting transfers between devices  59.1 us (41%)
  waiting for transfers between devices  56.7 us (39%)
  Pallas kernels  22 us (15%)
  local copies, waits for them, and re-layouts  2.93 us (2%)
    ppermute x13, starting transfers between devices, shift_z(): return lax.ppermute(value, 'z', [(i, (i + by) % NZ) for i in range(NZ)])  28.9 us
    ppermute x12, waiting for transfers between devices, shift_x(): return lax.ppermute(value, 'x', [(i, (i + by) % NX) for i in range(NX)])  25.5 us
    pallas_call x22, Pallas kernels, call(): pl.pallas_call(body, out_shape=[jax.ShapeDtypeStruct(s, d) for s, d in ou...  22 us
    ppermute x13, waiting for transfers between devices, shift_z(): return lax.ppermute(value, 'z', [(i, (i + by) % NZ) for i in range(NZ)])  15.1 us
    ppermute x17, waiting for transfers between devices, swap(): return lax.ppermute(value, axis, [(0, 1), (1, 0)])  14.2 us
    ppermute x12, starting transfers between devices, shift_x(): return lax.ppermute(value, 'x', [(i, (i + by) % NX) for i in range(NX)])  13.1 us
    ppermute x17, starting transfers between devices, swap(): return lax.ppermute(value, axis, [(0, 1), (1, 0)])  9.89 us
  transfers between devices with their start and end apart: 46, of which 24 were waited for; matrix products, arithmetic and copies ran while one was open for 0% of the time, Pallas kernels for 9%

profile of v9, /device:TPU:8, one launch (start us, length us, event | category | flops | bytes accessed | tf_op | source)
XLA Modules:
  0.0 142.5 jit_solution(14983952190073074008)
XLA Ops:
  3.5 2.4 %collective-permute-start = (bf16[320,128]{1,0:T(8,128)(2,1)S(1)}, bf16[320,128]{1,0:T(8,128)(2,1)S(1)}, u32[]{:S(2)}, u32[]{:S(2)}) collective-permute-start(bf16[320,128]{1,0:T(8,128)(2,1)S(1)} %pad_maximum_fusion), channel_id=1, source_target_pairs={{0,32},{1,36},{2,160},{3,164},{4,96},{5,100},{6,224},{7,228},{8,40... | collective-permute-start | bytes 245768 | tf_op jit(solution)/shard_map/ppermute | solution.py:435
  9.2 2.1 %collective-permute-start.2 = (f32[1,128]{1,0:T(1,128)S(1)}, f32[1,128]{1,0:T(1,128)S(1)}, u32[]{:S(2)}, u32[]{:S(2)}) collective-permute-start(f32[1,128]{1,0:T(1,128)S(1)} %get-tuple-element.74), channel_id=1, source_target_pairs={{0,1},{1,0},{2,3},{3,2},{4,5},{5,4},{6,7},{7,6},{8,9},{9,8},{10,11... | collective-permute-start | bytes 1544 | tf_op jit(solution)/shard_map/ppermute | solution.py:56
  12.1 6.4 %collective-permute-start.8 = (bf16[640,128]{1,0:T(8,128)(2,1)S(1)}, bf16[640,128]{1,0:T(8,128)(2,1)S(1)}, u32[]{:S(2)}, u32[]{:S(2)}) collective-permute-start(bf16[640,128]{1,0:T(8,128)(2,1)S(1)} %maximum_select_fusion.both), channel_id=1, source_target_pairs={{0,24},{4,28},{8,0},{12,4},{16,8},{20,12},{24,16},{28,20},{1,25},{... | collective-permute-start | bytes 491528 | tf_op jit(solution)/shard_map/ppermute | solution.py:52
  19.8 2.2 %collective-permute-done.3 = f32[1,128]{1,0:T(1,128)S(1)} collective-permute-done((f32[1,128]{1,0:T(1,128)S(1)}, f32[1,128]{1,0:T(1,128)S(1)}, u32[]{:S(2)}, u32[]{:S(2)}) %collective-permute-start.3) | collective-permute-done | bytes 544 | tf_op jit(solution)/shard_map/ppermute | solution.py:56
  22.6 1.9 %collective-permute-start.4 = (bf16[272,512]{1,0:T(8,128)(2,1)S(1)}, bf16[272,512]{1,0:T(8,128)(2,1)S(1)}, u32[]{:S(2)}, u32[]{:S(2)}) collective-permute-start(bf16[272,512]{1,0:T(8,128)(2,1)S(1)} %get-tuple-element.81), channel_id=1, source_target_pairs={{0,32},{32,64},{64,96},{96,0},{1,33},{33,65},{65,97},{97,1},{2,34}... | collective-permute-start | bytes 835592 | tf_op jit(solution)/shard_map/ppermute | solution.py:48
  24.5 2.3 %collective-permute-start.5 = (bf16[272,512]{1,0:T(8,128)(2,1)S(1)}, bf16[272,512]{1,0:T(8,128)(2,1)S(1)}, u32[]{:S(2)}, u32[]{:S(2)}) collective-permute-start(bf16[272,512]{1,0:T(8,128)(2,1)S(1)} %get-tuple-element.82), channel_id=1, source_target_pairs={{0,64},{32,96},{64,0},{96,32},{1,65},{33,97},{65,1},{97,33},{2,66}... | collective-permute-start | bytes 835592 | tf_op jit(solution)/shard_map/ppermute | solution.py:48
  26.8 2.5 %collective-permute-done.7.prev.prev2 = bf16[640,128]{1,0:T(8,128)(2,1)S(1)} collective-permute-done((bf16[640,128]{1,0:T(8,128)(2,1)S(1)}, bf16[640,128]{1,0:T(8,128)(2,1)S(1)}, u32[]{:S(2)}, u32[]{:S(2)}) %collective-permute-start.7) | collective-permute-done | bytes 163872 | tf_op jit(solution)/shard_map/ppermute | solution.py:52
  30.0 1.6 %collective-permute-start.9 = (bf16[1280,128]{1,0:T(8,128)(2,1)S(1)}, bf16[1280,128]{1,0:T(8,128)(2,1)S(1)}, u32[]{:S(2)}, u32[]{:S(2)}) collective-permute-start(bf16[1280,128]{1,0:T(8,128)(2,1)S(1)} %get-tuple-element.88), channel_id=1, source_target_pairs={{0,4},{4,8},{8,12},{12,16},{16,20},{20,24},{24,28},{28,0},{1,5},{5... | collective-permute-start | bytes 983048 | tf_op jit(solution)/shard_map/ppermute | solution.py:52
  31.6 1.7 %collective-permute-start.10 = (bf16[1280,128]{1,0:T(8,128)(2,1)S(1)}, bf16[1280,128]{1,0:T(8,128)(2,1)S(1)}, u32[]{:S(2)}, u32[]{:S(2)}) collective-permute-start(bf16[1280,128]{1,0:T(8,128)(2,1)S(1)} %get-tuple-element.89), channel_id=1, source_target_pairs={{0,28},{4,0},{8,4},{12,8},{16,12},{20,16},{24,20},{28,24},{1,29},{... | collective-permute-start | bytes 983048 | tf_op jit(solution)/shard_map/ppermute | solution.py:52
  34.1 4.0 %collective-permute-done.5.refs_2_ = bf16[272,512]{1,0:T(8,128)(2,1)S(1)} collective-permute-done((bf16[272,512]{1,0:T(8,128)(2,1)S(1)}, bf16[272,512]{1,0:T(8,128)(2,1)S(1)}, u32[]{:S(2)}, u32[]{:S(2)}) %collective-permute-start.5) | collective-permute-done | bytes 278560 | tf_op jit(solution)/shard_map/ppermute | solution.py:48
  38.1 3.9 %collective-permute-start.12 = (bf16[320,128]{1,0:T(8,128)(2,1)S(1)}, bf16[320,128]{1,0:T(8,128)(2,1)S(1)}, u32[]{:S(2)}, u32[]{:S(2)}) collective-permute-start(bf16[320,128]{1,0:T(8,128)(2,1)S(1)} %get-tuple-element.91), channel_id=1, source_target_pairs={{0,24},{4,28},{8,0},{12,4},{16,8},{20,12},{24,16},{28,20},{1,25},{... | collective-permute-start | bytes 245768 | tf_op jit(solution)/shard_map/ppermute | solution.py:52
  44.5 1.6 %shard_map.122 = (f32[128,640]{1,0:T(8,128)S(1)}, f32[128,640]{1,0:T(8,128)S(1)}, f32[128,640]{1,0:T(8,128)S(1)}, f32[128,640]{1,0:T(8,128)S(1)}, bf16[512,768]{...) custom-call(s32[5]{0:T(128)S(1)} %stack.23.ids, bf16[640,128]{1,0:T(8,128)(2,1)S(1)} %maximum_select_fusion.both, ...), custom_call_target="tpu_custom_call" | custom-call | tf_op jit(solution)/shard_map/pallas_call | solution.py:73
  49.6 1.7 %collective-permute-start.17 = (bf16[128,1024]{1,0:T(8,128)(2,1)S(1)}, bf16[128,1024]{1,0:T(8,128)(2,1)S(1)}, u32[]{:S(2)}, u32[]{:S(2)}) collective-permute-start(bf16[128,1024]{1,0:T(8,128)(2,1)S(1)} %shard_map.126), channel_id=1, source_target_pairs={{0,64},{32,96},{64,0},{96,32},{1,65},{33,97},{65,1},{97,33},{2,66}... | collective-permute-start | bytes 786440 | tf_op jit(solution)/shard_map/ppermute | solution.py:48
  53.6 4.5 %collective-permute-done.15.a = bf16[128,1024]{1,0:T(8,128)(2,1)S(1)} collective-permute-done((bf16[128,1024]{1,0:T(8,128)(2,1)S(1)}, bf16[128,1024]{1,0:T(8,128)(2,1)S(1)}, u32[]{:S(2)}, u32[]{:S(2)}) %collective-permute-start.15) | collective-permute-done | bytes 262176 | tf_op jit(solution)/shard_map/ppermute | solution.py:48
  58.1 2.3 %collective-permute-done.17.b = bf16[128,1024]{1,0:T(8,128)(2,1)S(1)} collective-permute-done((bf16[128,1024]{1,0:T(8,128)(2,1)S(1)}, bf16[128,1024]{1,0:T(8,128)(2,1)S(1)}, u32[]{:S(2)}, u32[]{:S(2)}) %collective-permute-start.17) | collective-permute-done | bytes 262176 | tf_op jit(solution)/shard_map/ppermute | solution.py:48
  60.4 4.7 %collective-permute-done.19.c = bf16[128,1024]{1,0:T(8,128)(2,1)S(1)} collective-permute-done((bf16[128,1024]{1,0:T(8,128)(2,1)S(1)}, bf16[128,1024]{1,0:T(8,128)(2,1)S(1)}, u32[]{:S(2)}, u32[]{:S(2)}) %collective-permute-start.19) | collective-permute-done | bytes 262176 | tf_op jit(solution)/shard_map/ppermute | solution.py:48
  67.3 6.8 %collective-permute-done.20.got = bf16[128,1024]{1,0:T(8,128)(2,1)S(1)} collective-permute-done((bf16[128,1024]{1,0:T(8,128)(2,1)S(1)}, bf16[128,1024]{1,0:T(8,128)(2,1)S(1)}, u32[]{:S(2)}, u32[]{:S(2)}) %collective-permute-start.20) | collective-permute-done | bytes 262176 | tf_op jit(solution)/shard_map/ppermute | solution.py:56
  76.0 1.7 %shard_map.130 = (bf16[128,768]{1,0:T(8,128)(2,1)S(1)}, f32[1,128]{1,0:T(1,128)S(1)}) custom-call(s32[5]{0:T(128)S(1)} %stack.23.ids, bf16[128,512]{1,0:T(8,128)(2,1)S(1)} %get-tuple-element.103.qa, bf16[128,128]{1,0:T(8,128)(2,1)S(1)} %get-tuple-element.104.kv_mine, bf16[128,128]{1,0:T(8,128)(2,1)S(1)} %collective-permute-done.21.kv_theirs), custom_call_target="tpu_custom_call" | custom-call | tf_op jit(solution)/shard_map/pallas_call | solution.py:73
  80.5 5.0 %collective-permute-done.24.refs_3_ = bf16[128,768]{1,0:T(8,128)(2,1)S(1)} collective-permute-done((bf16[128,768]{1,0:T(8,128)(2,1)S(1)}, bf16[128,768]{1,0:T(8,128)(2,1)S(1)}, u32[]{:S(2)}, u32[]{:S(2)}) %collective-permute-start.24) | collective-permute-done | bytes 196640 | tf_op jit(solution)/shard_map/ppermute | solution.py:48
  85.5 1.6 %collective-permute-done.23.refs_2_ = bf16[128,768]{1,0:T(8,128)(2,1)S(1)} collective-permute-done((bf16[128,768]{1,0:T(8,128)(2,1)S(1)}, bf16[128,768]{1,0:T(8,128)(2,1)S(1)}, u32[]{:S(2)}, u32[]{:S(2)}) %collective-permute-start.23) | collective-permute-done | bytes 196640 | tf_op jit(solution)/shard_map/ppermute | solution.py:48
  87.2 3.4 %collective-permute-done.22.refs_1_ = bf16[128,768]{1,0:T(8,128)(2,1)S(1)} collective-permute-done((bf16[128,768]{1,0:T(8,128)(2,1)S(1)}, bf16[128,768]{1,0:T(8,128)(2,1)S(1)}, u32[]{:S(2)}, u32[]{:S(2)}) %collective-permute-start.22) | collective-permute-done | bytes 196640 | tf_op jit(solution)/shard_map/ppermute | solution.py:48
  92.0 2.5 %shard_map.131 = (bf16[1296,128]{1,0:T(8,128)(2,1)S(1)}, bf16[1296,128]{1,0:T(8,128)(2,1)S(1)}, bf16[336,128]{1,0:T(8,128)(2,1)S(1)}, bf16[336,128]{1,0:T(8,128)...) custom-call(s32[5]{0:T(128)S(1)} %stack.23.ids, ...), custom_call_target="tpu_custom_call" | custom-call | tf_op jit(solution)/shard_map/pallas_call | solution.py:73
  95.9 1.9 %collective-permute-start.31 = (bf16[1296,128]{1,0:T(8,128)(2,1)S(1)}, bf16[1296,128]{1,0:T(8,128)(2,1)S(1)}, u32[]{:S(2)}, u32[]{:S(2)}) collective-permute-start(bf16[1296,128]{1,0:T(8,128)(2,1)S(1)} %get-tuple-element.114), channel_id=1, source_target_pairs={{0,28},{4,0},{8,4},{12,8},{16,12},{20,16},{24,20},{28,24},{1,29},{... | collective-permute-start | bytes 995336 | tf_op jit(solution)/shard_map/ppermute | solution.py:52
  98.9 3.0 %collective-permute-start.33 = (bf16[336,128]{1,0:T(8,128)(2,1)S(1)}, bf16[336,128]{1,0:T(8,128)(2,1)S(1)}, u32[]{:S(2)}, u32[]{:S(2)}) collective-permute-start(bf16[336,128]{1,0:T(8,128)(2,1)S(1)} %get-tuple-element.118), channel_id=1, source_target_pairs={{0,24},{4,28},{8,0},{12,4},{16,8},{20,12},{24,16},{28,20},{1,25},{... | collective-permute-start | bytes 258056 | tf_op jit(solution)/shard_map/ppermute | solution.py:52
  104.1 2.3 %collective-permute-done.29.a = bf16[1296,128]{1,0:T(8,128)(2,1)S(1)} collective-permute-done((bf16[1296,128]{1,0:T(8,128)(2,1)S(1)}, bf16[1296,128]{1,0:T(8,128)(2,1)S(1)}, u32[]{:S(2)}, u32[]{:S(2)}) %collective-permute-start.29) | collective-permute-done | bytes 331808 | tf_op jit(solution)/shard_map/ppermute | solution.py:52
  106.4 3.1 %collective-permute-done.32.c = bf16[336,128]{1,0:T(8,128)(2,1)S(1)} collective-permute-done((bf16[336,128]{1,0:T(8,128)(2,1)S(1)}, bf16[336,128]{1,0:T(8,128)(2,1)S(1)}, u32[]{:S(2)}, u32[]{:S(2)}) %collective-permute-start.32) | collective-permute-done | bytes 86048 | tf_op jit(solution)/shard_map/ppermute | solution.py:52
  111.1 3.1 %collective-permute-start.34 = (bf16[640,128]{1,0:T(8,128)(2,1)S(1)}, bf16[640,128]{1,0:T(8,128)(2,1)S(1)}, u32[]{:S(2)}, u32[]{:S(2)}) collective-permute-start(bf16[640,128]{1,0:T(8,128)(2,1)S(1)} %get-tuple-element.124), channel_id=1, source_target_pairs={{0,8},{4,12},{8,16},{12,20},{16,24},{20,28},{24,0},{28,4},{1,9},{5... | collective-permute-start | bytes 491528 | tf_op jit(solution)/shard_map/ppermute | solution.py:52
  117.7 3.6 %collective-permute-done.34.up = bf16[640,128]{1,0:T(8,128)(2,1)S(1)} collective-permute-done((bf16[640,128]{1,0:T(8,128)(2,1)S(1)}, bf16[640,128]{1,0:T(8,128)(2,1)S(1)}, u32[]{:S(2)}, u32[]{:S(2)}) %collective-permute-start.34) | collective-permute-done | bytes 163872 | tf_op jit(solution)/shard_map/ppermute | solution.py:52
  123.9 2.7 %collective-permute-start.37 = (bf16[320,128]{1,0:T(8,128)(2,1)S(1)}, bf16[320,128]{1,0:T(8,128)(2,1)S(1)}, u32[]{:S(2)}, u32[]{:S(2)}) collective-permute-start(bf16[320,128]{1,0:T(8,128)(2,1)S(1)} %get-tuple-element.127), channel_id=1, source_target_pairs={{160,0},{164,1},{32,2},{36,3},{224,4},{228,5},{96,6},{100,7},{168,... | collective-permute-start | bytes 245768 | tf_op jit(solution)/shard_map/ppermute | solution.py:536
  130.7 2.2 %collective-permute-start.38 = (bf16[64,128]{1,0:T(8,128)(2,1)S(1)}, bf16[64,128]{1,0:T(8,128)(2,1)S(1)}, u32[]{:S(2)}, u32[]{:S(2)}) collective-permute-start(bf16[64,128]{1,0:T(8,128)(2,1)S(1)} %shard_map.135.own), channel_id=1, source_target_pairs={{0,2},{2,0},{1,3},{3,1},{4,6},{6,4},{5,7},{7,5},{8,10},{10,8},{9,1... | collective-permute-start | bytes 49160 | tf_op jit(solution)/shard_map/ppermute | solution.py:56
  132.9 3.6 %collective-permute-start.45 = (f32[16,128]{1,0:T(8,128)S(1)}, f32[16,128]{1,0:T(8,128)S(1)}, u32[]{:S(2)}, u32[]{:S(2)}) collective-permute-start(f32[16,128]{1,0:T(8,128)S(1)} %slice.9), channel_id=1, source_target_pairs={{0,16},{4,20},{8,24},{12,28},{16,0},{20,4},{24,8},{28,12},{1,17},{... | collective-permute-start | bytes 24584 | tf_op jit(solution)/shard_map/ppermute | solution.py:52
  136.5 2.1 %shard_map.136 = f32[128,2048]{1,0:T(8,128)} custom-call(s32[5]{0:T(128)S(1)} %stack.23.ids, bf16[144,512]{1,0:T(8,128)(2,1)S(1)} %get-tuple-element.128.a.refs_0_, bf16[144,512]{1,0:T(8,128)(2,1)S(1)} %collective-permute-done.39.b.refs_1_, bf16[144,512]{1,0:T(8,128)(2,1)S(1)} %collective-permute-done.40.c.refs_2_, ...), custom_call_target="tpu_custom_call" | custom-call | tf_op jit(solution)/shard_map/pallas_call | solution.py:73
  (103 shorter events, 47.4 us)
Async XLA Ops:
  2.2 9.9 %collective-permute-start.1 = (bf16[320,128]{1,0:T(8,128)(2,1)S(1)}, bf16[320,128]{1,0:T(8,128)(2,1)S(1)}, u32[]{:S(2)}, u32[]{:S(2)}) collective-permute-start(bf16[320,128]{1,0:T(8,128)(2,1)S(1)} %pad_maximum_fusion), channel_id=1, source_target_pairs={{0,160},{1,164},{2,32},{3,36},{4,224},{5,228},{6,96},{7,100},{8,16... | collective-permute-start | bytes 245768 | tf_op jit(solution)/shard_map/ppermute | solution.py:436
  3.5 8.5 %collective-permute-start = (bf16[320,128]{1,0:T(8,128)(2,1)S(1)}, bf16[320,128]{1,0:T(8,128)(2,1)S(1)}, u32[]{:S(2)}, u32[]{:S(2)}) collective-permute-start(bf16[320,128]{1,0:T(8,128)(2,1)S(1)} %pad_maximum_fusion), channel_id=1, source_target_pairs={{0,32},{1,36},{2,160},{3,164},{4,96},{5,100},{6,224},{7,228},{8,40... | collective-permute-start | bytes 245768 | tf_op jit(solution)/shard_map/ppermute | solution.py:435
  12.1 14.7 %collective-permute-start.8 = (bf16[640,128]{1,0:T(8,128)(2,1)S(1)}, bf16[640,128]{1,0:T(8,128)(2,1)S(1)}, u32[]{:S(2)}, u32[]{:S(2)}) collective-permute-start(bf16[640,128]{1,0:T(8,128)(2,1)S(1)} %maximum_select_fusion.both), channel_id=1, source_target_pairs={{0,24},{4,28},{8,0},{12,4},{16,8},{20,12},{24,16},{28,20},{1,25},{... | collective-permute-start | bytes 491528 | tf_op jit(solution)/shard_map/ppermute | solution.py:52
  18.5 10.8 %collective-permute-start.7 = (bf16[640,128]{1,0:T(8,128)(2,1)S(1)}, bf16[640,128]{1,0:T(8,128)(2,1)S(1)}, u32[]{:S(2)}, u32[]{:S(2)}) collective-permute-start(bf16[640,128]{1,0:T(8,128)(2,1)S(1)} %maximum_select_fusion.both), channel_id=1, source_target_pairs={{0,8},{4,12},{8,16},{12,20},{16,24},{20,28},{24,0},{28,4},{1,9},{5... | collective-permute-start | bytes 491528 | tf_op jit(solution)/shard_map/ppermute | solution.py:52
  22.6 11.4 %collective-permute-start.4 = (bf16[272,512]{1,0:T(8,128)(2,1)S(1)}, bf16[272,512]{1,0:T(8,128)(2,1)S(1)}, u32[]{:S(2)}, u32[]{:S(2)}) collective-permute-start(bf16[272,512]{1,0:T(8,128)(2,1)S(1)} %get-tuple-element.81), channel_id=1, source_target_pairs={{0,32},{32,64},{64,96},{96,0},{1,33},{33,65},{65,97},{97,1},{2,34}... | collective-permute-start | bytes 835592 | tf_op jit(solution)/shard_map/ppermute | solution.py:48
  24.5 13.6 %collective-permute-start.5 = (bf16[272,512]{1,0:T(8,128)(2,1)S(1)}, bf16[272,512]{1,0:T(8,128)(2,1)S(1)}, u32[]{:S(2)}, u32[]{:S(2)}) collective-permute-start(bf16[272,512]{1,0:T(8,128)(2,1)S(1)} %get-tuple-element.82), channel_id=1, source_target_pairs={{0,64},{32,96},{64,0},{96,32},{1,65},{33,97},{65,1},{97,33},{2,66}... | collective-permute-start | bytes 835592 | tf_op jit(solution)/shard_map/ppermute | solution.py:48
  30.0 14.5 %collective-permute-start.9 = (bf16[1280,128]{1,0:T(8,128)(2,1)S(1)}, bf16[1280,128]{1,0:T(8,128)(2,1)S(1)}, u32[]{:S(2)}, u32[]{:S(2)}) collective-permute-start(bf16[1280,128]{1,0:T(8,128)(2,1)S(1)} %get-tuple-element.88), channel_id=1, source_target_pairs={{0,4},{4,8},{8,12},{12,16},{16,20},{20,24},{24,28},{28,0},{1,5},{5... | collective-permute-start | bytes 983048 | tf_op jit(solution)/shard_map/ppermute | solution.py:52
  31.6 12.9 %collective-permute-start.10 = (bf16[1280,128]{1,0:T(8,128)(2,1)S(1)}, bf16[1280,128]{1,0:T(8,128)(2,1)S(1)}, u32[]{:S(2)}, u32[]{:S(2)}) collective-permute-start(bf16[1280,128]{1,0:T(8,128)(2,1)S(1)} %get-tuple-element.89), channel_id=1, source_target_pairs={{0,28},{4,0},{8,4},{12,8},{16,12},{20,16},{24,20},{28,24},{1,29},{... | collective-permute-start | bytes 983048 | tf_op jit(solution)/shard_map/ppermute | solution.py:52
  33.3 8.7 %collective-permute-start.6 = (bf16[272,512]{1,0:T(8,128)(2,1)S(1)}, bf16[272,512]{1,0:T(8,128)(2,1)S(1)}, u32[]{:S(2)}, u32[]{:S(2)}) collective-permute-start(bf16[272,512]{1,0:T(8,128)(2,1)S(1)} %get-tuple-element.83), channel_id=1, source_target_pairs={{0,96},{32,0},{64,32},{96,64},{1,97},{33,1},{65,33},{97,65},{2,98}... | collective-permute-start | bytes 835592 | tf_op jit(solution)/shard_map/ppermute | solution.py:48
  34.0 9.3 %collective-permute-start.11 = (bf16[320,128]{1,0:T(8,128)(2,1)S(1)}, bf16[320,128]{1,0:T(8,128)(2,1)S(1)}, u32[]{:S(2)}, u32[]{:S(2)}) collective-permute-start(bf16[320,128]{1,0:T(8,128)(2,1)S(1)} %get-tuple-element.90), channel_id=1, source_target_pairs={{0,8},{4,12},{8,16},{12,20},{16,24},{20,28},{24,0},{28,4},{1,9},{5... | collective-permute-start | bytes 245768 | tf_op jit(solution)/shard_map/ppermute | solution.py:52
  38.1 6.4 %collective-permute-start.12 = (bf16[320,128]{1,0:T(8,128)(2,1)S(1)}, bf16[320,128]{1,0:T(8,128)(2,1)S(1)}, u32[]{:S(2)}, u32[]{:S(2)}) collective-permute-start(bf16[320,128]{1,0:T(8,128)(2,1)S(1)} %get-tuple-element.91), channel_id=1, source_target_pairs={{0,24},{4,28},{8,0},{12,4},{16,8},{20,12},{24,16},{28,20},{1,25},{... | collective-permute-start | bytes 245768 | tf_op jit(solution)/shard_map/ppermute | solution.py:52
  46.8 6.3 %collective-permute-start.13 = (f32[128,640]{1,0:T(8,128)S(1)}, f32[128,640]{1,0:T(8,128)S(1)}, u32[]{:S(2)}, u32[]{:S(2)}) collective-permute-start(f32[128,640]{1,0:T(8,128)S(1)} %get-tuple-element.96), channel_id=1, source_target_pairs={{0,1},{1,0},{2,3},{3,2},{4,5},{5,4},{6,7},{7,6},{8,9},{9,8},{10,11... | collective-permute-start | bytes 983048 | tf_op jit(solution)/shard_map/ppermute | solution.py:56
  48.9 9.2 %collective-permute-start.15 = (bf16[128,1024]{1,0:T(8,128)(2,1)S(1)}, bf16[128,1024]{1,0:T(8,128)(2,1)S(1)}, u32[]{:S(2)}, u32[]{:S(2)}) collective-permute-start(bf16[128,1024]{1,0:T(8,128)(2,1)S(1)} %shard_map.125), channel_id=1, source_target_pairs={{0,96},{32,0},{64,32},{96,64},{1,97},{33,1},{65,33},{97,65},{2,98}... | collective-permute-start | bytes 786440 | tf_op jit(solution)/shard_map/ppermute | solution.py:48
  49.6 10.8 %collective-permute-start.17 = (bf16[128,1024]{1,0:T(8,128)(2,1)S(1)}, bf16[128,1024]{1,0:T(8,128)(2,1)S(1)}, u32[]{:S(2)}, u32[]{:S(2)}) collective-permute-start(bf16[128,1024]{1,0:T(8,128)(2,1)S(1)} %shard_map.126), channel_id=1, source_target_pairs={{0,64},{32,96},{64,0},{96,32},{1,65},{33,97},{65,1},{97,33},{2,66}... | collective-permute-start | bytes 786440 | tf_op jit(solution)/shard_map/ppermute | solution.py:48
  51.9 13.3 %collective-permute-start.19 = (bf16[128,1024]{1,0:T(8,128)(2,1)S(1)}, bf16[128,1024]{1,0:T(8,128)(2,1)S(1)}, u32[]{:S(2)}, u32[]{:S(2)}) collective-permute-start(bf16[128,1024]{1,0:T(8,128)(2,1)S(1)} %shard_map.127), channel_id=1, source_target_pairs={{0,32},{32,64},{64,96},{96,0},{1,33},{33,65},{65,97},{97,1},{2,34}... | collective-permute-start | bytes 786440 | tf_op jit(solution)/shard_map/ppermute | solution.py:48
  65.8 8.3 %collective-permute-start.20 = (bf16[128,1024]{1,0:T(8,128)(2,1)S(1)}, bf16[128,1024]{1,0:T(8,128)(2,1)S(1)}, u32[]{:S(2)}, u32[]{:S(2)}) collective-permute-start(bf16[128,1024]{1,0:T(8,128)(2,1)S(1)} %shard_map.128.mine), channel_id=1, source_target_pairs={{0,2},{2,0},{1,3},{3,1},{4,6},{6,4},{5,7},{7,5},{8,10},{10,8},{9,1... | collective-permute-start | bytes 786440 | tf_op jit(solution)/shard_map/ppermute | solution.py:56
  77.7 7.8 %collective-permute-start.24 = (bf16[128,768]{1,0:T(8,128)(2,1)S(1)}, bf16[128,768]{1,0:T(8,128)(2,1)S(1)}, u32[]{:S(2)}, u32[]{:S(2)}) collective-permute-start(bf16[128,768]{1,0:T(8,128)(2,1)S(1)} %get-tuple-element.105.refs_0_), channel_id=1, source_target_pairs={{0,96},{32,0},{64,32},{96,64},{1,97},{33,1},{65,33},{97,65},{2,98}... | collective-permute-start | bytes 589832 | tf_op jit(solution)/shard_map/ppermute | solution.py:48
  77.8 9.4 %collective-permute-start.23 = (bf16[128,768]{1,0:T(8,128)(2,1)S(1)}, bf16[128,768]{1,0:T(8,128)(2,1)S(1)}, u32[]{:S(2)}, u32[]{:S(2)}) collective-permute-start(bf16[128,768]{1,0:T(8,128)(2,1)S(1)} %get-tuple-element.105.refs_0_), channel_id=1, source_target_pairs={{0,64},{32,96},{64,0},{96,32},{1,65},{33,97},{65,1},{97,33},{2,66}... | collective-permute-start | bytes 589832 | tf_op jit(solution)/shard_map/ppermute | solution.py:48
  79.2 11.4 %collective-permute-start.22 = (bf16[128,768]{1,0:T(8,128)(2,1)S(1)}, bf16[128,768]{1,0:T(8,128)(2,1)S(1)}, u32[]{:S(2)}, u32[]{:S(2)}) collective-permute-start(bf16[128,768]{1,0:T(8,128)(2,1)S(1)} %get-tuple-element.105.refs_0_), channel_id=1, source_target_pairs={{0,32},{32,64},{64,96},{96,0},{1,33},{33,65},{65,97},{97,1},{2,34}... | collective-permute-start | bytes 589832 | tf_op jit(solution)/shard_map/ppermute | solution.py:48
  80.5 10.1 %collective-permute-start.25 = (bf16[128,768]{1,0:T(8,128)(2,1)S(1)}, bf16[128,768]{1,0:T(8,128)(2,1)S(1)}, u32[]{:S(2)}, u32[]{:S(2)}) collective-permute-start(bf16[128,768]{1,0:T(8,128)(2,1)S(1)} %get-tuple-element.105.refs_0_), channel_id=1, source_target_pairs={{0,1},{1,0},{2,3},{3,2},{4,5},{5,4},{6,7},{7,6},{8,9},{9,8},{10,11... | collective-permute-start | bytes 589832 | tf_op jit(solution)/shard_map/ppermute | solution.py:56
  94.5 11.9 %collective-permute-start.29 = (bf16[1296,128]{1,0:T(8,128)(2,1)S(1)}, bf16[1296,128]{1,0:T(8,128)(2,1)S(1)}, u32[]{:S(2)}, u32[]{:S(2)}) collective-permute-start(bf16[1296,128]{1,0:T(8,128)(2,1)S(1)} %get-tuple-element.111), channel_id=1, source_target_pairs={{0,4},{4,8},{8,12},{12,16},{16,20},{20,24},{24,28},{28,0},{1,5},{5... | collective-permute-start | bytes 995336 | tf_op jit(solution)/shard_map/ppermute | solution.py:52
  95.9 14.5 %collective-permute-start.31 = (bf16[1296,128]{1,0:T(8,128)(2,1)S(1)}, bf16[1296,128]{1,0:T(8,128)(2,1)S(1)}, u32[]{:S(2)}, u32[]{:S(2)}) collective-permute-start(bf16[1296,128]{1,0:T(8,128)(2,1)S(1)} %get-tuple-element.114), channel_id=1, source_target_pairs={{0,28},{4,0},{8,4},{12,8},{16,12},{20,16},{24,20},{28,24},{1,29},{... | collective-permute-start | bytes 995336 | tf_op jit(solution)/shard_map/ppermute | solution.py:52
  97.8 11.7 %collective-permute-start.32 = (bf16[336,128]{1,0:T(8,128)(2,1)S(1)}, bf16[336,128]{1,0:T(8,128)(2,1)S(1)}, u32[]{:S(2)}, u32[]{:S(2)}) collective-permute-start(bf16[336,128]{1,0:T(8,128)(2,1)S(1)} %get-tuple-element.117), channel_id=1, source_target_pairs={{0,8},{4,12},{8,16},{12,20},{16,24},{20,28},{24,0},{28,4},{1,9},{5... | collective-permute-start | bytes 258056 | tf_op jit(solution)/shard_map/ppermute | solution.py:52
  98.9 11.5 %collective-permute-start.33 = (bf16[336,128]{1,0:T(8,128)(2,1)S(1)}, bf16[336,128]{1,0:T(8,128)(2,1)S(1)}, u32[]{:S(2)}, u32[]{:S(2)}) collective-permute-start(bf16[336,128]{1,0:T(8,128)(2,1)S(1)} %get-tuple-element.118), channel_id=1, source_target_pairs={{0,24},{4,28},{8,0},{12,4},{16,8},{20,12},{24,16},{28,20},{1,25},{... | collective-permute-start | bytes 258056 | tf_op jit(solution)/shard_map/ppermute | solution.py:52
  111.1 10.3 %collective-permute-start.34 = (bf16[640,128]{1,0:T(8,128)(2,1)S(1)}, bf16[640,128]{1,0:T(8,128)(2,1)S(1)}, u32[]{:S(2)}, u32[]{:S(2)}) collective-permute-start(bf16[640,128]{1,0:T(8,128)(2,1)S(1)} %get-tuple-element.124), channel_id=1, source_target_pairs={{0,8},{4,12},{8,16},{12,20},{16,24},{20,28},{24,0},{28,4},{1,9},{5... | collective-permute-start | bytes 491528 | tf_op jit(solution)/shard_map/ppermute | solution.py:52
  114.1 8.3 %collective-permute-start.35 = (bf16[640,128]{1,0:T(8,128)(2,1)S(1)}, bf16[640,128]{1,0:T(8,128)(2,1)S(1)}, u32[]{:S(2)}, u32[]{:S(2)}) collective-permute-start(bf16[640,128]{1,0:T(8,128)(2,1)S(1)} %get-tuple-element.125), channel_id=1, source_target_pairs={{0,24},{4,28},{8,0},{12,4},{16,8},{20,12},{24,16},{28,20},{1,25},{... | collective-permute-start | bytes 491528 | tf_op jit(solution)/shard_map/ppermute | solution.py:52
  115.3 11.3 %collective-permute-start.39 = (bf16[144,512]{1,0:T(8,128)(2,1)S(1)}, bf16[144,512]{1,0:T(8,128)(2,1)S(1)}, u32[]{:S(2)}, u32[]{:S(2)}) collective-permute-start(bf16[144,512]{1,0:T(8,128)(2,1)S(1)} %get-tuple-element.129), channel_id=1, source_target_pairs={{0,96},{32,0},{64,32},{96,64},{1,97},{33,1},{65,33},{97,65},{2,98}... | collective-permute-start | bytes 442376 | tf_op jit(solution)/shard_map/ppermute | solution.py:48
  116.7 9.9 %collective-permute-start.40 = (bf16[144,512]{1,0:T(8,128)(2,1)S(1)}, bf16[144,512]{1,0:T(8,128)(2,1)S(1)}, u32[]{:S(2)}, u32[]{:S(2)}) collective-permute-start(bf16[144,512]{1,0:T(8,128)(2,1)S(1)} %get-tuple-element.130), channel_id=1, source_target_pairs={{0,64},{32,96},{64,0},{96,32},{1,65},{33,97},{65,1},{97,33},{2,66}... | collective-permute-start | bytes 442376 | tf_op jit(solution)/shard_map/ppermute | solution.py:48
  117.3 9.3 %collective-permute-start.41 = (bf16[144,512]{1,0:T(8,128)(2,1)S(1)}, bf16[144,512]{1,0:T(8,128)(2,1)S(1)}, u32[]{:S(2)}, u32[]{:S(2)}) collective-permute-start(bf16[144,512]{1,0:T(8,128)(2,1)S(1)} %get-tuple-element.131), channel_id=1, source_target_pairs={{0,32},{32,64},{64,96},{96,0},{1,33},{33,65},{65,97},{97,1},{2,34}... | collective-permute-start | bytes 442376 | tf_op jit(solution)/shard_map/ppermute | solution.py:48
  123.9 6.2 %collective-permute-start.37 = (bf16[320,128]{1,0:T(8,128)(2,1)S(1)}, bf16[320,128]{1,0:T(8,128)(2,1)S(1)}, u32[]{:S(2)}, u32[]{:S(2)}) collective-permute-start(bf16[320,128]{1,0:T(8,128)(2,1)S(1)} %get-tuple-element.127), channel_id=1, source_target_pairs={{160,0},{164,1},{32,2},{36,3},{224,4},{228,5},{96,6},{100,7},{168,... | collective-permute-start | bytes 245768 | tf_op jit(solution)/shard_map/ppermute | solution.py:536
  130.7 9.4 %collective-permute-start.38 = (bf16[64,128]{1,0:T(8,128)(2,1)S(1)}, bf16[64,128]{1,0:T(8,128)(2,1)S(1)}, u32[]{:S(2)}, u32[]{:S(2)}) collective-permute-start(bf16[64,128]{1,0:T(8,128)(2,1)S(1)} %shard_map.135.own), channel_id=1, source_target_pairs={{0,2},{2,0},{1,3},{3,1},{4,6},{6,4},{5,7},{7,5},{8,10},{10,8},{9,1... | collective-permute-start | bytes 49160 | tf_op jit(solution)/shard_map/ppermute | solution.py:56
  132.9 7.7 %collective-permute-start.45 = (f32[16,128]{1,0:T(8,128)S(1)}, f32[16,128]{1,0:T(8,128)S(1)}, u32[]{:S(2)}, u32[]{:S(2)}) collective-permute-start(f32[16,128]{1,0:T(8,128)S(1)} %slice.9), channel_id=1, source_target_pairs={{0,16},{4,20},{8,24},{12,28},{16,0},{20,4},{24,8},{28,12},{1,17},{... | collective-permute-start | bytes 24584 | tf_op jit(solution)/shard_map/ppermute | solution.py:52
  (19 other events, 71.7 us)
